TPU v7x, 32 devices: a whole 2x2x4 slice. The times are simulated.
32 devices in a mesh: dp: 8 (over z, core), seq: 4 (over y, x).
Axes of the slice: x: 2, y: 2, z: 4, core: 2. Of those that a mesh axis runs over, the one named last changes fastest.
Arguments:
- q_pre: bfloat16 [8, 512, 16, 128], P('dp', 'seq'), may hold values from -6 to 6
- k_pre: bfloat16 [8, 512, 8, 128], P('dp', 'seq'), may hold values from -6 to 6
- values: bfloat16 [8, 512, 8, 128], P('dp', 'seq'), may hold values from -6 to 6
- grad_out: bfloat16 [8, 512, 16, 128], P('dp', 'seq'), may hold values from -6 to 6
- segment_ids: int32 [8, 512], P('dp', 'seq'), may hold values from 0 to 7, never falling along the last dimension, each value on 1 to 256 neighbouring positions
- q_gain: float32 [128], replicated, may hold values from 0.1 to 1.9
- k_gain: float32 [128], replicated, may hold values from 0.1 to 1.9
Outputs:
- grad_q: bfloat16 [8, 512, 16, 128], P('dp', 'seq')
- grad_k: bfloat16 [8, 512, 8, 128], P('dp', 'seq')
- grad_v: bfloat16 [8, 512, 8, 128], P('dp', 'seq')
- grad_q_gain: float32 [128], replicated
- grad_k_gain: float32 [128], replicated
Inputs may be any that keep to these rules, and one draw needn't show every extreme that they name: `segment_ids`: along a span the ids never fall, and each id from 0 to 7 names one run of consecutive tokens.
All inputs are finite; a program needn't handle non-finite values.
Results may differ from a plain program's by a relative error of at most 0.017.
Values may be sent and summed in bfloat16 or wider, within the bound.
No kernel may reach another device: no remote copies, remote signals or barrier semaphores. Data moves between devices by JAX's collectives and lax.ppermute only.
A program may use at most 64 MiB of HBM per device.

v0:
```python
import jax
import jax.numpy as jnp
from jax import lax
from jax.sharding import PartitionSpec as P

PRESCALE = 168
DOCS = 8


norm_epsilon = 1e-06
rope_base = 1000000.0
rope_factor = 8.0


def document_positions(segments, docs):
    labels = jnp.arange(docs, dtype=jnp.int32)
    member = (segments[:, None] == labels[None, :]).astype(jnp.int32)
    counts = jnp.sum(member, axis=0)
    starts = jnp.cumsum(counts) - counts
    first = jnp.sum(member * starts[None, :], axis=1)
    return (jnp.arange(segments.shape[0], dtype=jnp.int32) - first, first)


def embed(rows, gain, positions):
    width = rows.shape[-1]
    half = width // 2
    scale = lax.rsqrt(jnp.mean(rows * rows, axis=-1, keepdims=True) + norm_epsilon)
    normed = rows * scale * gain
    freqs = rope_base ** (-(jnp.arange(half, dtype=jnp.float32) * 2.0 / width))
    angles = (positions.astype(jnp.float32) / rope_factor)[:, None] * freqs[None, :]
    cosine = jnp.cos(angles)[:, None, :]
    sine = jnp.sin(angles)[:, None, :]
    first_half = normed[..., :half]
    second_half = normed[..., half:]
    return jnp.concatenate(
        [first_half * cosine - second_half * sine, second_half * cosine + first_half * sine],
        axis=-1,
    )


def attend_blocks(queries, keys, vals, upstream, segments):
    total = queries.shape[0]
    group = queries.shape[1]
    width = queries.shape[2]
    block = min(512, total)
    count = total // block
    rows = block * group
    score_scale = float(PRESCALE) ** (-0.5)
    contract_last = (((1,), (1,)), ((), ()))
    contract_first = (((0,), (0,)), ((), ()))

    def query_block(query_index, carry):
        query_grads, key_grads, value_grads = carry
        start = query_index * block
        query_rows = lax.dynamic_slice_in_dim(queries, start, block, 0).reshape(rows, width)
        upstream_rows = lax.dynamic_slice_in_dim(upstream, start, block, 0).reshape(rows, width)
        query_segs = jnp.repeat(lax.dynamic_slice_in_dim(segments, start, block, 0), group)
        query_places = jnp.repeat(start + jnp.arange(block, dtype=jnp.int32), group)
        lower = 0

        def key_scores(key_index):
            key_start = key_index * block
            key_rows = lax.dynamic_slice_in_dim(keys, key_start, block, 0)
            value_rows = lax.dynamic_slice_in_dim(vals, key_start, block, 0)
            key_segs = lax.dynamic_slice_in_dim(segments, key_start, block, 0)
            key_places = key_start + jnp.arange(block, dtype=jnp.int32)
            scores = score_scale * lax.dot_general(
                query_rows, key_rows, contract_last, preferred_element_type=jnp.float32
            )
            visible = (query_segs[:, None] == key_segs[None, :]) & (
                query_places[:, None] >= key_places[None, :]
            )
            return (scores, visible, key_rows, value_rows, key_start)

        def forward_step(key_index, state):
            totals, numer = state
            scores, visible, key_rows, value_rows, key_start = key_scores(key_index)
            raw = jnp.where(visible, jnp.exp(scores), 0.0)
            numer = numer + jnp.dot(
                raw.astype(jnp.bfloat16), value_rows, preferred_element_type=jnp.float32
            )
            return (totals + jnp.sum(raw, axis=1), numer)

        totals, numer = lax.fori_loop(
            lower,
            query_index + 1,
            forward_step,
            (jnp.zeros((rows,), jnp.float32), jnp.zeros((rows, width), jnp.float32)),
        )
        outputs = numer / totals[:, None]
        delta = jnp.sum(upstream_rows.astype(jnp.float32) * outputs, axis=1)
        logsum = jnp.log(totals)

        def backward_step(key_index, state):
            query_part, key_acc, value_acc = state
            scores, visible, key_rows, value_rows, key_start = key_scores(key_index)
            probs = jnp.where(visible, jnp.exp(scores - logsum[:, None]), 0.0).astype(jnp.bfloat16)
            prob_grads = lax.dot_general(
                upstream_rows, value_rows, contract_last, preferred_element_type=jnp.float32
            )
            score_grads = (
                probs.astype(jnp.float32) * (prob_grads - delta[:, None]) * score_scale
            ).astype(jnp.bfloat16)
            query_part = query_part + jnp.dot(
                score_grads, key_rows, preferred_element_type=jnp.float32
            )
            key_part = lax.dot_general(
                score_grads, query_rows, contract_first, preferred_element_type=jnp.float32
            )
            value_part = lax.dot_general(
                probs, upstream_rows, contract_first, preferred_element_type=jnp.float32
            )
            key_acc = lax.dynamic_update_slice_in_dim(
                key_acc,
                lax.dynamic_slice_in_dim(key_acc, key_start, block, 0) + key_part,
                key_start,
                0,
            )
            value_acc = lax.dynamic_update_slice_in_dim(
                value_acc,
                lax.dynamic_slice_in_dim(value_acc, key_start, block, 0) + value_part,
                key_start,
                0,
            )
            return (query_part, key_acc, value_acc)

        query_part, key_grads, value_grads = lax.fori_loop(
            lower,
            query_index + 1,
            backward_step,
            (jnp.zeros((rows, width), jnp.float32), key_grads, value_grads),
        )
        query_grads = lax.dynamic_update_slice_in_dim(query_grads, query_part, start * group, 0)
        return (query_grads, key_grads, value_grads)

    initial = (
        jnp.zeros((total * group, width), jnp.float32),
        jnp.zeros((total, width), jnp.float32),
        jnp.zeros((total, width), jnp.float32),
    )
    query_grads, key_grads, value_grads = lax.fori_loop(0, count, query_block, initial)
    return (query_grads.reshape(total, group, width), key_grads, value_grads)


def body(q_pre, k_pre, values, grad_out, segment_ids, q_gain, k_gain):
    segments = lax.all_gather(segment_ids, "seq", axis=1, tiled=True)[0]
    positions, first = document_positions(segments, DOCS)
    local = q_pre.shape[1]
    heads = q_pre.shape[2]
    kv_heads = k_pre.shape[2]
    width = q_pre.shape[3]
    group = heads // kv_heads

    def embed_rows(rows, gain):
        return embed(rows, gain, positions)

    key_copies = jnp.repeat(k_pre[0], group, axis=1)
    value_copies = jnp.repeat(values[0], group, axis=1)
    query_here, upstream_here, key_here, value_here = (
        lax.all_to_all(q_pre[0], "seq", split_axis=1, concat_axis=0, tiled=True),
        lax.all_to_all(grad_out[0], "seq", split_axis=1, concat_axis=0, tiled=True),
        lax.all_to_all(key_copies, "seq", split_axis=1, concat_axis=0, tiled=True),
        lax.all_to_all(value_copies, "seq", split_axis=1, concat_axis=0, tiled=True),
    )
    query_rot, query_back = jax.vjp(embed_rows, query_here.astype(jnp.float32), q_gain)
    key_rot, key_back = jax.vjp(embed_rows, key_here.astype(jnp.float32), k_gain)
    query_hat = query_rot.astype(jnp.bfloat16)
    key_hat = key_rot.astype(jnp.bfloat16)
    query_list, key_list, value_list = ([], [], [])
    for head in range(query_here.shape[1]):
        query_part, key_part, value_part = attend_blocks(
            query_hat[:, head : head + 1],
            key_hat[:, head],
            value_here[:, head],
            upstream_here[:, head : head + 1],
            segments,
        )
        query_list.append(query_part)
        key_list.append(key_part)
        value_list.append(value_part)
    query_input, query_gain_part = query_back(jnp.concatenate(query_list, axis=1))
    key_input, key_gain_part = key_back(jnp.stack(key_list, axis=1))
    value_input = jnp.stack(value_list, axis=1)
    query_return, key_return, value_return = (
        lax.all_to_all(
            query_input.astype(jnp.bfloat16), "seq", split_axis=0, concat_axis=1, tiled=True
        ).astype(query_input.dtype),
        lax.all_to_all(
            key_input.astype(jnp.bfloat16), "seq", split_axis=0, concat_axis=1, tiled=True
        ).astype(key_input.dtype),
        lax.all_to_all(
            value_input.astype(jnp.bfloat16), "seq", split_axis=0, concat_axis=1, tiled=True
        ).astype(value_input.dtype),
    )
    grad_q = query_return.astype(jnp.bfloat16)
    grad_k = jnp.sum(key_return.reshape(local, kv_heads, group, width), axis=2).astype(jnp.bfloat16)
    grad_v = jnp.sum(value_return.reshape(local, kv_heads, group, width), axis=2).astype(
        jnp.bfloat16
    )
    gain_totals = lax.psum((query_gain_part, key_gain_part), ("dp", "seq"))
    return (grad_q[None], grad_k[None], grad_v[None], gain_totals[0], gain_totals[1])


def solution(mesh):
    return jax.shard_map(
        body,
        mesh=mesh,
        in_specs=(
            P("dp", "seq", None, None),
            P("dp", "seq", None, None),
            P("dp", "seq", None, None),
            P("dp", "seq", None, None),
            P("dp", "seq"),
            P(),
            P(),
        ),
        out_specs=(
            P("dp", "seq", None, None),
            P("dp", "seq", None, None),
            P("dp", "seq", None, None),
            P(),
            P(),
        ),
        check_vma=False,
    )
```

profile of v0, /device:TPU:0, one launch (start us, length us, event | category | flops | bytes accessed | tf_op | source)
XLA Modules:
  0.0 144.0 jit_solution(3450268209742466574)
XLA Ops:
  0.6 1.0 copy.147
  1.6 0.9 broadcast_in_dim.75
  2.5 5.3 %all-to-all-start.1 = ((bf16[128,16,128]{2,0,1:T(8,128)(2,1)}), bf16[128,16,128]{2,0,1:T(8,128)(2,1)S(1)}, u32[]{:S(2)}, u32[]{:S(2)}) async-start(bf16[128,16,128]{2,0,1:T(8,128)(2,1)} %bitcast.11), calls=%async_computation.1 | async-start | bytes 1048576 | tf_op jit(solution)/shard_map/all_to_all | solution.py:162
  7.9 0.6 copy-done.24
  8.5 9.1 %all_gather.3 = s32[1,512]{1,0:T(1,128)S(1)} all-gather(s32[1,128]{1,0:T(1,128)S(1)} %copy-done.24), channel_id=1, replica_groups=mesh['dp'=8,'seq'=4] {'seq'}, dimensions={1}, use_global_device_ids=true | all-gather | bytes 2560 | tf_op jit(solution)/shard_map/all_gather | solution.py:146
  17.9 0.9 broadcast_in_dim.84
  18.8 4.2 %all-to-all-start.3 = ((bf16[128,16,128]{2,0,1:T(8,128)(2,1)}), bf16[128,16,128]{2,0,1:T(8,128)(2,1)S(1)}, u32[]{:S(2)}, u32[]{:S(2)}) async-start(bf16[128,16,128]{2,0,1:T(8,128)(2,1)} %bitcast.23), calls=%async_computation.3 | async-start | bytes 1048576 | tf_op jit(solution)/shard_map/all_to_all | solution.py:163
  22.9 0.9 copy.175
  24.0 5.5 %all-to-all-done.3 = bf16[128,16,128]{2,0,1:T(8,128)(2,1)S(1)} async-done(((bf16[128,16,128]{2,0,1:T(8,128)(2,1)}), bf16[128,16,128]{2,0,1:T(8,128)(2,1)S(1)}, u32[]{:S(2)}, u32[]{:S(2)}) %all-to-all-start.3) | async-done | bytes 524320 | tf_op jit(solution)/shard_map/all_to_all | solution.py:163
  29.5 3.6 %all-to-all-start = ((bf16[128,16,128]{2,0,1:T(8,128)(2,1)}), bf16[128,16,128]{2,0,1:T(8,128)(2,1)S(1)}, u32[]{:S(2)}, u32[]{:S(2)}) async-start(bf16[128,16,128]{2,0,1:T(8,128)(2,1)} %bitcast.163), calls=%async_computation | async-start | bytes 1048576 | tf_op jit(solution)/shard_map/all_to_all | solution.py:160
  33.1 0.5 multiply_cosine_fusion
  33.7 0.9 copy.174
  35.0 0.6 copy-done.16
  35.6 0.8 copy.152
  36.5 0.4 copy.148
  36.9 0.4 reshape.337
  37.4 2.3 %all-to-all-done = bf16[128,16,128]{2,0,1:T(8,128)(2,1)S(1)} async-done(((bf16[128,16,128]{2,0,1:T(8,128)(2,1)}), bf16[128,16,128]{2,0,1:T(8,128)(2,1)S(1)}, u32[]{:S(2)}, u32[]{:S(2)}) %all-to-all-start) | async-done | bytes 524320 | tf_op jit(solution)/shard_map/all_to_all | solution.py:160
  39.7 4.3 %all-to-all-start.2 = ((bf16[128,16,128]{2,0,1:T(8,128)(2,1)}), bf16[128,16,128]{2,0,1:T(8,128)(2,1)}, u32[]{:S(2)}, u32[]{:S(2)}) async-start(bf16[128,16,128]{2,0,1:T(8,128)(2,1)} %bitcast.162), calls=%async_computation.2 | async-start | bytes 1048576 | tf_op jit(solution)/shard_map/all_to_all | solution.py:161
  44.4 0.6 copy-done.14
  45.3 0.4 reshape.334
  46.1 0.5 copy-done.20
  46.8 0.4 subtract_convert_fusion.1
  47.2 1.4 convolution_multiply_fusion.2
  48.5 1.3 convolution_multiply_fusion.1
  49.9 0.6 all-to-all-done.2
  50.5 2.1 %copy.150 = bf16[128,4,4,128]{0,1,3,2:T(4,128)(2,1)} copy(bf16[128,4,4,128]{3,0,2,1:T(8,128)(2,1)} %bitcast.19) | data formatting | bytes 1048576 | tf_op jit(solution)/shard_map/all_to_all | solution.py:161
  52.6 2.0 %all_to_all.70 = bf16[512,4,128]{0,2,1:T(8,128)(2,1)} reshape(bf16[4,128,4,128]{1,0,3,2:T(4,128)(2,1)} %bitcast.170) | data formatting | bytes 1048576 | tf_op jit(solution)/shard_map/all_to_all | solution.py:161
  55.0 0.9 copy-done.2
  55.9 2.0 %fusion.28 = (f32[512]{0:T(512)S(1)}, f32[512]{0:T(512)S(1)}, f32[512]{0:T(512)S(1)}, f32[512]{0:T(512)S(1)}, f32[512,512]{0,1:T(8,128)S(1)}) fusion(s32[512]{0:T(512)S(1)} %bitcast.193, f32[512,512]{0,1:T(8,128)S(1)} %copy-done.2, f32[512,512]{0,1:T(8,128)} %convolution_multiply_fusion.1, f32[512,512]{0,1:T(8,128)S(1)} %convolution_multiply_fusion, ...), kind=kOutput, calls=%fused_computation.75 | convolution fusion | flops 70776832 | bytes 5255168 | tf_op jit(solution)/shard_map/while/body/eval_jaxpr/while/body/dot_general | solution.py:67
  57.9 0.4 fusion.18
  58.3 0.8 copy-done.3
  59.1 0.4 fusion.17
  59.5 0.4 fusion.16
  60.2 0.4 fusion.8
  60.6 1.0 convolution_bitcast_fusion.4
  61.6 0.9 convolution_bitcast_fusion
  62.6 0.4 fusion.19
  63.3 0.4 fusion.11
  63.7 1.0 convolution_bitcast_fusion.7
  65.0 0.4 fusion.22
  65.4 0.4 fusion.9
  65.8 1.0 convolution_bitcast_fusion.5
  66.8 0.9 convolution_bitcast_fusion.1
  68.1 0.4 fusion.10
  68.5 1.0 convolution_bitcast_fusion.6
  69.5 0.9 convolution_bitcast_fusion.2
  70.5 1.2 copy.162
  71.7 4.3 %all-to-all-start.6 = ((bf16[512,4,128]{2,1,0:T(4,128)(2,1)}), bf16[512,4,128]{2,1,0:T(4,128)(2,1)}, u32[]{:S(2)}, u32[]{:S(2)}) async-start(bf16[512,4,128]{2,1,0:T(4,128)(2,1)} %copy.162), calls=%async_computation.6 | async-start | bytes 1048576 | tf_op jit(solution)/shard_map/all_to_all | solution.py:191
  76.0 1.2 pad_maximum_fusion
  77.4 0.8 copy-done.1
  78.6 0.6 copy-done.21
  79.5 0.4 copy-done.17
  79.9 1.1 fusion.25
  81.0 2.1 %copy.159 = bf16[512,4,128]{2,1,0:T(4,128)(2,1)} copy(bf16[512,4,128]{0,2,1:T(8,128)(2,1)} %fusion.25) | data formatting | bytes 1048576 | tf_op jit(solution)/shard_map/convert_element_type | solution.py:189
  83.2 0.7 copy-done.23
  84.1 4.1 %all-to-all-start.5 = ((bf16[512,4,128]{2,1,0:T(4,128)(2,1)}), bf16[512,4,128]{2,1,0:T(4,128)(2,1)S(1)}, u32[]{:S(2)}, u32[]{:S(2)}) async-start(bf16[512,4,128]{2,1,0:T(4,128)(2,1)} %copy.159), calls=%async_computation.5 | async-start | bytes 1048576 | tf_op jit(solution)/shard_map/all_to_all | solution.py:188
  88.5 1.1 copy.157
  89.6 5.5 %all-to-all-done.5 = bf16[512,4,128]{2,1,0:T(4,128)(2,1)S(1)} async-done(((bf16[512,4,128]{2,1,0:T(4,128)(2,1)}), bf16[512,4,128]{2,1,0:T(4,128)(2,1)S(1)}, u32[]{:S(2)}, u32[]{:S(2)}) %all-to-all-start.5) | async-done | bytes 524320 | tf_op jit(solution)/shard_map/all_to_all | solution.py:188
  95.1 3.5 %all-to-all-start.4 = ((bf16[512,4,128]{2,1,0:T(4,128)(2,1)}), bf16[512,4,128]{2,1,0:T(4,128)(2,1)S(1)}, u32[]{:S(2)}, u32[]{:S(2)}) async-start(bf16[512,4,128]{2,1,0:T(4,128)(2,1)} %copy.157), calls=%async_computation.4 | async-start | bytes 1048576 | tf_op jit(solution)/shard_map/all_to_all | solution.py:185
  98.6 41.1 %all-reduce.4 = (f32[128]{0:T(128)}, f32[128]{0:T(128)}) all-reduce(f32[128]{0:T(128)S(1)} %get-tuple-element.824, f32[128]{0:T(128)S(1)} %get-tuple-element.822), channel_id=1, replica_groups=mesh['dp'=8,'seq'=4] {'dp','seq'}, use_global_device_ids=true, to_apply=%region_18.19 | all-reduce | flops 256 | bytes 2048 | tf_op jit(solution)/shard_map/psum | solution.py:200
  139.7 1.1 copy.163
  141.0 0.9 copy.166
  142.1 0.9 copy.165
  143.0 1.0 copy.158
  (83 shorter events, 5.7 us)
Async XLA Ops:
  2.5 5.3 %copy-start.13 = (bf16[1,128,8,128]{3,2,1,0:T(8,128)(2,1)S(1)}, bf16[1,128,8,128]{3,2,1,0:T(8,128)(2,1)}, u32[]{:S(2)}) copy-start(bf16[1,128,8,128]{3,2,1,0:T(8,128)(2,1)} %param.9) | copy-start | bytes 786436
  2.5 15.4 %all-to-all-start.1 = ((bf16[128,16,128]{2,0,1:T(8,128)(2,1)}), bf16[128,16,128]{2,0,1:T(8,128)(2,1)S(1)}, u32[]{:S(2)}, u32[]{:S(2)}) async-start(bf16[128,16,128]{2,0,1:T(8,128)(2,1)} %bitcast.11), calls=%async_computation.1 | async-start | bytes 1048576 | tf_op jit(solution)/shard_map/all_to_all | solution.py:162
  7.8 0.7 copy-start.24
  17.6 6.3 %copy-start.18 = (s32[1,512]{1,0:T(1,128)}, s32[1,512]{1,0:T(1,128)S(1)}, u32[]{:S(2)}) copy-start(s32[1,512]{1,0:T(1,128)S(1)} %all_gather.3) | copy-start | bytes 6148
  18.8 4.2 %copy-start.9 = (bf16[1,128,16,128]{3,2,1,0:T(8,128)(2,1)S(1)}, bf16[1,128,16,128]{3,2,1,0:T(8,128)(2,1)}, u32[]{:S(2)}) copy-start(bf16[1,128,16,128]{3,2,1,0:T(8,128)(2,1)} %param.7) | copy-start | bytes 1572868
  18.8 10.7 %all-to-all-start.3 = ((bf16[128,16,128]{2,0,1:T(8,128)(2,1)}), bf16[128,16,128]{2,0,1:T(8,128)(2,1)S(1)}, u32[]{:S(2)}, u32[]{:S(2)}) async-start(bf16[128,16,128]{2,0,1:T(8,128)(2,1)} %bitcast.23), calls=%async_computation.3 | async-start | bytes 1048576 | tf_op jit(solution)/shard_map/all_to_all | solution.py:163
  29.5 4.2 %copy-start.10 = (bf16[1,128,16,128]{3,2,1,0:T(8,128)(2,1)S(1)}, bf16[1,128,16,128]{3,2,1,0:T(8,128)(2,1)}, u32[]{:S(2)}) copy-start(bf16[1,128,16,128]{3,2,1,0:T(8,128)(2,1)} %param.10) | copy-start | bytes 1572868
  29.5 10.2 %all-to-all-start = ((bf16[128,16,128]{2,0,1:T(8,128)(2,1)}), bf16[128,16,128]{2,0,1:T(8,128)(2,1)S(1)}, u32[]{:S(2)}, u32[]{:S(2)}) async-start(bf16[128,16,128]{2,0,1:T(8,128)(2,1)} %bitcast.163), calls=%async_computation | async-start | bytes 1048576 | tf_op jit(solution)/shard_map/all_to_all | solution.py:160
  33.7 13.1 %copy-start = (f32[512,64]{0,1:T(8,128)}, f32[512,64]{0,1:T(8,128)S(1)}, u32[]{:S(2)}) copy-start(f32[512,64]{0,1:T(8,128)S(1)} %get-tuple-element.845) | copy-start | bytes 393220
  35.0 0.6 copy-start.16
  39.7 10.8 %all-to-all-start.2 = ((bf16[128,16,128]{2,0,1:T(8,128)(2,1)}), bf16[128,16,128]{2,0,1:T(8,128)(2,1)}, u32[]{:S(2)}, u32[]{:S(2)}) async-start(bf16[128,16,128]{2,0,1:T(8,128)(2,1)} %bitcast.162), calls=%async_computation.2 | async-start | bytes 1048576 | tf_op jit(solution)/shard_map/all_to_all | solution.py:161
  44.4 0.6 copy-start.14
  45.2 0.7 copy-start.22
  45.9 0.7 copy-start.20
  54.6 1.2 copy-start.2
  54.6 1.2 copy-start.19
  55.9 2.0 %copy-start.11 = (bf16[4,128,4,128]{3,1,0,2:T(8,128)(2,1)S(1)}, bf16[4,128,4,128]{3,1,0,2:T(8,128)(2,1)}, u32[]{:S(2)}) copy-start(bf16[4,128,4,128]{3,1,0,2:T(8,128)(2,1)} %copy.152) | copy-start | bytes 1572868
  55.9 2.0 %copy-start.12 = (bf16[512,4,128]{0,2,1:T(8,128)(2,1)S(1)}, bf16[512,4,128]{0,2,1:T(8,128)(2,1)}, u32[]{:S(2)}) copy-start(bf16[512,4,128]{0,2,1:T(8,128)(2,1)} %all_to_all.70) | copy-start | bytes 1572868
  57.9 1.2 copy-start.3
  71.7 4.3 %copy-start.5 = (f32[512,1,128]{0,2,1:T(8,128)S(1)}, f32[512,1,128]{0,2,1:T(8,128)}, u32[]{:S(2)}) copy-start(f32[512,1,128]{0,2,1:T(8,128)} %convolution_bitcast_fusion) | copy-start | bytes 786436
  71.7 12.3 %all-to-all-start.6 = ((bf16[512,4,128]{2,1,0:T(4,128)(2,1)}), bf16[512,4,128]{2,1,0:T(4,128)(2,1)}, u32[]{:S(2)}, u32[]{:S(2)}) async-start(bf16[512,4,128]{2,1,0:T(4,128)(2,1)} %copy.162), calls=%async_computation.6 | async-start | bytes 1048576 | tf_op jit(solution)/shard_map/all_to_all | solution.py:191
  76.0 1.3 copy-start.4
  76.0 1.3 copy-start.6
  76.0 1.3 copy-start.7
  76.0 1.3 copy-start.8
  77.3 0.9 copy-start.1
  78.5 0.7 copy-start.21
  79.2 0.7 copy-start.17
  83.2 0.7 copy-start.23
  84.1 4.2 %copy-start.15 = (f32[128,16]{0,1:T(8,128)S(1)}, f32[128,16]{0,1:T(8,128)}, u32[]{:S(2)}) copy-start(f32[128,16]{0,1:T(8,128)} %copy-done.14) | copy-start | bytes 24580
  84.1 11.1 %all-to-all-start.5 = ((bf16[512,4,128]{2,1,0:T(4,128)(2,1)}), bf16[512,4,128]{2,1,0:T(4,128)(2,1)S(1)}, u32[]{:S(2)}, u32[]{:S(2)}) async-start(bf16[512,4,128]{2,1,0:T(4,128)(2,1)} %copy.159), calls=%async_computation.5 | async-start | bytes 1048576 | tf_op jit(solution)/shard_map/all_to_all | solution.py:188
  95.1 47.9 %all-to-all-start.4 = ((bf16[512,4,128]{2,1,0:T(4,128)(2,1)}), bf16[512,4,128]{2,1,0:T(4,128)(2,1)S(1)}, u32[]{:S(2)}, u32[]{:S(2)}) async-start(bf16[512,4,128]{2,1,0:T(4,128)(2,1)} %copy.157), calls=%async_computation.4 | async-start | bytes 1048576 | tf_op jit(solution)/shard_map/all_to_all | solution.py:185
where the time goes:
time: 145 us; the launch traced here: 144 us
  blocking collectives  50.2 us (35%)
  starting transfers between devices  29.2 us (20%)
  local copies, waits for them, and re-layouts  26.5 us (18%)
  matrix products  16.6 us (11%)
  waiting for transfers between devices  14 us (10%)
  other arithmetic  6.38 us (4%)
    psum x1, blocking collectives, body(): gain_totals = lax.psum((query_gain_part, key_gain_part), ('dp', 'seq'))  41.1 us
    unnamed x54, local copies, waits for them, and re-layouts  10.5 us
    all_gather x1, blocking collectives, body(): segments = lax.all_gather(segment_ids, 'seq', axis=1, tiled=True)[0]  9.09 us
    all_to_all x1, waiting for transfers between devices, body(): lax.all_to_all(key_input.astype(jnp.bfloat16), 'seq', split_axis=0, conca...  5.54 us
    all_to_all x1, waiting for transfers between devices, body(): lax.all_to_all(value_copies, 'seq', split_axis=1, concat_axis=0, tiled=True)  5.53 us
    all_to_all x1, starting transfers between devices, body(): lax.all_to_all(key_copies, 'seq', split_axis=1, concat_axis=0, tiled=True)  5.29 us
    dot_general x4, matrix products, key_scores(): lax.dot_general(query_rows, key_rows, contract_last, preferred_element_ty...  5.02 us
    all_to_all x1, starting transfers between devices, body(): lax.all_to_all(grad_out[0], 'seq', split_axis=1, concat_axis=0, tiled=True)  4.32 us
  transfers between devices with their start and end apart: 7, of which 4 were waited for; matrix products, arithmetic and copies ran while one was open for 14% of the time, Pallas kernels for 0%

commit v1 on v0

v1 whole, which is shorter than its diff:
```python
import functools

import jax
import jax.numpy as jnp
import numpy as np
from jax import lax
from jax.experimental import pallas as pl
from jax.experimental.pallas import tpu as pltpu
from jax.sharding import PartitionSpec as P

PRESCALE = 168
EPS = 1e-06
ROPE_BASE = 1000000.0
ROPE_FACTOR = 8.0
GROUPS = 2
NEG = -1e30
SCALE = float(PRESCALE) ** (-0.5)
LOG2E = 1.4426950408889634
VMEM_LIMIT = 48 * 1024 * 1024
NT = (((1,), (1,)), ((), ()))
TN = (((0,), (0,)), ((), ()))


def rope_tables(block, width, blocks):
    half = width // 2
    freqs = ROPE_BASE ** (-(np.arange(half, dtype=np.float64) * 2.0 / width))
    freqs = np.concatenate([freqs, freqs])
    inner = (np.arange(block) / ROPE_FACTOR)[:, None] * freqs[None, :]
    outer = (np.asarray(blocks) * block / ROPE_FACTOR)[:, None] * freqs[None, :]
    f32 = lambda x: jnp.asarray(x.astype(np.float32))
    return f32(np.stack([np.cos(inner), np.sin(inner)])), f32(np.stack([np.cos(outer), np.sin(outer)], axis=1))


def rope_of(inner_ref, outer_ref, row):
    both = outer_ref[row]
    cb, sb = both[0:1, :], both[1:2, :]
    ct, st = inner_ref[0], inner_ref[1]
    cos = ct * cb - st * sb
    sin = st * cb + ct * sb
    lane = lax.broadcasted_iota(jnp.int32, sin.shape, 1)
    return cos, jnp.where(lane < sin.shape[1] // 2, -sin, sin)


def swap_halves(x):
    return pltpu.roll(x, x.shape[1] // 2, 1)


def unrotate(y, cos, sin):
    return y * cos + swap_halves(y * sin)


def pack_kernel(kv_heads, back, axis, k_ref, v_ref, seg_ref, gain_ref, inner_ref, outer_ref, *rest):
    outs, scratch = rest[:-1], rest[-1]
    block = seg_ref.shape[1]
    per = kv_heads // len(outs)
    cos, sin = rope_of(inner_ref, outer_ref, lax.axis_index(axis) + back)
    gain = gain_ref[...]
    scratch[...] = k_ref[...].astype(jnp.float32)
    for h in range(kv_heads):
        x = scratch[pl.ds(h, block, stride=kv_heads), :]
        r = x * lax.rsqrt(jnp.mean(x * x, axis=1, keepdims=True) + EPS) * gain
        y = r * cos + swap_halves(r) * sin
        outs[h // per][pl.ds((h % per) * block, block), :] = y.astype(jnp.bfloat16)
    scratch[...] = v_ref[...].astype(jnp.float32)
    seg = jnp.broadcast_to(seg_ref[...].astype(jnp.float32) + 1.0, (16, block)).astype(jnp.bfloat16)
    for h in range(kv_heads):
        x = scratch[pl.ds(h, block, stride=kv_heads), :]
        outs[h // per][pl.ds((per + h % per) * block, block), :] = x.astype(jnp.bfloat16)
    for out in outs:
        out[pl.ds(2 * per * block, 16), :] = seg


def query_kernel(heads, back, axis, q_ref, g_ref, gain_ref, inner_ref, outer_ref, qo_ref, go_ref, scratch):
    block = q_ref.shape[0] // heads
    cos, sin = rope_of(inner_ref, outer_ref, lax.axis_index(axis) + back)
    gain = gain_ref[...]
    scratch[...] = q_ref[...].astype(jnp.float32)
    for h in range(heads):
        x = scratch[pl.ds(h, block, stride=heads), :]
        r = x * lax.rsqrt(jnp.mean(x * x, axis=1, keepdims=True) + EPS) * gain
        y = r * cos + swap_halves(r) * sin
        qo_ref[pl.ds(h * block, block), :] = y.astype(jnp.bfloat16)
    scratch[...] = g_ref[...].astype(jnp.float32)
    for h in range(heads):
        go_ref[pl.ds(h * block, block), :] = scratch[pl.ds(h, block, stride=heads), :].astype(jnp.bfloat16)


def attend_kernel(per, group, back, q_ref, g_ref, *rest):
    blocks = rest[: back + 1]
    dq_ref, own_ref = rest[back + 1 : back + 3]
    part_refs = rest[back + 3 : 2 * back + 3]
    bias_ref = rest[-1]
    block = own_ref.shape[0] // (2 * per)
    rows = group * block
    ids = blocks[0][pl.ds(2 * per * block, 16), :].astype(jnp.float32)[0:1, :]
    ids = jnp.concatenate([ids] * group, axis=1)
    for d in range(back + 1):
        key_row = blocks[d][pl.ds(2 * per * block, 16), :].astype(jnp.float32)[0:1, :]
        key_ids = jnp.broadcast_to(key_row, (block, block)).T
        key_ids = jnp.concatenate([key_ids] * group, axis=1)
        seen = key_ids == ids
        if d == 0:
            key_at = lax.broadcasted_iota(jnp.int32, (block, rows), 0)
            query_at = lax.broadcasted_iota(jnp.int32, (block, rows), 1) & (block - 1)
            seen = seen & (key_at <= query_at)
        bias_ref[pl.ds(d * block, block), :] = jnp.where(seen, 0.0, NEG)
    for h in range(per):
        q = q_ref[pl.ds(h * rows, rows), :]
        g = g_ref[pl.ds(h * rows, rows), :]
        k = jnp.concatenate([b[pl.ds(h * block, block), :] for b in blocks], axis=0)
        v = jnp.concatenate([b[pl.ds((per + h) * block, block), :] for b in blocks], axis=0)
        scores = lax.dot_general(k, q, NT, preferred_element_type=jnp.float32)
        expo = jnp.exp2(scores * (SCALE * LOG2E) + bias_ref[...])
        prob_grads = lax.dot_general(v, g, NT, preferred_element_type=jnp.float32)
        inverse = 1.0 / jnp.sum(expo, axis=0, keepdims=True)
        delta = jnp.sum(expo * prob_grads, axis=0, keepdims=True) * inverse
        probs = expo * inverse
        score_grads = (probs * (prob_grads - delta)).astype(jnp.bfloat16)
        dv = jnp.dot(probs.astype(jnp.bfloat16), g, preferred_element_type=jnp.float32)
        dk = jnp.dot(score_grads, q, preferred_element_type=jnp.float32) * SCALE
        dq = lax.dot_general(score_grads, k, TN, preferred_element_type=jnp.float32) * SCALE
        dq_ref[pl.ds(h * rows, rows), :] = dq
        own_ref[pl.ds(h * block, block), :] = dk[:block]
        own_ref[pl.ds((per + h) * block, block), :] = dv[:block]
        for d in range(1, back + 1):
            part = part_refs[d - 1]
            part[pl.ds(h * block, block), :] = dk[d * block : (d + 1) * block].astype(jnp.bfloat16)
            part[pl.ds((per + h) * block, block), :] = dv[d * block : (d + 1) * block].astype(jnp.bfloat16)


def query_back_kernel(heads, kv_heads, groups, back, axis, *rest):
    q_ref, qgain_ref, kgain_ref, inner_ref, outer_ref = rest[:5]
    rest = rest[5:]
    dq_refs, own_refs = rest[:groups], rest[groups : 2 * groups]
    msg_refs = rest[2 * groups : (3 + back) * groups]
    part_refs = rest[(3 + back) * groups : (3 + 2 * back) * groups]
    gq_ref, gains_ref, scratch = rest[-3:]
    block = q_ref.shape[0] // heads
    width = q_ref.shape[1]
    per = kv_heads // groups
    here = lax.axis_index(axis) + back
    total = jnp.zeros((block, width), jnp.float32)
    for d in range(back + 1):
        cos, sin = rope_of(inner_ref, outer_ref, here - d)
        for g in range(groups):
            for h in range(per):
                at = pl.ds(h * block, block)
                dk = own_refs[g][at, :] if d == 0 else part_refs[g * back + d - 1][at, :].astype(jnp.float32)
                k = msg_refs[g * (back + 1) + d][at, :].astype(jnp.float32)
                total = total + unrotate(dk, cos, sin) * unrotate(k, cos, sin)
    kgain = jnp.sum(total, axis=0, keepdims=True) / kgain_ref[...]
    cos, sin = rope_of(inner_ref, outer_ref, here)
    scratch[...] = q_ref[...].astype(jnp.float32)
    gain = qgain_ref[...]
    total = jnp.zeros((block, width), jnp.float32)
    each = heads // groups
    for h in range(heads):
        x = scratch[pl.ds(h, block, stride=heads), :]
        scale = lax.rsqrt(jnp.mean(x * x, axis=1, keepdims=True) + EPS)
        normed = x * scale
        dr = unrotate(dq_refs[h // each][pl.ds((h % each) * block, block), :], cos, sin)
        total = total + dr * normed
        dn = dr * gain
        dx = scale * (dn - normed * jnp.mean(dn * normed, axis=1, keepdims=True))
        scratch[pl.ds(h, block, stride=heads), :] = dx
    gq_ref[...] = scratch[...].astype(jnp.bfloat16)
    qgain = jnp.sum(total, axis=0, keepdims=True)
    gains_ref[...] = jnp.concatenate([qgain, kgain, jnp.zeros((6, width), jnp.float32)], axis=0)


def key_back_kernel(kv_heads, groups, back, axis, *rest):
    k_ref, gain_ref, inner_ref, outer_ref = rest[:4]
    own_refs = rest[4 : 4 + groups]
    got_refs = rest[4 + groups : 4 + (1 + back) * groups]
    gk_ref, gv_ref, scratch = rest[-3:]
    block = k_ref.shape[0] // kv_heads
    per = kv_heads // groups
    cos, sin = rope_of(inner_ref, outer_ref, lax.axis_index(axis) + back)
    gain = gain_ref[...]

    def total(g, row):
        at = pl.ds(row * block, block)
        value = own_refs[g][at, :]
        for d in range(back):
            value = value + got_refs[g * back + d][at, :].astype(jnp.float32)
        return value

    scratch[...] = k_ref[...].astype(jnp.float32)
    for h in range(kv_heads):
        x = scratch[pl.ds(h, block, stride=kv_heads), :]
        scale = lax.rsqrt(jnp.mean(x * x, axis=1, keepdims=True) + EPS)
        normed = x * scale
        dn = unrotate(total(h // per, h % per), cos, sin) * gain
        dx = scale * (dn - normed * jnp.mean(dn * normed, axis=1, keepdims=True))
        scratch[pl.ds(h, block, stride=kv_heads), :] = dx
    gk_ref[...] = scratch[...].astype(jnp.bfloat16)
    for h in range(kv_heads):
        scratch[pl.ds(h, block, stride=kv_heads), :] = total(h // per, per + h % per)
    gv_ref[...] = scratch[...].astype(jnp.bfloat16)


def call(kernel, outs, scratch, cost, *args):
    vmem = pl.BlockSpec(memory_space=pltpu.VMEM)
    return pl.pallas_call(
        kernel,
        out_shape=[jax.ShapeDtypeStruct(s, t) for s, t in outs],
        in_specs=[vmem] * len(args),
        out_specs=[vmem] * len(outs),
        scratch_shapes=[pltpu.VMEM(s, jnp.float32) for s in scratch],
        compiler_params=pltpu.CompilerParams(vmem_limit_bytes=VMEM_LIMIT),
        cost_estimate=pl.CostEstimate(flops=cost, bytes_accessed=1 << 20, transcendentals=0),
    )(*args)


def sum_over(x, axis, size):
    if size & (size - 1):
        return lax.psum(x, axis)
    step = 1
    while step < size:
        x = x + lax.ppermute(x, axis, [(i, i ^ step) for i in range(size)])
        step *= 2
    return x


def body(spans, parts, q_pre, k_pre, values, grad_out, segment_ids, q_gain, k_gain):
    block, heads, width = q_pre.shape[1:]
    kv_heads = k_pre.shape[2]
    group = heads // kv_heads
    groups = GROUPS
    per = kv_heads // groups
    longest = parts * block // 2
    back = min(parts - 1, (longest - 2) // block + 1)
    bf16, f32 = jnp.bfloat16, jnp.float32
    inner, outer = rope_tables(block, width, range(-back, parts))
    q2, g2 = (x.reshape(block * heads, width) for x in (q_pre, grad_out))
    k2, v2 = (x.reshape(block * kv_heads, width) for x in (k_pre, values))
    qg, kg = q_gain.reshape(1, width), k_gain.reshape(1, width)

    message = (2 * per * block + 16, width)
    own = call(
        functools.partial(pack_kernel, kv_heads, back, "seq"),
        [(message, bf16)] * groups, [(block * kv_heads, width)], 1 << 28,
        k2, v2, segment_ids, kg, inner, outer,
    )
    window = [
        [own[g]] + [lax.ppermute(own[g], "seq", [(i, i + d) for i in range(parts - d)]) for d in range(1, back + 1)]
        for g in range(groups)
    ]
    q_rot, g_rot = call(
        functools.partial(query_kernel, heads, back, "seq"),
        [((heads * block, width), bf16)] * 2, [(heads * block, width)], 1 << 29,
        q2, g2, qg, inner, outer,
    )
    dqs, owns, shares, returned = [], [], [], []
    rows = group * block * per
    for g in range(groups):
        dq, kept, *share = call(
            functools.partial(attend_kernel, per, group, back),
            [((rows, width), f32), ((2 * per * block, width), f32)] + [((2 * per * block, width), bf16)] * back,
            [((back + 1) * block, group * block)], 1 << 30,
            lax.slice_in_dim(q_rot, g * rows, (g + 1) * rows), lax.slice_in_dim(g_rot, g * rows, (g + 1) * rows),
            *window[g],
        )
        dqs.append(dq)
        owns.append(kept)
        shares += share
        returned += [
            lax.ppermute(share[d - 1], "seq", [(i + d, i) for i in range(parts - d)]) for d in range(1, back + 1)
        ]
    grad_q, gains = call(
        functools.partial(query_back_kernel, heads, kv_heads, groups, back, "seq"),
        [((heads * block, width), bf16), ((8, width), f32)], [(heads * block, width)], 1 << 29,
        q2, qg, kg, inner, outer, *dqs, *owns, *[m for w in window for m in w], *shares,
    )
    gains = sum_over(sum_over(gains, "seq", parts), "dp", spans)
    grad_k, grad_v = call(
        functools.partial(key_back_kernel, kv_heads, groups, back, "seq"),
        [((kv_heads * block, width), bf16)] * 2, [(kv_heads * block, width)], 1 << 28,
        k2, kg, inner, outer, *owns, *returned,
    )
    return (
        grad_q.reshape(q_pre.shape),
        grad_k.reshape(k_pre.shape),
        grad_v.reshape(values.shape),
        gains[0],
        gains[1],
    )


def solution(mesh):
    tokens = P("dp", "seq", None, None)
    return jax.shard_map(
        functools.partial(body, mesh.shape["dp"], mesh.shape["seq"]),
        mesh=mesh,
        in_specs=(tokens, tokens, tokens, tokens, P("dp", "seq"), P(), P()),
        out_specs=(tokens, tokens, tokens, P(), P()),
        check_vma=False,
    )
```

time: 145 us -> 69.7 us (0.48)
  the two profiles are of different devices: /device:TPU:0 before, /device:TPU:10 now
where the time goes in v1:
time: 69.7 us; the launch traced here: 69.3 us
  starting transfers between devices  30.7 us (44%)
  waiting for transfers between devices  17.1 us (25%)
  Pallas kernels  12.9 us (19%)
  local copies, waits for them, and re-layouts  7.78 us (11%)
  between operations  0.86 us (1%)
    ppermute x5, waiting for transfers between devices, sum_over(): x = x + lax.ppermute(x, axis, [(i, i ^ step) for i in range(size)])  17.1 us
    ppermute x4, starting transfers between devices, body(): lax.ppermute(share[d - 1], 'seq', [(i + d, i) for i in range(parts - d)])  15.6 us
    pallas_call x6, Pallas kernels, call(): pl.pallas_call(kernel, out_shape=[jax.ShapeDtypeStruct(s, t) for s, t in...  12.9 us
    ppermute x4, starting transfers between devices, body(): lax.ppermute(own[g], 'seq', [(i, i + d) for i in range(parts - d)])  9.4 us
    unnamed x26, local copies, waits for them, and re-layouts  7.19 us
    ppermute x5, starting transfers between devices, sum_over(): x = x + lax.ppermute(x, axis, [(i, i ^ step) for i in range(size)])  5.7 us
  transfers between devices with their start and end apart: 13, of which 5 were waited for; matrix products, arithmetic and copies ran while one was open for 1% of the time, Pallas kernels for 14%

profile of v1, /device:TPU:10, one launch (start us, length us, event | category | flops | bytes accessed | tf_op | source)
XLA Modules:
  0.0 69.3 jit_solution(18165299439122162093)
XLA Ops:
  0.6 0.0 copy-start
  0.6 0.0 copy-start.1
  0.7 1.0 %copy-done.1 = f32[2,128,128]{2,1,0:T(8,128)S(1)} copy-done((f32[2,128,128]{2,1,0:T(8,128)S(1)}, f32[2,128,128]{2,1,0:T(8,128)}, u32[]{:S(2)}) %copy-start.1) | copy-done | bytes 131096
  1.6 0.0 copy-start.3
  1.6 0.9 %copy-done.3 = bf16[1,128,8,128]{3,2,1,0:T(8,128)(2,1)S(1)} copy-done((bf16[1,128,8,128]{3,2,1,0:T(8,128)(2,1)S(1)}, bf16[1,128,8,128]{3,2,1,0:T(8,128)(2,1)}, u32[]{:S(2)}) %copy-start.3) | copy-done | bytes 262168
  2.6 0.0 copy-start.5
  2.6 0.7 copy-done.5
  3.2 0.0 copy-start.7
  3.3 0.7 copy-done.7
  3.9 0.0 copy-start.11
  3.9 0.9 %copy-done.11 = bf16[1,128,8,128]{3,2,1,0:T(8,128)(2,1)S(1)} copy-done((bf16[1,128,8,128]{3,2,1,0:T(8,128)(2,1)S(1)}, bf16[1,128,8,128]{3,2,1,0:T(8,128)(2,1)}, u32[]{:S(2)}) %copy-start.11) | copy-done | bytes 262168
  4.9 0.0 copy-start.12
  4.9 0.7 copy-done.12
  5.5 0.9 %shard_map.129 = (bf16[1040,128]{1,0:T(8,128)(2,1)S(1)}, bf16[1040,128]{1,0:T(8,128)(2,1)S(1)}) custom-call(bf16[1024,128]{1,0:T(8,128)(2,1)S(1)} %bitcast.15, bf16[1024,128]{1,0:T(8,128)(2,1)S(1)} %bitcast.23, s32[1,128]{1,0:T(1,128)S(1)} %copy-done.12, f32[1,128]{1,0:T(1,128)S(1)} %bitcast.17, f32[2,128,128]{2,1,0:T(8,128)S(1)} %copy-done.1, ...), custom_call_target="tpu_custom_call" | custom-call | flops 268435456 | bytes 1048576 | tf_op jit(solution)/shard_map/pallas_call | solution.py:204
  6.4 3.4 %collective-permute-start.2 = (bf16[1040,128]{1,0:T(8,128)(2,1)S(1)}, bf16[1040,128]{1,0:T(8,128)(2,1)S(1)}, u32[]{:S(2)}, u32[]{:S(2)}) collective-permute-start(bf16[1040,128]{1,0:T(8,128)(2,1)S(1)} %get-tuple-element.25.rest_0_.rest_12_), channel_id=1, source_target_pairs={{0,1},{1,2},{2,3},{4,5},{5,6},{6,7},{8,9},{9,10},{10,11},{12,13},{... | collective-permute-start | bytes 798728 | tf_op jit(solution)/shard_map/ppermute | solution.py:246
  9.8 1.3 %collective-permute-start.3 = (bf16[1040,128]{1,0:T(8,128)(2,1)S(1)}, bf16[1040,128]{1,0:T(8,128)(2,1)S(1)}, u32[]{:S(2)}, u32[]{:S(2)}) collective-permute-start(bf16[1040,128]{1,0:T(8,128)(2,1)S(1)} %get-tuple-element.25.rest_0_.rest_12_), channel_id=1, source_target_pairs={{0,2},{1,3},{4,6},{5,7},{8,10},{9,11},{12,14},{13,15},{16,18},{17,... | collective-permute-start | bytes 798728 | tf_op jit(solution)/shard_map/ppermute | solution.py:246
  11.1 3.4 %collective-permute-start = (bf16[1040,128]{1,0:T(8,128)(2,1)S(1)}, bf16[1040,128]{1,0:T(8,128)(2,1)S(1)}, u32[]{:S(2)}, u32[]{:S(2)}) collective-permute-start(bf16[1040,128]{1,0:T(8,128)(2,1)S(1)} %get-tuple-element.23.rest_0_.rest_9_), channel_id=1, source_target_pairs={{0,1},{1,2},{2,3},{4,5},{5,6},{6,7},{8,9},{9,10},{10,11},{12,13},{... | collective-permute-start | bytes 798728 | tf_op jit(solution)/shard_map/ppermute | solution.py:246
  14.5 1.3 %collective-permute-start.1 = (bf16[1040,128]{1,0:T(8,128)(2,1)S(1)}, bf16[1040,128]{1,0:T(8,128)(2,1)S(1)}, u32[]{:S(2)}, u32[]{:S(2)}) collective-permute-start(bf16[1040,128]{1,0:T(8,128)(2,1)S(1)} %get-tuple-element.23.rest_0_.rest_9_), channel_id=1, source_target_pairs={{0,2},{1,3},{4,6},{5,7},{8,10},{9,11},{12,14},{13,15},{16,18},{17,... | collective-permute-start | bytes 798728 | tf_op jit(solution)/shard_map/ppermute | solution.py:246
  15.8 0.0 copy-start.9
  15.8 0.0 copy-done
  15.8 0.6 copy-done.9
  16.5 0.0 copy-start.10
  16.5 1.0 %copy-done.10 = bf16[1,128,16,128]{3,2,1,0:T(8,128)(2,1)S(1)} copy-done((bf16[1,128,16,128]{3,2,1,0:T(8,128)(2,1)S(1)}, bf16[1,128,16,128]{3,2,1,0:T(8,128)(2,1)}, u32[]{:S(2)}) %copy-start.10) | copy-done | bytes 524312
  17.5 2.1 %shard_map.128 = (bf16[2048,128]{1,0:T(8,128)(2,1)S(1)}, bf16[2048,128]{1,0:T(8,128)(2,1)S(1)}) custom-call(bf16[2048,128]{1,0:T(8,128)(2,1)S(1)} %bitcast.13, bf16[2048,128]{1,0:T(8,128)(2,1)S(1)} %bitcast.22, f32[1,128]{1,0:T(1,128)S(1)} %bitcast.20, f32[2,128,128]{2,1,0:T(8,128)S(1)} %copy-done.1, f32[6,2,128]{2,1,0:T(2,128)S(1)} %copy-done.5), custom_call_target="tpu_custom_call" | custom-call | flops 536870912 | bytes 1048576 | tf_op jit(solution)/shard_map/pallas_call | solution.py:204
  19.6 0.1 fusion
  19.7 0.0 collective-permute-done.2.rest_1_.rest_13_
  19.7 0.0 collective-permute-done.3.rest_2_.rest_14_
  19.7 1.9 %shard_map.131 = (f32[1024,128]{1,0:T(8,128)S(1)}, f32[1024,128]{1,0:T(8,128)S(1)}, bf16[1024,128]{1,0:T(8,128)(2,1)S(1)}, bf16[1024,128]{1,0:T(8,128)(2,1)S(1)}) custom-call(bf16[1024,128]{1,0:T(8,128)(2,1)S(1)} %get-tuple-element.44.q_ref, bf16[1024,128]{1,0:T(8,128)(2,1)S(1)} %get-tuple-element.37.g_ref, ...), custom_call_target="tpu_custom_call" | custom-call | flops 1073741824 | bytes 1048576 | tf_op jit(solution)/shard_map/pallas_call | solution.py:204
  21.6 10.6 %collective-permute-start.6 = (bf16[1024,128]{1,0:T(8,128)(2,1)S(1)}, bf16[1024,128]{1,0:T(8,128)(2,1)S(1)}, u32[]{:S(2)}, u32[]{:S(2)}) collective-permute-start(bf16[1024,128]{1,0:T(8,128)(2,1)S(1)} %get-tuple-element.31.rest_17_), channel_id=1, source_target_pairs={{1,0},{2,1},{3,2},{5,4},{6,5},{7,6},{9,8},{10,9},{11,10},{13,12},{... | collective-permute-start | bytes 786440 | tf_op jit(solution)/shard_map/ppermute | solution.py:268
  32.2 1.3 %collective-permute-start.7 = (bf16[1024,128]{1,0:T(8,128)(2,1)S(1)}, bf16[1024,128]{1,0:T(8,128)(2,1)S(1)}, u32[]{:S(2)}, u32[]{:S(2)}) collective-permute-start(bf16[1024,128]{1,0:T(8,128)(2,1)S(1)} %get-tuple-element.32.rest_18_), channel_id=1, source_target_pairs={{2,0},{3,1},{6,4},{7,5},{10,8},{11,9},{14,12},{15,13},{18,16},{19,... | collective-permute-start | bytes 786440 | tf_op jit(solution)/shard_map/ppermute | solution.py:268
  33.5 0.0 collective-permute-done.rest_1_.rest_10_
  33.5 0.0 collective-permute-done.1.rest_2_.rest_11_
  33.5 0.0 copy-start.2
  33.5 1.9 %shard_map.130 = (f32[1024,128]{1,0:T(8,128)S(1)}, f32[1024,128]{1,0:T(8,128)S(1)}, bf16[1024,128]{1,0:T(8,128)(2,1)S(1)}, bf16[1024,128]{1,0:T(8,128)(2,1)S(1)}) custom-call(bf16[1024,128]{1,0:T(8,128)(2,1)S(1)} %get-tuple-element.43.q_ref, bf16[1024,128]{1,0:T(8,128)(2,1)S(1)} %get-tuple-element.38.g_ref, ...), custom_call_target="tpu_custom_call" | custom-call | flops 1073741824 | bytes 1048576 | tf_op jit(solution)/shard_map/pallas_call | solution.py:204
  35.4 0.0 copy-start.6
  35.5 2.4 %collective-permute-start.4 = (bf16[1024,128]{1,0:T(8,128)(2,1)S(1)}, bf16[1024,128]{1,0:T(8,128)(2,1)S(1)}, u32[]{:S(2)}, u32[]{:S(2)}) collective-permute-start(bf16[1024,128]{1,0:T(8,128)(2,1)S(1)} %get-tuple-element.29.rest_15_), channel_id=1, source_target_pairs={{1,0},{2,1},{3,2},{5,4},{6,5},{7,6},{9,8},{10,9},{11,10},{13,12},{... | collective-permute-start | bytes 786440 | tf_op jit(solution)/shard_map/ppermute | solution.py:268
  37.8 1.3 %collective-permute-start.5 = (bf16[1024,128]{1,0:T(8,128)(2,1)S(1)}, bf16[1024,128]{1,0:T(8,128)(2,1)S(1)}, u32[]{:S(2)}, u32[]{:S(2)}) collective-permute-start(bf16[1024,128]{1,0:T(8,128)(2,1)S(1)} %get-tuple-element.30.rest_16_), channel_id=1, source_target_pairs={{2,0},{3,1},{6,4},{7,5},{10,8},{11,9},{14,12},{15,13},{18,16},{19,... | collective-permute-start | bytes 786440 | tf_op jit(solution)/shard_map/ppermute | solution.py:268
  39.1 0.0 copy-start.8
  39.2 0.0 copy-done.2
  39.2 0.0 copy-done.6
  39.2 0.6 copy-done.8
  39.8 0.0 copy-start.4
  39.8 4.2 %shard_map.132 = (bf16[2048,128]{1,0:T(8,128)(2,1)}, f32[8,128]{1,0:T(8,128)S(1)}) custom-call(bf16[2048,128]{1,0:T(8,128)(2,1)S(1)} %bitcast.14, f32[1,128]{1,0:T(1,128)S(1)} %bitcast.21, f32[1,128]{1,0:T(1,128)S(1)} %bitcast.18, f32[2,128,128]{2,1,0:T(8,128)S(1)} %copy-done.2, f32[6,2,128]{2,1,0:T(2,128)S(1)} %copy-done.6, ...), custom_call_target="tpu_custom_call" | custom-call | flops 536870912 | bytes 1048576 | tf_op jit(solution)/shard_map/pallas_call | solution.py:204
  44.0 0.0 collective-permute-start.8
  44.0 3.6 %collective-permute-done.8 = f32[8,128]{1,0:T(8,128)S(1)} collective-permute-done((f32[8,128]{1,0:T(8,128)S(1)}, f32[8,128]{1,0:T(8,128)S(1)}, u32[]{:S(2)}, u32[]{:S(2)}) %collective-permute-start.8) | collective-permute-done | bytes 4128 | tf_op jit(solution)/shard_map/ppermute | solution.py:220
  47.6 2.7 %collective-permute-start.9 = (f32[8,128]{1,0:T(8,128)S(1)}, f32[8,128]{1,0:T(8,128)S(1)}, u32[]{:S(2)}, u32[]{:S(2)}) collective-permute-start(f32[8,128]{1,0:T(8,128)S(1)} %add.15), channel_id=1, source_target_pairs={{0,2},{1,3},{2,0},{3,1},{4,6},{5,7},{6,4},{7,5},{8,10},{9,11},{10,... | collective-permute-start | bytes 12296 | tf_op jit(solution)/shard_map/ppermute | solution.py:220
  50.2 7.2 %collective-permute-done.9 = f32[8,128]{1,0:T(8,128)S(1)} collective-permute-done((f32[8,128]{1,0:T(8,128)S(1)}, f32[8,128]{1,0:T(8,128)S(1)}, u32[]{:S(2)}, u32[]{:S(2)}) %collective-permute-start.9) | collective-permute-done | bytes 4128 | tf_op jit(solution)/shard_map/ppermute | solution.py:220
  57.5 0.0 collective-permute-start.10
  57.5 1.1 %collective-permute-done.10 = f32[8,128]{1,0:T(8,128)S(1)} collective-permute-done((f32[8,128]{1,0:T(8,128)S(1)}, f32[8,128]{1,0:T(8,128)S(1)}, u32[]{:S(2)}, u32[]{:S(2)}) %collective-permute-start.10) | collective-permute-done | bytes 4128 | tf_op jit(solution)/shard_map/ppermute | solution.py:220
  58.6 0.4 collective-permute-start.11
  59.1 3.2 %collective-permute-done.11 = f32[8,128]{1,0:T(8,128)S(1)} collective-permute-done((f32[8,128]{1,0:T(8,128)S(1)}, f32[8,128]{1,0:T(8,128)S(1)}, u32[]{:S(2)}, u32[]{:S(2)}) %collective-permute-start.11) | collective-permute-done | bytes 4128 | tf_op jit(solution)/shard_map/ppermute | solution.py:220
  62.2 2.6 %collective-permute-start.12 = (f32[8,128]{1,0:T(8,128)S(1)}, f32[8,128]{1,0:T(8,128)S(1)}, u32[]{:S(2)}, u32[]{:S(2)}) collective-permute-start(f32[8,128]{1,0:T(8,128)S(1)} %add.18), channel_id=1, source_target_pairs={{0,16},{4,20},{8,24},{12,28},{16,0},{20,4},{24,8},{28,12},{1,17},{... | collective-permute-start | bytes 12296 | tf_op jit(solution)/shard_map/ppermute | solution.py:220
  64.8 1.9 %collective-permute-done.12 = f32[8,128]{1,0:T(8,128)S(1)} collective-permute-done((f32[8,128]{1,0:T(8,128)S(1)}, f32[8,128]{1,0:T(8,128)S(1)}, u32[]{:S(2)}, u32[]{:S(2)}) %collective-permute-start.12) | collective-permute-done | bytes 4128 | tf_op jit(solution)/shard_map/ppermute | solution.py:220
  66.7 0.5 slice_bitcast_fusion
  67.3 0.0 collective-permute-done.6.rest_8_
  67.3 0.0 collective-permute-done.7.rest_9_
  67.3 0.0 collective-permute-done.4.rest_6_
  67.3 0.0 collective-permute-done.5.rest_7_
  67.3 0.0 copy-done.4
  67.3 2.0 %shard_map.133 = (bf16[1024,128]{1,0:T(8,128)(2,1)}, bf16[1024,128]{1,0:T(8,128)(2,1)}) custom-call(bf16[1024,128]{1,0:T(8,128)(2,1)S(1)} %bitcast.16, f32[1,128]{1,0:T(1,128)S(1)} %bitcast.19, f32[2,128,128]{2,1,0:T(8,128)S(1)} %copy-done.2, f32[6,2,128]{2,1,0:T(2,128)S(1)} %copy-done.6, f32[1024,128]{1,0:T(8,128)S(1)} %get-tuple-element.27.rest_7_.rest_4_, ...), custom_call_target="tpu_custom_call" | custom-call | flops 268435456 | bytes 1048576 | tf_op jit(solution)/shard_map/pallas_call | solution.py:204
  (5 shorter events, 0.0 us)
Async XLA Ops:
  0.6 15.2 %copy-start = (bf16[1,128,16,128]{3,2,1,0:T(8,128)(2,1)S(1)}, bf16[1,128,16,128]{3,2,1,0:T(8,128)(2,1)}, u32[]{:S(2)}) copy-start(bf16[1,128,16,128]{3,2,1,0:T(8,128)(2,1)} %param.9) | copy-start | bytes 1572868
  0.6 1.0 %copy-start.1 = (f32[2,128,128]{2,1,0:T(8,128)S(1)}, f32[2,128,128]{2,1,0:T(8,128)}, u32[]{:S(2)}) copy-start(f32[2,128,128]{2,1,0:T(8,128)} %constant.4.clone.inner_ref.rest_3_.rest_2_) | copy-start | bytes 393220
  1.6 0.9 %copy-start.3 = (bf16[1,128,8,128]{3,2,1,0:T(8,128)(2,1)S(1)}, bf16[1,128,8,128]{3,2,1,0:T(8,128)(2,1)}, u32[]{:S(2)}) copy-start(bf16[1,128,8,128]{3,2,1,0:T(8,128)(2,1)} %param.10) | copy-start | bytes 786436
  2.6 0.7 copy-start.5
  3.2 0.7 copy-start.7
  3.9 0.9 %copy-start.11 = (bf16[1,128,8,128]{3,2,1,0:T(8,128)(2,1)S(1)}, bf16[1,128,8,128]{3,2,1,0:T(8,128)(2,1)}, u32[]{:S(2)}) copy-start(bf16[1,128,8,128]{3,2,1,0:T(8,128)(2,1)} %param.11) | copy-start | bytes 786436
  4.9 0.7 copy-start.12
  6.4 13.3 %collective-permute-start.2 = (bf16[1040,128]{1,0:T(8,128)(2,1)S(1)}, bf16[1040,128]{1,0:T(8,128)(2,1)S(1)}, u32[]{:S(2)}, u32[]{:S(2)}) collective-permute-start(bf16[1040,128]{1,0:T(8,128)(2,1)S(1)} %get-tuple-element.25.rest_0_.rest_12_), channel_id=1, source_target_pairs={{0,1},{1,2},{2,3},{4,5},{5,6},{6,7},{8,9},{9,10},{10,11},{12,13},{... | collective-permute-start | bytes 798728 | tf_op jit(solution)/shard_map/ppermute | solution.py:246
  9.8 9.9 %collective-permute-start.3 = (bf16[1040,128]{1,0:T(8,128)(2,1)S(1)}, bf16[1040,128]{1,0:T(8,128)(2,1)S(1)}, u32[]{:S(2)}, u32[]{:S(2)}) collective-permute-start(bf16[1040,128]{1,0:T(8,128)(2,1)S(1)} %get-tuple-element.25.rest_0_.rest_12_), channel_id=1, source_target_pairs={{0,2},{1,3},{4,6},{5,7},{8,10},{9,11},{12,14},{13,15},{16,18},{17,... | collective-permute-start | bytes 798728 | tf_op jit(solution)/shard_map/ppermute | solution.py:246
  11.1 22.4 %collective-permute-start = (bf16[1040,128]{1,0:T(8,128)(2,1)S(1)}, bf16[1040,128]{1,0:T(8,128)(2,1)S(1)}, u32[]{:S(2)}, u32[]{:S(2)}) collective-permute-start(bf16[1040,128]{1,0:T(8,128)(2,1)S(1)} %get-tuple-element.23.rest_0_.rest_9_), channel_id=1, source_target_pairs={{0,1},{1,2},{2,3},{4,5},{5,6},{6,7},{8,9},{9,10},{10,11},{12,13},{... | collective-permute-start | bytes 798728 | tf_op jit(solution)/shard_map/ppermute | solution.py:246
  14.5 19.0 %collective-permute-start.1 = (bf16[1040,128]{1,0:T(8,128)(2,1)S(1)}, bf16[1040,128]{1,0:T(8,128)(2,1)S(1)}, u32[]{:S(2)}, u32[]{:S(2)}) collective-permute-start(bf16[1040,128]{1,0:T(8,128)(2,1)S(1)} %get-tuple-element.23.rest_0_.rest_9_), channel_id=1, source_target_pairs={{0,2},{1,3},{4,6},{5,7},{8,10},{9,11},{12,14},{13,15},{16,18},{17,... | collective-permute-start | bytes 798728 | tf_op jit(solution)/shard_map/ppermute | solution.py:246
  15.8 0.7 copy-start.9
  16.5 1.0 %copy-start.10 = (bf16[1,128,16,128]{3,2,1,0:T(8,128)(2,1)S(1)}, bf16[1,128,16,128]{3,2,1,0:T(8,128)(2,1)}, u32[]{:S(2)}) copy-start(bf16[1,128,16,128]{3,2,1,0:T(8,128)(2,1)} %param.12) | copy-start | bytes 1572868
  21.6 45.7 %collective-permute-start.6 = (bf16[1024,128]{1,0:T(8,128)(2,1)S(1)}, bf16[1024,128]{1,0:T(8,128)(2,1)S(1)}, u32[]{:S(2)}, u32[]{:S(2)}) collective-permute-start(bf16[1024,128]{1,0:T(8,128)(2,1)S(1)} %get-tuple-element.31.rest_17_), channel_id=1, source_target_pairs={{1,0},{2,1},{3,2},{5,4},{6,5},{7,6},{9,8},{10,9},{11,10},{13,12},{... | collective-permute-start | bytes 786440 | tf_op jit(solution)/shard_map/ppermute | solution.py:268
  32.2 35.1 %collective-permute-start.7 = (bf16[1024,128]{1,0:T(8,128)(2,1)S(1)}, bf16[1024,128]{1,0:T(8,128)(2,1)S(1)}, u32[]{:S(2)}, u32[]{:S(2)}) collective-permute-start(bf16[1024,128]{1,0:T(8,128)(2,1)S(1)} %get-tuple-element.32.rest_18_), channel_id=1, source_target_pairs={{2,0},{3,1},{6,4},{7,5},{10,8},{11,9},{14,12},{15,13},{18,16},{19,... | collective-permute-start | bytes 786440 | tf_op jit(solution)/shard_map/ppermute | solution.py:268
  33.5 5.6 %copy-start.2 = (f32[2,128,128]{2,1,0:T(8,128)S(1)}, f32[2,128,128]{2,1,0:T(8,128)}, u32[]{:S(2)}) copy-start(f32[2,128,128]{2,1,0:T(8,128)} %constant.4.clone.inner_ref.rest_3_.rest_2_) | copy-start | bytes 393220
  35.4 3.7 %copy-start.6 = (f32[6,2,128]{2,1,0:T(2,128)S(1)}, f32[6,2,128]{2,1,0:T(2,128)}, u32[]{:S(2)}) copy-start(f32[6,2,128]{2,1,0:T(2,128)} %constant.5.clone.outer_ref.rest_4_.rest_3_) | copy-start | bytes 18436
  35.5 31.8 %collective-permute-start.4 = (bf16[1024,128]{1,0:T(8,128)(2,1)S(1)}, bf16[1024,128]{1,0:T(8,128)(2,1)S(1)}, u32[]{:S(2)}, u32[]{:S(2)}) collective-permute-start(bf16[1024,128]{1,0:T(8,128)(2,1)S(1)} %get-tuple-element.29.rest_15_), channel_id=1, source_target_pairs={{1,0},{2,1},{3,2},{5,4},{6,5},{7,6},{9,8},{10,9},{11,10},{13,12},{... | collective-permute-start | bytes 786440 | tf_op jit(solution)/shard_map/ppermute | solution.py:268
  37.8 29.4 %collective-permute-start.5 = (bf16[1024,128]{1,0:T(8,128)(2,1)S(1)}, bf16[1024,128]{1,0:T(8,128)(2,1)S(1)}, u32[]{:S(2)}, u32[]{:S(2)}) collective-permute-start(bf16[1024,128]{1,0:T(8,128)(2,1)S(1)} %get-tuple-element.30.rest_16_), channel_id=1, source_target_pairs={{2,0},{3,1},{6,4},{7,5},{10,8},{11,9},{14,12},{15,13},{18,16},{19,... | collective-permute-start | bytes 786440 | tf_op jit(solution)/shard_map/ppermute | solution.py:268
  39.1 0.7 copy-start.8
  39.8 27.5 %copy-start.4 = (bf16[1,128,8,128]{3,2,1,0:T(8,128)(2,1)S(1)}, bf16[1,128,8,128]{3,2,1,0:T(8,128)(2,1)}, u32[]{:S(2)}) copy-start(bf16[1,128,8,128]{3,2,1,0:T(8,128)(2,1)} %param.10) | copy-start | bytes 786436
  44.0 3.6 %collective-permute-start.8 = (f32[8,128]{1,0:T(8,128)S(1)}, f32[8,128]{1,0:T(8,128)S(1)}, u32[]{:S(2)}, u32[]{:S(2)}) collective-permute-start(f32[8,128]{1,0:T(8,128)S(1)} %get-tuple-element.36), channel_id=1, source_target_pairs={{0,1},{1,0},{2,3},{3,2},{4,5},{5,4},{6,7},{7,6},{8,9},{9,8},{10,11... | collective-permute-start | bytes 12296 | tf_op jit(solution)/shard_map/ppermute | solution.py:220
  47.6 9.9 %collective-permute-start.9 = (f32[8,128]{1,0:T(8,128)S(1)}, f32[8,128]{1,0:T(8,128)S(1)}, u32[]{:S(2)}, u32[]{:S(2)}) collective-permute-start(f32[8,128]{1,0:T(8,128)S(1)} %add.15), channel_id=1, source_target_pairs={{0,2},{1,3},{2,0},{3,1},{4,6},{5,7},{6,4},{7,5},{8,10},{9,11},{10,... | collective-permute-start | bytes 12296 | tf_op jit(solution)/shard_map/ppermute | solution.py:220
  57.5 1.2 %collective-permute-start.10 = (f32[8,128]{1,0:T(8,128)S(1)}, f32[8,128]{1,0:T(8,128)S(1)}, u32[]{:S(2)}, u32[]{:S(2)}) collective-permute-start(f32[8,128]{1,0:T(8,128)S(1)} %add.16), channel_id=1, source_target_pairs={{0,4},{4,0},{8,12},{12,8},{16,20},{20,16},{24,28},{28,24},{1,5},{5... | collective-permute-start | bytes 12296 | tf_op jit(solution)/shard_map/ppermute | solution.py:220
  58.6 3.6 %collective-permute-start.11 = (f32[8,128]{1,0:T(8,128)S(1)}, f32[8,128]{1,0:T(8,128)S(1)}, u32[]{:S(2)}, u32[]{:S(2)}) collective-permute-start(f32[8,128]{1,0:T(8,128)S(1)} %add.17), channel_id=1, source_target_pairs={{0,8},{4,12},{8,0},{12,4},{16,24},{20,28},{24,16},{28,20},{1,9},{5... | collective-permute-start | bytes 12296 | tf_op jit(solution)/shard_map/ppermute | solution.py:220
  62.2 4.5 %collective-permute-start.12 = (f32[8,128]{1,0:T(8,128)S(1)}, f32[8,128]{1,0:T(8,128)S(1)}, u32[]{:S(2)}, u32[]{:S(2)}) collective-permute-start(f32[8,128]{1,0:T(8,128)S(1)} %add.18), channel_id=1, source_target_pairs={{0,16},{4,20},{8,24},{12,28},{16,0},{20,4},{24,8},{28,12},{1,17},{... | collective-permute-start | bytes 12296 | tf_op jit(solution)/shard_map/ppermute | solution.py:220

commit v2 on v1

--- a/solution.py
+++ b/solution.py
@@ -222,7 +222,7 @@
     return x
 
 
-def body(spans, parts, q_pre, k_pre, values, grad_out, segment_ids, q_gain, k_gain):
+def by_tokens(spans, parts, q_pre, k_pre, values, grad_out, segment_ids, q_gain, k_gain):
     block, heads, width = q_pre.shape[1:]
     kv_heads = k_pre.shape[2]
     group = heads // kv_heads
@@ -287,10 +287,272 @@
     )
 
 
+def dma_all(pairs, sems):
+    copies = [pltpu.make_async_copy(src, dst, sems.at[i]) for i, (src, dst) in enumerate(pairs)]
+    for copy in copies:
+        copy.start()
+    return copies
+
+
+def spread_kernel(axis, parts, groups, heads, kv_heads, q_hbm, g_hbm, k_hbm, v_hbm, seg_hbm, *rest):
+    outs = rest[: parts * groups]
+    q_in, g_in, k_in, v_in, seg_in, q_f32, g_f32, k_f32, v_f32, msg, in_sems, out_sems = rest[parts * groups :]
+    block = seg_in.shape[1]
+    group = heads // kv_heads
+    per = kv_heads // parts // groups
+    me = lax.axis_index(axis)
+    loads = dma_all(
+        [(k_hbm, k_in), (v_hbm, v_in), (q_hbm, q_in), (g_hbm, g_in), (seg_hbm, seg_in)], in_sems
+    )
+    for copy, src, dst in zip(loads, (k_in, v_in, q_in, g_in), (k_f32, v_f32, q_f32, g_f32)):
+        copy.wait()
+        dst[...] = src[...].astype(jnp.float32)
+    loads[4].wait()
+    ids = jnp.broadcast_to(seg_in[...].astype(jnp.float32), (16, block)).astype(jnp.bfloat16)
+    stores = []
+    for grp in range(groups):
+        for part in range(parts):
+            slot = grp * parts + part
+            at = 0
+            for p in range(per):
+                kv = (part * groups + grp) * per + p
+                pieces = [(q_f32, kv * group + i, heads) for i in range(group)]
+                pieces += [(g_f32, kv * group + i, heads) for i in range(group)]
+                pieces += [(k_f32, kv, kv_heads), (v_f32, kv, kv_heads)]
+                for src, head, stride in pieces:
+                    rows = src[pl.ds(head, block, stride=stride), :]
+                    msg[slot, pl.ds(at, block), :] = rows.astype(jnp.bfloat16)
+                    at += block
+            msg[slot, pl.ds(at, 16), :] = ids
+        for m in range(parts):
+            i = grp * parts + m
+            copy = pltpu.make_async_copy(msg.at[grp * parts + (me ^ m)], outs[i], out_sems.at[i])
+            copy.start()
+            stores.append(copy)
+    for copy in stores:
+        copy.wait()
+
+
+def heads_kernel(axis, parts, per, group, back, inner_hbm, outer_hbm, gains_hbm, *rest):
+    msgs, outs = rest[:parts], rest[parts : 2 * parts]
+    share_ref, inner_ref, outer_ref, gains_ref, buf, res, in_sems, out_sems = rest[2 * parts :]
+    block, width = inner_ref.shape[1:]
+    rows = group * block
+    me = lax.axis_index(axis)
+    loads = dma_all(
+        [(inner_hbm, inner_ref), (outer_hbm, outer_ref), (gains_hbm, gains_ref)]
+        + [(msgs[m], buf.at[me ^ m]) for m in range(parts)],
+        in_sems,
+    )
+    for copy in loads:
+        copy.wait()
+    q_gain, k_gain = gains_ref[0:1, :], gains_ref[1:2, :]
+    f32, bf16 = jnp.float32, jnp.bfloat16
+    ropes = [rope_of(inner_ref, outer_ref, b) for b in range(parts)]
+    last = per * (2 * group + 2) * block
+    id_rows = [buf[b, pl.ds(last, 16), :].astype(f32)[0:1, :] for b in range(parts)]
+    id_columns = [jnp.broadcast_to(row, (block, block)).T for row in id_rows]
+    key_at = lax.broadcasted_iota(jnp.int32, (block, block), 0)
+    query_at = lax.broadcasted_iota(jnp.int32, (block, block), 1)
+    causal = key_at <= query_at
+
+    def seen(key_block, query_block):
+        same = id_columns[key_block] == id_rows[query_block]
+        if key_block == query_block:
+            same = same & causal
+        return jnp.concatenate([same.astype(f32)] * group, axis=1) > 0.5
+
+    def embed(x, gain, rope):
+        scale = lax.rsqrt(jnp.mean(x * x, axis=1, keepdims=True) + EPS)
+        normed = x * scale
+        r = normed * gain
+        return (r * rope[0] + swap_halves(r) * rope[1]).astype(bf16), normed, scale
+
+    def embed_back(dy, gain, rope, normed, scale):
+        dr = unrotate(dy, *rope)
+        dn = dr * gain
+        dx = scale * (dn - normed * jnp.mean(dn * normed, axis=1, keepdims=True))
+        return dx.astype(bf16), dr * normed
+
+    q_total = jnp.zeros((block, width), f32)
+    k_total = jnp.zeros((block, width), f32)
+    for p in range(per):
+        base = p * (2 * group + 2) * block
+        out_base = p * (group + 2) * block
+
+        def piece(b, i):
+            return buf[b, pl.ds(base + i * block, block), :]
+
+        keys = [embed(piece(b, 2 * group).astype(f32), k_gain, ropes[b]) for b in range(parts)]
+        dk = [jnp.zeros((block, width), f32)] * parts
+        dv = [jnp.zeros((block, width), f32)] * parts
+        for b in range(parts):
+            first = max(0, b - back)
+            queries = [embed(piece(b, i).astype(f32), q_gain, ropes[b]) for i in range(group)]
+            q = jnp.concatenate([x[0] for x in queries], axis=0)
+            g = buf[b, pl.ds(base + rows, rows), :]
+            k = jnp.concatenate([keys[j][0] for j in range(first, b + 1)], axis=0)
+            v = jnp.concatenate([piece(j, 2 * group + 1) for j in range(first, b + 1)], axis=0)
+            mask = jnp.concatenate([seen(j, b) for j in range(first, b + 1)], axis=0)
+            scores = lax.dot_general(k, q, NT, preferred_element_type=f32)
+            expo = jnp.where(mask, jnp.exp2(scores * (SCALE * LOG2E)), 0.0)
+            prob_grads = lax.dot_general(v, g, NT, preferred_element_type=f32)
+            inverse = 1.0 / jnp.sum(expo, axis=0, keepdims=True)
+            delta = jnp.sum(expo * prob_grads, axis=0, keepdims=True) * inverse
+            probs = expo * inverse
+            score_grads = (probs * (prob_grads - delta)).astype(bf16)
+            dvs = jnp.dot(probs.astype(bf16), g, preferred_element_type=f32)
+            dks = jnp.dot(score_grads, q, preferred_element_type=f32)
+            dq = lax.dot_general(score_grads, k, TN, preferred_element_type=f32) * SCALE
+            for i in range(group):
+                dx, share = embed_back(dq[i * block : (i + 1) * block], q_gain, ropes[b], *queries[i][1:])
+                res[b, pl.ds(out_base + i * block, block), :] = dx
+                q_total = q_total + share
+            for j in range(first, b + 1):
+                at = slice((j - first) * block, (j - first + 1) * block)
+                dk[j] = dk[j] + dks[at]
+                dv[j] = dv[j] + dvs[at]
+        for b in range(parts):
+            dx, share = embed_back(dk[b] * SCALE, k_gain, ropes[b], *keys[b][1:])
+            res[b, pl.ds(out_base + rows, block), :] = dx
+            res[b, pl.ds(out_base + rows + block, block), :] = dv[b].astype(bf16)
+            k_total = k_total + share
+    stores = [pltpu.make_async_copy(res.at[me ^ m], outs[m], out_sems.at[m]) for m in range(parts)]
+    for copy in stores:
+        copy.start()
+    share_ref[...] = jnp.concatenate(
+        [
+            jnp.sum(q_total, axis=0, keepdims=True),
+            jnp.sum(k_total, axis=0, keepdims=True),
+            jnp.zeros((6, width), f32),
+        ],
+        axis=0,
+    )
+    for copy in stores:
+        copy.wait()
+
+
+def collect_kernel(axis, parts, groups, heads, kv_heads, *rest):
+    msgs = rest[: parts * groups]
+    gq_hbm, gk_hbm, gv_hbm, buf, q_f32, k_f32, v_f32, q_out, k_out, v_out, in_sems, out_sems = rest[parts * groups :]
+    group = heads // kv_heads
+    per = kv_heads // parts // groups
+    block = q_out.shape[0] // heads
+    me = lax.axis_index(axis)
+    loads = dma_all(
+        [
+            (msgs[grp * parts + m], buf.at[grp * parts + (me ^ m)])
+            for grp in range(groups)
+            for m in range(parts)
+        ],
+        in_sems,
+    )
+    for copy in loads:
+        copy.wait()
+    for grp in range(groups):
+        for part in range(parts):
+            at = 0
+            for p in range(per):
+                kv = (part * groups + grp) * per + p
+                pieces = [(q_f32, kv * group + i, heads) for i in range(group)]
+                pieces += [(k_f32, kv, kv_heads), (v_f32, kv, kv_heads)]
+                for dst, head, stride in pieces:
+                    rows = buf[grp * parts + part, pl.ds(at, block), :].astype(jnp.float32)
+                    dst[pl.ds(head, block, stride=stride), :] = rows
+                    at += block
+    stores = []
+    for i, (src, out, dst) in enumerate(((q_f32, q_out, gq_hbm), (k_f32, k_out, gk_hbm), (v_f32, v_out, gv_hbm))):
+        out[...] = src[...].astype(jnp.bfloat16)
+        copy = pltpu.make_async_copy(out, dst, out_sems.at[i])
+        copy.start()
+        stores.append(copy)
+    for copy in stores:
+        copy.wait()
+
+
+def call_any(kernel, outs, scratch, cost, *args):
+    return pl.pallas_call(
+        kernel,
+        out_shape=[jax.ShapeDtypeStruct(s, t) for s, t, _ in outs],
+        in_specs=[pl.BlockSpec(memory_space=pl.ANY)] * len(args),
+        out_specs=[pl.BlockSpec(memory_space=m) for _, _, m in outs],
+        scratch_shapes=scratch,
+        compiler_params=pltpu.CompilerParams(vmem_limit_bytes=VMEM_LIMIT),
+        cost_estimate=pl.CostEstimate(flops=cost, bytes_accessed=1 << 20, transcendentals=0),
+    )(*args)
+
+
+def exchange_sum(x, axis, size, *partners):
+    got = [lax.ppermute(x, axis, [(i, i ^ m) for i in range(size)]) for m in partners]
+    return x + got[0] if len(got) == 1 else (x + got[0]) + (got[1] + got[2])
+
+
+def by_heads(spans, parts, q_pre, k_pre, values, grad_out, segment_ids, q_gain, k_gain):
+    block, heads, width = q_pre.shape[1:]
+    kv_heads = k_pre.shape[2]
+    group = heads // kv_heads
+    groups = min(GROUPS, kv_heads // parts)
+    per = kv_heads // parts // groups
+    longest = parts * block // 2
+    back = min(parts - 1, (longest - 2) // block + 1)
+    bf16, f32, vmem = jnp.bfloat16, jnp.float32, pltpu.VMEM
+    inner, outer = rope_tables(block, width, range(parts))
+    q2, g2 = (x.reshape(block * heads, width) for x in (q_pre, grad_out))
+    k2, v2 = (x.reshape(block * kv_heads, width) for x in (k_pre, values))
+    sent = (per * (2 * group + 2) * block + 16, width)
+    back_sent = (per * (group + 2) * block, width)
+    dma = pltpu.SemaphoreType.DMA
+    q_shape, k_shape = q2.shape, k2.shape
+
+    messages = call_any(
+        functools.partial(spread_kernel, "seq", parts, groups, heads, kv_heads),
+        [(sent, bf16, pl.ANY)] * (parts * groups),
+        [vmem(q_shape, bf16), vmem(q_shape, bf16), vmem(k_shape, bf16), vmem(k_shape, bf16), vmem((1, block), jnp.int32)]
+        + [vmem(q_shape, f32), vmem(q_shape, f32), vmem(k_shape, f32), vmem(k_shape, f32)]
+        + [vmem((parts * groups, *sent), bf16), dma((5,)), dma((parts * groups,))],
+        1 << 20, q2, g2, k2, v2, segment_ids,
+    )
+    gains = jnp.concatenate([q_gain[None], k_gain[None], jnp.zeros((6, width), f32)], axis=0)
+    xor = lambda m, size: [(i, i ^ m) for i in range(size)]
+    arrived = [
+        [messages[grp * parts]]
+        + [lax.ppermute(messages[grp * parts + m], "seq", xor(m, parts)) for m in range(1, parts)]
+        for grp in range(groups)
+    ]
+    returned, shares = [], []
+    for grp in range(groups):
+        *results, share = call_any(
+            functools.partial(heads_kernel, "seq", parts, per, group, back),
+            [(back_sent, bf16, pl.ANY)] * parts + [((8, width), f32, vmem)],
+            [vmem(inner.shape, f32), vmem(outer.shape, f32), vmem(gains.shape, f32)]
+            + [vmem((parts, *sent), bf16), vmem((parts, *back_sent), bf16), dma((3 + parts,)), dma((parts,))],
+            1 << 30, inner, outer, gains, *arrived[grp],
+        )
+        returned += [results[0]] + [lax.ppermute(results[m], "seq", xor(m, parts)) for m in range(1, parts)]
+        shares.append(share)
+    total = functools.reduce(jnp.add, shares)
+    total = exchange_sum(total, "dp", spans, 1)
+    total = exchange_sum(total, "seq", parts, 1, 2, 3)
+    total = exchange_sum(total, "dp", spans, 2, 4, 6)
+    grad_q, grad_k, grad_v = call_any(
+        functools.partial(collect_kernel, "seq", parts, groups, heads, kv_heads),
+        [(q_shape, bf16, pl.ANY), (k_shape, bf16, pl.ANY), (k_shape, bf16, pl.ANY)],
+        [vmem((parts * groups, *back_sent), bf16)]
+        + [vmem(q_shape, f32), vmem(k_shape, f32), vmem(k_shape, f32)]
+        + [vmem(q_shape, bf16), vmem(k_shape, bf16), vmem(k_shape, bf16), dma((parts * groups,)), dma((3,))],
+        1 << 20, *returned,
+    )
+    return (
+        grad_q.reshape(q_pre.shape), grad_k.reshape(k_pre.shape), grad_v.reshape(values.shape), total[0], total[1],
+    )
+
+
 def solution(mesh):
     tokens = P("dp", "seq", None, None)
+    spans, parts = mesh.shape["dp"], mesh.shape["seq"]
+    body = by_heads if (spans, parts) == (8, 4) else by_tokens
     return jax.shard_map(
-        functools.partial(body, mesh.shape["dp"], mesh.shape["seq"]),
+        functools.partial(body, spans, parts),
         mesh=mesh,
         in_specs=(tokens, tokens, tokens, tokens, P("dp", "seq"), P(), P()),
         out_specs=(tokens, tokens, tokens, P(), P()),

time: 69.7 us -> 65 us (0.933)
  the two profiles are of different devices: /device:TPU:10 before, /device:TPU:0 now
where the time goes in v2:
time: 65 us; the launch traced here: 64.7 us
  starting transfers between devices  26.3 us (40%)
  Pallas kernels  17.3 us (27%)
  waiting for transfers between devices  14.5 us (22%)
  local copies, waits for them, and re-layouts  5.9 us (9%)
  between operations  0.72 us (1%)
    pallas_call x4, Pallas kernels, call_any(): pl.pallas_call(kernel, out_shape=[jax.ShapeDtypeStruct(s, t) for s, t, _...  17.3 us
    ppermute x6, starting transfers between devices, by_heads(): lax.ppermute(messages[grp * parts + m], 'seq', xor(m, parts))  11 us
    ppermute x7, starting transfers between devices, exchange_sum(): lax.ppermute(x, axis, [(i, i ^ m) for i in range(size)])  7.95 us
    ppermute x6, starting transfers between devices, by_heads(): lax.ppermute(results[m], 'seq', xor(m, parts))  7.28 us
    unnamed x18, local copies, waits for them, and re-layouts  5.31 us
    ppermute x6, waiting for transfers between devices, by_heads(): lax.ppermute(messages[grp * parts + m], 'seq', xor(m, parts))  5.12 us
    ppermute x6, waiting for transfers between devices, by_heads(): lax.ppermute(results[m], 'seq', xor(m, parts))  5.12 us
    ppermute x7, waiting for transfers between devices, exchange_sum(): lax.ppermute(x, axis, [(i, i ^ m) for i in range(size)])  4.23 us
  transfers between devices with their start and end apart: 19, of which 12 were waited for; matrix products, arithmetic and copies ran while one was open for 1% of the time, Pallas kernels for 8%

profile of v2, /device:TPU:0, one launch (start us, length us, event | category | flops | bytes accessed | tf_op | source)
XLA Modules:
  0.0 64.7 jit_solution(9539362432554698255)
XLA Ops:
  0.6 0.0 copy-start.4
  0.6 0.6 copy-done.4
  1.3 0.0 copy-start
  1.3 1.0 %copy-done = bf16[1,128,16,128]{3,2,1,0:T(8,128)(2,1)S(1)} copy-done((bf16[1,128,16,128]{3,2,1,0:T(8,128)(2,1)S(1)}, bf16[1,128,16,128]{3,2,1,0:T(8,128)(2,1)}, u32[]{:S(2)}) %copy-start) | copy-done | bytes 524312
  2.3 0.0 copy-start.1
  2.3 1.0 %copy-done.1 = bf16[1,128,16,128]{3,2,1,0:T(8,128)(2,1)S(1)} copy-done((bf16[1,128,16,128]{3,2,1,0:T(8,128)(2,1)S(1)}, bf16[1,128,16,128]{3,2,1,0:T(8,128)(2,1)}, u32[]{:S(2)}) %copy-start.1) | copy-done | bytes 524312
  3.4 0.0 copy-start.2
  3.4 0.9 %copy-done.2 = bf16[1,128,8,128]{3,2,1,0:T(8,128)(2,1)S(1)} copy-done((bf16[1,128,8,128]{3,2,1,0:T(8,128)(2,1)S(1)}, bf16[1,128,8,128]{3,2,1,0:T(8,128)(2,1)}, u32[]{:S(2)}) %copy-start.2) | copy-done | bytes 262168
  4.3 0.0 copy-start.3
  4.3 0.9 %copy-done.3 = bf16[1,128,8,128]{3,2,1,0:T(8,128)(2,1)S(1)} copy-done((bf16[1,128,8,128]{3,2,1,0:T(8,128)(2,1)S(1)}, bf16[1,128,8,128]{3,2,1,0:T(8,128)(2,1)}, u32[]{:S(2)}) %copy-start.3) | copy-done | bytes 262168
  5.3 0.0 copy-start.5
  5.3 3.4 %shard_map.128 = (bf16[784,128]{1,0:T(8,128)(2,1)S(1)}, bf16[784,128]{1,0:T(8,128)(2,1)S(1)}, bf16[784,128]{1,0:T(8,128)(2,1)S(1)}, bf16[784,128]{1,0:T(8,128)(2...) custom-call(bf16[2048,128]{1,0:T(8,128)(2,1)S(1)} %bitcast.13, ...), custom_call_target="tpu_custom_call" | custom-call | flops 1048576 | bytes 1048576 | tf_op jit(solution)/shard_map/pallas_call | solution.py:474
  8.6 3.0 %collective-permute-start = (bf16[784,128]{1,0:T(8,128)(2,1)S(1)}, bf16[784,128]{1,0:T(8,128)(2,1)S(1)}, u32[]{:S(2)}, u32[]{:S(2)}) collective-permute-start(bf16[784,128]{1,0:T(8,128)(2,1)S(1)} %get-tuple-element.27), channel_id=1, source_target_pairs={{0,1},{1,0},{2,3},{3,2},{4,5},{5,4},{6,7},{7,6},{8,9},{9,8},{10,11... | collective-permute-start | bytes 602120 | tf_op jit(solution)/shard_map/ppermute | solution.py:519
  11.6 1.5 %collective-permute-start.1 = (bf16[784,128]{1,0:T(8,128)(2,1)S(1)}, bf16[784,128]{1,0:T(8,128)(2,1)S(1)}, u32[]{:S(2)}, u32[]{:S(2)}) collective-permute-start(bf16[784,128]{1,0:T(8,128)(2,1)S(1)} %get-tuple-element.28), channel_id=1, source_target_pairs={{0,2},{1,3},{2,0},{3,1},{4,6},{5,7},{6,4},{7,5},{8,10},{9,11},{10,... | collective-permute-start | bytes 602120 | tf_op jit(solution)/shard_map/ppermute | solution.py:519
  13.2 0.0 collective-permute-start.2
  13.2 1.9 %collective-permute-start.6 = (bf16[784,128]{1,0:T(8,128)(2,1)S(1)}, bf16[784,128]{1,0:T(8,128)(2,1)S(1)}, u32[]{:S(2)}, u32[]{:S(2)}) collective-permute-start(bf16[784,128]{1,0:T(8,128)(2,1)S(1)} %get-tuple-element.35), channel_id=1, source_target_pairs={{0,1},{1,0},{2,3},{3,2},{4,5},{5,4},{6,7},{7,6},{8,9},{9,8},{10,11... | collective-permute-start | bytes 602120 | tf_op jit(solution)/shard_map/ppermute | solution.py:519
  15.1 1.5 %collective-permute-start.7 = (bf16[784,128]{1,0:T(8,128)(2,1)S(1)}, bf16[784,128]{1,0:T(8,128)(2,1)S(1)}, u32[]{:S(2)}, u32[]{:S(2)}) collective-permute-start(bf16[784,128]{1,0:T(8,128)(2,1)S(1)} %get-tuple-element.36), channel_id=1, source_target_pairs={{0,2},{1,3},{2,0},{3,1},{4,6},{5,7},{6,4},{7,5},{8,10},{9,11},{10,... | collective-permute-start | bytes 602120 | tf_op jit(solution)/shard_map/ppermute | solution.py:519
  16.7 0.1 pad.2.clone
  16.7 0.7 %collective-permute-done.rest_1_ = bf16[784,128]{1,0:T(8,128)(2,1)S(1)} collective-permute-done((bf16[784,128]{1,0:T(8,128)(2,1)S(1)}, bf16[784,128]{1,0:T(8,128)(2,1)S(1)}, u32[]{:S(2)}, u32[]{:S(2)}) %collective-permute-start) | collective-permute-done | bytes 200736 | tf_op jit(solution)/shard_map/ppermute | solution.py:519
  17.5 3.0 %collective-permute-start.8 = (bf16[784,128]{1,0:T(8,128)(2,1)S(1)}, bf16[784,128]{1,0:T(8,128)(2,1)S(1)}, u32[]{:S(2)}, u32[]{:S(2)}) collective-permute-start(bf16[784,128]{1,0:T(8,128)(2,1)S(1)} %get-tuple-element.37), channel_id=1, source_target_pairs={{0,3},{1,2},{2,1},{3,0},{4,7},{5,6},{6,5},{7,4},{8,11},{9,10},{10,... | collective-permute-start | bytes 602120 | tf_op jit(solution)/shard_map/ppermute | solution.py:519
  20.5 0.0 copy-start.7
  20.5 0.0 copy-start.8
  20.5 0.7 %copy-done.7 = f32[128]{0:T(128)S(1)} copy-done((f32[128]{0:T(128)S(1)}, f32[128]{0:T(128)}, u32[]{:S(2)}) %copy-start.7) | copy-done | bytes 536
  21.1 0.0 copy-done.8
  21.1 0.0 copy-start.6
  21.1 0.1 maximum_maximum_fusion.gains_hbm
  21.2 2.6 %collective-permute-done.1.rest_2_ = bf16[784,128]{1,0:T(8,128)(2,1)S(1)} collective-permute-done((bf16[784,128]{1,0:T(8,128)(2,1)S(1)}, bf16[784,128]{1,0:T(8,128)(2,1)S(1)}, u32[]{:S(2)}, u32[]{:S(2)}) %collective-permute-start.1) | collective-permute-done | bytes 200736 | tf_op jit(solution)/shard_map/ppermute | solution.py:519
  23.9 0.0 collective-permute-done.2.rest_3_
  23.9 0.0 copy-done.5
  23.9 0.0 copy-done.6
  23.9 5.4 %shard_map.129 = (bf16[512,128]{1,0:T(8,128)(2,1)S(1)}, bf16[512,128]{1,0:T(8,128)(2,1)S(1)}, bf16[512,128]{1,0:T(8,128)(2,1)S(1)}, bf16[512,128]{1,0:T(8,128)(2,1)S(1)}, f32[8,128]{1,0:T(8,128)S(1)}) custom-call(f32[2,128,128]{2,1,0:T(8,128)S(1)} %copy-done.5, f32[4,2,128]{2,1,0:T(2,128)S(1)} %copy-done.6, f32[8,128]{1,0:T(8,128)S(1)} %maximum_maximum_fusion.gains_hbm, ...), custom_call_target="tpu_custom_call" | custom-call | flops 1073741824 | bytes 1048576 | tf_op jit(solution)/shard_map/pallas_call | solution.py:474
  29.2 0.0 collective-permute-done.6.rest_1_
  29.2 1.7 %collective-permute-done.7.rest_2_ = bf16[784,128]{1,0:T(8,128)(2,1)S(1)} collective-permute-done((bf16[784,128]{1,0:T(8,128)(2,1)S(1)}, bf16[784,128]{1,0:T(8,128)(2,1)S(1)}, u32[]{:S(2)}, u32[]{:S(2)}) %collective-permute-start.7) | collective-permute-done | bytes 200736 | tf_op jit(solution)/shard_map/ppermute | solution.py:519
  31.0 0.0 collective-permute-done.8.rest_3_
  31.0 5.3 %shard_map.130 = (bf16[512,128]{1,0:T(8,128)(2,1)S(1)}, bf16[512,128]{1,0:T(8,128)(2,1)S(1)}, bf16[512,128]{1,0:T(8,128)(2,1)S(1)}, bf16[512,128]{1,0:T(8,128)(2,1)S(1)}, f32[8,128]{1,0:T(8,128)S(1)}) custom-call(f32[2,128,128]{2,1,0:T(8,128)S(1)} %copy-done.5, f32[4,2,128]{2,1,0:T(2,128)S(1)} %copy-done.6, f32[8,128]{1,0:T(8,128)S(1)} %maximum_maximum_fusion.gains_hbm, ...), custom_call_target="tpu_custom_call" | custom-call | flops 1073741824 | bytes 1048576 | tf_op jit(solution)/shard_map/pallas_call | solution.py:474
  36.4 0.1 collective-permute-start.12
  36.4 1.2 %collective-permute-done.12 = f32[8,128]{1,0:T(8,128)S(1)} collective-permute-done((f32[8,128]{1,0:T(8,128)S(1)}, f32[8,128]{1,0:T(8,128)S(1)}, u32[]{:S(2)}, u32[]{:S(2)}) %collective-permute-start.12) | collective-permute-done | bytes 4128 | tf_op jit(solution)/shard_map/ppermute | solution.py:486
  37.6 1.5 %collective-permute-start.15 = (f32[8,128]{1,0:T(8,128)S(1)}, f32[8,128]{1,0:T(8,128)S(1)}, u32[]{:S(2)}, u32[]{:S(2)}) collective-permute-start(f32[8,128]{1,0:T(8,128)S(1)} %add.25), channel_id=1, source_target_pairs={{0,3},{1,2},{2,1},{3,0},{4,7},{5,6},{6,5},{7,4},{8,11},{9,10},{10,... | collective-permute-start | bytes 12296 | tf_op jit(solution)/shard_map/ppermute | solution.py:486
  39.1 1.2 %collective-permute-start.14 = (f32[8,128]{1,0:T(8,128)S(1)}, f32[8,128]{1,0:T(8,128)S(1)}, u32[]{:S(2)}, u32[]{:S(2)}) collective-permute-start(f32[8,128]{1,0:T(8,128)S(1)} %add.25), channel_id=1, source_target_pairs={{0,2},{1,3},{2,0},{3,1},{4,6},{5,7},{6,4},{7,5},{8,10},{9,11},{10,... | collective-permute-start | bytes 12296 | tf_op jit(solution)/shard_map/ppermute | solution.py:486
  40.3 0.8 %collective-permute-start.13 = (f32[8,128]{1,0:T(8,128)S(1)}, f32[8,128]{1,0:T(8,128)S(1)}, u32[]{:S(2)}, u32[]{:S(2)}) collective-permute-start(f32[8,128]{1,0:T(8,128)S(1)} %add.25), channel_id=1, source_target_pairs={{0,1},{1,0},{2,3},{3,2},{4,5},{5,4},{6,7},{7,6},{8,9},{9,8},{10,11... | collective-permute-start | bytes 12296 | tf_op jit(solution)/shard_map/ppermute | solution.py:486
  41.1 1.0 %collective-permute-done.15 = f32[8,128]{1,0:T(8,128)S(1)} collective-permute-done((f32[8,128]{1,0:T(8,128)S(1)}, f32[8,128]{1,0:T(8,128)S(1)}, u32[]{:S(2)}, u32[]{:S(2)}) %collective-permute-start.15) | collective-permute-done | bytes 4128 | tf_op jit(solution)/shard_map/ppermute | solution.py:486
  42.1 0.6 collective-permute-done.14
  42.7 1.2 %collective-permute-done.13 = f32[8,128]{1,0:T(8,128)S(1)} collective-permute-done((f32[8,128]{1,0:T(8,128)S(1)}, f32[8,128]{1,0:T(8,128)S(1)}, u32[]{:S(2)}, u32[]{:S(2)}) %collective-permute-start.13) | collective-permute-done | bytes 4128 | tf_op jit(solution)/shard_map/ppermute | solution.py:486
  43.9 3.6 %collective-permute-start.18 = (f32[8,128]{1,0:T(8,128)S(1)}, f32[8,128]{1,0:T(8,128)S(1)}, u32[]{:S(2)}, u32[]{:S(2)}) collective-permute-start(f32[8,128]{1,0:T(8,128)S(1)} %add_add_fusion.1), channel_id=1, source_target_pairs={{0,24},{4,28},{8,16},{12,20},{16,8},{20,12},{24,0},{28,4},{1,25},{... | collective-permute-start | bytes 12296 | tf_op jit(solution)/shard_map/ppermute | solution.py:486
  47.5 0.0 collective-permute-start.17
  47.5 0.8 %collective-permute-start.16 = (f32[8,128]{1,0:T(8,128)S(1)}, f32[8,128]{1,0:T(8,128)S(1)}, u32[]{:S(2)}, u32[]{:S(2)}) collective-permute-start(f32[8,128]{1,0:T(8,128)S(1)} %add_add_fusion.1), channel_id=1, source_target_pairs={{0,8},{4,12},{8,0},{12,4},{16,24},{20,28},{24,16},{28,20},{1,9},{5... | collective-permute-start | bytes 12296 | tf_op jit(solution)/shard_map/ppermute | solution.py:486
  48.3 0.8 %collective-permute-start.3 = (bf16[512,128]{1,0:T(8,128)(2,1)S(1)}, bf16[512,128]{1,0:T(8,128)(2,1)S(1)}, u32[]{:S(2)}, u32[]{:S(2)}) collective-permute-start(bf16[512,128]{1,0:T(8,128)(2,1)S(1)} %get-tuple-element.31), channel_id=1, source_target_pairs={{0,1},{1,0},{2,3},{3,2},{4,5},{5,4},{6,7},{7,6},{8,9},{9,8},{10,11... | collective-permute-start | bytes 393224 | tf_op jit(solution)/shard_map/ppermute | solution.py:531
  49.1 1.5 %collective-permute-start.4 = (bf16[512,128]{1,0:T(8,128)(2,1)S(1)}, bf16[512,128]{1,0:T(8,128)(2,1)S(1)}, u32[]{:S(2)}, u32[]{:S(2)}) collective-permute-start(bf16[512,128]{1,0:T(8,128)(2,1)S(1)} %get-tuple-element.32), channel_id=1, source_target_pairs={{0,2},{1,3},{2,0},{3,1},{4,6},{5,7},{6,4},{7,5},{8,10},{9,11},{10,... | collective-permute-start | bytes 393224 | tf_op jit(solution)/shard_map/ppermute | solution.py:531
  50.6 0.0 collective-permute-done.18
  50.6 1.2 %collective-permute-start.5 = (bf16[512,128]{1,0:T(8,128)(2,1)S(1)}, bf16[512,128]{1,0:T(8,128)(2,1)S(1)}, u32[]{:S(2)}, u32[]{:S(2)}) collective-permute-start(bf16[512,128]{1,0:T(8,128)(2,1)S(1)} %get-tuple-element.33), channel_id=1, source_target_pairs={{0,3},{1,2},{2,1},{3,0},{4,7},{5,6},{6,5},{7,4},{8,11},{9,10},{10,... | collective-permute-start | bytes 393224 | tf_op jit(solution)/shard_map/ppermute | solution.py:531
  51.8 0.2 collective-permute-done.17
  52.0 0.8 %collective-permute-start.9 = (bf16[512,128]{1,0:T(8,128)(2,1)S(1)}, bf16[512,128]{1,0:T(8,128)(2,1)S(1)}, u32[]{:S(2)}, u32[]{:S(2)}) collective-permute-start(bf16[512,128]{1,0:T(8,128)(2,1)S(1)} %get-tuple-element.39), channel_id=1, source_target_pairs={{0,1},{1,0},{2,3},{3,2},{4,5},{5,4},{6,7},{7,6},{8,9},{9,8},{10,11... | collective-permute-start | bytes 393224 | tf_op jit(solution)/shard_map/ppermute | solution.py:531
  52.8 0.0 collective-permute-done.16
  52.8 1.5 %collective-permute-start.10 = (bf16[512,128]{1,0:T(8,128)(2,1)S(1)}, bf16[512,128]{1,0:T(8,128)(2,1)S(1)}, u32[]{:S(2)}, u32[]{:S(2)}) collective-permute-start(bf16[512,128]{1,0:T(8,128)(2,1)S(1)} %get-tuple-element.40), channel_id=1, source_target_pairs={{0,2},{1,3},{2,0},{3,1},{4,6},{5,7},{6,4},{7,5},{8,10},{9,11},{10,... | collective-permute-start | bytes 393224 | tf_op jit(solution)/shard_map/ppermute | solution.py:531
  54.3 0.4 collective-permute-done.3.rest_1_
  54.7 1.5 %collective-permute-start.11 = (bf16[512,128]{1,0:T(8,128)(2,1)S(1)}, bf16[512,128]{1,0:T(8,128)(2,1)S(1)}, u32[]{:S(2)}, u32[]{:S(2)}) collective-permute-start(bf16[512,128]{1,0:T(8,128)(2,1)S(1)} %get-tuple-element.41), channel_id=1, source_target_pairs={{0,3},{1,2},{2,1},{3,0},{4,7},{5,6},{6,5},{7,4},{8,11},{9,10},{10,... | collective-permute-start | bytes 393224 | tf_op jit(solution)/shard_map/ppermute | solution.py:531
  56.2 0.5 slice_bitcast_fusion
  56.8 1.6 %collective-permute-done.4.rest_2_ = bf16[512,128]{1,0:T(8,128)(2,1)S(1)} collective-permute-done((bf16[512,128]{1,0:T(8,128)(2,1)S(1)}, bf16[512,128]{1,0:T(8,128)(2,1)S(1)}, u32[]{:S(2)}, u32[]{:S(2)}) %collective-permute-start.4) | collective-permute-done | bytes 131104 | tf_op jit(solution)/shard_map/ppermute | solution.py:531
  58.4 0.0 collective-permute-done.5.rest_3_
  58.4 0.8 %collective-permute-done.9.rest_5_ = bf16[512,128]{1,0:T(8,128)(2,1)S(1)} collective-permute-done((bf16[512,128]{1,0:T(8,128)(2,1)S(1)}, bf16[512,128]{1,0:T(8,128)(2,1)S(1)}, u32[]{:S(2)}, u32[]{:S(2)}) %collective-permute-start.9) | collective-permute-done | bytes 131104 | tf_op jit(solution)/shard_map/ppermute | solution.py:531
  59.1 2.3 %collective-permute-done.10.rest_6_ = bf16[512,128]{1,0:T(8,128)(2,1)S(1)} collective-permute-done((bf16[512,128]{1,0:T(8,128)(2,1)S(1)}, bf16[512,128]{1,0:T(8,128)(2,1)S(1)}, u32[]{:S(2)}, u32[]{:S(2)}) %collective-permute-start.10) | collective-permute-done | bytes 131104 | tf_op jit(solution)/shard_map/ppermute | solution.py:531
  61.5 0.0 collective-permute-done.11.rest_7_
  61.5 3.3 %shard_map.131 = (bf16[2048,128]{1,0:T(8,128)(2,1)}, bf16[1024,128]{1,0:T(8,128)(2,1)}, bf16[1024,128]{1,0:T(8,128)(2,1)}) custom-call(bf16[512,128]{1,0:T(8,128)(2,1)S(1)} %get-tuple-element.30.rest_0_, bf16[512,128]{1,0:T(8,128)(2,1)S(1)} %collective-permute-done.3.rest_1_, bf16[512,128]{1,0:T(8,128)(2,1)S(1)} %collective-permute-done.4.rest_2_, ...), custom_call_target="tpu_custom_call" | custom-call | flops 1048576 | bytes 1048576 | tf_op jit(solution)/shard_map/pallas_call | solution.py:474
  (5 shorter events, 0.0 us)
Async XLA Ops:
  0.6 0.7 %copy-start.4 = (s32[1,128]{1,0:T(1,128)S(1)}, s32[1,128]{1,0:T(1,128)}, u32[]{:S(2)}) copy-start(s32[1,128]{1,0:T(1,128)} %seg_hbm.1) | copy-start | bytes 1540
  1.3 1.0 %copy-start = (bf16[1,128,16,128]{3,2,1,0:T(8,128)(2,1)S(1)}, bf16[1,128,16,128]{3,2,1,0:T(8,128)(2,1)}, u32[]{:S(2)}) copy-start(bf16[1,128,16,128]{3,2,1,0:T(8,128)(2,1)} %param.9) | copy-start | bytes 1572868
  2.3 1.0 %copy-start.1 = (bf16[1,128,16,128]{3,2,1,0:T(8,128)(2,1)S(1)}, bf16[1,128,16,128]{3,2,1,0:T(8,128)(2,1)}, u32[]{:S(2)}) copy-start(bf16[1,128,16,128]{3,2,1,0:T(8,128)(2,1)} %param.12) | copy-start | bytes 1572868
  3.4 0.9 %copy-start.2 = (bf16[1,128,8,128]{3,2,1,0:T(8,128)(2,1)S(1)}, bf16[1,128,8,128]{3,2,1,0:T(8,128)(2,1)}, u32[]{:S(2)}) copy-start(bf16[1,128,8,128]{3,2,1,0:T(8,128)(2,1)} %param.10) | copy-start | bytes 786436
  4.3 0.9 %copy-start.3 = (bf16[1,128,8,128]{3,2,1,0:T(8,128)(2,1)S(1)}, bf16[1,128,8,128]{3,2,1,0:T(8,128)(2,1)}, u32[]{:S(2)}) copy-start(bf16[1,128,8,128]{3,2,1,0:T(8,128)(2,1)} %param.11) | copy-start | bytes 786436
  5.3 18.6 %copy-start.5 = (f32[2,128,128]{2,1,0:T(8,128)S(1)}, f32[2,128,128]{2,1,0:T(8,128)}, u32[]{:S(2)}) copy-start(f32[2,128,128]{2,1,0:T(8,128)} %constant.6.clone.inner_hbm) | copy-start | bytes 393220
  8.6 8.8 %collective-permute-start = (bf16[784,128]{1,0:T(8,128)(2,1)S(1)}, bf16[784,128]{1,0:T(8,128)(2,1)S(1)}, u32[]{:S(2)}, u32[]{:S(2)}) collective-permute-start(bf16[784,128]{1,0:T(8,128)(2,1)S(1)} %get-tuple-element.27), channel_id=1, source_target_pairs={{0,1},{1,0},{2,3},{3,2},{4,5},{5,4},{6,7},{7,6},{8,9},{9,8},{10,11... | collective-permute-start | bytes 602120 | tf_op jit(solution)/shard_map/ppermute | solution.py:519
  11.6 12.2 %collective-permute-start.1 = (bf16[784,128]{1,0:T(8,128)(2,1)S(1)}, bf16[784,128]{1,0:T(8,128)(2,1)S(1)}, u32[]{:S(2)}, u32[]{:S(2)}) collective-permute-start(bf16[784,128]{1,0:T(8,128)(2,1)S(1)} %get-tuple-element.28), channel_id=1, source_target_pairs={{0,2},{1,3},{2,0},{3,1},{4,6},{5,7},{6,4},{7,5},{8,10},{9,11},{10,... | collective-permute-start | bytes 602120 | tf_op jit(solution)/shard_map/ppermute | solution.py:519
  13.2 10.7 %collective-permute-start.2 = (bf16[784,128]{1,0:T(8,128)(2,1)S(1)}, bf16[784,128]{1,0:T(8,128)(2,1)S(1)}, u32[]{:S(2)}, u32[]{:S(2)}) collective-permute-start(bf16[784,128]{1,0:T(8,128)(2,1)S(1)} %get-tuple-element.29), channel_id=1, source_target_pairs={{0,3},{1,2},{2,1},{3,0},{4,7},{5,6},{6,5},{7,4},{8,11},{9,10},{10,... | collective-permute-start | bytes 602120 | tf_op jit(solution)/shard_map/ppermute | solution.py:519
  13.2 16.1 %collective-permute-start.6 = (bf16[784,128]{1,0:T(8,128)(2,1)S(1)}, bf16[784,128]{1,0:T(8,128)(2,1)S(1)}, u32[]{:S(2)}, u32[]{:S(2)}) collective-permute-start(bf16[784,128]{1,0:T(8,128)(2,1)S(1)} %get-tuple-element.35), channel_id=1, source_target_pairs={{0,1},{1,0},{2,3},{3,2},{4,5},{5,4},{6,7},{7,6},{8,9},{9,8},{10,11... | collective-permute-start | bytes 602120 | tf_op jit(solution)/shard_map/ppermute | solution.py:519
  15.1 15.9 %collective-permute-start.7 = (bf16[784,128]{1,0:T(8,128)(2,1)S(1)}, bf16[784,128]{1,0:T(8,128)(2,1)S(1)}, u32[]{:S(2)}, u32[]{:S(2)}) collective-permute-start(bf16[784,128]{1,0:T(8,128)(2,1)S(1)} %get-tuple-element.36), channel_id=1, source_target_pairs={{0,2},{1,3},{2,0},{3,1},{4,6},{5,7},{6,4},{7,5},{8,10},{9,11},{10,... | collective-permute-start | bytes 602120 | tf_op jit(solution)/shard_map/ppermute | solution.py:519
  17.5 13.5 %collective-permute-start.8 = (bf16[784,128]{1,0:T(8,128)(2,1)S(1)}, bf16[784,128]{1,0:T(8,128)(2,1)S(1)}, u32[]{:S(2)}, u32[]{:S(2)}) collective-permute-start(bf16[784,128]{1,0:T(8,128)(2,1)S(1)} %get-tuple-element.37), channel_id=1, source_target_pairs={{0,3},{1,2},{2,1},{3,0},{4,7},{5,6},{6,5},{7,4},{8,11},{9,10},{10,... | collective-permute-start | bytes 602120 | tf_op jit(solution)/shard_map/ppermute | solution.py:519
  20.5 0.7 %copy-start.7 = (f32[128]{0:T(128)S(1)}, f32[128]{0:T(128)}, u32[]{:S(2)}) copy-start(f32[128]{0:T(128)} %param.15) | copy-start | bytes 1540
  20.5 0.7 %copy-start.8 = (f32[128]{0:T(128)S(1)}, f32[128]{0:T(128)}, u32[]{:S(2)}) copy-start(f32[128]{0:T(128)} %param.14) | copy-start | bytes 1540
  21.1 2.7 %copy-start.6 = (f32[4,2,128]{2,1,0:T(2,128)S(1)}, f32[4,2,128]{2,1,0:T(2,128)}, u32[]{:S(2)}) copy-start(f32[4,2,128]{2,1,0:T(2,128)} %constant.7.clone.outer_hbm) | copy-start | bytes 12292
  36.4 1.2 %collective-permute-start.12 = (f32[8,128]{1,0:T(8,128)S(1)}, f32[8,128]{1,0:T(8,128)S(1)}, u32[]{:S(2)}, u32[]{:S(2)}) collective-permute-start(f32[8,128]{1,0:T(8,128)S(1)} %add.24), channel_id=1, source_target_pairs={{0,4},{4,0},{8,12},{12,8},{16,20},{20,16},{24,28},{28,24},{1,5},{5... | collective-permute-start | bytes 12296 | tf_op jit(solution)/shard_map/ppermute | solution.py:486
  37.6 4.5 %collective-permute-start.15 = (f32[8,128]{1,0:T(8,128)S(1)}, f32[8,128]{1,0:T(8,128)S(1)}, u32[]{:S(2)}, u32[]{:S(2)}) collective-permute-start(f32[8,128]{1,0:T(8,128)S(1)} %add.25), channel_id=1, source_target_pairs={{0,3},{1,2},{2,1},{3,0},{4,7},{5,6},{6,5},{7,4},{8,11},{9,10},{10,... | collective-permute-start | bytes 12296 | tf_op jit(solution)/shard_map/ppermute | solution.py:486
  39.1 3.6 %collective-permute-start.14 = (f32[8,128]{1,0:T(8,128)S(1)}, f32[8,128]{1,0:T(8,128)S(1)}, u32[]{:S(2)}, u32[]{:S(2)}) collective-permute-start(f32[8,128]{1,0:T(8,128)S(1)} %add.25), channel_id=1, source_target_pairs={{0,2},{1,3},{2,0},{3,1},{4,6},{5,7},{6,4},{7,5},{8,10},{9,11},{10,... | collective-permute-start | bytes 12296 | tf_op jit(solution)/shard_map/ppermute | solution.py:486
  40.3 3.6 %collective-permute-start.13 = (f32[8,128]{1,0:T(8,128)S(1)}, f32[8,128]{1,0:T(8,128)S(1)}, u32[]{:S(2)}, u32[]{:S(2)}) collective-permute-start(f32[8,128]{1,0:T(8,128)S(1)} %add.25), channel_id=1, source_target_pairs={{0,1},{1,0},{2,3},{3,2},{4,5},{5,4},{6,7},{7,6},{8,9},{9,8},{10,11... | collective-permute-start | bytes 12296 | tf_op jit(solution)/shard_map/ppermute | solution.py:486
  43.9 6.7 %collective-permute-start.18 = (f32[8,128]{1,0:T(8,128)S(1)}, f32[8,128]{1,0:T(8,128)S(1)}, u32[]{:S(2)}, u32[]{:S(2)}) collective-permute-start(f32[8,128]{1,0:T(8,128)S(1)} %add_add_fusion.1), channel_id=1, source_target_pairs={{0,24},{4,28},{8,16},{12,20},{16,8},{20,12},{24,0},{28,4},{1,25},{... | collective-permute-start | bytes 12296 | tf_op jit(solution)/shard_map/ppermute | solution.py:486
  47.5 4.5 %collective-permute-start.17 = (f32[8,128]{1,0:T(8,128)S(1)}, f32[8,128]{1,0:T(8,128)S(1)}, u32[]{:S(2)}, u32[]{:S(2)}) collective-permute-start(f32[8,128]{1,0:T(8,128)S(1)} %add_add_fusion.1), channel_id=1, source_target_pairs={{0,16},{4,20},{8,24},{12,28},{16,0},{20,4},{24,8},{28,12},{1,17},{... | collective-permute-start | bytes 12296 | tf_op jit(solution)/shard_map/ppermute | solution.py:486
  47.5 5.3 %collective-permute-start.16 = (f32[8,128]{1,0:T(8,128)S(1)}, f32[8,128]{1,0:T(8,128)S(1)}, u32[]{:S(2)}, u32[]{:S(2)}) collective-permute-start(f32[8,128]{1,0:T(8,128)S(1)} %add_add_fusion.1), channel_id=1, source_target_pairs={{0,8},{4,12},{8,0},{12,4},{16,24},{20,28},{24,16},{28,20},{1,9},{5... | collective-permute-start | bytes 12296 | tf_op jit(solution)/shard_map/ppermute | solution.py:486
  48.3 6.4 %collective-permute-start.3 = (bf16[512,128]{1,0:T(8,128)(2,1)S(1)}, bf16[512,128]{1,0:T(8,128)(2,1)S(1)}, u32[]{:S(2)}, u32[]{:S(2)}) collective-permute-start(bf16[512,128]{1,0:T(8,128)(2,1)S(1)} %get-tuple-element.31), channel_id=1, source_target_pairs={{0,1},{1,0},{2,3},{3,2},{4,5},{5,4},{6,7},{7,6},{8,9},{9,8},{10,11... | collective-permute-start | bytes 393224 | tf_op jit(solution)/shard_map/ppermute | solution.py:531
  49.1 9.3 %collective-permute-start.4 = (bf16[512,128]{1,0:T(8,128)(2,1)S(1)}, bf16[512,128]{1,0:T(8,128)(2,1)S(1)}, u32[]{:S(2)}, u32[]{:S(2)}) collective-permute-start(bf16[512,128]{1,0:T(8,128)(2,1)S(1)} %get-tuple-element.32), channel_id=1, source_target_pairs={{0,2},{1,3},{2,0},{3,1},{4,6},{5,7},{6,4},{7,5},{8,10},{9,11},{10,... | collective-permute-start | bytes 393224 | tf_op jit(solution)/shard_map/ppermute | solution.py:531
  50.6 7.8 %collective-permute-start.5 = (bf16[512,128]{1,0:T(8,128)(2,1)S(1)}, bf16[512,128]{1,0:T(8,128)(2,1)S(1)}, u32[]{:S(2)}, u32[]{:S(2)}) collective-permute-start(bf16[512,128]{1,0:T(8,128)(2,1)S(1)} %get-tuple-element.33), channel_id=1, source_target_pairs={{0,3},{1,2},{2,1},{3,0},{4,7},{5,6},{6,5},{7,4},{8,11},{9,10},{10,... | collective-permute-start | bytes 393224 | tf_op jit(solution)/shard_map/ppermute | solution.py:531
  52.0 7.1 %collective-permute-start.9 = (bf16[512,128]{1,0:T(8,128)(2,1)S(1)}, bf16[512,128]{1,0:T(8,128)(2,1)S(1)}, u32[]{:S(2)}, u32[]{:S(2)}) collective-permute-start(bf16[512,128]{1,0:T(8,128)(2,1)S(1)} %get-tuple-element.39), channel_id=1, source_target_pairs={{0,1},{1,0},{2,3},{3,2},{4,5},{5,4},{6,7},{7,6},{8,9},{9,8},{10,11... | collective-permute-start | bytes 393224 | tf_op jit(solution)/shard_map/ppermute | solution.py:531
  52.8 8.7 %collective-permute-start.10 = (bf16[512,128]{1,0:T(8,128)(2,1)S(1)}, bf16[512,128]{1,0:T(8,128)(2,1)S(1)}, u32[]{:S(2)}, u32[]{:S(2)}) collective-permute-start(bf16[512,128]{1,0:T(8,128)(2,1)S(1)} %get-tuple-element.40), channel_id=1, source_target_pairs={{0,2},{1,3},{2,0},{3,1},{4,6},{5,7},{6,4},{7,5},{8,10},{9,11},{10,... | collective-permute-start | bytes 393224 | tf_op jit(solution)/shard_map/ppermute | solution.py:531
  54.7 6.8 %collective-permute-start.11 = (bf16[512,128]{1,0:T(8,128)(2,1)S(1)}, bf16[512,128]{1,0:T(8,128)(2,1)S(1)}, u32[]{:S(2)}, u32[]{:S(2)}) collective-permute-start(bf16[512,128]{1,0:T(8,128)(2,1)S(1)} %get-tuple-element.41), channel_id=1, source_target_pairs={{0,3},{1,2},{2,1},{3,0},{4,7},{5,6},{6,5},{7,4},{8,11},{9,10},{10,... | collective-permute-start | bytes 393224 | tf_op jit(solution)/shard_map/ppermute | solution.py:531

commit v3 on v2

--- a/solution.py
+++ b/solution.py
@@ -333,9 +333,11 @@
         copy.wait()
 
 
-def heads_kernel(axis, parts, per, group, back, inner_hbm, outer_hbm, gains_hbm, *rest):
-    msgs, outs = rest[:parts], rest[parts : 2 * parts]
-    share_ref, inner_ref, outer_ref, gains_ref, buf, res, in_sems, out_sems = rest[2 * parts :]
+def heads_kernel(axis, parts, grp, per, group, back, *rest):
+    outs = rest[-8 - parts : -8]
+    msgs = rest[-11 - 2 * parts : -11 - parts]
+    inner_hbm, outer_hbm, gains_hbm = rest[-11 - parts : -8 - parts]
+    share_ref, inner_ref, outer_ref, gains_ref, buf, res, in_sems, out_sems = rest[-8:]
     block, width = inner_ref.shape[1:]
     rows = group * block
     me = lax.axis_index(axis)
@@ -417,7 +419,8 @@
             res[b, pl.ds(out_base + rows, block), :] = dx
             res[b, pl.ds(out_base + rows + block, block), :] = dv[b].astype(bf16)
             k_total = k_total + share
-    stores = [pltpu.make_async_copy(res.at[me ^ m], outs[m], out_sems.at[m]) for m in range(parts)]
+    mine = pl.ds(grp * res.shape[1], res.shape[1])
+    stores = [pltpu.make_async_copy(res.at[me ^ m], outs[m].at[mine], out_sems.at[m]) for m in range(parts)]
     for copy in stores:
         copy.start()
     share_ref[...] = jnp.concatenate(
@@ -433,31 +436,24 @@
 
 
 def collect_kernel(axis, parts, groups, heads, kv_heads, *rest):
-    msgs = rest[: parts * groups]
-    gq_hbm, gk_hbm, gv_hbm, buf, q_f32, k_f32, v_f32, q_out, k_out, v_out, in_sems, out_sems = rest[parts * groups :]
+    msgs = rest[:parts]
+    gq_hbm, gk_hbm, gv_hbm, buf, q_f32, k_f32, v_f32, q_out, k_out, v_out, in_sems, out_sems = rest[parts:]
     group = heads // kv_heads
     per = kv_heads // parts // groups
     block = q_out.shape[0] // heads
     me = lax.axis_index(axis)
-    loads = dma_all(
-        [
-            (msgs[grp * parts + m], buf.at[grp * parts + (me ^ m)])
-            for grp in range(groups)
-            for m in range(parts)
-        ],
-        in_sems,
-    )
+    loads = dma_all([(msgs[m], buf.at[me ^ m]) for m in range(parts)], in_sems)
     for copy in loads:
         copy.wait()
-    for grp in range(groups):
-        for part in range(parts):
-            at = 0
+    for part in range(parts):
+        at = 0
+        for grp in range(groups):
             for p in range(per):
                 kv = (part * groups + grp) * per + p
                 pieces = [(q_f32, kv * group + i, heads) for i in range(group)]
                 pieces += [(k_f32, kv, kv_heads), (v_f32, kv, kv_heads)]
                 for dst, head, stride in pieces:
-                    rows = buf[grp * parts + part, pl.ds(at, block), :].astype(jnp.float32)
+                    rows = buf[part, pl.ds(at, block), :].astype(jnp.float32)
                     dst[pl.ds(head, block, stride=stride), :] = rows
                     at += block
     stores = []
@@ -470,21 +466,23 @@
         copy.wait()
 
 
-def call_any(kernel, outs, scratch, cost, *args):
+def call_any(kernel, outs, scratch, cost, *args, limit=VMEM_LIMIT, aliases=None):
     return pl.pallas_call(
         kernel,
         out_shape=[jax.ShapeDtypeStruct(s, t) for s, t, _ in outs],
-        in_specs=[pl.BlockSpec(memory_space=pl.ANY)] * len(args),
+        in_specs=[pl.BlockSpec(memory_space=pltpu.HBM)] * len(args),
         out_specs=[pl.BlockSpec(memory_space=m) for _, _, m in outs],
         scratch_shapes=scratch,
-        compiler_params=pltpu.CompilerParams(vmem_limit_bytes=VMEM_LIMIT),
+        input_output_aliases=aliases or {},
+        compiler_params=pltpu.CompilerParams(vmem_limit_bytes=limit),
         cost_estimate=pl.CostEstimate(flops=cost, bytes_accessed=1 << 20, transcendentals=0),
     )(*args)
 
 
-def exchange_sum(x, axis, size, *partners):
-    got = [lax.ppermute(x, axis, [(i, i ^ m) for i in range(size)]) for m in partners]
-    return x + got[0] if len(got) == 1 else (x + got[0]) + (got[1] + got[2])
+def exchange_sum(x, axis, size, *steps):
+    for step in steps:
+        x = x + lax.ppermute(x, axis, [(i, i ^ step) for i in range(size)])
+    return x
 
 
 def by_heads(spans, parts, q_pre, k_pre, values, grad_out, segment_ids, q_gain, k_gain):
@@ -506,11 +504,11 @@
 
     messages = call_any(
         functools.partial(spread_kernel, "seq", parts, groups, heads, kv_heads),
-        [(sent, bf16, pl.ANY)] * (parts * groups),
+        [(sent, bf16, pltpu.HBM)] * (parts * groups),
         [vmem(q_shape, bf16), vmem(q_shape, bf16), vmem(k_shape, bf16), vmem(k_shape, bf16), vmem((1, block), jnp.int32)]
         + [vmem(q_shape, f32), vmem(q_shape, f32), vmem(k_shape, f32), vmem(k_shape, f32)]
         + [vmem((parts * groups, *sent), bf16), dma((5,)), dma((parts * groups,))],
-        1 << 20, q2, g2, k2, v2, segment_ids,
+        1 << 20, q2, g2, k2, v2, segment_ids, limit=62 * 1024 * 1024,
     )
     gains = jnp.concatenate([q_gain[None], k_gain[None], jnp.zeros((6, width), f32)], axis=0)
     xor = lambda m, size: [(i, i ^ m) for i in range(size)]
@@ -519,27 +517,26 @@
         + [lax.ppermute(messages[grp * parts + m], "seq", xor(m, parts)) for m in range(1, parts)]
         for grp in range(groups)
     ]
-    returned, shares = [], []
+    results, shares = [], []
     for grp in range(groups):
         *results, share = call_any(
-            functools.partial(heads_kernel, "seq", parts, per, group, back),
-            [(back_sent, bf16, pl.ANY)] * parts + [((8, width), f32, vmem)],
+            functools.partial(heads_kernel, "seq", parts, grp, per, group, back),
+            [((groups * back_sent[0], width), bf16, pltpu.HBM)] * parts + [((8, width), f32, vmem)],
             [vmem(inner.shape, f32), vmem(outer.shape, f32), vmem(gains.shape, f32)]
             + [vmem((parts, *sent), bf16), vmem((parts, *back_sent), bf16), dma((3 + parts,)), dma((parts,))],
-            1 << 30, inner, outer, gains, *arrived[grp],
+            1 << 34, *results, *arrived[grp], inner, outer, gains, aliases={m: m for m in range(len(results))},
         )
-        returned += [results[0]] + [lax.ppermute(results[m], "seq", xor(m, parts)) for m in range(1, parts)]
         shares.append(share)
+    returned = [results[0]] + [lax.ppermute(results[m], "seq", xor(m, parts)) for m in range(1, parts)]
     total = functools.reduce(jnp.add, shares)
-    total = exchange_sum(total, "dp", spans, 1)
-    total = exchange_sum(total, "seq", parts, 1, 2, 3)
-    total = exchange_sum(total, "dp", spans, 2, 4, 6)
+    total = exchange_sum(total, "dp", spans, 1, 2, 4)
+    total = exchange_sum(total, "seq", parts, 1, 2)
     grad_q, grad_k, grad_v = call_any(
         functools.partial(collect_kernel, "seq", parts, groups, heads, kv_heads),
-        [(q_shape, bf16, pl.ANY), (k_shape, bf16, pl.ANY), (k_shape, bf16, pl.ANY)],
-        [vmem((parts * groups, *back_sent), bf16)]
+        [(q_shape, bf16, pltpu.HBM), (k_shape, bf16, pltpu.HBM), (k_shape, bf16, pltpu.HBM)],
+        [vmem((parts, groups * back_sent[0], width), bf16)]
         + [vmem(q_shape, f32), vmem(k_shape, f32), vmem(k_shape, f32)]
-        + [vmem(q_shape, bf16), vmem(k_shape, bf16), vmem(k_shape, bf16), dma((parts * groups,)), dma((3,))],
+        + [vmem(q_shape, bf16), vmem(k_shape, bf16), vmem(k_shape, bf16), dma((parts,)), dma((3,))],
         1 << 20, *returned,
     )
     return (

time: 65 us -> 54.6 us (0.84)
  starting transfers between devices: 26.3 us -> 21.5 us
  local copies, waits for them, and re-layouts: 5.9 us -> 2.21 us
  Pallas kernels: 17.3 us -> 15.9 us
    ppermute x7 -> x5, waiting for transfers between devices: 4.23 us -> 9.53 us  [exchange_sum(): x = x + lax.ppermute(x, axis, [(i, i ^ step) for i in range(size)])]
    ppermute x6 -> x3, waiting for transfers between devices: 5.12 us -> 0.01 us  [by_heads(): lax.ppermute(results[m], 'seq', xor(m, parts))]
    ppermute x6 -> x3, starting transfers between devices: 7.28 us -> 3.55 us  [by_heads(): lax.ppermute(results[m], 'seq', xor(m, parts))]
    unnamed x18 -> x12, local copies, waits for them, and re-layouts: 5.31 us -> 1.61 us
    pallas_call x4, Pallas kernels: 17.3 us -> 15.9 us  [call_any(): pl.pallas_call(kernel, out_shape=[jax.ShapeDtypeStruct(s, t) for s, t, _...]
    ppermute x7 -> x5, starting transfers between devices: 7.95 us -> 6.96 us  [exchange_sum(): x = x + lax.ppermute(x, axis, [(i, i ^ step) for i in range(size)])]
    ppermute x6, waiting for transfers between devices: 5.12 us -> 4.43 us  [by_heads(): lax.ppermute(messages[grp * parts + m], 'seq', xor(m, parts))]
  transfers between devices with their start and end apart: 19 -> 14, of which waited for: 12 -> 8; matrix products, arithmetic and copies ran while one was open for 1% -> 1% of each run, Pallas kernels for 8% -> 10%
where the time goes in v3:
time: 54.6 us; the launch traced here: 54.5 us
  starting transfers between devices  21.5 us (39%)
  Pallas kernels  15.9 us (29%)
  waiting for transfers between devices  14 us (26%)
  local copies, waits for them, and re-layouts  2.21 us (4%)
  between operations  0.71 us (1%)
    pallas_call x4, Pallas kernels, call_any(): pl.pallas_call(kernel, out_shape=[jax.ShapeDtypeStruct(s, t) for s, t, _...  15.9 us
    ppermute x6, starting transfers between devices, by_heads(): lax.ppermute(messages[grp * parts + m], 'seq', xor(m, parts))  11 us
    ppermute x5, waiting for transfers between devices, exchange_sum(): x = x + lax.ppermute(x, axis, [(i, i ^ step) for i in range(size)])  9.53 us
    ppermute x5, starting transfers between devices, exchange_sum(): x = x + lax.ppermute(x, axis, [(i, i ^ step) for i in range(size)])  6.96 us
    ppermute x6, waiting for transfers between devices, by_heads(): lax.ppermute(messages[grp * parts + m], 'seq', xor(m, parts))  4.43 us
    ppermute x3, starting transfers between devices, by_heads(): lax.ppermute(results[m], 'seq', xor(m, parts))  3.55 us
    unnamed x12, local copies, waits for them, and re-layouts  1.61 us
  transfers between devices with their start and end apart: 14, of which 8 were waited for; matrix products, arithmetic and copies ran while one was open for 1% of the time, Pallas kernels for 10%

profile of v3, /device:TPU:0, one launch (start us, length us, event | category | flops | bytes accessed | tf_op | source)
XLA Modules:
  0.0 54.5 jit_solution(8043981097175263060)
XLA Ops:
  0.6 0.0 copy-start.2
  0.6 3.3 %shard_map.128 = (bf16[784,128]{1,0:T(8,128)(2,1)}, bf16[784,128]{1,0:T(8,128)(2,1)}, bf16[784,128]{1,0:T(8,128)(2,1)}, bf16[784,128]{1,0:T(8,128)(2,1)}, bf16[7...) custom-call(bf16[2048,128]{1,0:T(8,128)(2,1)} %bitcast.13, ...), custom_call_target="tpu_custom_call" | custom-call | flops 1048576 | bytes 1048576 | tf_op jit(solution)/shard_map/pallas_call | solution.py:470
  4.0 3.0 %collective-permute-start = (bf16[784,128]{1,0:T(8,128)(2,1)}, bf16[784,128]{1,0:T(8,128)(2,1)S(1)}, u32[]{:S(2)}, u32[]{:S(2)}) collective-permute-start(bf16[784,128]{1,0:T(8,128)(2,1)} %get-tuple-element.27), channel_id=1, source_target_pairs={{0,1},{1,0},{2,3},{3,2},{4,5},{5,4},{6,7},{7,6},{8,9},{9,8},{10,11... | collective-permute-start | bytes 602120 | tf_op jit(solution)/shard_map/ppermute | solution.py:517
  7.0 1.5 %collective-permute-start.1 = (bf16[784,128]{1,0:T(8,128)(2,1)}, bf16[784,128]{1,0:T(8,128)(2,1)S(1)}, u32[]{:S(2)}, u32[]{:S(2)}) collective-permute-start(bf16[784,128]{1,0:T(8,128)(2,1)} %get-tuple-element.28), channel_id=1, source_target_pairs={{0,2},{1,3},{2,0},{3,1},{4,6},{5,7},{6,4},{7,5},{8,10},{9,11},{10,... | collective-permute-start | bytes 602120 | tf_op jit(solution)/shard_map/ppermute | solution.py:517
  8.5 0.0 collective-permute-start.2
  8.5 1.9 %collective-permute-start.3 = (bf16[784,128]{1,0:T(8,128)(2,1)}, bf16[784,128]{1,0:T(8,128)(2,1)S(1)}, u32[]{:S(2)}, u32[]{:S(2)}) collective-permute-start(bf16[784,128]{1,0:T(8,128)(2,1)} %get-tuple-element.35), channel_id=1, source_target_pairs={{0,1},{1,0},{2,3},{3,2},{4,5},{5,4},{6,7},{7,6},{8,9},{9,8},{10,11... | collective-permute-start | bytes 602120 | tf_op jit(solution)/shard_map/ppermute | solution.py:517
  10.4 1.5 %collective-permute-start.4 = (bf16[784,128]{1,0:T(8,128)(2,1)}, bf16[784,128]{1,0:T(8,128)(2,1)S(1)}, u32[]{:S(2)}, u32[]{:S(2)}) collective-permute-start(bf16[784,128]{1,0:T(8,128)(2,1)} %get-tuple-element.36), channel_id=1, source_target_pairs={{0,2},{1,3},{2,0},{3,1},{4,6},{5,7},{6,4},{7,5},{8,10},{9,11},{10,... | collective-permute-start | bytes 602120 | tf_op jit(solution)/shard_map/ppermute | solution.py:517
  12.0 0.1 pad.2.clone
  12.0 0.0 copy-start.4
  12.0 0.0 copy-start.5
  12.1 0.7 %copy-done.4 = f32[128]{0:T(128)S(1)} copy-done((f32[128]{0:T(128)S(1)}, f32[128]{0:T(128)}, u32[]{:S(2)}) %copy-start.4) | copy-done | bytes 536
  12.7 0.0 copy-done.5
  12.7 0.0 copy-start.3
  12.7 0.1 maximum_maximum_fusion.rest_6_.rest_10_
  12.8 0.2 collective-permute-done.rest_1_
  13.0 3.0 %collective-permute-start.5 = (bf16[784,128]{1,0:T(8,128)(2,1)}, bf16[784,128]{1,0:T(8,128)(2,1)S(1)}, u32[]{:S(2)}, u32[]{:S(2)}) collective-permute-start(bf16[784,128]{1,0:T(8,128)(2,1)} %get-tuple-element.37), channel_id=1, source_target_pairs={{0,3},{1,2},{2,1},{3,0},{4,7},{5,6},{6,5},{7,4},{8,11},{9,10},{10,... | collective-permute-start | bytes 602120 | tf_op jit(solution)/shard_map/ppermute | solution.py:517
  16.0 3.4 %collective-permute-done.1.rest_2_ = bf16[784,128]{1,0:T(8,128)(2,1)S(1)} collective-permute-done((bf16[784,128]{1,0:T(8,128)(2,1)}, bf16[784,128]{1,0:T(8,128)(2,1)S(1)}, u32[]{:S(2)}, u32[]{:S(2)}) %collective-permute-start.1) | collective-permute-done | bytes 200736 | tf_op jit(solution)/shard_map/ppermute | solution.py:517
  19.4 0.0 collective-permute-done.2.rest_3_
  19.4 0.0 copy-done.2
  19.4 0.0 copy-done.3
  19.4 0.0 copy-start.1
  19.4 0.9 %copy-done.1 = bf16[784,128]{1,0:T(8,128)(2,1)S(1)} copy-done((bf16[784,128]{1,0:T(8,128)(2,1)S(1)}, bf16[784,128]{1,0:T(8,128)(2,1)}, u32[]{:S(2)}) %copy-start.1) | copy-done | bytes 200728
  20.3 0.0 copy-start
  20.3 5.3 %shard_map.129 = (bf16[1024,128]{1,0:T(8,128)(2,1)S(1)}, bf16[1024,128]{1,0:T(8,128)(2,1)S(1)}, bf16[1024,128]{1,0:T(8,128)(2,1)S(1)}, bf16[1024,128]{1,0:T(8,128)(2,1)S(1)}, f32[8,128]{1,0:T(8,128)S(1)}) custom-call(bf16[784,128]{1,0:T(8,128)(2,1)S(1)} %copy-done.1, bf16[784,128]{1,0:T(8,128)(2,1)S(1)} %collective-permute-done.rest_1_, ...), custom_call_target="tpu_custom_call" | custom-call | flops 17179869184 | bytes 1048576 | tf_op jit(solution)/shard_map/pallas_call | solution.py:470
  25.7 0.0 collective-permute-done.3.rest_5_
  25.7 0.8 %collective-permute-done.4.rest_6_ = bf16[784,128]{1,0:T(8,128)(2,1)S(1)} collective-permute-done((bf16[784,128]{1,0:T(8,128)(2,1)}, bf16[784,128]{1,0:T(8,128)(2,1)S(1)}, u32[]{:S(2)}, u32[]{:S(2)}) %collective-permute-start.4) | collective-permute-done | bytes 200736 | tf_op jit(solution)/shard_map/ppermute | solution.py:517
  26.5 0.0 collective-permute-done.5.rest_7_
  26.5 0.0 copy-done
  26.5 5.3 %shard_map.130 = (bf16[1024,128]{1,0:T(8,128)(2,1)S(1)}, bf16[1024,128]{1,0:T(8,128)(2,1)S(1)}, bf16[1024,128]{1,0:T(8,128)(2,1)S(1)}, bf16[1024,128]{1,0:T(8,128)(2,1)S(1)}, f32[8,128]{1,0:T(8,128)S(1)}) custom-call(bf16[1024,128]{1,0:T(8,128)(2,1)S(1)} %get-tuple-element.30.rest_0_, ...), custom_call_target="tpu_custom_call", output_to_operand_aliasing={{0}: (0, {}), {1}: (1, {}), {2}: (2, {}), {3}: (3, {})} | custom-call | flops 17179869184 | bytes 1048576 | tf_op jit(solution)/shard_map/pallas_call | solution.py:470
  31.9 1.3 %collective-permute-start.6 = (bf16[1024,128]{1,0:T(8,128)(2,1)S(1)}, bf16[1024,128]{1,0:T(8,128)(2,1)S(1)}, u32[]{:S(2)}, u32[]{:S(2)}) collective-permute-start(bf16[1024,128]{1,0:T(8,128)(2,1)S(1)} %get-tuple-element.39), channel_id=1, source_target_pairs={{0,1},{1,0},{2,3},{3,2},{4,5},{5,4},{6,7},{7,6},{8,9},{9,8},{10,11... | collective-permute-start | bytes 786440 | tf_op jit(solution)/shard_map/ppermute | solution.py:530
  33.2 0.8 %collective-permute-start.7 = (bf16[1024,128]{1,0:T(8,128)(2,1)S(1)}, bf16[1024,128]{1,0:T(8,128)(2,1)S(1)}, u32[]{:S(2)}, u32[]{:S(2)}) collective-permute-start(bf16[1024,128]{1,0:T(8,128)(2,1)S(1)} %get-tuple-element.40), channel_id=1, source_target_pairs={{0,2},{1,3},{2,0},{3,1},{4,6},{5,7},{6,4},{7,5},{8,10},{9,11},{10,... | collective-permute-start | bytes 786440 | tf_op jit(solution)/shard_map/ppermute | solution.py:530
  34.0 1.4 %collective-permute-start.8 = (bf16[1024,128]{1,0:T(8,128)(2,1)S(1)}, bf16[1024,128]{1,0:T(8,128)(2,1)S(1)}, u32[]{:S(2)}, u32[]{:S(2)}) collective-permute-start(bf16[1024,128]{1,0:T(8,128)(2,1)S(1)} %get-tuple-element.41), channel_id=1, source_target_pairs={{0,3},{1,2},{2,1},{3,0},{4,7},{5,6},{6,5},{7,4},{8,11},{9,10},{10,... | collective-permute-start | bytes 786440 | tf_op jit(solution)/shard_map/ppermute | solution.py:530
  35.4 0.0 collective-permute-start.9
  35.4 1.2 %collective-permute-done.9 = f32[8,128]{1,0:T(8,128)S(1)} collective-permute-done((f32[8,128]{1,0:T(8,128)S(1)}, f32[8,128]{1,0:T(8,128)S(1)}, u32[]{:S(2)}, u32[]{:S(2)}) %collective-permute-start.9) | collective-permute-done | bytes 4128 | tf_op jit(solution)/shard_map/ppermute | solution.py:484
  36.6 1.6 %collective-permute-start.10 = (f32[8,128]{1,0:T(8,128)S(1)}, f32[8,128]{1,0:T(8,128)S(1)}, u32[]{:S(2)}, u32[]{:S(2)}) collective-permute-start(f32[8,128]{1,0:T(8,128)S(1)} %add.19), channel_id=1, source_target_pairs={{0,8},{4,12},{8,0},{12,4},{16,24},{20,28},{24,16},{28,20},{1,9},{5... | collective-permute-start | bytes 12296 | tf_op jit(solution)/shard_map/ppermute | solution.py:484
  38.2 2.0 %collective-permute-done.10 = f32[8,128]{1,0:T(8,128)S(1)} collective-permute-done((f32[8,128]{1,0:T(8,128)S(1)}, f32[8,128]{1,0:T(8,128)S(1)}, u32[]{:S(2)}, u32[]{:S(2)}) %collective-permute-start.10) | collective-permute-done | bytes 4128 | tf_op jit(solution)/shard_map/ppermute | solution.py:484
  40.2 2.6 %collective-permute-start.11 = (f32[8,128]{1,0:T(8,128)S(1)}, f32[8,128]{1,0:T(8,128)S(1)}, u32[]{:S(2)}, u32[]{:S(2)}) collective-permute-start(f32[8,128]{1,0:T(8,128)S(1)} %add.20), channel_id=1, source_target_pairs={{0,16},{4,20},{8,24},{12,28},{16,0},{20,4},{24,8},{28,12},{1,17},{... | collective-permute-start | bytes 12296 | tf_op jit(solution)/shard_map/ppermute | solution.py:484
  42.8 1.9 %collective-permute-done.11 = f32[8,128]{1,0:T(8,128)S(1)} collective-permute-done((f32[8,128]{1,0:T(8,128)S(1)}, f32[8,128]{1,0:T(8,128)S(1)}, u32[]{:S(2)}, u32[]{:S(2)}) %collective-permute-start.11) | collective-permute-done | bytes 4128 | tf_op jit(solution)/shard_map/ppermute | solution.py:484
  44.7 1.3 %collective-permute-start.12 = (f32[8,128]{1,0:T(8,128)S(1)}, f32[8,128]{1,0:T(8,128)S(1)}, u32[]{:S(2)}, u32[]{:S(2)}) collective-permute-start(f32[8,128]{1,0:T(8,128)S(1)} %add.21), channel_id=1, source_target_pairs={{0,1},{1,0},{2,3},{3,2},{4,5},{5,4},{6,7},{7,6},{8,9},{9,8},{10,11... | collective-permute-start | bytes 12296 | tf_op jit(solution)/shard_map/ppermute | solution.py:484
  46.0 2.3 %collective-permute-done.12 = f32[8,128]{1,0:T(8,128)S(1)} collective-permute-done((f32[8,128]{1,0:T(8,128)S(1)}, f32[8,128]{1,0:T(8,128)S(1)}, u32[]{:S(2)}, u32[]{:S(2)}) %collective-permute-start.12) | collective-permute-done | bytes 4128 | tf_op jit(solution)/shard_map/ppermute | solution.py:484
  48.3 1.5 %collective-permute-start.13 = (f32[8,128]{1,0:T(8,128)S(1)}, f32[8,128]{1,0:T(8,128)S(1)}, u32[]{:S(2)}, u32[]{:S(2)}) collective-permute-start(f32[8,128]{1,0:T(8,128)S(1)} %add.22), channel_id=1, source_target_pairs={{0,2},{1,3},{2,0},{3,1},{4,6},{5,7},{6,4},{7,5},{8,10},{9,11},{10,... | collective-permute-start | bytes 12296 | tf_op jit(solution)/shard_map/ppermute | solution.py:484
  49.9 2.1 %collective-permute-done.13 = f32[8,128]{1,0:T(8,128)S(1)} collective-permute-done((f32[8,128]{1,0:T(8,128)S(1)}, f32[8,128]{1,0:T(8,128)S(1)}, u32[]{:S(2)}, u32[]{:S(2)}) %collective-permute-start.13) | collective-permute-done | bytes 4128 | tf_op jit(solution)/shard_map/ppermute | solution.py:484
  52.0 0.5 slice_bitcast_fusion
  52.5 0.0 collective-permute-done.6.rest_1_
  52.5 0.0 collective-permute-done.7.rest_2_
  52.5 0.0 collective-permute-done.8.rest_3_
  52.5 2.0 %shard_map.131 = (bf16[2048,128]{1,0:T(8,128)(2,1)}, bf16[1024,128]{1,0:T(8,128)(2,1)}, bf16[1024,128]{1,0:T(8,128)(2,1)}) custom-call(bf16[1024,128]{1,0:T(8,128)(2,1)S(1)} %get-tuple-element.38.rest_0_, bf16[1024,128]{1,0:T(8,128)(2,1)S(1)} %collective-permute-done.6.rest_1_, bf16[1024,128]{1,0:T(8,128)(2,1)S(1)} %collective-permute-done.7.rest_2_, ...), custom_call_target="tpu_custom_call" | custom-call | flops 1048576 | bytes 1048576 | tf_op jit(solution)/shard_map/pallas_call | solution.py:470
  (7 shorter events, 0.0 us)
Async XLA Ops:
  0.6 18.8 %copy-start.2 = (f32[2,128,128]{2,1,0:T(8,128)S(1)}, f32[2,128,128]{2,1,0:T(8,128)}, u32[]{:S(2)}) copy-start(f32[2,128,128]{2,1,0:T(8,128)} %constant.6.clone.rest_4_.rest_8_) | copy-start | bytes 393220
  4.0 9.0 %collective-permute-start = (bf16[784,128]{1,0:T(8,128)(2,1)}, bf16[784,128]{1,0:T(8,128)(2,1)S(1)}, u32[]{:S(2)}, u32[]{:S(2)}) collective-permute-start(bf16[784,128]{1,0:T(8,128)(2,1)} %get-tuple-element.27), channel_id=1, source_target_pairs={{0,1},{1,0},{2,3},{3,2},{4,5},{5,4},{6,7},{7,6},{8,9},{9,8},{10,11... | collective-permute-start | bytes 602120 | tf_op jit(solution)/shard_map/ppermute | solution.py:517
  7.0 12.4 %collective-permute-start.1 = (bf16[784,128]{1,0:T(8,128)(2,1)}, bf16[784,128]{1,0:T(8,128)(2,1)S(1)}, u32[]{:S(2)}, u32[]{:S(2)}) collective-permute-start(bf16[784,128]{1,0:T(8,128)(2,1)} %get-tuple-element.28), channel_id=1, source_target_pairs={{0,2},{1,3},{2,0},{3,1},{4,6},{5,7},{6,4},{7,5},{8,10},{9,11},{10,... | collective-permute-start | bytes 602120 | tf_op jit(solution)/shard_map/ppermute | solution.py:517
  8.5 10.9 %collective-permute-start.2 = (bf16[784,128]{1,0:T(8,128)(2,1)}, bf16[784,128]{1,0:T(8,128)(2,1)S(1)}, u32[]{:S(2)}, u32[]{:S(2)}) collective-permute-start(bf16[784,128]{1,0:T(8,128)(2,1)} %get-tuple-element.29), channel_id=1, source_target_pairs={{0,3},{1,2},{2,1},{3,0},{4,7},{5,6},{6,5},{7,4},{8,11},{9,10},{10,... | collective-permute-start | bytes 602120 | tf_op jit(solution)/shard_map/ppermute | solution.py:517
  8.5 17.2 %collective-permute-start.3 = (bf16[784,128]{1,0:T(8,128)(2,1)}, bf16[784,128]{1,0:T(8,128)(2,1)S(1)}, u32[]{:S(2)}, u32[]{:S(2)}) collective-permute-start(bf16[784,128]{1,0:T(8,128)(2,1)} %get-tuple-element.35), channel_id=1, source_target_pairs={{0,1},{1,0},{2,3},{3,2},{4,5},{5,4},{6,7},{7,6},{8,9},{9,8},{10,11... | collective-permute-start | bytes 602120 | tf_op jit(solution)/shard_map/ppermute | solution.py:517
  10.4 16.1 %collective-permute-start.4 = (bf16[784,128]{1,0:T(8,128)(2,1)}, bf16[784,128]{1,0:T(8,128)(2,1)S(1)}, u32[]{:S(2)}, u32[]{:S(2)}) collective-permute-start(bf16[784,128]{1,0:T(8,128)(2,1)} %get-tuple-element.36), channel_id=1, source_target_pairs={{0,2},{1,3},{2,0},{3,1},{4,6},{5,7},{6,4},{7,5},{8,10},{9,11},{10,... | collective-permute-start | bytes 602120 | tf_op jit(solution)/shard_map/ppermute | solution.py:517
  12.0 0.7 %copy-start.4 = (f32[128]{0:T(128)S(1)}, f32[128]{0:T(128)}, u32[]{:S(2)}) copy-start(f32[128]{0:T(128)} %param.15) | copy-start | bytes 1540
  12.0 0.7 %copy-start.5 = (f32[128]{0:T(128)S(1)}, f32[128]{0:T(128)}, u32[]{:S(2)}) copy-start(f32[128]{0:T(128)} %param.14) | copy-start | bytes 1540
  12.7 6.7 %copy-start.3 = (f32[4,2,128]{2,1,0:T(2,128)S(1)}, f32[4,2,128]{2,1,0:T(2,128)}, u32[]{:S(2)}) copy-start(f32[4,2,128]{2,1,0:T(2,128)} %constant.7.clone.rest_5_.rest_9_) | copy-start | bytes 12292
  13.0 13.5 %collective-permute-start.5 = (bf16[784,128]{1,0:T(8,128)(2,1)}, bf16[784,128]{1,0:T(8,128)(2,1)S(1)}, u32[]{:S(2)}, u32[]{:S(2)}) collective-permute-start(bf16[784,128]{1,0:T(8,128)(2,1)} %get-tuple-element.37), channel_id=1, source_target_pairs={{0,3},{1,2},{2,1},{3,0},{4,7},{5,6},{6,5},{7,4},{8,11},{9,10},{10,... | collective-permute-start | bytes 602120 | tf_op jit(solution)/shard_map/ppermute | solution.py:517
  19.4 0.9 %copy-start.1 = (bf16[784,128]{1,0:T(8,128)(2,1)S(1)}, bf16[784,128]{1,0:T(8,128)(2,1)}, u32[]{:S(2)}) copy-start(bf16[784,128]{1,0:T(8,128)(2,1)} %get-tuple-element.26.rest_0_) | copy-start | bytes 602116
  20.3 6.2 %copy-start = (bf16[784,128]{1,0:T(8,128)(2,1)S(1)}, bf16[784,128]{1,0:T(8,128)(2,1)}, u32[]{:S(2)}) copy-start(bf16[784,128]{1,0:T(8,128)(2,1)} %get-tuple-element.34.rest_4_) | copy-start | bytes 602116
  31.9 20.6 %collective-permute-start.6 = (bf16[1024,128]{1,0:T(8,128)(2,1)S(1)}, bf16[1024,128]{1,0:T(8,128)(2,1)S(1)}, u32[]{:S(2)}, u32[]{:S(2)}) collective-permute-start(bf16[1024,128]{1,0:T(8,128)(2,1)S(1)} %get-tuple-element.39), channel_id=1, source_target_pairs={{0,1},{1,0},{2,3},{3,2},{4,5},{5,4},{6,7},{7,6},{8,9},{9,8},{10,11... | collective-permute-start | bytes 786440 | tf_op jit(solution)/shard_map/ppermute | solution.py:530
  33.2 19.3 %collective-permute-start.7 = (bf16[1024,128]{1,0:T(8,128)(2,1)S(1)}, bf16[1024,128]{1,0:T(8,128)(2,1)S(1)}, u32[]{:S(2)}, u32[]{:S(2)}) collective-permute-start(bf16[1024,128]{1,0:T(8,128)(2,1)S(1)} %get-tuple-element.40), channel_id=1, source_target_pairs={{0,2},{1,3},{2,0},{3,1},{4,6},{5,7},{6,4},{7,5},{8,10},{9,11},{10,... | collective-permute-start | bytes 786440 | tf_op jit(solution)/shard_map/ppermute | solution.py:530
  34.0 18.5 %collective-permute-start.8 = (bf16[1024,128]{1,0:T(8,128)(2,1)S(1)}, bf16[1024,128]{1,0:T(8,128)(2,1)S(1)}, u32[]{:S(2)}, u32[]{:S(2)}) collective-permute-start(bf16[1024,128]{1,0:T(8,128)(2,1)S(1)} %get-tuple-element.41), channel_id=1, source_target_pairs={{0,3},{1,2},{2,1},{3,0},{4,7},{5,6},{6,5},{7,4},{8,11},{9,10},{10,... | collective-permute-start | bytes 786440 | tf_op jit(solution)/shard_map/ppermute | solution.py:530
  35.4 1.2 %collective-permute-start.9 = (f32[8,128]{1,0:T(8,128)S(1)}, f32[8,128]{1,0:T(8,128)S(1)}, u32[]{:S(2)}, u32[]{:S(2)}) collective-permute-start(f32[8,128]{1,0:T(8,128)S(1)} %add.18), channel_id=1, source_target_pairs={{0,4},{4,0},{8,12},{12,8},{16,20},{20,16},{24,28},{28,24},{1,5},{5... | collective-permute-start | bytes 12296 | tf_op jit(solution)/shard_map/ppermute | solution.py:484
  36.6 3.6 %collective-permute-start.10 = (f32[8,128]{1,0:T(8,128)S(1)}, f32[8,128]{1,0:T(8,128)S(1)}, u32[]{:S(2)}, u32[]{:S(2)}) collective-permute-start(f32[8,128]{1,0:T(8,128)S(1)} %add.19), channel_id=1, source_target_pairs={{0,8},{4,12},{8,0},{12,4},{16,24},{20,28},{24,16},{28,20},{1,9},{5... | collective-permute-start | bytes 12296 | tf_op jit(solution)/shard_map/ppermute | solution.py:484
  40.2 4.5 %collective-permute-start.11 = (f32[8,128]{1,0:T(8,128)S(1)}, f32[8,128]{1,0:T(8,128)S(1)}, u32[]{:S(2)}, u32[]{:S(2)}) collective-permute-start(f32[8,128]{1,0:T(8,128)S(1)} %add.20), channel_id=1, source_target_pairs={{0,16},{4,20},{8,24},{12,28},{16,0},{20,4},{24,8},{28,12},{1,17},{... | collective-permute-start | bytes 12296 | tf_op jit(solution)/shard_map/ppermute | solution.py:484
  44.7 3.6 %collective-permute-start.12 = (f32[8,128]{1,0:T(8,128)S(1)}, f32[8,128]{1,0:T(8,128)S(1)}, u32[]{:S(2)}, u32[]{:S(2)}) collective-permute-start(f32[8,128]{1,0:T(8,128)S(1)} %add.21), channel_id=1, source_target_pairs={{0,1},{1,0},{2,3},{3,2},{4,5},{5,4},{6,7},{7,6},{8,9},{9,8},{10,11... | collective-permute-start | bytes 12296 | tf_op jit(solution)/shard_map/ppermute | solution.py:484
  48.3 3.6 %collective-permute-start.13 = (f32[8,128]{1,0:T(8,128)S(1)}, f32[8,128]{1,0:T(8,128)S(1)}, u32[]{:S(2)}, u32[]{:S(2)}) collective-permute-start(f32[8,128]{1,0:T(8,128)S(1)} %add.22), channel_id=1, source_target_pairs={{0,2},{1,3},{2,0},{3,1},{4,6},{5,7},{6,4},{7,5},{8,10},{9,11},{10,... | collective-permute-start | bytes 12296 | tf_op jit(solution)/shard_map/ppermute | solution.py:484

commit v4 on v1

--- a/solution.py
+++ b/solution.py
@@ -17,6 +17,8 @@
 SCALE = float(PRESCALE) ** (-0.5)
 LOG2E = 1.4426950408889634
 VMEM_LIMIT = 48 * 1024 * 1024
+HEADS_VMEM = 24 * 1024 * 1024
+SPREAD_VMEM = 61 * 1024 * 1024
 NT = (((1,), (1,)), ((), ()))
 TN = (((0,), (0,)), ((), ()))
 
@@ -222,7 +224,7 @@
     return x
 
 
-def body(spans, parts, q_pre, k_pre, values, grad_out, segment_ids, q_gain, k_gain):
+def by_tokens(spans, parts, q_pre, k_pre, values, grad_out, segment_ids, q_gain, k_gain):
     block, heads, width = q_pre.shape[1:]
     kv_heads = k_pre.shape[2]
     group = heads // kv_heads
@@ -287,10 +289,287 @@
     )
 
 
+def spread_kernel(axis, parts, groups, heads, kv_heads, q_hbm, g_hbm, k_hbm, v_hbm, seg_hbm, *rest):
+    outs = rest[: parts * groups]
+    q_in, g_in, k_in, v_in, seg_in, q_f32, g_f32, k_f32, v_f32, sems = rest[parts * groups :]
+    block = seg_in.shape[1]
+    group = heads // kv_heads
+    per = kv_heads // parts // groups
+    me = lax.axis_index(axis)
+    pairs = [(seg_hbm, seg_in)]
+    for src, dst in ((k_hbm, k_in), (v_hbm, v_in), (q_hbm, q_in), (g_hbm, g_in)):
+        half = dst.shape[0] // 2
+        pairs += [(src.at[pl.ds(i * half, half)], dst.at[pl.ds(i * half, half)]) for i in range(2)]
+    loads = [pltpu.make_async_copy(src, dst, sems.at[i]) for i, (src, dst) in enumerate(pairs)]
+    for copy in loads:
+        copy.start()
+    loads[0].wait()
+    ids = jnp.broadcast_to(seg_in[...].astype(jnp.float32), (16, block)).astype(jnp.bfloat16)
+    for n, (src, dst) in enumerate(((k_in, k_f32), (v_in, v_f32), (q_in, q_f32), (g_in, g_f32))):
+        half = dst.shape[0] // 2
+        for i in range(2):
+            loads[1 + 2 * n + i].wait()
+            dst[pl.ds(i * half, half), :] = src[pl.ds(i * half, half), :].astype(jnp.float32)
+    for grp in range(groups):
+        for m in range(parts):
+            out = outs[grp * parts + m]
+            at = 0
+            for p in range(per):
+                kv = ((me ^ m) * groups + grp) * per + p
+                pieces = [(q_f32, kv * group + i, heads) for i in range(group)]
+                pieces += [(g_f32, kv * group + i, heads) for i in range(group)]
+                pieces += [(k_f32, kv, kv_heads), (v_f32, kv, kv_heads)]
+                for src, head, stride in pieces:
+                    rows = src[pl.ds(head, block, stride=stride), :]
+                    out[pl.ds(at, block), :] = rows.astype(jnp.bfloat16)
+                    at += block
+            out[pl.ds(at, 16), :] = ids
+
+
+def eye(size):
+    row = lax.broadcasted_iota(jnp.int32, (size, size), 0)
+    return (row == lax.broadcasted_iota(jnp.int32, (size, size), 1)).astype(jnp.bfloat16)
+
+
+def turned(x, unit):
+    return lax.dot_general(unit, x, NT, preferred_element_type=jnp.float32)
+
+
+def heads_kernel(axis, parts, grp, per, group, back, *rest):
+    earlier, msgs = rest[: grp * parts], rest[grp * parts : grp * parts + parts]
+    table_ref, gains_ref = rest[parts + grp * parts : parts + grp * parts + 2]
+    outs = rest[-parts - 12 : -12]
+    share_ref, qt_ref, kt_ref, k_ref, v_ref, g_ref, qn_ref, kn_ref, qs_ref, ks_ref, id_ref, res_ref = rest[-12:]
+    block, width = table_ref.shape[3], msgs[0].shape[1]
+    half = width // 2
+    rows = group * block
+    f32, bf16 = jnp.float32, jnp.bfloat16
+    me = lax.axis_index(axis)
+    unit, unit_rows = eye(width), eye(rows)
+    q_gain = jnp.broadcast_to(gains_ref[0:1, :], (width, width)).T
+    k_gain = jnp.broadcast_to(gains_ref[1:2, :], (width, width)).T
+    q_gain = jnp.concatenate([q_gain] * group, axis=1)
+    last = per * (2 * group + 2) * block
+
+    def rotated(x, c, s):
+        a, b = x[:half], x[half:]
+        return jnp.concatenate([a * c - b * s, b * c + a * s], axis=0)
+
+    def embed(x, gain, c, s):
+        scale = lax.rsqrt(jnp.sum(x * x, axis=0, keepdims=True) * (1.0 / width) + EPS)
+        normed = x * scale
+        return rotated(normed * gain, c, s).astype(bf16), normed, scale
+
+    def embed_back(dy, gain, c, s, normed, scale):
+        dr = rotated(dy, c, -s)
+        share = dr * normed
+        dn = dr * gain
+        mean = jnp.sum(dn * normed, axis=0, keepdims=True) * (1.0 / width)
+        return ((scale * SCALE) * (dn - normed * mean)).astype(bf16), share
+
+    def rope(b, copies):
+        c, s = table_ref[b, 0], table_ref[b, 1]
+        return jnp.concatenate([c] * copies, axis=1), jnp.concatenate([s] * copies, axis=1)
+
+    for m in range(parts):
+        b = me ^ m
+        id_ref[b] = jnp.broadcast_to(msgs[m][pl.ds(last, 16), :].astype(f32)[0:1, :], (8, block))
+        for p in range(per):
+            base = p * (2 * group + 2) * block
+            at = b * per + p
+            y, normed, scale = embed(turned(msgs[m][pl.ds(base, rows), :], unit), q_gain, *rope(b, group))
+            qt_ref[at], qn_ref[at], qs_ref[at] = y, normed, jnp.broadcast_to(scale, (8, rows))
+            g_ref[at] = msgs[m][pl.ds(base + rows, rows), :]
+            y, normed, scale = embed(turned(msgs[m][pl.ds(base + 2 * rows, block), :], unit), k_gain, *rope(b, 1))
+            kt_ref[at], kn_ref[at], ks_ref[at] = y, normed, jnp.broadcast_to(scale, (8, block))
+            k_ref[at] = turned(y, unit).astype(bf16)
+            v_ref[at] = msgs[m][pl.ds(base + 2 * rows + block, block), :]
+
+    id_rows = [id_ref[b][0:1, :] for b in range(parts)]
+    id_columns = [turned(jnp.broadcast_to(row, (block, block)).astype(bf16), unit) for row in id_rows]
+    key_at = lax.broadcasted_iota(jnp.int32, (block, block), 0)
+    query_at = lax.broadcasted_iota(jnp.int32, (block, block), 1)
+    causal = jnp.where(key_at <= query_at, 0.0, NEG)
+
+    def bias(key_block, query_block):
+        value = jnp.where(id_columns[key_block] == id_rows[query_block], 0.0, NEG)
+        if key_block == query_block:
+            value = value + causal
+        return jnp.concatenate([value] * group, axis=1)
+
+    q_total = jnp.zeros((width, rows), f32)
+    k_total = jnp.zeros((width, block), f32)
+    for p in range(per):
+        out_base = p * (group + 2) * block
+        dk = [None] * parts
+        dv = [None] * parts
+        for b in range(parts):
+            span = range(max(0, b - back), b + 1)
+            qt, g = qt_ref[b * per + p], g_ref[b * per + p]
+            k = jnp.concatenate([k_ref[j * per + p] for j in span], axis=0)
+            kt = jnp.concatenate([kt_ref[j * per + p] for j in span], axis=1)
+            v = jnp.concatenate([v_ref[j * per + p] for j in span], axis=0)
+            hidden = jnp.concatenate([bias(j, b) for j in span], axis=0)
+            scores = jnp.dot(k, qt, preferred_element_type=f32)
+            expo = jnp.exp2(scores * (SCALE * LOG2E) + hidden)
+            prob_grads = lax.dot_general(v, g, NT, preferred_element_type=f32)
+            inverse = 1.0 / jnp.sum(expo, axis=0, keepdims=True)
+            delta = jnp.sum(expo * prob_grads, axis=0, keepdims=True) * inverse
+            probs = expo * inverse
+            score_grads = (probs * (prob_grads - delta)).astype(bf16)
+            dvs = jnp.dot(probs.astype(bf16), g, preferred_element_type=f32)
+            dks = lax.dot_general(qt, score_grads, NT, preferred_element_type=f32)
+            dq = jnp.dot(kt, score_grads, preferred_element_type=f32)
+            for i, j in enumerate(span):
+                cut = slice(i * block, (i + 1) * block)
+                dk[j] = dks[:, cut] if dk[j] is None else dk[j] + dks[:, cut]
+                dv[j] = dvs[cut] if dv[j] is None else dv[j] + dvs[cut]
+            at = b * per + p
+            dx, share = embed_back(dq, q_gain, *rope(b, group), qn_ref[at], qs_ref[at][0:1, :])
+            q_total = q_total + share
+            res_ref[b, pl.ds(out_base, rows), :] = turned(dx, unit_rows).astype(bf16)
+        for b in range(parts):
+            at = b * per + p
+            dx, share = embed_back(dk[b], k_gain, *rope(b, 1), kn_ref[at], ks_ref[at][0:1, :])
+            k_total = k_total + share
+            res_ref[b, pl.ds(out_base + rows, block), :] = turned(dx, unit).astype(bf16)
+            res_ref[b, pl.ds(out_base + rows + block, block), :] = dv[b].astype(bf16)
+    size = res_ref.shape[1]
+    for m in range(parts):
+        for i in range(grp):
+            outs[m][pl.ds(i * size, size), :] = earlier[i * parts + m][...]
+        outs[m][pl.ds(grp * size, size), :] = res_ref[me ^ m]
+    ones = jnp.ones((8, rows), f32)
+    exact = functools.partial(
+        lax.dot_general, dimension_numbers=NT, precision=lax.Precision.HIGHEST, preferred_element_type=f32
+    )
+    q_share, k_share = exact(ones, q_total), exact(ones[:, :block], k_total)
+    row = lax.broadcasted_iota(jnp.int32, (8, width), 0)
+    share_ref[...] = jnp.where(row == 0, q_share, jnp.where(row == 1, k_share, 0.0)) * SCALE
+
+
+def collect_kernel(axis, parts, groups, heads, kv_heads, *rest):
+    msgs = rest[:parts]
+    gq_hbm, gk_hbm, gv_hbm, q_f32, k_f32, v_f32, q_out, k_out, v_out, sems = rest[parts:]
+    group = heads // kv_heads
+    per = kv_heads // parts // groups
+    block = q_out.shape[0] // heads
+    me = lax.axis_index(axis)
+    for m in range(parts):
+        at = 0
+        for grp in range(groups):
+            for p in range(per):
+                kv = ((me ^ m) * groups + grp) * per + p
+                pieces = [(q_f32, kv * group + i, heads) for i in range(group)]
+                pieces += [(k_f32, kv, kv_heads), (v_f32, kv, kv_heads)]
+                for dst, head, stride in pieces:
+                    rows = msgs[m][pl.ds(at, block), :].astype(jnp.float32)
+                    dst[pl.ds(head, block, stride=stride), :] = rows
+                    at += block
+    stores = []
+    for src, out, dst in ((q_f32, q_out, gq_hbm), (k_f32, k_out, gk_hbm), (v_f32, v_out, gv_hbm)):
+        half = out.shape[0] // 2
+        for i in range(2):
+            cut = pl.ds(i * half, half)
+            out[cut, :] = src[cut, :].astype(jnp.bfloat16)
+            copy = pltpu.make_async_copy(out.at[cut], dst.at[cut], sems.at[len(stores)])
+            copy.start()
+            stores.append(copy)
+    for copy in stores:
+        copy.wait()
+
+
+def call_in(kernel, ins, outs, scratch, cost, *args, limit=HEADS_VMEM):
+    return pl.pallas_call(
+        kernel,
+        out_shape=[jax.ShapeDtypeStruct(s, t) for s, t, _ in outs],
+        in_specs=[pl.BlockSpec(memory_space=m) for m in ins],
+        out_specs=[pl.BlockSpec(memory_space=m) for _, _, m in outs],
+        scratch_shapes=scratch,
+        compiler_params=pltpu.CompilerParams(vmem_limit_bytes=limit),
+        cost_estimate=pl.CostEstimate(flops=cost, bytes_accessed=1 << 20, transcendentals=0),
+    )(*args)
+
+
+def exchange_sum(x, axis, size, *partners):
+    got = [lax.ppermute(x, axis, [(i, i ^ m) for i in range(size)]) for m in partners]
+    return x + got[0] if len(got) == 1 else (x + got[0]) + (got[1] + got[2])
+
+
+def by_heads(spans, parts, q_pre, k_pre, values, grad_out, segment_ids, q_gain, k_gain):
+    block, heads, width = q_pre.shape[1:]
+    kv_heads = k_pre.shape[2]
+    group = heads // kv_heads
+    groups = min(GROUPS, kv_heads // parts)
+    per = kv_heads // parts // groups
+    rows = group * block
+    longest = parts * block // 2
+    back = min(parts - 1, (longest - 2) // block + 1)
+    bf16, f32, vmem, hbm = jnp.bfloat16, jnp.float32, pltpu.VMEM, pltpu.HBM
+    freqs = ROPE_BASE ** (-(np.arange(width // 2, dtype=np.float64) * 2.0 / width))
+    angles = (np.arange(parts * block) / ROPE_FACTOR).reshape(parts, 1, block) * freqs[:, None]
+    table = jnp.asarray(np.stack([np.cos(angles), np.sin(angles)], axis=1).astype(np.float32))
+    q2, g2 = (x.reshape(block * heads, width) for x in (q_pre, grad_out))
+    k2, v2 = (x.reshape(block * kv_heads, width) for x in (k_pre, values))
+    sent = (per * (2 * group + 2) * block + 16, width)
+    back_sent = (per * (group + 2) * block, width)
+    dma = pltpu.SemaphoreType.DMA
+    q_shape, k_shape = q2.shape, k2.shape
+
+    messages = call_in(
+        functools.partial(spread_kernel, "seq", parts, groups, heads, kv_heads),
+        [hbm] * 5, [(sent, bf16, vmem)] * (parts * groups),
+        [vmem(q_shape, bf16), vmem(q_shape, bf16), vmem(k_shape, bf16), vmem(k_shape, bf16), vmem((1, block), jnp.int32)]
+        + [vmem(q_shape, f32), vmem(q_shape, f32), vmem(k_shape, f32), vmem(k_shape, f32), dma((9,))],
+        1 << 20, q2, g2, k2, v2, segment_ids, limit=SPREAD_VMEM,
+    )
+    gains = jnp.concatenate([q_gain[None], k_gain[None], jnp.zeros((6, width), f32)], axis=0)
+    xor = lambda m, size: [(i, i ^ m) for i in range(size)]
+    arrived = [
+        [messages[grp * parts]]
+        + [lax.ppermute(messages[grp * parts + m], "seq", xor(m, parts)) for m in range(1, parts)]
+        for grp in range(groups)
+    ]
+    results, shares = [], []
+    for grp in range(groups):
+        inputs = [*results, *arrived[grp], table, gains]
+        *made, share = call_in(
+            functools.partial(heads_kernel, "seq", parts, grp, per, group, back),
+            [vmem] * len(inputs),
+            [(((grp + 1) * back_sent[0], width), bf16, vmem)] * parts + [((8, width), f32, vmem)],
+            [vmem((parts * per, width, rows), bf16), vmem((parts * per, width, block), bf16)]
+            + [vmem((parts * per, block, width), bf16), vmem((parts * per, block, width), bf16)]
+            + [vmem((parts * per, rows, width), bf16)]
+            + [vmem((parts * per, width, rows), f32), vmem((parts * per, width, block), f32)]
+            + [vmem((parts * per, 8, rows), f32), vmem((parts * per, 8, block), f32), vmem((parts, 8, block), f32)]
+            + [vmem((parts, *back_sent), bf16)],
+            1 << 34, *inputs,
+        )
+        results = made
+        shares.append(share)
+    first, second, third = (lax.ppermute(results[m], "seq", xor(m, parts)) for m in (1, 2, 3))
+    total = exchange_sum(functools.reduce(jnp.add, shares), "dp", spans, 1)
+    total = exchange_sum(exchange_sum(total, "dp", spans, 2), "dp", spans, 4)
+    total, first, second = lax.optimization_barrier((total, first, second))
+    total = exchange_sum(total, "seq", parts, 1, 2, 3)
+    grad_q, grad_k, grad_v = call_in(
+        functools.partial(collect_kernel, "seq", parts, groups, heads, kv_heads),
+        [vmem] * parts, [(q_shape, bf16, hbm), (k_shape, bf16, hbm), (k_shape, bf16, hbm)],
+        [vmem(q_shape, f32), vmem(k_shape, f32), vmem(k_shape, f32)]
+        + [vmem(q_shape, bf16), vmem(k_shape, bf16), vmem(k_shape, bf16), dma((6,))],
+        1 << 20, results[0], first, second, third,
+    )
+    return (
+        grad_q.reshape(q_pre.shape), grad_k.reshape(k_pre.shape), grad_v.reshape(values.shape), total[0], total[1],
+    )
+
+
 def solution(mesh):
     tokens = P("dp", "seq", None, None)
+    spans, parts = mesh.shape["dp"], mesh.shape["seq"]
+    body = by_heads if (spans, parts) == (8, 4) else by_tokens
     return jax.shard_map(
-        functools.partial(body, mesh.shape["dp"], mesh.shape["seq"]),
+        functools.partial(body, spans, parts),
         mesh=mesh,
         in_specs=(tokens, tokens, tokens, tokens, P("dp", "seq"), P(), P()),
         out_specs=(tokens, tokens, tokens, P(), P()),

time: 69.7 us -> 50.6 us (0.73)
  the two profiles are of different devices: /device:TPU:10 before, /device:TPU:0 now
where the time goes in v4:
time: 50.6 us; the launch traced here: 50.4 us
  starting transfers between devices  22.2 us (44%)
  Pallas kernels  12.7 us (25%)
  waiting for transfers between devices  12.5 us (25%)
  local copies, waits for them, and re-layouts  2.21 us (4%)
  between operations  0.7 us (1%)
    pallas_call x4, Pallas kernels, call_in(): pl.pallas_call(kernel, out_shape=[jax.ShapeDtypeStruct(s, t) for s, t, _...  12.7 us
    ppermute x6, starting transfers between devices, by_heads(): lax.ppermute(messages[grp * parts + m], 'seq', xor(m, parts))  11 us
    ppermute x6, starting transfers between devices, exchange_sum(): lax.ppermute(x, axis, [(i, i ^ m) for i in range(size)])  7.66 us
    ppermute x6, waiting for transfers between devices, by_heads(): lax.ppermute(messages[grp * parts + m], 'seq', xor(m, parts))  6.04 us
    ppermute x6, waiting for transfers between devices, exchange_sum(): lax.ppermute(x, axis, [(i, i ^ m) for i in range(size)])  5.48 us
    ppermute x3, starting transfers between devices, by_heads(): lax.ppermute(results[m], 'seq', xor(m, parts))  3.52 us
    unnamed x10, local copies, waits for them, and re-layouts  1.61 us
  transfers between devices with their start and end apart: 15, of which 8 were waited for; matrix products, arithmetic and copies ran while one was open for 0% of the time, Pallas kernels for 11%

profile of v4, /device:TPU:0, one launch (start us, length us, event | category | flops | bytes accessed | tf_op | source)
XLA Modules:
  0.0 50.4 jit_solution(15333964927679498624)
XLA Ops:
  0.6 0.0 copy-start.2
  0.6 3.4 %shard_map.119 = (bf16[784,128]{1,0:T(8,128)(2,1)}, bf16[784,128]{1,0:T(8,128)(2,1)}, bf16[784,128]{1,0:T(8,128)(2,1)}, bf16[784,128]{1,0:T(8,128)(2,1)}, bf16[7...) custom-call(bf16[2048,128]{1,0:T(8,128)(2,1)} %bitcast.13, ...), custom_call_target="tpu_custom_call" | custom-call | flops 1048576 | bytes 1048576 | tf_op jit(solution)/shard_map/pallas_call | solution.py:483
  4.1 3.0 %collective-permute-start = (bf16[784,128]{1,0:T(8,128)(2,1)}, bf16[784,128]{1,0:T(8,128)(2,1)S(1)}, u32[]{:S(2)}, u32[]{:S(2)}) collective-permute-start(bf16[784,128]{1,0:T(8,128)(2,1)} %get-tuple-element.30), channel_id=1, source_target_pairs={{0,1},{1,0},{2,3},{3,2},{4,5},{5,4},{6,7},{7,6},{8,9},{9,8},{10,11... | collective-permute-start | bytes 602120 | tf_op jit(solution)/shard_map/ppermute | solution.py:530
  7.1 1.5 %collective-permute-start.1 = (bf16[784,128]{1,0:T(8,128)(2,1)}, bf16[784,128]{1,0:T(8,128)(2,1)S(1)}, u32[]{:S(2)}, u32[]{:S(2)}) collective-permute-start(bf16[784,128]{1,0:T(8,128)(2,1)} %get-tuple-element.31), channel_id=1, source_target_pairs={{0,2},{1,3},{2,0},{3,1},{4,6},{5,7},{6,4},{7,5},{8,10},{9,11},{10,... | collective-permute-start | bytes 602120 | tf_op jit(solution)/shard_map/ppermute | solution.py:530
  8.6 0.0 collective-permute-start.2
  8.6 1.9 %collective-permute-start.3 = (bf16[784,128]{1,0:T(8,128)(2,1)}, bf16[784,128]{1,0:T(8,128)(2,1)S(1)}, u32[]{:S(2)}, u32[]{:S(2)}) collective-permute-start(bf16[784,128]{1,0:T(8,128)(2,1)} %get-tuple-element.38), channel_id=1, source_target_pairs={{0,1},{1,0},{2,3},{3,2},{4,5},{5,4},{6,7},{7,6},{8,9},{9,8},{10,11... | collective-permute-start | bytes 602120 | tf_op jit(solution)/shard_map/ppermute | solution.py:530
  10.6 1.5 %collective-permute-start.4 = (bf16[784,128]{1,0:T(8,128)(2,1)}, bf16[784,128]{1,0:T(8,128)(2,1)S(1)}, u32[]{:S(2)}, u32[]{:S(2)}) collective-permute-start(bf16[784,128]{1,0:T(8,128)(2,1)} %get-tuple-element.39), channel_id=1, source_target_pairs={{0,2},{1,3},{2,0},{3,1},{4,6},{5,7},{6,4},{7,5},{8,10},{9,11},{10,... | collective-permute-start | bytes 602120 | tf_op jit(solution)/shard_map/ppermute | solution.py:530
  12.1 0.1 pad.2.clone
  12.1 0.0 copy-start.3
  12.1 0.0 copy-start.4
  12.1 0.7 %copy-done.3 = f32[128]{0:T(128)S(1)} copy-done((f32[128]{0:T(128)S(1)}, f32[128]{0:T(128)}, u32[]{:S(2)}) %copy-start.3) | copy-done | bytes 536
  12.8 0.0 copy-done.4
  12.8 0.1 maximum_maximum_fusion.rest_5_.rest_9_
  12.9 0.2 collective-permute-done.rest_1_
  13.1 3.0 %collective-permute-start.5 = (bf16[784,128]{1,0:T(8,128)(2,1)}, bf16[784,128]{1,0:T(8,128)(2,1)S(1)}, u32[]{:S(2)}, u32[]{:S(2)}) collective-permute-start(bf16[784,128]{1,0:T(8,128)(2,1)} %get-tuple-element.40), channel_id=1, source_target_pairs={{0,3},{1,2},{2,1},{3,0},{4,7},{5,6},{6,5},{7,4},{8,11},{9,10},{10,... | collective-permute-start | bytes 602120 | tf_op jit(solution)/shard_map/ppermute | solution.py:530
  16.1 3.4 %collective-permute-done.1.rest_2_ = bf16[784,128]{1,0:T(8,128)(2,1)S(1)} collective-permute-done((bf16[784,128]{1,0:T(8,128)(2,1)}, bf16[784,128]{1,0:T(8,128)(2,1)S(1)}, u32[]{:S(2)}, u32[]{:S(2)}) %collective-permute-start.1) | collective-permute-done | bytes 200736 | tf_op jit(solution)/shard_map/ppermute | solution.py:530
  19.5 0.0 collective-permute-done.2.rest_3_
  19.5 0.0 copy-done.2
  19.5 0.0 copy-start.1
  19.5 0.9 %copy-done.1 = bf16[784,128]{1,0:T(8,128)(2,1)S(1)} copy-done((bf16[784,128]{1,0:T(8,128)(2,1)S(1)}, bf16[784,128]{1,0:T(8,128)(2,1)}, u32[]{:S(2)}) %copy-start.1) | copy-done | bytes 200728
  20.4 0.0 copy-start
  20.4 3.8 %shard_map.120 = (bf16[512,128]{1,0:T(8,128)(2,1)S(1)}, bf16[512,128]{1,0:T(8,128)(2,1)S(1)}, bf16[512,128]{1,0:T(8,128)(2,1)S(1)}, bf16[512,128]{1,0:T(8,128)(2,1)S(1)}, f32[8,128]{1,0:T(8,128)S(1)}) custom-call(bf16[784,128]{1,0:T(8,128)(2,1)S(1)} %copy-done.1, bf16[784,128]{1,0:T(8,128)(2,1)S(1)} %collective-permute-done.rest_1_, ...), custom_call_target="tpu_custom_call" | custom-call | flops 17179869184 | bytes 1048576 | tf_op jit(solution)/shard_map/pallas_call | solution.py:483
  24.2 0.0 collective-permute-done.3.rest_5_
  24.2 2.4 %collective-permute-done.4.rest_6_ = bf16[784,128]{1,0:T(8,128)(2,1)S(1)} collective-permute-done((bf16[784,128]{1,0:T(8,128)(2,1)}, bf16[784,128]{1,0:T(8,128)(2,1)S(1)}, u32[]{:S(2)}, u32[]{:S(2)}) %collective-permute-start.4) | collective-permute-done | bytes 200736 | tf_op jit(solution)/shard_map/ppermute | solution.py:530
  26.6 0.0 collective-permute-done.5.rest_7_
  26.6 0.0 copy-done
  26.6 3.8 %shard_map.121 = (bf16[1024,128]{1,0:T(8,128)(2,1)S(1)}, bf16[1024,128]{1,0:T(8,128)(2,1)S(1)}, bf16[1024,128]{1,0:T(8,128)(2,1)S(1)}, bf16[1024,128]{1,0:T(8,128)(2,1)S(1)}, f32[8,128]{1,0:T(8,128)S(1)}) custom-call(bf16[512,128]{1,0:T(8,128)(2,1)S(1)} %get-tuple-element.33.rest_0_, bf16[512,128]{1,0:T(8,128)(2,1)S(1)} %get-tuple-element.34.rest_1_, ...), custom_call_target="tpu_custom_call" | custom-call | flops 17179869184 | bytes 1048576 | tf_op jit(solution)/shard_map/pallas_call | solution.py:483
  30.4 1.3 %collective-permute-start.9 = (bf16[1024,128]{1,0:T(8,128)(2,1)S(1)}, bf16[1024,128]{1,0:T(8,128)(2,1)S(1)}, u32[]{:S(2)}, u32[]{:S(2)}) collective-permute-start(bf16[1024,128]{1,0:T(8,128)(2,1)S(1)} %get-tuple-element.44), channel_id=1, source_target_pairs={{0,1},{1,0},{2,3},{3,2},{4,5},{5,4},{6,7},{7,6},{8,9},{9,8},{10,11... | collective-permute-start | bytes 786440 | tf_op jit(solution)/shard_map/ppermute | solution.py:550
  31.7 0.8 %collective-permute-start.10 = (bf16[1024,128]{1,0:T(8,128)(2,1)S(1)}, bf16[1024,128]{1,0:T(8,128)(2,1)S(1)}, u32[]{:S(2)}, u32[]{:S(2)}) collective-permute-start(bf16[1024,128]{1,0:T(8,128)(2,1)S(1)} %get-tuple-element.45), channel_id=1, source_target_pairs={{0,2},{1,3},{2,0},{3,1},{4,6},{5,7},{6,4},{7,5},{8,10},{9,11},{10,... | collective-permute-start | bytes 786440 | tf_op jit(solution)/shard_map/ppermute | solution.py:550
  32.5 1.4 %collective-permute-start.11 = (bf16[1024,128]{1,0:T(8,128)(2,1)S(1)}, bf16[1024,128]{1,0:T(8,128)(2,1)S(1)}, u32[]{:S(2)}, u32[]{:S(2)}) collective-permute-start(bf16[1024,128]{1,0:T(8,128)(2,1)S(1)} %get-tuple-element.48), channel_id=1, source_target_pairs={{0,3},{1,2},{2,1},{3,0},{4,7},{5,6},{6,5},{7,4},{8,11},{9,10},{10,... | collective-permute-start | bytes 786440 | tf_op jit(solution)/shard_map/ppermute | solution.py:550
  33.9 0.0 collective-permute-start.6
  33.9 1.2 %collective-permute-done.6 = f32[8,128]{1,0:T(8,128)S(1)} collective-permute-done((f32[8,128]{1,0:T(8,128)S(1)}, f32[8,128]{1,0:T(8,128)S(1)}, u32[]{:S(2)}, u32[]{:S(2)}) %collective-permute-start.6) | collective-permute-done | bytes 4128 | tf_op jit(solution)/shard_map/ppermute | solution.py:495
  35.1 1.6 %collective-permute-start.7 = (f32[8,128]{1,0:T(8,128)S(1)}, f32[8,128]{1,0:T(8,128)S(1)}, u32[]{:S(2)}, u32[]{:S(2)}) collective-permute-start(f32[8,128]{1,0:T(8,128)S(1)} %add.22), channel_id=1, source_target_pairs={{0,8},{4,12},{8,0},{12,4},{16,24},{20,28},{24,16},{28,20},{1,9},{5... | collective-permute-start | bytes 12296 | tf_op jit(solution)/shard_map/ppermute | solution.py:495
  36.7 2.0 %collective-permute-done.7 = f32[8,128]{1,0:T(8,128)S(1)} collective-permute-done((f32[8,128]{1,0:T(8,128)S(1)}, f32[8,128]{1,0:T(8,128)S(1)}, u32[]{:S(2)}, u32[]{:S(2)}) %collective-permute-start.7) | collective-permute-done | bytes 4128 | tf_op jit(solution)/shard_map/ppermute | solution.py:495
  38.7 2.6 %collective-permute-start.8 = (f32[8,128]{1,0:T(8,128)S(1)}, f32[8,128]{1,0:T(8,128)S(1)}, u32[]{:S(2)}, u32[]{:S(2)}) collective-permute-start(f32[8,128]{1,0:T(8,128)S(1)} %add.23), channel_id=1, source_target_pairs={{0,16},{4,20},{8,24},{12,28},{16,0},{20,4},{24,8},{28,12},{1,17},{... | collective-permute-start | bytes 12296 | tf_op jit(solution)/shard_map/ppermute | solution.py:495
  41.3 1.9 %collective-permute-done.8 = f32[8,128]{1,0:T(8,128)S(1)} collective-permute-done((f32[8,128]{1,0:T(8,128)S(1)}, f32[8,128]{1,0:T(8,128)S(1)}, u32[]{:S(2)}, u32[]{:S(2)}) %collective-permute-start.8) | collective-permute-done | bytes 4128 | tf_op jit(solution)/shard_map/ppermute | solution.py:495
  43.2 0.0 collective-permute-done.9.rest_1_
  43.2 1.0 %collective-permute-done.10.rest_2_ = bf16[1024,128]{1,0:T(8,128)(2,1)S(1)} collective-permute-done((bf16[1024,128]{1,0:T(8,128)(2,1)S(1)}, bf16[1024,128]{1,0:T(8,128)(2,1)S(1)}, u32[]{:S(2)}, u32[]{:S(2)}) %collective-permute-start.10) | collective-permute-done | bytes 262176 | tf_op jit(solution)/shard_map/ppermute | solution.py:550
  44.2 0.6 %collective-permute-start.14 = (f32[8,128]{1,0:T(8,128)S(1)}, f32[8,128]{1,0:T(8,128)S(1)}, u32[]{:S(2)}, u32[]{:S(2)}) collective-permute-start(f32[8,128]{1,0:T(8,128)S(1)} %add.24), channel_id=1, source_target_pairs={{0,3},{1,2},{2,1},{3,0},{4,7},{5,6},{6,5},{7,4},{8,11},{9,10},{10,... | collective-permute-start | bytes 12296 | tf_op jit(solution)/shard_map/ppermute | solution.py:495
  44.8 1.4 %collective-permute-start.13 = (f32[8,128]{1,0:T(8,128)S(1)}, f32[8,128]{1,0:T(8,128)S(1)}, u32[]{:S(2)}, u32[]{:S(2)}) collective-permute-start(f32[8,128]{1,0:T(8,128)S(1)} %add.24), channel_id=1, source_target_pairs={{0,2},{1,3},{2,0},{3,1},{4,6},{5,7},{6,4},{7,5},{8,10},{9,11},{10,... | collective-permute-start | bytes 12296 | tf_op jit(solution)/shard_map/ppermute | solution.py:495
  46.3 1.4 %collective-permute-start.12 = (f32[8,128]{1,0:T(8,128)S(1)}, f32[8,128]{1,0:T(8,128)S(1)}, u32[]{:S(2)}, u32[]{:S(2)}) collective-permute-start(f32[8,128]{1,0:T(8,128)S(1)} %add.24), channel_id=1, source_target_pairs={{0,1},{1,0},{2,3},{3,2},{4,5},{5,4},{6,7},{7,6},{8,9},{9,8},{10,11... | collective-permute-start | bytes 12296 | tf_op jit(solution)/shard_map/ppermute | solution.py:495
  47.7 0.0 collective-permute-done.11.rest_3_
  47.7 1.8 %shard_map.122 = (bf16[2048,128]{1,0:T(8,128)(2,1)}, bf16[1024,128]{1,0:T(8,128)(2,1)}, bf16[1024,128]{1,0:T(8,128)(2,1)}) custom-call(bf16[1024,128]{1,0:T(8,128)(2,1)S(1)} %get-tuple-element.41.rest_0_, bf16[1024,128]{1,0:T(8,128)(2,1)S(1)} %collective-permute-done.9.rest_1_, bf16[1024,128]{1,0:T(8,128)(2,1)S(1)} %collective-permute-done.10.rest_2_, ...), custom_call_target="tpu_custom_call" | custom-call | flops 1048576 | bytes 1048576 | tf_op jit(solution)/shard_map/pallas_call | solution.py:483
  49.5 0.0 collective-permute-done.14
  49.5 0.0 collective-permute-done.13
  49.5 0.4 collective-permute-done.12
  49.9 0.5 %slice_bitcast_fusion = (f32[128]{0:T(128)}, f32[128]{0:T(128)}) fusion(f32[8,128]{1,0:T(8,128)S(1)} %add_add_fusion), kind=kLoop, calls=%fused_computation.2 | loop fusion | bytes 2048 | tf_op jit(solution)/shard_map/squeeze | solution.py:563
  (6 shorter events, 0.0 us)
Async XLA Ops:
  0.6 18.9 %copy-start.2 = (f32[4,2,64,128]{3,2,1,0:T(8,128)S(1)}, f32[4,2,64,128]{3,2,1,0:T(8,128)}, u32[]{:S(2)}) copy-start(f32[4,2,64,128]{3,2,1,0:T(8,128)} %constant.4.clone.rest_4_.rest_8_) | copy-start | bytes 786436
  4.1 9.0 %collective-permute-start = (bf16[784,128]{1,0:T(8,128)(2,1)}, bf16[784,128]{1,0:T(8,128)(2,1)S(1)}, u32[]{:S(2)}, u32[]{:S(2)}) collective-permute-start(bf16[784,128]{1,0:T(8,128)(2,1)} %get-tuple-element.30), channel_id=1, source_target_pairs={{0,1},{1,0},{2,3},{3,2},{4,5},{5,4},{6,7},{7,6},{8,9},{9,8},{10,11... | collective-permute-start | bytes 602120 | tf_op jit(solution)/shard_map/ppermute | solution.py:530
  7.1 12.4 %collective-permute-start.1 = (bf16[784,128]{1,0:T(8,128)(2,1)}, bf16[784,128]{1,0:T(8,128)(2,1)S(1)}, u32[]{:S(2)}, u32[]{:S(2)}) collective-permute-start(bf16[784,128]{1,0:T(8,128)(2,1)} %get-tuple-element.31), channel_id=1, source_target_pairs={{0,2},{1,3},{2,0},{3,1},{4,6},{5,7},{6,4},{7,5},{8,10},{9,11},{10,... | collective-permute-start | bytes 602120 | tf_op jit(solution)/shard_map/ppermute | solution.py:530
  8.6 10.9 %collective-permute-start.2 = (bf16[784,128]{1,0:T(8,128)(2,1)}, bf16[784,128]{1,0:T(8,128)(2,1)S(1)}, u32[]{:S(2)}, u32[]{:S(2)}) collective-permute-start(bf16[784,128]{1,0:T(8,128)(2,1)} %get-tuple-element.32), channel_id=1, source_target_pairs={{0,3},{1,2},{2,1},{3,0},{4,7},{5,6},{6,5},{7,4},{8,11},{9,10},{10,... | collective-permute-start | bytes 602120 | tf_op jit(solution)/shard_map/ppermute | solution.py:530
  8.6 15.6 %collective-permute-start.3 = (bf16[784,128]{1,0:T(8,128)(2,1)}, bf16[784,128]{1,0:T(8,128)(2,1)S(1)}, u32[]{:S(2)}, u32[]{:S(2)}) collective-permute-start(bf16[784,128]{1,0:T(8,128)(2,1)} %get-tuple-element.38), channel_id=1, source_target_pairs={{0,1},{1,0},{2,3},{3,2},{4,5},{5,4},{6,7},{7,6},{8,9},{9,8},{10,11... | collective-permute-start | bytes 602120 | tf_op jit(solution)/shard_map/ppermute | solution.py:530
  10.6 16.1 %collective-permute-start.4 = (bf16[784,128]{1,0:T(8,128)(2,1)}, bf16[784,128]{1,0:T(8,128)(2,1)S(1)}, u32[]{:S(2)}, u32[]{:S(2)}) collective-permute-start(bf16[784,128]{1,0:T(8,128)(2,1)} %get-tuple-element.39), channel_id=1, source_target_pairs={{0,2},{1,3},{2,0},{3,1},{4,6},{5,7},{6,4},{7,5},{8,10},{9,11},{10,... | collective-permute-start | bytes 602120 | tf_op jit(solution)/shard_map/ppermute | solution.py:530
  12.1 0.7 %copy-start.3 = (f32[128]{0:T(128)S(1)}, f32[128]{0:T(128)}, u32[]{:S(2)}) copy-start(f32[128]{0:T(128)} %param.14) | copy-start | bytes 1540
  12.1 0.7 %copy-start.4 = (f32[128]{0:T(128)S(1)}, f32[128]{0:T(128)}, u32[]{:S(2)}) copy-start(f32[128]{0:T(128)} %param.13) | copy-start | bytes 1540
  13.1 13.5 %collective-permute-start.5 = (bf16[784,128]{1,0:T(8,128)(2,1)}, bf16[784,128]{1,0:T(8,128)(2,1)S(1)}, u32[]{:S(2)}, u32[]{:S(2)}) collective-permute-start(bf16[784,128]{1,0:T(8,128)(2,1)} %get-tuple-element.40), channel_id=1, source_target_pairs={{0,3},{1,2},{2,1},{3,0},{4,7},{5,6},{6,5},{7,4},{8,11},{9,10},{10,... | collective-permute-start | bytes 602120 | tf_op jit(solution)/shard_map/ppermute | solution.py:530
  19.5 0.9 %copy-start.1 = (bf16[784,128]{1,0:T(8,128)(2,1)S(1)}, bf16[784,128]{1,0:T(8,128)(2,1)}, u32[]{:S(2)}) copy-start(bf16[784,128]{1,0:T(8,128)(2,1)} %get-tuple-element.29.rest_0_) | copy-start | bytes 602116
  20.4 6.2 %copy-start = (bf16[784,128]{1,0:T(8,128)(2,1)S(1)}, bf16[784,128]{1,0:T(8,128)(2,1)}, u32[]{:S(2)}) copy-start(bf16[784,128]{1,0:T(8,128)(2,1)} %get-tuple-element.37.rest_4_) | copy-start | bytes 602116
  30.4 12.8 %collective-permute-start.9 = (bf16[1024,128]{1,0:T(8,128)(2,1)S(1)}, bf16[1024,128]{1,0:T(8,128)(2,1)S(1)}, u32[]{:S(2)}, u32[]{:S(2)}) collective-permute-start(bf16[1024,128]{1,0:T(8,128)(2,1)S(1)} %get-tuple-element.44), channel_id=1, source_target_pairs={{0,1},{1,0},{2,3},{3,2},{4,5},{5,4},{6,7},{7,6},{8,9},{9,8},{10,11... | collective-permute-start | bytes 786440 | tf_op jit(solution)/shard_map/ppermute | solution.py:550
  31.7 12.5 %collective-permute-start.10 = (bf16[1024,128]{1,0:T(8,128)(2,1)S(1)}, bf16[1024,128]{1,0:T(8,128)(2,1)S(1)}, u32[]{:S(2)}, u32[]{:S(2)}) collective-permute-start(bf16[1024,128]{1,0:T(8,128)(2,1)S(1)} %get-tuple-element.45), channel_id=1, source_target_pairs={{0,2},{1,3},{2,0},{3,1},{4,6},{5,7},{6,4},{7,5},{8,10},{9,11},{10,... | collective-permute-start | bytes 786440 | tf_op jit(solution)/shard_map/ppermute | solution.py:550
  32.5 15.2 %collective-permute-start.11 = (bf16[1024,128]{1,0:T(8,128)(2,1)S(1)}, bf16[1024,128]{1,0:T(8,128)(2,1)S(1)}, u32[]{:S(2)}, u32[]{:S(2)}) collective-permute-start(bf16[1024,128]{1,0:T(8,128)(2,1)S(1)} %get-tuple-element.48), channel_id=1, source_target_pairs={{0,3},{1,2},{2,1},{3,0},{4,7},{5,6},{6,5},{7,4},{8,11},{9,10},{10,... | collective-permute-start | bytes 786440 | tf_op jit(solution)/shard_map/ppermute | solution.py:550
  33.9 1.2 %collective-permute-start.6 = (f32[8,128]{1,0:T(8,128)S(1)}, f32[8,128]{1,0:T(8,128)S(1)}, u32[]{:S(2)}, u32[]{:S(2)}) collective-permute-start(f32[8,128]{1,0:T(8,128)S(1)} %add.21), channel_id=1, source_target_pairs={{0,4},{4,0},{8,12},{12,8},{16,20},{20,16},{24,28},{28,24},{1,5},{5... | collective-permute-start | bytes 12296 | tf_op jit(solution)/shard_map/ppermute | solution.py:495
  35.1 3.6 %collective-permute-start.7 = (f32[8,128]{1,0:T(8,128)S(1)}, f32[8,128]{1,0:T(8,128)S(1)}, u32[]{:S(2)}, u32[]{:S(2)}) collective-permute-start(f32[8,128]{1,0:T(8,128)S(1)} %add.22), channel_id=1, source_target_pairs={{0,8},{4,12},{8,0},{12,4},{16,24},{20,28},{24,16},{28,20},{1,9},{5... | collective-permute-start | bytes 12296 | tf_op jit(solution)/shard_map/ppermute | solution.py:495
  38.7 4.5 %collective-permute-start.8 = (f32[8,128]{1,0:T(8,128)S(1)}, f32[8,128]{1,0:T(8,128)S(1)}, u32[]{:S(2)}, u32[]{:S(2)}) collective-permute-start(f32[8,128]{1,0:T(8,128)S(1)} %add.23), channel_id=1, source_target_pairs={{0,16},{4,20},{8,24},{12,28},{16,0},{20,4},{24,8},{28,12},{1,17},{... | collective-permute-start | bytes 12296 | tf_op jit(solution)/shard_map/ppermute | solution.py:495
  44.2 5.3 %collective-permute-start.14 = (f32[8,128]{1,0:T(8,128)S(1)}, f32[8,128]{1,0:T(8,128)S(1)}, u32[]{:S(2)}, u32[]{:S(2)}) collective-permute-start(f32[8,128]{1,0:T(8,128)S(1)} %add.24), channel_id=1, source_target_pairs={{0,3},{1,2},{2,1},{3,0},{4,7},{5,6},{6,5},{7,4},{8,11},{9,10},{10,... | collective-permute-start | bytes 12296 | tf_op jit(solution)/shard_map/ppermute | solution.py:495
  44.8 4.7 %collective-permute-start.13 = (f32[8,128]{1,0:T(8,128)S(1)}, f32[8,128]{1,0:T(8,128)S(1)}, u32[]{:S(2)}, u32[]{:S(2)}) collective-permute-start(f32[8,128]{1,0:T(8,128)S(1)} %add.24), channel_id=1, source_target_pairs={{0,2},{1,3},{2,0},{3,1},{4,6},{5,7},{6,4},{7,5},{8,10},{9,11},{10,... | collective-permute-start | bytes 12296 | tf_op jit(solution)/shard_map/ppermute | solution.py:495
  46.3 3.6 %collective-permute-start.12 = (f32[8,128]{1,0:T(8,128)S(1)}, f32[8,128]{1,0:T(8,128)S(1)}, u32[]{:S(2)}, u32[]{:S(2)}) collective-permute-start(f32[8,128]{1,0:T(8,128)S(1)} %add.24), channel_id=1, source_target_pairs={{0,1},{1,0},{2,3},{3,2},{4,5},{5,4},{6,7},{7,6},{8,9},{9,8},{10,11... | collective-permute-start | bytes 12296 | tf_op jit(solution)/shard_map/ppermute | solution.py:495

commit v5 on v4

--- a/solution.py
+++ b/solution.py
@@ -289,104 +289,119 @@
     )
 
 
-def spread_kernel(axis, parts, groups, heads, kv_heads, q_hbm, g_hbm, k_hbm, v_hbm, seg_hbm, *rest):
+def spread_kernel(axis, parts, groups, per, a_hbm, b_hbm, *rest):
+    with_ids = groups is None
+    groups = groups or 1
+    seg_hbm, rest = rest[:1], rest[1:]
     outs = rest[: parts * groups]
-    q_in, g_in, k_in, v_in, seg_in, q_f32, g_f32, k_f32, v_f32, sems = rest[parts * groups :]
+    a_in, b_in, a_f32, b_f32, seg_in, msg, in_sems, out_sems = rest[parts * groups :]
     block = seg_in.shape[1]
-    group = heads // kv_heads
-    per = kv_heads // parts // groups
+    heads = a_in.shape[0] // block
     me = lax.axis_index(axis)
-    pairs = [(seg_hbm, seg_in)]
-    for src, dst in ((k_hbm, k_in), (v_hbm, v_in), (q_hbm, q_in), (g_hbm, g_in)):
-        half = dst.shape[0] // 2
-        pairs += [(src.at[pl.ds(i * half, half)], dst.at[pl.ds(i * half, half)]) for i in range(2)]
-    loads = [pltpu.make_async_copy(src, dst, sems.at[i]) for i, (src, dst) in enumerate(pairs)]
+    pairs = [(a_hbm, a_in), (b_hbm, b_in)] + ([(seg_hbm[0], seg_in)] if with_ids else [])
+    loads = [pltpu.make_async_copy(src, dst, in_sems.at[i]) for i, (src, dst) in enumerate(pairs)]
     for copy in loads:
         copy.start()
-    loads[0].wait()
-    ids = jnp.broadcast_to(seg_in[...].astype(jnp.float32), (16, block)).astype(jnp.bfloat16)
-    for n, (src, dst) in enumerate(((k_in, k_f32), (v_in, v_f32), (q_in, q_f32), (g_in, g_f32))):
-        half = dst.shape[0] // 2
-        for i in range(2):
-            loads[1 + 2 * n + i].wait()
-            dst[pl.ds(i * half, half), :] = src[pl.ds(i * half, half), :].astype(jnp.float32)
+    for copy, src, dst in zip(loads, (a_in, b_in), (a_f32, b_f32)):
+        copy.wait()
+        dst[...] = src[...].astype(jnp.float32)
+    if with_ids:
+        loads[2].wait()
+        ids = jnp.broadcast_to(seg_in[...].astype(jnp.float32), (16, block)).astype(jnp.bfloat16)
+    stores = []
     for grp in range(groups):
-        for m in range(parts):
-            out = outs[grp * parts + m]
+        for m in (*range(1, parts), 0):
+            slot = grp * parts + m
+            first = ((me ^ m) * groups + grp) * per
             at = 0
-            for p in range(per):
-                kv = ((me ^ m) * groups + grp) * per + p
-                pieces = [(q_f32, kv * group + i, heads) for i in range(group)]
-                pieces += [(g_f32, kv * group + i, heads) for i in range(group)]
-                pieces += [(k_f32, kv, kv_heads), (v_f32, kv, kv_heads)]
-                for src, head, stride in pieces:
-                    rows = src[pl.ds(head, block, stride=stride), :]
-                    out[pl.ds(at, block), :] = rows.astype(jnp.bfloat16)
+            for src in (a_f32, b_f32):
+                for h in range(per):
+                    rows = src[pl.ds(first + h, block, stride=heads), :]
+                    msg[slot, pl.ds(at, block), :] = rows.astype(jnp.bfloat16)
                     at += block
-            out[pl.ds(at, 16), :] = ids
-
-
-def eye(size):
-    row = lax.broadcasted_iota(jnp.int32, (size, size), 0)
-    return (row == lax.broadcasted_iota(jnp.int32, (size, size), 1)).astype(jnp.bfloat16)
-
-
-def turned(x, unit):
-    return lax.dot_general(unit, x, NT, preferred_element_type=jnp.float32)
+            if with_ids:
+                msg[slot, pl.ds(at, 16), :] = ids
+            copy = pltpu.make_async_copy(msg.at[slot], outs[slot], out_sems.at[slot])
+            copy.start()
+            stores.append(copy)
+    for copy in stores:
+        copy.wait()
+
+
+def turned(x):
+    return x.astype(jnp.float32).T
+
+
+def rotated(x, c, s):
+    half = x.shape[0] // 2
+    a, b = x[:half], x[half:]
+    return jnp.concatenate([a * c - b * s, b * c + a * s], axis=0)
+
+
+def embed(x, gain, c, s):
+    scale = lax.rsqrt(jnp.sum(x * x, axis=0, keepdims=True) * (1.0 / x.shape[0]) + EPS)
+    normed = x * scale
+    return rotated(normed * gain, c, s).astype(jnp.bfloat16), normed, scale
+
+
+def embed_back(dy, gain, c, s, normed, scale):
+    dr = rotated(dy, c, -s)
+    share = dr * normed
+    dn = dr * gain
+    mean = jnp.sum(dn * normed, axis=0, keepdims=True) * (1.0 / dy.shape[0])
+    return ((scale * SCALE) * (dn - normed * mean)).astype(jnp.bfloat16), share
+
+
+def rope(table_ref, b, copies):
+    c, s = table_ref[b, 0], table_ref[b, 1]
+    return jnp.concatenate([c] * copies, axis=1), jnp.concatenate([s] * copies, axis=1)
+
+
+def gain_columns(gains_ref, row, copies):
+    width = gains_ref.shape[1]
+    return jnp.concatenate([jnp.broadcast_to(gains_ref[row : row + 1, :], (width, width)).T] * copies, axis=1)
+
+
+def keys_kernel(axis, parts, *rest):
+    msgs, table_ref, gains_ref = rest[:parts], rest[parts], rest[parts + 1]
+    kt_ref, k_ref, v_ref, kn_ref, ks_ref, id_ref = rest[parts + 2 :]
+    block = table_ref.shape[3]
+    owned = v_ref.shape[1]
+    f32, bf16 = jnp.float32, jnp.bfloat16
+    me = lax.axis_index(axis)
+    gain = gain_columns(gains_ref, 1, 1)
+    for m in range(parts):
+        b = me ^ m
+        id_ref[b] = jnp.broadcast_to(msgs[m][pl.ds(2 * owned * block, 16), :].astype(f32)[0:1, :], (8, block))
+        for h in range(owned):
+            y, normed, scale = embed(turned(msgs[m][pl.ds(h * block, block), :]), gain, *rope(table_ref, b, 1))
+            kt_ref[b, h], kn_ref[b, h], ks_ref[b, h] = y, normed, jnp.broadcast_to(scale, (8, block))
+            k_ref[b, h] = turned(y).astype(bf16)
+            v_ref[b, h] = msgs[m][pl.ds((owned + h) * block, block), :]
 
 
 def heads_kernel(axis, parts, grp, per, group, back, *rest):
-    earlier, msgs = rest[: grp * parts], rest[grp * parts : grp * parts + parts]
-    table_ref, gains_ref = rest[parts + grp * parts : parts + grp * parts + 2]
-    outs = rest[-parts - 12 : -12]
-    share_ref, qt_ref, kt_ref, k_ref, v_ref, g_ref, qn_ref, kn_ref, qs_ref, ks_ref, id_ref, res_ref = rest[-12:]
-    block, width = table_ref.shape[3], msgs[0].shape[1]
-    half = width // 2
+    earlier, rest = rest[: grp * parts], rest[grp * parts :]
+    msgs, rest = rest[:parts], rest[parts:]
+    kt_ref, k_ref, v_ref, kn_ref, ks_ref, id_ref, table_ref, gains_ref = rest[:8]
+    outs, share_ref = rest[8 : 8 + parts], rest[8 + parts]
+    qt_ref, g_ref, qn_ref, qs_ref, res_ref = rest[9 + parts :]
+    block, width = table_ref.shape[3], gains_ref.shape[1]
     rows = group * block
     f32, bf16 = jnp.float32, jnp.bfloat16
     me = lax.axis_index(axis)
-    unit, unit_rows = eye(width), eye(rows)
-    q_gain = jnp.broadcast_to(gains_ref[0:1, :], (width, width)).T
-    k_gain = jnp.broadcast_to(gains_ref[1:2, :], (width, width)).T
-    q_gain = jnp.concatenate([q_gain] * group, axis=1)
-    last = per * (2 * group + 2) * block
-
-    def rotated(x, c, s):
-        a, b = x[:half], x[half:]
-        return jnp.concatenate([a * c - b * s, b * c + a * s], axis=0)
-
-    def embed(x, gain, c, s):
-        scale = lax.rsqrt(jnp.sum(x * x, axis=0, keepdims=True) * (1.0 / width) + EPS)
-        normed = x * scale
-        return rotated(normed * gain, c, s).astype(bf16), normed, scale
-
-    def embed_back(dy, gain, c, s, normed, scale):
-        dr = rotated(dy, c, -s)
-        share = dr * normed
-        dn = dr * gain
-        mean = jnp.sum(dn * normed, axis=0, keepdims=True) * (1.0 / width)
-        return ((scale * SCALE) * (dn - normed * mean)).astype(bf16), share
-
-    def rope(b, copies):
-        c, s = table_ref[b, 0], table_ref[b, 1]
-        return jnp.concatenate([c] * copies, axis=1), jnp.concatenate([s] * copies, axis=1)
-
+    q_gain, k_gain = gain_columns(gains_ref, 0, group), gain_columns(gains_ref, 1, 1)
     for m in range(parts):
         b = me ^ m
-        id_ref[b] = jnp.broadcast_to(msgs[m][pl.ds(last, 16), :].astype(f32)[0:1, :], (8, block))
         for p in range(per):
-            base = p * (2 * group + 2) * block
             at = b * per + p
-            y, normed, scale = embed(turned(msgs[m][pl.ds(base, rows), :], unit), q_gain, *rope(b, group))
+            x = turned(msgs[m][pl.ds(p * rows, rows), :])
+            y, normed, scale = embed(x, q_gain, *rope(table_ref, b, group))
             qt_ref[at], qn_ref[at], qs_ref[at] = y, normed, jnp.broadcast_to(scale, (8, rows))
-            g_ref[at] = msgs[m][pl.ds(base + rows, rows), :]
-            y, normed, scale = embed(turned(msgs[m][pl.ds(base + 2 * rows, block), :], unit), k_gain, *rope(b, 1))
-            kt_ref[at], kn_ref[at], ks_ref[at] = y, normed, jnp.broadcast_to(scale, (8, block))
-            k_ref[at] = turned(y, unit).astype(bf16)
-            v_ref[at] = msgs[m][pl.ds(base + 2 * rows + block, block), :]
+            g_ref[at] = msgs[m][pl.ds((per + p) * rows, rows), :]
 
     id_rows = [id_ref[b][0:1, :] for b in range(parts)]
-    id_columns = [turned(jnp.broadcast_to(row, (block, block)).astype(bf16), unit) for row in id_rows]
+    id_columns = [jnp.broadcast_to(row, (block, block)).T for row in id_rows]
     key_at = lax.broadcasted_iota(jnp.int32, (block, block), 0)
     query_at = lax.broadcasted_iota(jnp.int32, (block, block), 1)
     causal = jnp.where(key_at <= query_at, 0.0, NEG)
@@ -406,9 +421,9 @@
         for b in range(parts):
             span = range(max(0, b - back), b + 1)
             qt, g = qt_ref[b * per + p], g_ref[b * per + p]
-            k = jnp.concatenate([k_ref[j * per + p] for j in span], axis=0)
-            kt = jnp.concatenate([kt_ref[j * per + p] for j in span], axis=1)
-            v = jnp.concatenate([v_ref[j * per + p] for j in span], axis=0)
+            k = jnp.concatenate([k_ref[j, grp * per + p] for j in span], axis=0)
+            kt = jnp.concatenate([kt_ref[j, grp * per + p] for j in span], axis=1)
+            v = jnp.concatenate([v_ref[j, grp * per + p] for j in span], axis=0)
             hidden = jnp.concatenate([bias(j, b) for j in span], axis=0)
             scores = jnp.dot(k, qt, preferred_element_type=f32)
             expo = jnp.exp2(scores * (SCALE * LOG2E) + hidden)
@@ -425,14 +440,13 @@
                 dk[j] = dks[:, cut] if dk[j] is None else dk[j] + dks[:, cut]
                 dv[j] = dvs[cut] if dv[j] is None else dv[j] + dvs[cut]
             at = b * per + p
-            dx, share = embed_back(dq, q_gain, *rope(b, group), qn_ref[at], qs_ref[at][0:1, :])
+            dx, share = embed_back(dq, q_gain, *rope(table_ref, b, group), qn_ref[at], qs_ref[at][0:1, :])
             q_total = q_total + share
-            res_ref[b, pl.ds(out_base, rows), :] = turned(dx, unit_rows).astype(bf16)
+            res_ref[b, pl.ds(out_base, rows), :] = turned(dx).astype(bf16)
         for b in range(parts):
-            at = b * per + p
-            dx, share = embed_back(dk[b], k_gain, *rope(b, 1), kn_ref[at], ks_ref[at][0:1, :])
+            dx, share = embed_back(dk[b], k_gain, *rope(table_ref, b, 1), kn_ref[b, grp * per + p], ks_ref[b, grp * per + p][0:1, :])
             k_total = k_total + share
-            res_ref[b, pl.ds(out_base + rows, block), :] = turned(dx, unit).astype(bf16)
+            res_ref[b, pl.ds(out_base + rows, block), :] = turned(dx).astype(bf16)
             res_ref[b, pl.ds(out_base + rows + block, block), :] = dv[b].astype(bf16)
     size = res_ref.shape[1]
     for m in range(parts):
@@ -511,38 +525,46 @@
     table = jnp.asarray(np.stack([np.cos(angles), np.sin(angles)], axis=1).astype(np.float32))
     q2, g2 = (x.reshape(block * heads, width) for x in (q_pre, grad_out))
     k2, v2 = (x.reshape(block * kv_heads, width) for x in (k_pre, values))
-    sent = (per * (2 * group + 2) * block + 16, width)
+    owned = kv_heads // parts
+    kv_sent = (2 * owned * block + 16, width)
+    sent = (per * 2 * rows, width)
     back_sent = (per * (group + 2) * block, width)
     dma = pltpu.SemaphoreType.DMA
     q_shape, k_shape = q2.shape, k2.shape
 
-    messages = call_in(
-        functools.partial(spread_kernel, "seq", parts, groups, heads, kv_heads),
-        [hbm] * 5, [(sent, bf16, vmem)] * (parts * groups),
-        [vmem(q_shape, bf16), vmem(q_shape, bf16), vmem(k_shape, bf16), vmem(k_shape, bf16), vmem((1, block), jnp.int32)]
-        + [vmem(q_shape, f32), vmem(q_shape, f32), vmem(k_shape, f32), vmem(k_shape, f32), dma((9,))],
-        1 << 20, q2, g2, k2, v2, segment_ids, limit=SPREAD_VMEM,
-    )
+    def spread(count, each, shape, message, cost, *arrays):
+        number = parts * (count or 1)
+        return call_in(
+            functools.partial(spread_kernel, "seq", parts, count, each),
+            [hbm] * len(arrays), [(message, bf16, hbm)] * number,
+            [vmem(shape, bf16), vmem(shape, bf16), vmem(shape, f32), vmem(shape, f32), vmem((1, block), jnp.int32)]
+            + [vmem((number, *message), bf16), dma((len(arrays),)), dma((number,))],
+            cost, *arrays, limit=SPREAD_VMEM,
+        )
+
+    xor = lambda m, size: [(i, i ^ m) for i in range(size)]
+    send = lambda out: [out[0]] + [lax.ppermute(out[m], "seq", xor(m, parts)) for m in range(1, parts)]
+    kv_messages = spread(None, owned, k_shape, kv_sent, 1 << 20, k2, v2, segment_ids)
+    kv_arrived = send(kv_messages)
+    messages = spread(groups, per * group, q_shape, sent, 1 << 33, q2, g2, kv_messages[0])
+    arrived = [send(messages[grp * parts : (grp + 1) * parts]) for grp in range(groups)]
     gains = jnp.concatenate([q_gain[None], k_gain[None], jnp.zeros((6, width), f32)], axis=0)
-    xor = lambda m, size: [(i, i ^ m) for i in range(size)]
-    arrived = [
-        [messages[grp * parts]]
-        + [lax.ppermute(messages[grp * parts + m], "seq", xor(m, parts)) for m in range(1, parts)]
-        for grp in range(groups)
-    ]
+    held = (parts, owned)
+    keys = call_in(
+        functools.partial(keys_kernel, "seq", parts), [vmem] * (parts + 2),
+        [((*held, width, block), bf16, vmem), ((*held, block, width), bf16, vmem), ((*held, block, width), bf16, vmem)]
+        + [((*held, width, block), f32, vmem), ((*held, 8, block), f32, vmem), ((parts, 8, block), f32, vmem)],
+        [], 1 << 33, *kv_arrived, table, gains,
+    )
     results, shares = [], []
     for grp in range(groups):
-        inputs = [*results, *arrived[grp], table, gains]
+        inputs = [*results, *arrived[grp], *keys, table, gains]
         *made, share = call_in(
             functools.partial(heads_kernel, "seq", parts, grp, per, group, back),
             [vmem] * len(inputs),
             [(((grp + 1) * back_sent[0], width), bf16, vmem)] * parts + [((8, width), f32, vmem)],
-            [vmem((parts * per, width, rows), bf16), vmem((parts * per, width, block), bf16)]
-            + [vmem((parts * per, block, width), bf16), vmem((parts * per, block, width), bf16)]
-            + [vmem((parts * per, rows, width), bf16)]
-            + [vmem((parts * per, width, rows), f32), vmem((parts * per, width, block), f32)]
-            + [vmem((parts * per, 8, rows), f32), vmem((parts * per, 8, block), f32), vmem((parts, 8, block), f32)]
-            + [vmem((parts, *back_sent), bf16)],
+            [vmem((parts * per, width, rows), bf16), vmem((parts * per, rows, width), bf16)]
+            + [vmem((parts * per, width, rows), f32), vmem((parts * per, 8, rows), f32), vmem((parts, *back_sent), bf16)],
             1 << 34, *inputs,
         )
         results = made

time: 50.6 us -> 47.6 us (0.941)
  waiting for transfers between devices: 12.5 us -> 10 us
  starting transfers between devices: 22.2 us -> 23.3 us
  local copies, waits for them, and re-layouts: 2.21 us -> 1.29 us
  Pallas kernels: 12.7 us -> 12 us
    ppermute x6 -> x9, waiting for transfers between devices: 6.04 us -> 4.03 us  [by_heads(): lax.ppermute(out[m], 'seq', xor(m, parts))]
    ppermute x6 -> x9, starting transfers between devices: 11 us -> 12.1 us  [by_heads(): lax.ppermute(out[m], 'seq', xor(m, parts))]
    ppermute x3, waiting for transfers between devices: 1 us -> 0.04 us  [by_heads(): lax.ppermute(results[m], 'seq', xor(m, parts))]
    unnamed x10 -> x14, local copies, waits for them, and re-layouts: 1.61 us -> 0.69 us
    pallas_call x4 -> x6, Pallas kernels: 12.7 us -> 12 us  [call_in(): pl.pallas_call(kernel, out_shape=[jax.ShapeDtypeStruct(s, t) for s, t, _...]
  transfers between devices with their start and end apart: 15 -> 18, of which waited for: 8 -> 7; matrix products, arithmetic and copies ran while one was open for 0% -> 0% of each run, Pallas kernels for 11% -> 16%
where the time goes in v5:
time: 47.6 us; the launch traced here: 47.4 us
  starting transfers between devices  23.3 us (49%)
  Pallas kernels  12 us (25%)
  waiting for transfers between devices  10 us (21%)
  local copies, waits for them, and re-layouts  1.29 us (3%)
  between operations  0.73 us (2%)
    ppermute x9, starting transfers between devices, by_heads(): lax.ppermute(out[m], 'seq', xor(m, parts))  12.1 us
    pallas_call x6, Pallas kernels, call_in(): pl.pallas_call(kernel, out_shape=[jax.ShapeDtypeStruct(s, t) for s, t, _...  12 us
    ppermute x6, starting transfers between devices, exchange_sum(): lax.ppermute(x, axis, [(i, i ^ m) for i in range(size)])  7.68 us
    ppermute x6, waiting for transfers between devices, exchange_sum(): lax.ppermute(x, axis, [(i, i ^ m) for i in range(size)])  5.97 us
    ppermute x9, waiting for transfers between devices, by_heads(): lax.ppermute(out[m], 'seq', xor(m, parts))  4.03 us
    ppermute x3, starting transfers between devices, by_heads(): lax.ppermute(results[m], 'seq', xor(m, parts))  3.55 us
  transfers between devices with their start and end apart: 18, of which 7 were waited for; matrix products, arithmetic and copies ran while one was open for 0% of the time, Pallas kernels for 16%

profile of v5, /device:TPU:0, one launch (start us, length us, event | category | flops | bytes accessed | tf_op | source)
XLA Modules:
  0.0 47.4 jit_solution(14170525596202020522)
XLA Ops:
  0.6 2.0 %shard_map.119 = (bf16[528,128]{1,0:T(8,128)(2,1)}, bf16[528,128]{1,0:T(8,128)(2,1)}, bf16[528,128]{1,0:T(8,128)(2,1)}, bf16[528,128]{1,0:T(8,128)(2,1)}) custom-call(bf16[1024,128]{1,0:T(8,128)(2,1)} %bitcast.13, bf16[1024,128]{1,0:T(8,128)(2,1)} %bitcast.14, s32[1,128]{1,0:T(1,128)} %rest_0_.1), custom_call_target="tpu_custom_call" | custom-call | flops 1048576 | bytes 1048576 | tf_op jit(solution)/shard_map/pallas_call | solution.py:497
  2.6 3.0 %collective-permute-start.3 = (bf16[528,128]{1,0:T(8,128)(2,1)}, bf16[528,128]{1,0:T(8,128)(2,1)S(1)}, u32[]{:S(2)}, u32[]{:S(2)}) collective-permute-start(bf16[528,128]{1,0:T(8,128)(2,1)} %get-tuple-element.44), channel_id=1, source_target_pairs={{0,1},{1,0},{2,3},{3,2},{4,5},{5,4},{6,7},{7,6},{8,9},{9,8},{10,11... | collective-permute-start | bytes 405512 | tf_op jit(solution)/shard_map/ppermute | solution.py:546
  5.6 1.5 %collective-permute-start.4 = (bf16[528,128]{1,0:T(8,128)(2,1)}, bf16[528,128]{1,0:T(8,128)(2,1)S(1)}, u32[]{:S(2)}, u32[]{:S(2)}) collective-permute-start(bf16[528,128]{1,0:T(8,128)(2,1)} %get-tuple-element.45), channel_id=1, source_target_pairs={{0,2},{1,3},{2,0},{3,1},{4,6},{5,7},{6,4},{7,5},{8,10},{9,11},{10,... | collective-permute-start | bytes 405512 | tf_op jit(solution)/shard_map/ppermute | solution.py:546
  7.1 0.0 collective-permute-start.5
  7.1 0.0 copy-start
  7.1 0.0 copy-start.1
  7.1 2.7 %shard_map.120 = (bf16[512,128]{1,0:T(8,128)(2,1)}, bf16[512,128]{1,0:T(8,128)(2,1)}, bf16[512,128]{1,0:T(8,128)(2,1)}, bf16[512,128]{1,0:T(8,128)(2,1)}, bf16[5...) custom-call(bf16[2048,128]{1,0:T(8,128)(2,1)} %bitcast.17, ...), custom_call_target="tpu_custom_call" | custom-call | flops 8589934592 | bytes 1048576 | tf_op jit(solution)/shard_map/pallas_call | solution.py:497
  9.9 2.0 %collective-permute-start = (bf16[512,128]{1,0:T(8,128)(2,1)}, bf16[512,128]{1,0:T(8,128)(2,1)S(1)}, u32[]{:S(2)}, u32[]{:S(2)}) collective-permute-start(bf16[512,128]{1,0:T(8,128)(2,1)} %get-tuple-element.41), channel_id=1, source_target_pairs={{0,1},{1,0},{2,3},{3,2},{4,5},{5,4},{6,7},{7,6},{8,9},{9,8},{10,11... | collective-permute-start | bytes 393224 | tf_op jit(solution)/shard_map/ppermute | solution.py:546
  11.9 1.5 %collective-permute-start.1 = (bf16[512,128]{1,0:T(8,128)(2,1)}, bf16[512,128]{1,0:T(8,128)(2,1)S(1)}, u32[]{:S(2)}, u32[]{:S(2)}) collective-permute-start(bf16[512,128]{1,0:T(8,128)(2,1)} %get-tuple-element.42), channel_id=1, source_target_pairs={{0,2},{1,3},{2,0},{3,1},{4,6},{5,7},{6,4},{7,5},{8,10},{9,11},{10,... | collective-permute-start | bytes 393224 | tf_op jit(solution)/shard_map/ppermute | solution.py:546
  13.4 0.1 pad.2.clone
  13.5 0.0 copy-start.4
  13.5 0.0 copy-start.5
  13.5 0.7 %copy-done.4 = f32[128]{0:T(128)S(1)} copy-done((f32[128]{0:T(128)S(1)}, f32[128]{0:T(128)}, u32[]{:S(2)}) %copy-start.4) | copy-done | bytes 536
  14.1 0.0 copy-done.5
  14.2 0.1 maximum_maximum_fusion.rest_5_.rest_11_.rest_15_
  14.2 0.0 collective-permute-done.3.rest_1_
  14.2 0.0 collective-permute-start.2
  14.3 0.0 collective-permute-done.4.rest_2_
  14.3 1.9 %collective-permute-start.6 = (bf16[512,128]{1,0:T(8,128)(2,1)}, bf16[512,128]{1,0:T(8,128)(2,1)S(1)}, u32[]{:S(2)}, u32[]{:S(2)}) collective-permute-start(bf16[512,128]{1,0:T(8,128)(2,1)} %get-tuple-element.58), channel_id=1, source_target_pairs={{0,1},{1,0},{2,3},{3,2},{4,5},{5,4},{6,7},{7,6},{8,9},{9,8},{10,11... | collective-permute-start | bytes 393224 | tf_op jit(solution)/shard_map/ppermute | solution.py:546
  16.2 0.0 collective-permute-done.5.rest_3_
  16.2 0.0 copy-start.6
  16.2 0.0 copy-start.3
  16.2 1.5 %collective-permute-start.7 = (bf16[512,128]{1,0:T(8,128)(2,1)}, bf16[512,128]{1,0:T(8,128)(2,1)S(1)}, u32[]{:S(2)}, u32[]{:S(2)}) collective-permute-start(bf16[512,128]{1,0:T(8,128)(2,1)} %get-tuple-element.59), channel_id=1, source_target_pairs={{0,2},{1,3},{2,0},{3,1},{4,6},{5,7},{6,4},{7,5},{8,10},{9,11},{10,... | collective-permute-start | bytes 393224 | tf_op jit(solution)/shard_map/ppermute | solution.py:546
  17.7 0.0 copy-done
  17.8 0.0 copy-done.1
  17.8 0.9 %shard_map.121 = (bf16[4,2,128,128]{3,2,1,0:T(8,128)(2,1)S(1)}, bf16[4,2,128,128]{3,2,1,0:T(8,128)(2,1)S(1)}, bf16[4,2,128,128]{3,2,1,0:T(8,128)(2,1)S(1)}, f32[...) custom-call(bf16[528,128]{1,0:T(8,128)(2,1)S(1)} %copy-done, ...), custom_call_target="tpu_custom_call" | custom-call | flops 8589934592 | bytes 1048576 | tf_op jit(solution)/shard_map/pallas_call | solution.py:497
  18.6 0.0 collective-permute-done.rest_1_
  18.6 0.0 copy-done.6
  18.6 0.5 %collective-permute-start.8 = (bf16[512,128]{1,0:T(8,128)(2,1)S(1)}, bf16[512,128]{1,0:T(8,128)(2,1)S(1)}, u32[]{:S(2)}, u32[]{:S(2)}) collective-permute-start(bf16[512,128]{1,0:T(8,128)(2,1)S(1)} %copy-done.6), channel_id=1, source_target_pairs={{0,3},{1,2},{2,1},{3,0},{4,7},{5,6},{6,5},{7,4},{8,11},{9,10},{10,... | collective-permute-start | bytes 393224 | tf_op jit(solution)/shard_map/ppermute | solution.py:546
  19.1 2.1 %collective-permute-done.1.rest_2_ = bf16[512,128]{1,0:T(8,128)(2,1)S(1)} collective-permute-done((bf16[512,128]{1,0:T(8,128)(2,1)}, bf16[512,128]{1,0:T(8,128)(2,1)S(1)}, u32[]{:S(2)}, u32[]{:S(2)}) %collective-permute-start.1) | collective-permute-done | bytes 131104 | tf_op jit(solution)/shard_map/ppermute | solution.py:546
  21.3 0.6 %collective-permute-done.2.rest_3_ = bf16[512,128]{1,0:T(8,128)(2,1)S(1)} collective-permute-done((bf16[512,128]{1,0:T(8,128)(2,1)}, bf16[512,128]{1,0:T(8,128)(2,1)S(1)}, u32[]{:S(2)}, u32[]{:S(2)}) %collective-permute-start.2) | collective-permute-done | bytes 131104 | tf_op jit(solution)/shard_map/ppermute | solution.py:546
  21.9 0.0 copy-done.3
  21.9 0.0 copy-start.2
  21.9 2.3 %shard_map.122 = (bf16[512,128]{1,0:T(8,128)(2,1)S(1)}, bf16[512,128]{1,0:T(8,128)(2,1)S(1)}, bf16[512,128]{1,0:T(8,128)(2,1)S(1)}, bf16[512,128]{1,0:T(8,128)(2,1)S(1)}, f32[8,128]{1,0:T(8,128)S(1)}) custom-call(bf16[512,128]{1,0:T(8,128)(2,1)S(1)} %copy-done.3, bf16[512,128]{1,0:T(8,128)(2,1)S(1)} %collective-permute-done.rest_1_, ...), custom_call_target="tpu_custom_call" | custom-call | flops 17179869184 | bytes 1048576 | tf_op jit(solution)/shard_map/pallas_call | solution.py:497
  24.2 0.0 collective-permute-done.6.rest_5_
  24.2 1.3 %collective-permute-done.7.rest_6_ = bf16[512,128]{1,0:T(8,128)(2,1)S(1)} collective-permute-done((bf16[512,128]{1,0:T(8,128)(2,1)}, bf16[512,128]{1,0:T(8,128)(2,1)S(1)}, u32[]{:S(2)}, u32[]{:S(2)}) %collective-permute-start.7) | collective-permute-done | bytes 131104 | tf_op jit(solution)/shard_map/ppermute | solution.py:546
  25.5 0.0 collective-permute-done.8.rest_7_
  25.5 0.0 copy-done.2
  25.5 2.4 %shard_map.123 = (bf16[1024,128]{1,0:T(8,128)(2,1)S(1)}, bf16[1024,128]{1,0:T(8,128)(2,1)S(1)}, bf16[1024,128]{1,0:T(8,128)(2,1)S(1)}, bf16[1024,128]{1,0:T(8,128)(2,1)S(1)}, f32[8,128]{1,0:T(8,128)S(1)}) custom-call(bf16[512,128]{1,0:T(8,128)(2,1)S(1)} %get-tuple-element.53.rest_0_, bf16[512,128]{1,0:T(8,128)(2,1)S(1)} %get-tuple-element.54.rest_1_, ...), custom_call_target="tpu_custom_call" | custom-call | flops 17179869184 | bytes 1048576 | tf_op jit(solution)/shard_map/pallas_call | solution.py:497
  27.9 1.0 %collective-permute-start.12 = (bf16[1024,128]{1,0:T(8,128)(2,1)S(1)}, bf16[1024,128]{1,0:T(8,128)(2,1)S(1)}, u32[]{:S(2)}, u32[]{:S(2)}) collective-permute-start(bf16[1024,128]{1,0:T(8,128)(2,1)S(1)} %get-tuple-element.64), channel_id=1, source_target_pairs={{0,1},{1,0},{2,3},{3,2},{4,5},{5,4},{6,7},{7,6},{8,9},{9,8},{10,11... | collective-permute-start | bytes 786440 | tf_op jit(solution)/shard_map/ppermute | solution.py:572
  28.9 0.9 %collective-permute-start.13 = (bf16[1024,128]{1,0:T(8,128)(2,1)S(1)}, bf16[1024,128]{1,0:T(8,128)(2,1)S(1)}, u32[]{:S(2)}, u32[]{:S(2)}) collective-permute-start(bf16[1024,128]{1,0:T(8,128)(2,1)S(1)} %get-tuple-element.65), channel_id=1, source_target_pairs={{0,2},{1,3},{2,0},{3,1},{4,6},{5,7},{6,4},{7,5},{8,10},{9,11},{10,... | collective-permute-start | bytes 786440 | tf_op jit(solution)/shard_map/ppermute | solution.py:572
  29.8 1.6 %collective-permute-start.14 = (bf16[1024,128]{1,0:T(8,128)(2,1)S(1)}, bf16[1024,128]{1,0:T(8,128)(2,1)S(1)}, u32[]{:S(2)}, u32[]{:S(2)}) collective-permute-start(bf16[1024,128]{1,0:T(8,128)(2,1)S(1)} %get-tuple-element.68), channel_id=1, source_target_pairs={{0,3},{1,2},{2,1},{3,0},{4,7},{5,6},{6,5},{7,4},{8,11},{9,10},{10,... | collective-permute-start | bytes 786440 | tf_op jit(solution)/shard_map/ppermute | solution.py:572
  31.4 0.0 collective-permute-start.9
  31.4 1.2 %collective-permute-done.9 = f32[8,128]{1,0:T(8,128)S(1)} collective-permute-done((f32[8,128]{1,0:T(8,128)S(1)}, f32[8,128]{1,0:T(8,128)S(1)}, u32[]{:S(2)}, u32[]{:S(2)}) %collective-permute-start.9) | collective-permute-done | bytes 4128 | tf_op jit(solution)/shard_map/ppermute | solution.py:509
  32.6 1.6 %collective-permute-start.10 = (f32[8,128]{1,0:T(8,128)S(1)}, f32[8,128]{1,0:T(8,128)S(1)}, u32[]{:S(2)}, u32[]{:S(2)}) collective-permute-start(f32[8,128]{1,0:T(8,128)S(1)} %add.22), channel_id=1, source_target_pairs={{0,8},{4,12},{8,0},{12,4},{16,24},{20,28},{24,16},{28,20},{1,9},{5... | collective-permute-start | bytes 12296 | tf_op jit(solution)/shard_map/ppermute | solution.py:509
  34.2 2.0 %collective-permute-done.10 = f32[8,128]{1,0:T(8,128)S(1)} collective-permute-done((f32[8,128]{1,0:T(8,128)S(1)}, f32[8,128]{1,0:T(8,128)S(1)}, u32[]{:S(2)}, u32[]{:S(2)}) %collective-permute-start.10) | collective-permute-done | bytes 4128 | tf_op jit(solution)/shard_map/ppermute | solution.py:509
  36.2 2.6 %collective-permute-start.11 = (f32[8,128]{1,0:T(8,128)S(1)}, f32[8,128]{1,0:T(8,128)S(1)}, u32[]{:S(2)}, u32[]{:S(2)}) collective-permute-start(f32[8,128]{1,0:T(8,128)S(1)} %add.23), channel_id=1, source_target_pairs={{0,16},{4,20},{8,24},{12,28},{16,0},{20,4},{24,8},{28,12},{1,17},{... | collective-permute-start | bytes 12296 | tf_op jit(solution)/shard_map/ppermute | solution.py:509
  38.8 1.9 %collective-permute-done.11 = f32[8,128]{1,0:T(8,128)S(1)} collective-permute-done((f32[8,128]{1,0:T(8,128)S(1)}, f32[8,128]{1,0:T(8,128)S(1)}, u32[]{:S(2)}, u32[]{:S(2)}) %collective-permute-start.11) | collective-permute-done | bytes 4128 | tf_op jit(solution)/shard_map/ppermute | solution.py:509
  40.7 0.0 collective-permute-done.12.rest_1_
  40.7 0.0 collective-permute-done.13.rest_2_
  40.8 1.6 %collective-permute-start.17 = (f32[8,128]{1,0:T(8,128)S(1)}, f32[8,128]{1,0:T(8,128)S(1)}, u32[]{:S(2)}, u32[]{:S(2)}) collective-permute-start(f32[8,128]{1,0:T(8,128)S(1)} %add.24), channel_id=1, source_target_pairs={{0,3},{1,2},{2,1},{3,0},{4,7},{5,6},{6,5},{7,4},{8,11},{9,10},{10,... | collective-permute-start | bytes 12296 | tf_op jit(solution)/shard_map/ppermute | solution.py:509
  42.3 1.0 %collective-permute-start.16 = (f32[8,128]{1,0:T(8,128)S(1)}, f32[8,128]{1,0:T(8,128)S(1)}, u32[]{:S(2)}, u32[]{:S(2)}) collective-permute-start(f32[8,128]{1,0:T(8,128)S(1)} %add.24), channel_id=1, source_target_pairs={{0,2},{1,3},{2,0},{3,1},{4,6},{5,7},{6,4},{7,5},{8,10},{9,11},{10,... | collective-permute-start | bytes 12296 | tf_op jit(solution)/shard_map/ppermute | solution.py:509
  43.3 1.0 %collective-permute-start.15 = (f32[8,128]{1,0:T(8,128)S(1)}, f32[8,128]{1,0:T(8,128)S(1)}, u32[]{:S(2)}, u32[]{:S(2)}) collective-permute-start(f32[8,128]{1,0:T(8,128)S(1)} %add.24), channel_id=1, source_target_pairs={{0,1},{1,0},{2,3},{3,2},{4,5},{5,4},{6,7},{7,6},{8,9},{9,8},{10,11... | collective-permute-start | bytes 12296 | tf_op jit(solution)/shard_map/ppermute | solution.py:509
  44.3 0.0 collective-permute-done.14.rest_3_
  44.3 1.8 %shard_map.124 = (bf16[2048,128]{1,0:T(8,128)(2,1)}, bf16[1024,128]{1,0:T(8,128)(2,1)}, bf16[1024,128]{1,0:T(8,128)(2,1)}) custom-call(bf16[1024,128]{1,0:T(8,128)(2,1)S(1)} %get-tuple-element.61.rest_0_, bf16[1024,128]{1,0:T(8,128)(2,1)S(1)} %collective-permute-done.12.rest_1_, bf16[1024,128]{1,0:T(8,128)(2,1)S(1)} %collective-permute-done.13.rest_2_, ...), custom_call_target="tpu_custom_call" | custom-call | flops 1048576 | bytes 1048576 | tf_op jit(solution)/shard_map/pallas_call | solution.py:497
  46.1 0.0 collective-permute-done.17
  46.1 0.0 collective-permute-done.16
  46.1 0.8 %collective-permute-done.15 = f32[8,128]{1,0:T(8,128)S(1)} collective-permute-done((f32[8,128]{1,0:T(8,128)S(1)}, f32[8,128]{1,0:T(8,128)S(1)}, u32[]{:S(2)}, u32[]{:S(2)}) %collective-permute-start.15) | collective-permute-done | bytes 4128 | tf_op jit(solution)/shard_map/ppermute | solution.py:509
  46.9 0.5 %slice_bitcast_fusion = (f32[128]{0:T(128)}, f32[128]{0:T(128)}) fusion(f32[8,128]{1,0:T(8,128)S(1)} %add_add_fusion), kind=kLoop, calls=%fused_computation.2 | loop fusion | bytes 2048 | tf_op jit(solution)/shard_map/squeeze | solution.py:585
  (6 shorter events, 0.0 us)
Async XLA Ops:
  2.6 11.6 %collective-permute-start.3 = (bf16[528,128]{1,0:T(8,128)(2,1)}, bf16[528,128]{1,0:T(8,128)(2,1)S(1)}, u32[]{:S(2)}, u32[]{:S(2)}) collective-permute-start(bf16[528,128]{1,0:T(8,128)(2,1)} %get-tuple-element.44), channel_id=1, source_target_pairs={{0,1},{1,0},{2,3},{3,2},{4,5},{5,4},{6,7},{7,6},{8,9},{9,8},{10,11... | collective-permute-start | bytes 405512 | tf_op jit(solution)/shard_map/ppermute | solution.py:546
  5.6 8.7 %collective-permute-start.4 = (bf16[528,128]{1,0:T(8,128)(2,1)}, bf16[528,128]{1,0:T(8,128)(2,1)S(1)}, u32[]{:S(2)}, u32[]{:S(2)}) collective-permute-start(bf16[528,128]{1,0:T(8,128)(2,1)} %get-tuple-element.45), channel_id=1, source_target_pairs={{0,2},{1,3},{2,0},{3,1},{4,6},{5,7},{6,4},{7,5},{8,10},{9,11},{10,... | collective-permute-start | bytes 405512 | tf_op jit(solution)/shard_map/ppermute | solution.py:546
  7.1 9.1 %collective-permute-start.5 = (bf16[528,128]{1,0:T(8,128)(2,1)}, bf16[528,128]{1,0:T(8,128)(2,1)S(1)}, u32[]{:S(2)}, u32[]{:S(2)}) collective-permute-start(bf16[528,128]{1,0:T(8,128)(2,1)} %get-tuple-element.46), channel_id=1, source_target_pairs={{0,3},{1,2},{2,1},{3,0},{4,7},{5,6},{6,5},{7,4},{8,11},{9,10},{10,... | collective-permute-start | bytes 405512 | tf_op jit(solution)/shard_map/ppermute | solution.py:546
  7.1 10.6 %copy-start = (bf16[528,128]{1,0:T(8,128)(2,1)S(1)}, bf16[528,128]{1,0:T(8,128)(2,1)}, u32[]{:S(2)}) copy-start(bf16[528,128]{1,0:T(8,128)(2,1)} %get-tuple-element.39.rest_0_) | copy-start | bytes 405508
  7.1 10.6 %copy-start.1 = (f32[4,2,64,128]{3,2,1,0:T(8,128)S(1)}, f32[4,2,64,128]{3,2,1,0:T(8,128)}, u32[]{:S(2)}) copy-start(f32[4,2,64,128]{3,2,1,0:T(8,128)} %constant.4.clone.rest_4_.rest_10_.rest_14_) | copy-start | bytes 786436
  9.9 8.8 %collective-permute-start = (bf16[512,128]{1,0:T(8,128)(2,1)}, bf16[512,128]{1,0:T(8,128)(2,1)S(1)}, u32[]{:S(2)}, u32[]{:S(2)}) collective-permute-start(bf16[512,128]{1,0:T(8,128)(2,1)} %get-tuple-element.41), channel_id=1, source_target_pairs={{0,1},{1,0},{2,3},{3,2},{4,5},{5,4},{6,7},{7,6},{8,9},{9,8},{10,11... | collective-permute-start | bytes 393224 | tf_op jit(solution)/shard_map/ppermute | solution.py:546
  11.9 9.4 %collective-permute-start.1 = (bf16[512,128]{1,0:T(8,128)(2,1)}, bf16[512,128]{1,0:T(8,128)(2,1)S(1)}, u32[]{:S(2)}, u32[]{:S(2)}) collective-permute-start(bf16[512,128]{1,0:T(8,128)(2,1)} %get-tuple-element.42), channel_id=1, source_target_pairs={{0,2},{1,3},{2,0},{3,1},{4,6},{5,7},{6,4},{7,5},{8,10},{9,11},{10,... | collective-permute-start | bytes 393224 | tf_op jit(solution)/shard_map/ppermute | solution.py:546
  13.5 0.7 %copy-start.4 = (f32[128]{0:T(128)S(1)}, f32[128]{0:T(128)}, u32[]{:S(2)}) copy-start(f32[128]{0:T(128)} %param.14) | copy-start | bytes 1540
  13.5 0.7 %copy-start.5 = (f32[128]{0:T(128)S(1)}, f32[128]{0:T(128)}, u32[]{:S(2)}) copy-start(f32[128]{0:T(128)} %param.13) | copy-start | bytes 1540
  14.2 7.7 %collective-permute-start.2 = (bf16[512,128]{1,0:T(8,128)(2,1)}, bf16[512,128]{1,0:T(8,128)(2,1)S(1)}, u32[]{:S(2)}, u32[]{:S(2)}) collective-permute-start(bf16[512,128]{1,0:T(8,128)(2,1)} %get-tuple-element.43), channel_id=1, source_target_pairs={{0,3},{1,2},{2,1},{3,0},{4,7},{5,6},{6,5},{7,4},{8,11},{9,10},{10,... | collective-permute-start | bytes 393224 | tf_op jit(solution)/shard_map/ppermute | solution.py:546
  14.3 10.0 %collective-permute-start.6 = (bf16[512,128]{1,0:T(8,128)(2,1)}, bf16[512,128]{1,0:T(8,128)(2,1)S(1)}, u32[]{:S(2)}, u32[]{:S(2)}) collective-permute-start(bf16[512,128]{1,0:T(8,128)(2,1)} %get-tuple-element.58), channel_id=1, source_target_pairs={{0,1},{1,0},{2,3},{3,2},{4,5},{5,4},{6,7},{7,6},{8,9},{9,8},{10,11... | collective-permute-start | bytes 393224 | tf_op jit(solution)/shard_map/ppermute | solution.py:546
  16.2 2.4 %copy-start.6 = (bf16[512,128]{1,0:T(8,128)(2,1)S(1)}, bf16[512,128]{1,0:T(8,128)(2,1)}, u32[]{:S(2)}) copy-start(bf16[512,128]{1,0:T(8,128)(2,1)} %get-tuple-element.60) | copy-start | bytes 393220
  16.2 5.7 %copy-start.3 = (bf16[512,128]{1,0:T(8,128)(2,1)S(1)}, bf16[512,128]{1,0:T(8,128)(2,1)}, u32[]{:S(2)}) copy-start(bf16[512,128]{1,0:T(8,128)(2,1)} %get-tuple-element.40.rest_0_) | copy-start | bytes 393220
  16.2 9.3 %collective-permute-start.7 = (bf16[512,128]{1,0:T(8,128)(2,1)}, bf16[512,128]{1,0:T(8,128)(2,1)S(1)}, u32[]{:S(2)}, u32[]{:S(2)}) collective-permute-start(bf16[512,128]{1,0:T(8,128)(2,1)} %get-tuple-element.59), channel_id=1, source_target_pairs={{0,2},{1,3},{2,0},{3,1},{4,6},{5,7},{6,4},{7,5},{8,10},{9,11},{10,... | collective-permute-start | bytes 393224 | tf_op jit(solution)/shard_map/ppermute | solution.py:546
  18.6 6.8 %collective-permute-start.8 = (bf16[512,128]{1,0:T(8,128)(2,1)S(1)}, bf16[512,128]{1,0:T(8,128)(2,1)S(1)}, u32[]{:S(2)}, u32[]{:S(2)}) collective-permute-start(bf16[512,128]{1,0:T(8,128)(2,1)S(1)} %copy-done.6), channel_id=1, source_target_pairs={{0,3},{1,2},{2,1},{3,0},{4,7},{5,6},{6,5},{7,4},{8,11},{9,10},{10,... | collective-permute-start | bytes 393224 | tf_op jit(solution)/shard_map/ppermute | solution.py:546
  21.9 3.6 %copy-start.2 = (bf16[512,128]{1,0:T(8,128)(2,1)S(1)}, bf16[512,128]{1,0:T(8,128)(2,1)}, u32[]{:S(2)}) copy-start(bf16[512,128]{1,0:T(8,128)(2,1)} %get-tuple-element.57.rest_4_) | copy-start | bytes 393220
  27.9 12.9 %collective-permute-start.12 = (bf16[1024,128]{1,0:T(8,128)(2,1)S(1)}, bf16[1024,128]{1,0:T(8,128)(2,1)S(1)}, u32[]{:S(2)}, u32[]{:S(2)}) collective-permute-start(bf16[1024,128]{1,0:T(8,128)(2,1)S(1)} %get-tuple-element.64), channel_id=1, source_target_pairs={{0,1},{1,0},{2,3},{3,2},{4,5},{5,4},{6,7},{7,6},{8,9},{9,8},{10,11... | collective-permute-start | bytes 786440 | tf_op jit(solution)/shard_map/ppermute | solution.py:572
  28.9 11.9 %collective-permute-start.13 = (bf16[1024,128]{1,0:T(8,128)(2,1)S(1)}, bf16[1024,128]{1,0:T(8,128)(2,1)S(1)}, u32[]{:S(2)}, u32[]{:S(2)}) collective-permute-start(bf16[1024,128]{1,0:T(8,128)(2,1)S(1)} %get-tuple-element.65), channel_id=1, source_target_pairs={{0,2},{1,3},{2,0},{3,1},{4,6},{5,7},{6,4},{7,5},{8,10},{9,11},{10,... | collective-permute-start | bytes 786440 | tf_op jit(solution)/shard_map/ppermute | solution.py:572
  29.8 14.5 %collective-permute-start.14 = (bf16[1024,128]{1,0:T(8,128)(2,1)S(1)}, bf16[1024,128]{1,0:T(8,128)(2,1)S(1)}, u32[]{:S(2)}, u32[]{:S(2)}) collective-permute-start(bf16[1024,128]{1,0:T(8,128)(2,1)S(1)} %get-tuple-element.68), channel_id=1, source_target_pairs={{0,3},{1,2},{2,1},{3,0},{4,7},{5,6},{6,5},{7,4},{8,11},{9,10},{10,... | collective-permute-start | bytes 786440 | tf_op jit(solution)/shard_map/ppermute | solution.py:572
  31.4 1.2 %collective-permute-start.9 = (f32[8,128]{1,0:T(8,128)S(1)}, f32[8,128]{1,0:T(8,128)S(1)}, u32[]{:S(2)}, u32[]{:S(2)}) collective-permute-start(f32[8,128]{1,0:T(8,128)S(1)} %add.21), channel_id=1, source_target_pairs={{0,4},{4,0},{8,12},{12,8},{16,20},{20,16},{24,28},{28,24},{1,5},{5... | collective-permute-start | bytes 12296 | tf_op jit(solution)/shard_map/ppermute | solution.py:509
  32.6 3.6 %collective-permute-start.10 = (f32[8,128]{1,0:T(8,128)S(1)}, f32[8,128]{1,0:T(8,128)S(1)}, u32[]{:S(2)}, u32[]{:S(2)}) collective-permute-start(f32[8,128]{1,0:T(8,128)S(1)} %add.22), channel_id=1, source_target_pairs={{0,8},{4,12},{8,0},{12,4},{16,24},{20,28},{24,16},{28,20},{1,9},{5... | collective-permute-start | bytes 12296 | tf_op jit(solution)/shard_map/ppermute | solution.py:509
  36.2 4.5 %collective-permute-start.11 = (f32[8,128]{1,0:T(8,128)S(1)}, f32[8,128]{1,0:T(8,128)S(1)}, u32[]{:S(2)}, u32[]{:S(2)}) collective-permute-start(f32[8,128]{1,0:T(8,128)S(1)} %add.23), channel_id=1, source_target_pairs={{0,16},{4,20},{8,24},{12,28},{16,0},{20,4},{24,8},{28,12},{1,17},{... | collective-permute-start | bytes 12296 | tf_op jit(solution)/shard_map/ppermute | solution.py:509
  40.8 5.3 %collective-permute-start.17 = (f32[8,128]{1,0:T(8,128)S(1)}, f32[8,128]{1,0:T(8,128)S(1)}, u32[]{:S(2)}, u32[]{:S(2)}) collective-permute-start(f32[8,128]{1,0:T(8,128)S(1)} %add.24), channel_id=1, source_target_pairs={{0,3},{1,2},{2,1},{3,0},{4,7},{5,6},{6,5},{7,4},{8,11},{9,10},{10,... | collective-permute-start | bytes 12296 | tf_op jit(solution)/shard_map/ppermute | solution.py:509
  42.3 3.7 %collective-permute-start.16 = (f32[8,128]{1,0:T(8,128)S(1)}, f32[8,128]{1,0:T(8,128)S(1)}, u32[]{:S(2)}, u32[]{:S(2)}) collective-permute-start(f32[8,128]{1,0:T(8,128)S(1)} %add.24), channel_id=1, source_target_pairs={{0,2},{1,3},{2,0},{3,1},{4,6},{5,7},{6,4},{7,5},{8,10},{9,11},{10,... | collective-permute-start | bytes 12296 | tf_op jit(solution)/shard_map/ppermute | solution.py:509
  43.3 3.6 %collective-permute-start.15 = (f32[8,128]{1,0:T(8,128)S(1)}, f32[8,128]{1,0:T(8,128)S(1)}, u32[]{:S(2)}, u32[]{:S(2)}) collective-permute-start(f32[8,128]{1,0:T(8,128)S(1)} %add.24), channel_id=1, source_target_pairs={{0,1},{1,0},{2,3},{3,2},{4,5},{5,4},{6,7},{7,6},{8,9},{9,8},{10,11... | collective-permute-start | bytes 12296 | tf_op jit(solution)/shard_map/ppermute | solution.py:509

commit v6 on v5

--- a/solution.py
+++ b/solution.py
@@ -13,6 +13,7 @@
 ROPE_BASE = 1000000.0
 ROPE_FACTOR = 8.0
 GROUPS = 2
+PIECES = 4
 NEG = -1e30
 SCALE = float(PRESCALE) ** (-0.5)
 LOG2E = 1.4426950408889634
@@ -469,22 +470,24 @@
     per = kv_heads // parts // groups
     block = q_out.shape[0] // heads
     me = lax.axis_index(axis)
-    for m in range(parts):
-        at = 0
-        for grp in range(groups):
-            for p in range(per):
-                kv = ((me ^ m) * groups + grp) * per + p
-                pieces = [(q_f32, kv * group + i, heads) for i in range(group)]
-                pieces += [(k_f32, kv, kv_heads), (v_f32, kv, kv_heads)]
-                for dst, head, stride in pieces:
-                    rows = msgs[m][pl.ds(at, block), :].astype(jnp.float32)
-                    dst[pl.ds(head, block, stride=stride), :] = rows
-                    at += block
+    arrays = ((q_f32, q_out, gq_hbm, heads), (k_f32, k_out, gk_hbm, kv_heads), (v_f32, v_out, gv_hbm, kv_heads))
+    tokens = block // PIECES
     stores = []
-    for src, out, dst in ((q_f32, q_out, gq_hbm), (k_f32, k_out, gk_hbm), (v_f32, v_out, gv_hbm)):
-        half = out.shape[0] // 2
-        for i in range(2):
-            cut = pl.ds(i * half, half)
+    for piece in range(PIECES):
+        start = piece * tokens
+        for m in range(parts):
+            at = start
+            for grp in range(groups):
+                for p in range(per):
+                    kv = ((me ^ m) * groups + grp) * per + p
+                    places = [(0, kv * group + i) for i in range(group)] + [(1, kv), (2, kv)]
+                    for which, head in places:
+                        dst, _, _, stride = arrays[which]
+                        rows = msgs[m][pl.ds(at, tokens), :].astype(jnp.float32)
+                        dst[pl.ds(start * stride + head, tokens, stride=stride), :] = rows
+                        at += block
+        for src, out, dst, stride in arrays:
+            cut = pl.ds(start * stride, tokens * stride)
             out[cut, :] = src[cut, :].astype(jnp.bfloat16)
             copy = pltpu.make_async_copy(out.at[cut], dst.at[cut], sems.at[len(stores)])
             copy.start()
@@ -569,16 +572,16 @@
         )
         results = made
         shares.append(share)
-    first, second, third = (lax.ppermute(results[m], "seq", xor(m, parts)) for m in (1, 2, 3))
-    total = exchange_sum(functools.reduce(jnp.add, shares), "dp", spans, 1)
-    total = exchange_sum(exchange_sum(total, "dp", spans, 2), "dp", spans, 4)
-    total, first, second = lax.optimization_barrier((total, first, second))
+    go = lambda m: lax.ppermute(results[m], "seq", xor(m, parts))
+    total = functools.reduce(jnp.add, shares)
+    first, second, third = go(1), go(2), go(3)
     total = exchange_sum(total, "seq", parts, 1, 2, 3)
+    total = exchange_sum(exchange_sum(exchange_sum(total, "dp", spans, 1), "dp", spans, 2), "dp", spans, 4)
     grad_q, grad_k, grad_v = call_in(
         functools.partial(collect_kernel, "seq", parts, groups, heads, kv_heads),
         [vmem] * parts, [(q_shape, bf16, hbm), (k_shape, bf16, hbm), (k_shape, bf16, hbm)],
         [vmem(q_shape, f32), vmem(k_shape, f32), vmem(k_shape, f32)]
-        + [vmem(q_shape, bf16), vmem(k_shape, bf16), vmem(k_shape, bf16), dma((6,))],
+        + [vmem(q_shape, bf16), vmem(k_shape, bf16), vmem(k_shape, bf16), dma((3 * PIECES,))],
         1 << 20, results[0], first, second, third,
     )
     return (

time: 47.6 us -> 46.5 us (0.977)
  waiting for transfers between devices: 10 us -> 9.15 us
    ppermute x6, waiting for transfers between devices: 5.97 us -> 5.11 us  [exchange_sum(): lax.ppermute(x, axis, [(i, i ^ m) for i in range(size)])]
  transfers between devices with their start and end apart: 18 -> 18, of which waited for: 7 -> 6; matrix products, arithmetic and copies ran while one was open for 0% -> 1% of each run, Pallas kernels for 16% -> 13%
where the time goes in v6:
time: 46.5 us; the launch traced here: 46.3 us
  starting transfers between devices  23.3 us (50%)
  Pallas kernels  11.7 us (25%)
  waiting for transfers between devices  9.15 us (20%)
  local copies, waits for them, and re-layouts  1.29 us (3%)
  between operations  0.72 us (2%)
    ppermute x9, starting transfers between devices, by_heads(): lax.ppermute(out[m], 'seq', xor(m, parts))  12.1 us
    pallas_call x6, Pallas kernels, call_in(): pl.pallas_call(kernel, out_shape=[jax.ShapeDtypeStruct(s, t) for s, t, _...  11.7 us
    ppermute x6, starting transfers between devices, exchange_sum(): lax.ppermute(x, axis, [(i, i ^ m) for i in range(size)])  7.78 us
    ppermute x6, waiting for transfers between devices, exchange_sum(): lax.ppermute(x, axis, [(i, i ^ m) for i in range(size)])  5.11 us
    ppermute x9, waiting for transfers between devices, by_heads(): lax.ppermute(out[m], 'seq', xor(m, parts))  4.03 us
    ppermute x3, starting transfers between devices, by_heads(): go = lambda m: lax.ppermute(results[m], 'seq', xor(m, parts))  3.49 us
  transfers between devices with their start and end apart: 18, of which 6 were waited for; matrix products, arithmetic and copies ran while one was open for 1% of the time, Pallas kernels for 13%

profile of v6, /device:TPU:0, one launch (start us, length us, event | category | flops | bytes accessed | tf_op | source)
XLA Modules:
  0.0 46.3 jit_solution(8598018874355379976)
XLA Ops:
  0.6 2.0 %shard_map.119 = (bf16[528,128]{1,0:T(8,128)(2,1)}, bf16[528,128]{1,0:T(8,128)(2,1)}, bf16[528,128]{1,0:T(8,128)(2,1)}, bf16[528,128]{1,0:T(8,128)(2,1)}) custom-call(bf16[1024,128]{1,0:T(8,128)(2,1)} %bitcast.13, bf16[1024,128]{1,0:T(8,128)(2,1)} %bitcast.14, s32[1,128]{1,0:T(1,128)} %rest_0_.1), custom_call_target="tpu_custom_call" | custom-call | flops 1048576 | bytes 1048576 | tf_op jit(solution)/shard_map/pallas_call | solution.py:500
  2.6 3.0 %collective-permute-start.3 = (bf16[528,128]{1,0:T(8,128)(2,1)}, bf16[528,128]{1,0:T(8,128)(2,1)S(1)}, u32[]{:S(2)}, u32[]{:S(2)}) collective-permute-start(bf16[528,128]{1,0:T(8,128)(2,1)} %get-tuple-element.41), channel_id=1, source_target_pairs={{0,1},{1,0},{2,3},{3,2},{4,5},{5,4},{6,7},{7,6},{8,9},{9,8},{10,11... | collective-permute-start | bytes 405512 | tf_op jit(solution)/shard_map/ppermute | solution.py:549
  5.6 1.5 %collective-permute-start.4 = (bf16[528,128]{1,0:T(8,128)(2,1)}, bf16[528,128]{1,0:T(8,128)(2,1)S(1)}, u32[]{:S(2)}, u32[]{:S(2)}) collective-permute-start(bf16[528,128]{1,0:T(8,128)(2,1)} %get-tuple-element.42), channel_id=1, source_target_pairs={{0,2},{1,3},{2,0},{3,1},{4,6},{5,7},{6,4},{7,5},{8,10},{9,11},{10,... | collective-permute-start | bytes 405512 | tf_op jit(solution)/shard_map/ppermute | solution.py:549
  7.1 0.0 collective-permute-start.5
  7.1 0.0 copy-start
  7.1 0.0 copy-start.1
  7.1 2.7 %shard_map.120 = (bf16[512,128]{1,0:T(8,128)(2,1)}, bf16[512,128]{1,0:T(8,128)(2,1)}, bf16[512,128]{1,0:T(8,128)(2,1)}, bf16[512,128]{1,0:T(8,128)(2,1)}, bf16[5...) custom-call(bf16[2048,128]{1,0:T(8,128)(2,1)} %bitcast.17, ...), custom_call_target="tpu_custom_call" | custom-call | flops 8589934592 | bytes 1048576 | tf_op jit(solution)/shard_map/pallas_call | solution.py:500
  9.9 2.0 %collective-permute-start = (bf16[512,128]{1,0:T(8,128)(2,1)}, bf16[512,128]{1,0:T(8,128)(2,1)S(1)}, u32[]{:S(2)}, u32[]{:S(2)}) collective-permute-start(bf16[512,128]{1,0:T(8,128)(2,1)} %get-tuple-element.38), channel_id=1, source_target_pairs={{0,1},{1,0},{2,3},{3,2},{4,5},{5,4},{6,7},{7,6},{8,9},{9,8},{10,11... | collective-permute-start | bytes 393224 | tf_op jit(solution)/shard_map/ppermute | solution.py:549
  11.9 1.5 %collective-permute-start.1 = (bf16[512,128]{1,0:T(8,128)(2,1)}, bf16[512,128]{1,0:T(8,128)(2,1)S(1)}, u32[]{:S(2)}, u32[]{:S(2)}) collective-permute-start(bf16[512,128]{1,0:T(8,128)(2,1)} %get-tuple-element.39), channel_id=1, source_target_pairs={{0,2},{1,3},{2,0},{3,1},{4,6},{5,7},{6,4},{7,5},{8,10},{9,11},{10,... | collective-permute-start | bytes 393224 | tf_op jit(solution)/shard_map/ppermute | solution.py:549
  13.4 0.1 pad.2.clone
  13.5 0.0 copy-start.4
  13.5 0.0 copy-start.5
  13.5 0.7 %copy-done.4 = f32[128]{0:T(128)S(1)} copy-done((f32[128]{0:T(128)S(1)}, f32[128]{0:T(128)}, u32[]{:S(2)}) %copy-start.4) | copy-done | bytes 536
  14.1 0.0 copy-done.5
  14.2 0.1 maximum_maximum_fusion.rest_5_.rest_11_.rest_15_
  14.2 0.0 collective-permute-done.3.rest_1_
  14.2 0.0 collective-permute-start.2
  14.3 0.0 collective-permute-done.4.rest_2_
  14.3 1.9 %collective-permute-start.6 = (bf16[512,128]{1,0:T(8,128)(2,1)}, bf16[512,128]{1,0:T(8,128)(2,1)S(1)}, u32[]{:S(2)}, u32[]{:S(2)}) collective-permute-start(bf16[512,128]{1,0:T(8,128)(2,1)} %get-tuple-element.55), channel_id=1, source_target_pairs={{0,1},{1,0},{2,3},{3,2},{4,5},{5,4},{6,7},{7,6},{8,9},{9,8},{10,11... | collective-permute-start | bytes 393224 | tf_op jit(solution)/shard_map/ppermute | solution.py:549
  16.2 0.0 collective-permute-done.5.rest_3_
  16.2 0.0 copy-start.6
  16.2 0.0 copy-start.3
  16.2 1.5 %collective-permute-start.7 = (bf16[512,128]{1,0:T(8,128)(2,1)}, bf16[512,128]{1,0:T(8,128)(2,1)S(1)}, u32[]{:S(2)}, u32[]{:S(2)}) collective-permute-start(bf16[512,128]{1,0:T(8,128)(2,1)} %get-tuple-element.56), channel_id=1, source_target_pairs={{0,2},{1,3},{2,0},{3,1},{4,6},{5,7},{6,4},{7,5},{8,10},{9,11},{10,... | collective-permute-start | bytes 393224 | tf_op jit(solution)/shard_map/ppermute | solution.py:549
  17.7 0.0 copy-done
  17.8 0.0 copy-done.1
  17.8 0.9 %shard_map.121 = (bf16[4,2,128,128]{3,2,1,0:T(8,128)(2,1)S(1)}, bf16[4,2,128,128]{3,2,1,0:T(8,128)(2,1)S(1)}, bf16[4,2,128,128]{3,2,1,0:T(8,128)(2,1)S(1)}, f32[...) custom-call(bf16[528,128]{1,0:T(8,128)(2,1)S(1)} %copy-done, ...), custom_call_target="tpu_custom_call" | custom-call | flops 8589934592 | bytes 1048576 | tf_op jit(solution)/shard_map/pallas_call | solution.py:500
  18.6 0.0 collective-permute-done.rest_1_
  18.6 0.0 copy-done.6
  18.6 0.5 %collective-permute-start.8 = (bf16[512,128]{1,0:T(8,128)(2,1)S(1)}, bf16[512,128]{1,0:T(8,128)(2,1)S(1)}, u32[]{:S(2)}, u32[]{:S(2)}) collective-permute-start(bf16[512,128]{1,0:T(8,128)(2,1)S(1)} %copy-done.6), channel_id=1, source_target_pairs={{0,3},{1,2},{2,1},{3,0},{4,7},{5,6},{6,5},{7,4},{8,11},{9,10},{10,... | collective-permute-start | bytes 393224 | tf_op jit(solution)/shard_map/ppermute | solution.py:549
  19.1 2.1 %collective-permute-done.1.rest_2_ = bf16[512,128]{1,0:T(8,128)(2,1)S(1)} collective-permute-done((bf16[512,128]{1,0:T(8,128)(2,1)}, bf16[512,128]{1,0:T(8,128)(2,1)S(1)}, u32[]{:S(2)}, u32[]{:S(2)}) %collective-permute-start.1) | collective-permute-done | bytes 131104 | tf_op jit(solution)/shard_map/ppermute | solution.py:549
  21.3 0.6 %collective-permute-done.2.rest_3_ = bf16[512,128]{1,0:T(8,128)(2,1)S(1)} collective-permute-done((bf16[512,128]{1,0:T(8,128)(2,1)}, bf16[512,128]{1,0:T(8,128)(2,1)S(1)}, u32[]{:S(2)}, u32[]{:S(2)}) %collective-permute-start.2) | collective-permute-done | bytes 131104 | tf_op jit(solution)/shard_map/ppermute | solution.py:549
  21.9 0.0 copy-done.3
  21.9 0.0 copy-start.2
  21.9 2.3 %shard_map.122 = (bf16[512,128]{1,0:T(8,128)(2,1)S(1)}, bf16[512,128]{1,0:T(8,128)(2,1)S(1)}, bf16[512,128]{1,0:T(8,128)(2,1)S(1)}, bf16[512,128]{1,0:T(8,128)(2,1)S(1)}, f32[8,128]{1,0:T(8,128)S(1)}) custom-call(bf16[512,128]{1,0:T(8,128)(2,1)S(1)} %copy-done.3, bf16[512,128]{1,0:T(8,128)(2,1)S(1)} %collective-permute-done.rest_1_, ...), custom_call_target="tpu_custom_call" | custom-call | flops 17179869184 | bytes 1048576 | tf_op jit(solution)/shard_map/pallas_call | solution.py:500
  24.2 0.0 collective-permute-done.6.rest_5_
  24.2 1.3 %collective-permute-done.7.rest_6_ = bf16[512,128]{1,0:T(8,128)(2,1)S(1)} collective-permute-done((bf16[512,128]{1,0:T(8,128)(2,1)}, bf16[512,128]{1,0:T(8,128)(2,1)S(1)}, u32[]{:S(2)}, u32[]{:S(2)}) %collective-permute-start.7) | collective-permute-done | bytes 131104 | tf_op jit(solution)/shard_map/ppermute | solution.py:549
  25.5 0.0 collective-permute-done.8.rest_7_
  25.5 0.0 copy-done.2
  25.5 2.4 %shard_map.123 = (bf16[1024,128]{1,0:T(8,128)(2,1)S(1)}, bf16[1024,128]{1,0:T(8,128)(2,1)S(1)}, bf16[1024,128]{1,0:T(8,128)(2,1)S(1)}, bf16[1024,128]{1,0:T(8,128)(2,1)S(1)}, f32[8,128]{1,0:T(8,128)S(1)}) custom-call(bf16[512,128]{1,0:T(8,128)(2,1)S(1)} %get-tuple-element.50.rest_0_, bf16[512,128]{1,0:T(8,128)(2,1)S(1)} %get-tuple-element.51.rest_1_, ...), custom_call_target="tpu_custom_call" | custom-call | flops 17179869184 | bytes 1048576 | tf_op jit(solution)/shard_map/pallas_call | solution.py:500
  27.9 1.4 %collective-permute-start.14 = (f32[8,128]{1,0:T(8,128)S(1)}, f32[8,128]{1,0:T(8,128)S(1)}, u32[]{:S(2)}, u32[]{:S(2)}) collective-permute-start(f32[8,128]{1,0:T(8,128)S(1)} %add.21), channel_id=1, source_target_pairs={{0,3},{1,2},{2,1},{3,0},{4,7},{5,6},{6,5},{7,4},{8,11},{9,10},{10,... | collective-permute-start | bytes 12296 | tf_op jit(solution)/shard_map/ppermute | solution.py:512
  29.2 1.1 %collective-permute-start.13 = (f32[8,128]{1,0:T(8,128)S(1)}, f32[8,128]{1,0:T(8,128)S(1)}, u32[]{:S(2)}, u32[]{:S(2)}) collective-permute-start(f32[8,128]{1,0:T(8,128)S(1)} %add.21), channel_id=1, source_target_pairs={{0,2},{1,3},{2,0},{3,1},{4,6},{5,7},{6,4},{7,5},{8,10},{9,11},{10,... | collective-permute-start | bytes 12296 | tf_op jit(solution)/shard_map/ppermute | solution.py:512
  30.4 1.1 %collective-permute-start.12 = (f32[8,128]{1,0:T(8,128)S(1)}, f32[8,128]{1,0:T(8,128)S(1)}, u32[]{:S(2)}, u32[]{:S(2)}) collective-permute-start(f32[8,128]{1,0:T(8,128)S(1)} %add.21), channel_id=1, source_target_pairs={{0,1},{1,0},{2,3},{3,2},{4,5},{5,4},{6,7},{7,6},{8,9},{9,8},{10,11... | collective-permute-start | bytes 12296 | tf_op jit(solution)/shard_map/ppermute | solution.py:512
  31.4 1.0 %collective-permute-start.9 = (bf16[1024,128]{1,0:T(8,128)(2,1)S(1)}, bf16[1024,128]{1,0:T(8,128)(2,1)S(1)}, u32[]{:S(2)}, u32[]{:S(2)}) collective-permute-start(bf16[1024,128]{1,0:T(8,128)(2,1)S(1)} %get-tuple-element.59), channel_id=1, source_target_pairs={{0,1},{1,0},{2,3},{3,2},{4,5},{5,4},{6,7},{7,6},{8,9},{9,8},{10,11... | collective-permute-start | bytes 786440 | tf_op jit(solution)/shard_map/ppermute | solution.py:575
  32.4 0.9 %collective-permute-start.10 = (bf16[1024,128]{1,0:T(8,128)(2,1)S(1)}, bf16[1024,128]{1,0:T(8,128)(2,1)S(1)}, u32[]{:S(2)}, u32[]{:S(2)}) collective-permute-start(bf16[1024,128]{1,0:T(8,128)(2,1)S(1)} %get-tuple-element.60), channel_id=1, source_target_pairs={{0,2},{1,3},{2,0},{3,1},{4,6},{5,7},{6,4},{7,5},{8,10},{9,11},{10,... | collective-permute-start | bytes 786440 | tf_op jit(solution)/shard_map/ppermute | solution.py:575
  33.3 0.0 collective-permute-done.14
  33.3 1.6 %collective-permute-start.11 = (bf16[1024,128]{1,0:T(8,128)(2,1)S(1)}, bf16[1024,128]{1,0:T(8,128)(2,1)S(1)}, u32[]{:S(2)}, u32[]{:S(2)}) collective-permute-start(bf16[1024,128]{1,0:T(8,128)(2,1)S(1)} %get-tuple-element.61), channel_id=1, source_target_pairs={{0,3},{1,2},{2,1},{3,0},{4,7},{5,6},{6,5},{7,4},{8,11},{9,10},{10,... | collective-permute-start | bytes 786440 | tf_op jit(solution)/shard_map/ppermute | solution.py:575
  34.9 0.0 collective-permute-done.13
  34.9 0.0 collective-permute-done.12
  34.9 0.1 collective-permute-start.15
  35.0 1.2 %collective-permute-done.15 = f32[8,128]{1,0:T(8,128)S(1)} collective-permute-done((f32[8,128]{1,0:T(8,128)S(1)}, f32[8,128]{1,0:T(8,128)S(1)}, u32[]{:S(2)}, u32[]{:S(2)}) %collective-permute-start.15) | collective-permute-done | bytes 4128 | tf_op jit(solution)/shard_map/ppermute | solution.py:512
  36.2 1.6 %collective-permute-start.16 = (f32[8,128]{1,0:T(8,128)S(1)}, f32[8,128]{1,0:T(8,128)S(1)}, u32[]{:S(2)}, u32[]{:S(2)}) collective-permute-start(f32[8,128]{1,0:T(8,128)S(1)} %add.25), channel_id=1, source_target_pairs={{0,8},{4,12},{8,0},{12,4},{16,24},{20,28},{24,16},{28,20},{1,9},{5... | collective-permute-start | bytes 12296 | tf_op jit(solution)/shard_map/ppermute | solution.py:512
  37.7 2.0 %collective-permute-done.16 = f32[8,128]{1,0:T(8,128)S(1)} collective-permute-done((f32[8,128]{1,0:T(8,128)S(1)}, f32[8,128]{1,0:T(8,128)S(1)}, u32[]{:S(2)}, u32[]{:S(2)}) %collective-permute-start.16) | collective-permute-done | bytes 4128 | tf_op jit(solution)/shard_map/ppermute | solution.py:512
  39.8 2.6 %collective-permute-start.17 = (f32[8,128]{1,0:T(8,128)S(1)}, f32[8,128]{1,0:T(8,128)S(1)}, u32[]{:S(2)}, u32[]{:S(2)}) collective-permute-start(f32[8,128]{1,0:T(8,128)S(1)} %add.26), channel_id=1, source_target_pairs={{0,16},{4,20},{8,24},{12,28},{16,0},{20,4},{24,8},{28,12},{1,17},{... | collective-permute-start | bytes 12296 | tf_op jit(solution)/shard_map/ppermute | solution.py:512
  42.4 1.9 %collective-permute-done.17 = f32[8,128]{1,0:T(8,128)S(1)} collective-permute-done((f32[8,128]{1,0:T(8,128)S(1)}, f32[8,128]{1,0:T(8,128)S(1)}, u32[]{:S(2)}, u32[]{:S(2)}) %collective-permute-start.17) | collective-permute-done | bytes 4128 | tf_op jit(solution)/shard_map/ppermute | solution.py:512
  44.3 0.5 %slice_bitcast_fusion = (f32[128]{0:T(128)}, f32[128]{0:T(128)}) fusion(f32[8,128]{1,0:T(8,128)S(1)} %add.27), kind=kLoop, calls=%fused_computation.2 | loop fusion | bytes 2048 | tf_op jit(solution)/shard_map/squeeze | solution.py:588
  44.8 0.0 collective-permute-done.9.rest_1_
  44.8 0.0 collective-permute-done.10.rest_2_
  44.8 0.0 collective-permute-done.11.rest_3_
  44.8 1.5 %shard_map.124 = (bf16[2048,128]{1,0:T(8,128)(2,1)}, bf16[1024,128]{1,0:T(8,128)(2,1)}, bf16[1024,128]{1,0:T(8,128)(2,1)}) custom-call(bf16[1024,128]{1,0:T(8,128)(2,1)S(1)} %get-tuple-element.58.rest_0_, bf16[1024,128]{1,0:T(8,128)(2,1)S(1)} %collective-permute-done.9.rest_1_, bf16[1024,128]{1,0:T(8,128)(2,1)S(1)} %collective-permute-done.10.rest_2_, ...), custom_call_target="tpu_custom_call" | custom-call | flops 1048576 | bytes 1048576 | tf_op jit(solution)/shard_map/pallas_call | solution.py:500
  (6 shorter events, 0.0 us)
Async XLA Ops:
  2.6 11.6 %collective-permute-start.3 = (bf16[528,128]{1,0:T(8,128)(2,1)}, bf16[528,128]{1,0:T(8,128)(2,1)S(1)}, u32[]{:S(2)}, u32[]{:S(2)}) collective-permute-start(bf16[528,128]{1,0:T(8,128)(2,1)} %get-tuple-element.41), channel_id=1, source_target_pairs={{0,1},{1,0},{2,3},{3,2},{4,5},{5,4},{6,7},{7,6},{8,9},{9,8},{10,11... | collective-permute-start | bytes 405512 | tf_op jit(solution)/shard_map/ppermute | solution.py:549
  5.6 8.7 %collective-permute-start.4 = (bf16[528,128]{1,0:T(8,128)(2,1)}, bf16[528,128]{1,0:T(8,128)(2,1)S(1)}, u32[]{:S(2)}, u32[]{:S(2)}) collective-permute-start(bf16[528,128]{1,0:T(8,128)(2,1)} %get-tuple-element.42), channel_id=1, source_target_pairs={{0,2},{1,3},{2,0},{3,1},{4,6},{5,7},{6,4},{7,5},{8,10},{9,11},{10,... | collective-permute-start | bytes 405512 | tf_op jit(solution)/shard_map/ppermute | solution.py:549
  7.1 9.1 %collective-permute-start.5 = (bf16[528,128]{1,0:T(8,128)(2,1)}, bf16[528,128]{1,0:T(8,128)(2,1)S(1)}, u32[]{:S(2)}, u32[]{:S(2)}) collective-permute-start(bf16[528,128]{1,0:T(8,128)(2,1)} %get-tuple-element.43), channel_id=1, source_target_pairs={{0,3},{1,2},{2,1},{3,0},{4,7},{5,6},{6,5},{7,4},{8,11},{9,10},{10,... | collective-permute-start | bytes 405512 | tf_op jit(solution)/shard_map/ppermute | solution.py:549
  7.1 10.6 %copy-start = (bf16[528,128]{1,0:T(8,128)(2,1)S(1)}, bf16[528,128]{1,0:T(8,128)(2,1)}, u32[]{:S(2)}) copy-start(bf16[528,128]{1,0:T(8,128)(2,1)} %get-tuple-element.36.rest_0_) | copy-start | bytes 405508
  7.1 10.6 %copy-start.1 = (f32[4,2,64,128]{3,2,1,0:T(8,128)S(1)}, f32[4,2,64,128]{3,2,1,0:T(8,128)}, u32[]{:S(2)}) copy-start(f32[4,2,64,128]{3,2,1,0:T(8,128)} %constant.4.clone.rest_4_.rest_10_.rest_14_) | copy-start | bytes 786436
  9.9 8.8 %collective-permute-start = (bf16[512,128]{1,0:T(8,128)(2,1)}, bf16[512,128]{1,0:T(8,128)(2,1)S(1)}, u32[]{:S(2)}, u32[]{:S(2)}) collective-permute-start(bf16[512,128]{1,0:T(8,128)(2,1)} %get-tuple-element.38), channel_id=1, source_target_pairs={{0,1},{1,0},{2,3},{3,2},{4,5},{5,4},{6,7},{7,6},{8,9},{9,8},{10,11... | collective-permute-start | bytes 393224 | tf_op jit(solution)/shard_map/ppermute | solution.py:549
  11.9 9.4 %collective-permute-start.1 = (bf16[512,128]{1,0:T(8,128)(2,1)}, bf16[512,128]{1,0:T(8,128)(2,1)S(1)}, u32[]{:S(2)}, u32[]{:S(2)}) collective-permute-start(bf16[512,128]{1,0:T(8,128)(2,1)} %get-tuple-element.39), channel_id=1, source_target_pairs={{0,2},{1,3},{2,0},{3,1},{4,6},{5,7},{6,4},{7,5},{8,10},{9,11},{10,... | collective-permute-start | bytes 393224 | tf_op jit(solution)/shard_map/ppermute | solution.py:549
  13.5 0.7 %copy-start.4 = (f32[128]{0:T(128)S(1)}, f32[128]{0:T(128)}, u32[]{:S(2)}) copy-start(f32[128]{0:T(128)} %param.14) | copy-start | bytes 1540
  13.5 0.7 %copy-start.5 = (f32[128]{0:T(128)S(1)}, f32[128]{0:T(128)}, u32[]{:S(2)}) copy-start(f32[128]{0:T(128)} %param.13) | copy-start | bytes 1540
  14.2 7.7 %collective-permute-start.2 = (bf16[512,128]{1,0:T(8,128)(2,1)}, bf16[512,128]{1,0:T(8,128)(2,1)S(1)}, u32[]{:S(2)}, u32[]{:S(2)}) collective-permute-start(bf16[512,128]{1,0:T(8,128)(2,1)} %get-tuple-element.40), channel_id=1, source_target_pairs={{0,3},{1,2},{2,1},{3,0},{4,7},{5,6},{6,5},{7,4},{8,11},{9,10},{10,... | collective-permute-start | bytes 393224 | tf_op jit(solution)/shard_map/ppermute | solution.py:549
  14.3 10.0 %collective-permute-start.6 = (bf16[512,128]{1,0:T(8,128)(2,1)}, bf16[512,128]{1,0:T(8,128)(2,1)S(1)}, u32[]{:S(2)}, u32[]{:S(2)}) collective-permute-start(bf16[512,128]{1,0:T(8,128)(2,1)} %get-tuple-element.55), channel_id=1, source_target_pairs={{0,1},{1,0},{2,3},{3,2},{4,5},{5,4},{6,7},{7,6},{8,9},{9,8},{10,11... | collective-permute-start | bytes 393224 | tf_op jit(solution)/shard_map/ppermute | solution.py:549
  16.2 2.4 %copy-start.6 = (bf16[512,128]{1,0:T(8,128)(2,1)S(1)}, bf16[512,128]{1,0:T(8,128)(2,1)}, u32[]{:S(2)}) copy-start(bf16[512,128]{1,0:T(8,128)(2,1)} %get-tuple-element.57) | copy-start | bytes 393220
  16.2 5.7 %copy-start.3 = (bf16[512,128]{1,0:T(8,128)(2,1)S(1)}, bf16[512,128]{1,0:T(8,128)(2,1)}, u32[]{:S(2)}) copy-start(bf16[512,128]{1,0:T(8,128)(2,1)} %get-tuple-element.37.rest_0_) | copy-start | bytes 393220
  16.2 9.3 %collective-permute-start.7 = (bf16[512,128]{1,0:T(8,128)(2,1)}, bf16[512,128]{1,0:T(8,128)(2,1)S(1)}, u32[]{:S(2)}, u32[]{:S(2)}) collective-permute-start(bf16[512,128]{1,0:T(8,128)(2,1)} %get-tuple-element.56), channel_id=1, source_target_pairs={{0,2},{1,3},{2,0},{3,1},{4,6},{5,7},{6,4},{7,5},{8,10},{9,11},{10,... | collective-permute-start | bytes 393224 | tf_op jit(solution)/shard_map/ppermute | solution.py:549
  18.6 6.8 %collective-permute-start.8 = (bf16[512,128]{1,0:T(8,128)(2,1)S(1)}, bf16[512,128]{1,0:T(8,128)(2,1)S(1)}, u32[]{:S(2)}, u32[]{:S(2)}) collective-permute-start(bf16[512,128]{1,0:T(8,128)(2,1)S(1)} %copy-done.6), channel_id=1, source_target_pairs={{0,3},{1,2},{2,1},{3,0},{4,7},{5,6},{6,5},{7,4},{8,11},{9,10},{10,... | collective-permute-start | bytes 393224 | tf_op jit(solution)/shard_map/ppermute | solution.py:549
  21.9 3.6 %copy-start.2 = (bf16[512,128]{1,0:T(8,128)(2,1)S(1)}, bf16[512,128]{1,0:T(8,128)(2,1)}, u32[]{:S(2)}) copy-start(bf16[512,128]{1,0:T(8,128)(2,1)} %get-tuple-element.54.rest_4_) | copy-start | bytes 393220
  27.9 5.4 %collective-permute-start.14 = (f32[8,128]{1,0:T(8,128)S(1)}, f32[8,128]{1,0:T(8,128)S(1)}, u32[]{:S(2)}, u32[]{:S(2)}) collective-permute-start(f32[8,128]{1,0:T(8,128)S(1)} %add.21), channel_id=1, source_target_pairs={{0,3},{1,2},{2,1},{3,0},{4,7},{5,6},{6,5},{7,4},{8,11},{9,10},{10,... | collective-permute-start | bytes 12296 | tf_op jit(solution)/shard_map/ppermute | solution.py:512
  29.2 5.7 %collective-permute-start.13 = (f32[8,128]{1,0:T(8,128)S(1)}, f32[8,128]{1,0:T(8,128)S(1)}, u32[]{:S(2)}, u32[]{:S(2)}) collective-permute-start(f32[8,128]{1,0:T(8,128)S(1)} %add.21), channel_id=1, source_target_pairs={{0,2},{1,3},{2,0},{3,1},{4,6},{5,7},{6,4},{7,5},{8,10},{9,11},{10,... | collective-permute-start | bytes 12296 | tf_op jit(solution)/shard_map/ppermute | solution.py:512
  30.4 4.6 %collective-permute-start.12 = (f32[8,128]{1,0:T(8,128)S(1)}, f32[8,128]{1,0:T(8,128)S(1)}, u32[]{:S(2)}, u32[]{:S(2)}) collective-permute-start(f32[8,128]{1,0:T(8,128)S(1)} %add.21), channel_id=1, source_target_pairs={{0,1},{1,0},{2,3},{3,2},{4,5},{5,4},{6,7},{7,6},{8,9},{9,8},{10,11... | collective-permute-start | bytes 12296 | tf_op jit(solution)/shard_map/ppermute | solution.py:512
  31.4 13.4 %collective-permute-start.9 = (bf16[1024,128]{1,0:T(8,128)(2,1)S(1)}, bf16[1024,128]{1,0:T(8,128)(2,1)S(1)}, u32[]{:S(2)}, u32[]{:S(2)}) collective-permute-start(bf16[1024,128]{1,0:T(8,128)(2,1)S(1)} %get-tuple-element.59), channel_id=1, source_target_pairs={{0,1},{1,0},{2,3},{3,2},{4,5},{5,4},{6,7},{7,6},{8,9},{9,8},{10,11... | collective-permute-start | bytes 786440 | tf_op jit(solution)/shard_map/ppermute | solution.py:575
  32.4 12.4 %collective-permute-start.10 = (bf16[1024,128]{1,0:T(8,128)(2,1)S(1)}, bf16[1024,128]{1,0:T(8,128)(2,1)S(1)}, u32[]{:S(2)}, u32[]{:S(2)}) collective-permute-start(bf16[1024,128]{1,0:T(8,128)(2,1)S(1)} %get-tuple-element.60), channel_id=1, source_target_pairs={{0,2},{1,3},{2,0},{3,1},{4,6},{5,7},{6,4},{7,5},{8,10},{9,11},{10,... | collective-permute-start | bytes 786440 | tf_op jit(solution)/shard_map/ppermute | solution.py:575
  33.3 11.5 %collective-permute-start.11 = (bf16[1024,128]{1,0:T(8,128)(2,1)S(1)}, bf16[1024,128]{1,0:T(8,128)(2,1)S(1)}, u32[]{:S(2)}, u32[]{:S(2)}) collective-permute-start(bf16[1024,128]{1,0:T(8,128)(2,1)S(1)} %get-tuple-element.61), channel_id=1, source_target_pairs={{0,3},{1,2},{2,1},{3,0},{4,7},{5,6},{6,5},{7,4},{8,11},{9,10},{10,... | collective-permute-start | bytes 786440 | tf_op jit(solution)/shard_map/ppermute | solution.py:575
  34.9 1.2 %collective-permute-start.15 = (f32[8,128]{1,0:T(8,128)S(1)}, f32[8,128]{1,0:T(8,128)S(1)}, u32[]{:S(2)}, u32[]{:S(2)}) collective-permute-start(f32[8,128]{1,0:T(8,128)S(1)} %add_add_fusion), channel_id=1, source_target_pairs={{0,4},{4,0},{8,12},{12,8},{16,20},{20,16},{24,28},{28,24},{1,5},{5... | collective-permute-start | bytes 12296 | tf_op jit(solution)/shard_map/ppermute | solution.py:512
  36.2 3.6 %collective-permute-start.16 = (f32[8,128]{1,0:T(8,128)S(1)}, f32[8,128]{1,0:T(8,128)S(1)}, u32[]{:S(2)}, u32[]{:S(2)}) collective-permute-start(f32[8,128]{1,0:T(8,128)S(1)} %add.25), channel_id=1, source_target_pairs={{0,8},{4,12},{8,0},{12,4},{16,24},{20,28},{24,16},{28,20},{1,9},{5... | collective-permute-start | bytes 12296 | tf_op jit(solution)/shard_map/ppermute | solution.py:512
  39.8 4.5 %collective-permute-start.17 = (f32[8,128]{1,0:T(8,128)S(1)}, f32[8,128]{1,0:T(8,128)S(1)}, u32[]{:S(2)}, u32[]{:S(2)}) collective-permute-start(f32[8,128]{1,0:T(8,128)S(1)} %add.26), channel_id=1, source_target_pairs={{0,16},{4,20},{8,24},{12,28},{16,0},{20,4},{24,8},{28,12},{1,17},{... | collective-permute-start | bytes 12296 | tf_op jit(solution)/shard_map/ppermute | solution.py:512

commit v7 on v6

--- a/solution.py
+++ b/solution.py
@@ -290,43 +290,48 @@
     )
 
 
-def spread_kernel(axis, parts, groups, per, a_hbm, b_hbm, *rest):
-    with_ids = groups is None
-    groups = groups or 1
-    seg_hbm, rest = rest[:1], rest[1:]
-    outs = rest[: parts * groups]
-    a_in, b_in, a_f32, b_f32, seg_in, msg, in_sems, out_sems = rest[parts * groups :]
+def head_rows(refs, first, per, block):
+    for ref in refs:
+        for h in range(per):
+            yield ref[pl.ds(first + h, block, stride=ref.shape[0] // block), :].astype(jnp.bfloat16)
+
+
+def spread_keys_kernel(axis, parts, per, a_hbm, b_hbm, seg_hbm, *rest):
+    outs = rest[:parts]
+    a_in, b_in, a_f32, b_f32, seg_in, msg, in_sems, out_sems = rest[parts:]
     block = seg_in.shape[1]
-    heads = a_in.shape[0] // block
     me = lax.axis_index(axis)
-    pairs = [(a_hbm, a_in), (b_hbm, b_in)] + ([(seg_hbm[0], seg_in)] if with_ids else [])
+    pairs = ((a_hbm, a_in), (b_hbm, b_in), (seg_hbm, seg_in))
     loads = [pltpu.make_async_copy(src, dst, in_sems.at[i]) for i, (src, dst) in enumerate(pairs)]
     for copy in loads:
         copy.start()
     for copy, src, dst in zip(loads, (a_in, b_in), (a_f32, b_f32)):
         copy.wait()
         dst[...] = src[...].astype(jnp.float32)
-    if with_ids:
-        loads[2].wait()
-        ids = jnp.broadcast_to(seg_in[...].astype(jnp.float32), (16, block)).astype(jnp.bfloat16)
+    loads[2].wait()
+    ids = jnp.broadcast_to(seg_in[...].astype(jnp.float32), (16, block)).astype(jnp.bfloat16)
     stores = []
-    for grp in range(groups):
-        for m in (*range(1, parts), 0):
-            slot = grp * parts + m
-            first = ((me ^ m) * groups + grp) * per
-            at = 0
-            for src in (a_f32, b_f32):
-                for h in range(per):
-                    rows = src[pl.ds(first + h, block, stride=heads), :]
-                    msg[slot, pl.ds(at, block), :] = rows.astype(jnp.bfloat16)
-                    at += block
-            if with_ids:
-                msg[slot, pl.ds(at, 16), :] = ids
-            copy = pltpu.make_async_copy(msg.at[slot], outs[slot], out_sems.at[slot])
-            copy.start()
-            stores.append(copy)
+    for m in (*range(1, parts), 0):
+        for i, rows in enumerate(head_rows((a_f32, b_f32), (me ^ m) * per, per, block)):
+            msg[m, pl.ds(i * block, block), :] = rows
+        msg[m, pl.ds(2 * per * block, 16), :] = ids
+        copy = pltpu.make_async_copy(msg.at[m], outs[m], out_sems.at[m])
+        copy.start()
+        stores.append(copy)
     for copy in stores:
         copy.wait()
+
+
+def spread_queries_kernel(axis, parts, groups, per, a_ref, b_ref, *rest):
+    outs, a_f32, b_f32 = rest[-2 - parts * groups : -2], rest[-2], rest[-1]
+    block = outs[0].shape[0] // (2 * per)
+    me = lax.axis_index(axis)
+    for src, dst in ((a_ref, a_f32), (b_ref, b_f32)):
+        dst[...] = src[...].astype(jnp.float32)
+    for grp in range(groups):
+        for m in range(parts):
+            for i, rows in enumerate(head_rows((a_f32, b_f32), ((me ^ m) * groups + grp) * per, per, block)):
+                outs[grp * parts + m][pl.ds(i * block, block), :] = rows
 
 
 def turned(x):
@@ -419,27 +424,38 @@
         out_base = p * (group + 2) * block
         dk = [None] * parts
         dv = [None] * parts
-        for b in range(parts):
-            span = range(max(0, b - back), b + 1)
-            qt, g = qt_ref[b * per + p], g_ref[b * per + p]
+        spans = [range(max(0, b - back), b + 1) for b in range(parts)]
+        qts = [qt_ref[b * per + p] for b in range(parts)]
+        gs = [g_ref[b * per + p] for b in range(parts)]
+        first = []
+        for b, span in enumerate(spans):
             k = jnp.concatenate([k_ref[j, grp * per + p] for j in span], axis=0)
-            kt = jnp.concatenate([kt_ref[j, grp * per + p] for j in span], axis=1)
             v = jnp.concatenate([v_ref[j, grp * per + p] for j in span], axis=0)
+            scores = jnp.dot(k, qts[b], preferred_element_type=f32)
+            prob_grads = lax.dot_general(v, gs[b], NT, preferred_element_type=f32)
+            first.append((scores, prob_grads))
+        second = []
+        for b, span in enumerate(spans):
+            scores, prob_grads = first[b]
             hidden = jnp.concatenate([bias(j, b) for j in span], axis=0)
-            scores = jnp.dot(k, qt, preferred_element_type=f32)
             expo = jnp.exp2(scores * (SCALE * LOG2E) + hidden)
-            prob_grads = lax.dot_general(v, g, NT, preferred_element_type=f32)
             inverse = 1.0 / jnp.sum(expo, axis=0, keepdims=True)
             delta = jnp.sum(expo * prob_grads, axis=0, keepdims=True) * inverse
             probs = expo * inverse
             score_grads = (probs * (prob_grads - delta)).astype(bf16)
-            dvs = jnp.dot(probs.astype(bf16), g, preferred_element_type=f32)
-            dks = lax.dot_general(qt, score_grads, NT, preferred_element_type=f32)
-            dq = jnp.dot(kt, score_grads, preferred_element_type=f32)
+            second.append((probs.astype(bf16), score_grads))
+        third = []
+        for b, span in enumerate(spans):
+            probs, score_grads = second[b]
+            kt = jnp.concatenate([kt_ref[j, grp * per + p] for j in span], axis=1)
+            third.append(jnp.dot(kt, score_grads, preferred_element_type=f32))
+            dvs = jnp.dot(probs, gs[b], preferred_element_type=f32)
+            dks = lax.dot_general(qts[b], score_grads, NT, preferred_element_type=f32)
             for i, j in enumerate(span):
                 cut = slice(i * block, (i + 1) * block)
                 dk[j] = dks[:, cut] if dk[j] is None else dk[j] + dks[:, cut]
                 dv[j] = dvs[cut] if dv[j] is None else dv[j] + dvs[cut]
+        for b, dq in enumerate(third):
             at = b * per + p
             dx, share = embed_back(dq, q_gain, *rope(table_ref, b, group), qn_ref[at], qs_ref[at][0:1, :])
             q_total = q_total + share
@@ -454,11 +470,9 @@
         for i in range(grp):
             outs[m][pl.ds(i * size, size), :] = earlier[i * parts + m][...]
         outs[m][pl.ds(grp * size, size), :] = res_ref[me ^ m]
-    ones = jnp.ones((8, rows), f32)
-    exact = functools.partial(
-        lax.dot_general, dimension_numbers=NT, precision=lax.Precision.HIGHEST, preferred_element_type=f32
-    )
-    q_share, k_share = exact(ones, q_total), exact(ones[:, :block], k_total)
+    q_share = sum(q_total[:, i * block : (i + 1) * block] for i in range(group))
+    q_share = jnp.sum(q_share.T, axis=0, keepdims=True)
+    k_share = jnp.sum(k_total.T, axis=0, keepdims=True)
     row = lax.broadcasted_iota(jnp.int32, (8, width), 0)
     share_ref[...] = jnp.where(row == 0, q_share, jnp.where(row == 1, k_share, 0.0)) * SCALE
 
@@ -535,21 +549,21 @@
     dma = pltpu.SemaphoreType.DMA
     q_shape, k_shape = q2.shape, k2.shape
 
-    def spread(count, each, shape, message, cost, *arrays):
-        number = parts * (count or 1)
-        return call_in(
-            functools.partial(spread_kernel, "seq", parts, count, each),
-            [hbm] * len(arrays), [(message, bf16, hbm)] * number,
-            [vmem(shape, bf16), vmem(shape, bf16), vmem(shape, f32), vmem(shape, f32), vmem((1, block), jnp.int32)]
-            + [vmem((number, *message), bf16), dma((len(arrays),)), dma((number,))],
-            cost, *arrays, limit=SPREAD_VMEM,
-        )
-
     xor = lambda m, size: [(i, i ^ m) for i in range(size)]
     send = lambda out: [out[0]] + [lax.ppermute(out[m], "seq", xor(m, parts)) for m in range(1, parts)]
-    kv_messages = spread(None, owned, k_shape, kv_sent, 1 << 20, k2, v2, segment_ids)
+    kv_messages = call_in(
+        functools.partial(spread_keys_kernel, "seq", parts, owned),
+        [hbm] * 3, [(kv_sent, bf16, hbm)] * parts,
+        [vmem(k_shape, bf16), vmem(k_shape, bf16), vmem(k_shape, f32), vmem(k_shape, f32), vmem((1, block), jnp.int32)]
+        + [vmem((parts, *kv_sent), bf16), dma((3,)), dma((parts,))],
+        1 << 20, k2, v2, segment_ids, limit=SPREAD_VMEM,
+    )
     kv_arrived = send(kv_messages)
-    messages = spread(groups, per * group, q_shape, sent, 1 << 33, q2, g2, kv_messages[0])
+    messages = call_in(
+        functools.partial(spread_queries_kernel, "seq", parts, groups, per * group),
+        [vmem] * 2, [(sent, bf16, vmem)] * (parts * groups),
+        [vmem(q_shape, f32), vmem(q_shape, f32)], 1 << 33, q2, g2,
+    )
     arrived = [send(messages[grp * parts : (grp + 1) * parts]) for grp in range(groups)]
     gains = jnp.concatenate([q_gain[None], k_gain[None], jnp.zeros((6, width), f32)], axis=0)
     held = (parts, owned)

time: 46.5 us -> 45.4 us (0.976)
  Pallas kernels: 11.7 us -> 8.4 us
  local copies, waits for them, and re-layouts: 1.29 us -> 2.32 us
  starting transfers between devices: 23.3 us -> 24 us
  waiting for transfers between devices: 9.15 us -> 9.66 us
    pallas_call x6, Pallas kernels: 11.7 us -> 8.4 us  [call_in(): pl.pallas_call(kernel, out_shape=[jax.ShapeDtypeStruct(s, t) for s, t, _...]
    unnamed x14 -> x12, local copies, waits for them, and re-layouts: 0.69 us -> 1.72 us
    ppermute x9, starting transfers between devices: 12.1 us -> 12.7 us  [by_heads(): lax.ppermute(out[m], 'seq', xor(m, parts))]
  transfers between devices with their start and end apart: 18 -> 18, of which waited for: 6 -> 7; matrix products, arithmetic and copies ran while one was open for 1% -> 2% of each run, Pallas kernels for 13% -> 7%
where the time goes in v7:
time: 45.4 us; the launch traced here: 45.2 us
  starting transfers between devices  24 us (53%)
  waiting for transfers between devices  9.66 us (21%)
  Pallas kernels  8.4 us (19%)
  local copies, waits for them, and re-layouts  2.32 us (5%)
  between operations  0.73 us (2%)
    ppermute x9, starting transfers between devices, by_heads(): lax.ppermute(out[m], 'seq', xor(m, parts))  12.7 us
    pallas_call x6, Pallas kernels, call_in(): pl.pallas_call(kernel, out_shape=[jax.ShapeDtypeStruct(s, t) for s, t, _...  8.4 us
    ppermute x6, starting transfers between devices, exchange_sum(): lax.ppermute(x, axis, [(i, i ^ m) for i in range(size)])  7.79 us
    ppermute x6, waiting for transfers between devices, exchange_sum(): lax.ppermute(x, axis, [(i, i ^ m) for i in range(size)])  5.11 us
    ppermute x9, waiting for transfers between devices, by_heads(): lax.ppermute(out[m], 'seq', xor(m, parts))  4.49 us
    ppermute x3, starting transfers between devices, by_heads(): go = lambda m: lax.ppermute(results[m], 'seq', xor(m, parts))  3.49 us
    unnamed x12, local copies, waits for them, and re-layouts  1.72 us
  transfers between devices with their start and end apart: 18, of which 7 were waited for; matrix products, arithmetic and copies ran while one was open for 2% of the time, Pallas kernels for 7%

profile of v7, /device:TPU:0, one launch (start us, length us, event | category | flops | bytes accessed | tf_op | source)
XLA Modules:
  0.0 45.2 jit_solution(17750911827261006074)
XLA Ops:
  0.6 0.0 copy-start
  0.6 2.0 %shard_map.120 = (bf16[528,128]{1,0:T(8,128)(2,1)}, bf16[528,128]{1,0:T(8,128)(2,1)}, bf16[528,128]{1,0:T(8,128)(2,1)}, bf16[528,128]{1,0:T(8,128)(2,1)}) custom-call(bf16[1024,128]{1,0:T(8,128)(2,1)} %bitcast.15, bf16[1024,128]{1,0:T(8,128)(2,1)} %bitcast.16, s32[1,128]{1,0:T(1,128)} %seg_hbm.1), custom_call_target="tpu_custom_call" | custom-call | flops 1048576 | bytes 1048576 | tf_op jit(solution)/shard_map/pallas_call | solution.py:514
  2.7 3.0 %collective-permute-start.3 = (bf16[528,128]{1,0:T(8,128)(2,1)}, bf16[528,128]{1,0:T(8,128)(2,1)S(1)}, u32[]{:S(2)}, u32[]{:S(2)}) collective-permute-start(bf16[528,128]{1,0:T(8,128)(2,1)} %get-tuple-element.41), channel_id=1, source_target_pairs={{0,1},{1,0},{2,3},{3,2},{4,5},{5,4},{6,7},{7,6},{8,9},{9,8},{10,11... | collective-permute-start | bytes 405512 | tf_op jit(solution)/shard_map/ppermute | solution.py:553
  5.7 1.5 %collective-permute-start.4 = (bf16[528,128]{1,0:T(8,128)(2,1)}, bf16[528,128]{1,0:T(8,128)(2,1)S(1)}, u32[]{:S(2)}, u32[]{:S(2)}) collective-permute-start(bf16[528,128]{1,0:T(8,128)(2,1)} %get-tuple-element.42), channel_id=1, source_target_pairs={{0,2},{1,3},{2,0},{3,1},{4,6},{5,7},{6,4},{7,5},{8,10},{9,11},{10,... | collective-permute-start | bytes 405512 | tf_op jit(solution)/shard_map/ppermute | solution.py:553
  7.2 0.0 collective-permute-start.5
  7.2 0.0 copy-done
  7.2 0.0 copy-start.1
  7.2 1.0 %copy-done.1 = bf16[1,128,16,128]{3,2,1,0:T(8,128)(2,1)S(1)} copy-done((bf16[1,128,16,128]{3,2,1,0:T(8,128)(2,1)S(1)}, bf16[1,128,16,128]{3,2,1,0:T(8,128)(2,1)}, u32[]{:S(2)}) %copy-start.1) | copy-done | bytes 524312
  8.3 0.0 copy-start.2
  8.3 0.0 copy-start.3
  8.3 0.8 %shard_map.119 = (bf16[512,128]{1,0:T(8,128)(2,1)S(1)}, bf16[512,128]{1,0:T(8,128)(2,1)S(1)}, bf16[512,128]{1,0:T(8,128)(2,1)S(1)}, bf16[512,128]{1,0:T(8,128)(2...) custom-call(bf16[2048,128]{1,0:T(8,128)(2,1)S(1)} %bitcast.13, ...), custom_call_target="tpu_custom_call" | custom-call | flops 8589934592 | bytes 1048576 | tf_op jit(solution)/shard_map/pallas_call | solution.py:514
  9.0 2.0 %collective-permute-start = (bf16[512,128]{1,0:T(8,128)(2,1)S(1)}, bf16[512,128]{1,0:T(8,128)(2,1)S(1)}, u32[]{:S(2)}, u32[]{:S(2)}) collective-permute-start(bf16[512,128]{1,0:T(8,128)(2,1)S(1)} %get-tuple-element.37), channel_id=1, source_target_pairs={{0,1},{1,0},{2,3},{3,2},{4,5},{5,4},{6,7},{7,6},{8,9},{9,8},{10,11... | collective-permute-start | bytes 393224 | tf_op jit(solution)/shard_map/ppermute | solution.py:553
  11.0 1.5 %collective-permute-start.1 = (bf16[512,128]{1,0:T(8,128)(2,1)S(1)}, bf16[512,128]{1,0:T(8,128)(2,1)S(1)}, u32[]{:S(2)}, u32[]{:S(2)}) collective-permute-start(bf16[512,128]{1,0:T(8,128)(2,1)S(1)} %get-tuple-element.38), channel_id=1, source_target_pairs={{0,2},{1,3},{2,0},{3,1},{4,6},{5,7},{6,4},{7,5},{8,10},{9,11},{10,... | collective-permute-start | bytes 393224 | tf_op jit(solution)/shard_map/ppermute | solution.py:553
  12.6 0.1 pad.2.clone
  12.6 0.0 copy-start.4
  12.6 0.0 copy-start.5
  12.7 0.7 %copy-done.4 = f32[128]{0:T(128)S(1)} copy-done((f32[128]{0:T(128)S(1)}, f32[128]{0:T(128)}, u32[]{:S(2)}) %copy-start.4) | copy-done | bytes 536
  13.3 0.0 copy-done.5
  13.3 0.1 maximum_maximum_fusion.rest_5_.rest_11_.rest_15_
  13.4 0.0 collective-permute-done.3.rest_1_
  13.4 0.0 collective-permute-start.2
  13.4 0.1 collective-permute-done.4.rest_2_
  13.5 1.9 %collective-permute-start.6 = (bf16[512,128]{1,0:T(8,128)(2,1)S(1)}, bf16[512,128]{1,0:T(8,128)(2,1)S(1)}, u32[]{:S(2)}, u32[]{:S(2)}) collective-permute-start(bf16[512,128]{1,0:T(8,128)(2,1)S(1)} %get-tuple-element.55), channel_id=1, source_target_pairs={{0,1},{1,0},{2,3},{3,2},{4,5},{5,4},{6,7},{7,6},{8,9},{9,8},{10,11... | collective-permute-start | bytes 393224 | tf_op jit(solution)/shard_map/ppermute | solution.py:553
  15.4 0.0 collective-permute-done.5.rest_3_
  15.4 1.5 %collective-permute-start.7 = (bf16[512,128]{1,0:T(8,128)(2,1)S(1)}, bf16[512,128]{1,0:T(8,128)(2,1)S(1)}, u32[]{:S(2)}, u32[]{:S(2)}) collective-permute-start(bf16[512,128]{1,0:T(8,128)(2,1)S(1)} %get-tuple-element.56), channel_id=1, source_target_pairs={{0,2},{1,3},{2,0},{3,1},{4,6},{5,7},{6,4},{7,5},{8,10},{9,11},{10,... | collective-permute-start | bytes 393224 | tf_op jit(solution)/shard_map/ppermute | solution.py:553
  16.9 0.0 copy-done.2
  16.9 0.0 copy-done.3
  16.9 0.9 %shard_map.121 = (bf16[4,2,128,128]{3,2,1,0:T(8,128)(2,1)S(1)}, bf16[4,2,128,128]{3,2,1,0:T(8,128)(2,1)S(1)}, bf16[4,2,128,128]{3,2,1,0:T(8,128)(2,1)S(1)}, f32[...) custom-call(bf16[528,128]{1,0:T(8,128)(2,1)S(1)} %copy-done.2, ...), custom_call_target="tpu_custom_call" | custom-call | flops 8589934592 | bytes 1048576 | tf_op jit(solution)/shard_map/pallas_call | solution.py:514
  17.8 0.0 collective-permute-done.rest_1_
  17.8 1.2 %collective-permute-start.8 = (bf16[512,128]{1,0:T(8,128)(2,1)S(1)}, bf16[512,128]{1,0:T(8,128)(2,1)S(1)}, u32[]{:S(2)}, u32[]{:S(2)}) collective-permute-start(bf16[512,128]{1,0:T(8,128)(2,1)S(1)} %get-tuple-element.57), channel_id=1, source_target_pairs={{0,3},{1,2},{2,1},{3,0},{4,7},{5,6},{6,5},{7,4},{8,11},{9,10},{10,... | collective-permute-start | bytes 393224 | tf_op jit(solution)/shard_map/ppermute | solution.py:553
  19.0 1.1 %collective-permute-done.1.rest_2_ = bf16[512,128]{1,0:T(8,128)(2,1)S(1)} collective-permute-done((bf16[512,128]{1,0:T(8,128)(2,1)S(1)}, bf16[512,128]{1,0:T(8,128)(2,1)S(1)}, u32[]{:S(2)}, u32[]{:S(2)}) %collective-permute-start.1) | collective-permute-done | bytes 131104 | tf_op jit(solution)/shard_map/ppermute | solution.py:553
  20.1 0.7 %collective-permute-done.2.rest_3_ = bf16[512,128]{1,0:T(8,128)(2,1)S(1)} collective-permute-done((bf16[512,128]{1,0:T(8,128)(2,1)S(1)}, bf16[512,128]{1,0:T(8,128)(2,1)S(1)}, u32[]{:S(2)}, u32[]{:S(2)}) %collective-permute-start.2) | collective-permute-done | bytes 131104 | tf_op jit(solution)/shard_map/ppermute | solution.py:553
  20.8 1.6 %shard_map.122 = (bf16[512,128]{1,0:T(8,128)(2,1)S(1)}, bf16[512,128]{1,0:T(8,128)(2,1)S(1)}, bf16[512,128]{1,0:T(8,128)(2,1)S(1)}, bf16[512,128]{1,0:T(8,128)(2,1)S(1)}, f32[8,128]{1,0:T(8,128)S(1)}) custom-call(bf16[512,128]{1,0:T(8,128)(2,1)S(1)} %get-tuple-element.36.rest_0_, bf16[512,128]{1,0:T(8,128)(2,1)S(1)} %collective-permute-done.rest_1_, ...), custom_call_target="tpu_custom_call" | custom-call | flops 17179869184 | bytes 1048576 | tf_op jit(solution)/shard_map/pallas_call | solution.py:514
  22.4 0.0 collective-permute-done.6.rest_5_
  22.4 2.6 %collective-permute-done.7.rest_6_ = bf16[512,128]{1,0:T(8,128)(2,1)S(1)} collective-permute-done((bf16[512,128]{1,0:T(8,128)(2,1)S(1)}, bf16[512,128]{1,0:T(8,128)(2,1)S(1)}, u32[]{:S(2)}, u32[]{:S(2)}) %collective-permute-start.7) | collective-permute-done | bytes 131104 | tf_op jit(solution)/shard_map/ppermute | solution.py:553
  25.1 0.0 collective-permute-done.8.rest_7_
  25.1 1.6 %shard_map.123 = (bf16[1024,128]{1,0:T(8,128)(2,1)S(1)}, bf16[1024,128]{1,0:T(8,128)(2,1)S(1)}, bf16[1024,128]{1,0:T(8,128)(2,1)S(1)}, bf16[1024,128]{1,0:T(8,128)(2,1)S(1)}, f32[8,128]{1,0:T(8,128)S(1)}) custom-call(bf16[512,128]{1,0:T(8,128)(2,1)S(1)} %get-tuple-element.50.rest_0_, bf16[512,128]{1,0:T(8,128)(2,1)S(1)} %get-tuple-element.51.rest_1_, ...), custom_call_target="tpu_custom_call" | custom-call | flops 17179869184 | bytes 1048576 | tf_op jit(solution)/shard_map/pallas_call | solution.py:514
  26.7 1.6 %collective-permute-start.14 = (f32[8,128]{1,0:T(8,128)S(1)}, f32[8,128]{1,0:T(8,128)S(1)}, u32[]{:S(2)}, u32[]{:S(2)}) collective-permute-start(f32[8,128]{1,0:T(8,128)S(1)} %add.21), channel_id=1, source_target_pairs={{0,3},{1,2},{2,1},{3,0},{4,7},{5,6},{6,5},{7,4},{8,11},{9,10},{10,... | collective-permute-start | bytes 12296 | tf_op jit(solution)/shard_map/ppermute | solution.py:526
  28.3 1.2 %collective-permute-start.13 = (f32[8,128]{1,0:T(8,128)S(1)}, f32[8,128]{1,0:T(8,128)S(1)}, u32[]{:S(2)}, u32[]{:S(2)}) collective-permute-start(f32[8,128]{1,0:T(8,128)S(1)} %add.21), channel_id=1, source_target_pairs={{0,2},{1,3},{2,0},{3,1},{4,6},{5,7},{6,4},{7,5},{8,10},{9,11},{10,... | collective-permute-start | bytes 12296 | tf_op jit(solution)/shard_map/ppermute | solution.py:526
  29.5 0.8 %collective-permute-start.12 = (f32[8,128]{1,0:T(8,128)S(1)}, f32[8,128]{1,0:T(8,128)S(1)}, u32[]{:S(2)}, u32[]{:S(2)}) collective-permute-start(f32[8,128]{1,0:T(8,128)S(1)} %add.21), channel_id=1, source_target_pairs={{0,1},{1,0},{2,3},{3,2},{4,5},{5,4},{6,7},{7,6},{8,9},{9,8},{10,11... | collective-permute-start | bytes 12296 | tf_op jit(solution)/shard_map/ppermute | solution.py:526
  30.3 1.2 %collective-permute-start.9 = (bf16[1024,128]{1,0:T(8,128)(2,1)S(1)}, bf16[1024,128]{1,0:T(8,128)(2,1)S(1)}, u32[]{:S(2)}, u32[]{:S(2)}) collective-permute-start(bf16[1024,128]{1,0:T(8,128)(2,1)S(1)} %get-tuple-element.59), channel_id=1, source_target_pairs={{0,1},{1,0},{2,3},{3,2},{4,5},{5,4},{6,7},{7,6},{8,9},{9,8},{10,11... | collective-permute-start | bytes 786440 | tf_op jit(solution)/shard_map/ppermute | solution.py:589
  31.5 0.9 %collective-permute-start.10 = (bf16[1024,128]{1,0:T(8,128)(2,1)S(1)}, bf16[1024,128]{1,0:T(8,128)(2,1)S(1)}, u32[]{:S(2)}, u32[]{:S(2)}) collective-permute-start(bf16[1024,128]{1,0:T(8,128)(2,1)S(1)} %get-tuple-element.60), channel_id=1, source_target_pairs={{0,2},{1,3},{2,0},{3,1},{4,6},{5,7},{6,4},{7,5},{8,10},{9,11},{10,... | collective-permute-start | bytes 786440 | tf_op jit(solution)/shard_map/ppermute | solution.py:589
  32.4 0.0 collective-permute-done.14
  32.4 1.4 %collective-permute-start.11 = (bf16[1024,128]{1,0:T(8,128)(2,1)S(1)}, bf16[1024,128]{1,0:T(8,128)(2,1)S(1)}, u32[]{:S(2)}, u32[]{:S(2)}) collective-permute-start(bf16[1024,128]{1,0:T(8,128)(2,1)S(1)} %get-tuple-element.61), channel_id=1, source_target_pairs={{0,3},{1,2},{2,1},{3,0},{4,7},{5,6},{6,5},{7,4},{8,11},{9,10},{10,... | collective-permute-start | bytes 786440 | tf_op jit(solution)/shard_map/ppermute | solution.py:589
  33.8 0.0 collective-permute-done.13
  33.8 0.0 collective-permute-done.12
  33.8 0.1 collective-permute-start.15
  33.8 1.2 %collective-permute-done.15 = f32[8,128]{1,0:T(8,128)S(1)} collective-permute-done((f32[8,128]{1,0:T(8,128)S(1)}, f32[8,128]{1,0:T(8,128)S(1)}, u32[]{:S(2)}, u32[]{:S(2)}) %collective-permute-start.15) | collective-permute-done | bytes 4128 | tf_op jit(solution)/shard_map/ppermute | solution.py:526
  35.0 1.6 %collective-permute-start.16 = (f32[8,128]{1,0:T(8,128)S(1)}, f32[8,128]{1,0:T(8,128)S(1)}, u32[]{:S(2)}, u32[]{:S(2)}) collective-permute-start(f32[8,128]{1,0:T(8,128)S(1)} %add.25), channel_id=1, source_target_pairs={{0,8},{4,12},{8,0},{12,4},{16,24},{20,28},{24,16},{28,20},{1,9},{5... | collective-permute-start | bytes 12296 | tf_op jit(solution)/shard_map/ppermute | solution.py:526
  36.6 2.0 %collective-permute-done.16 = f32[8,128]{1,0:T(8,128)S(1)} collective-permute-done((f32[8,128]{1,0:T(8,128)S(1)}, f32[8,128]{1,0:T(8,128)S(1)}, u32[]{:S(2)}, u32[]{:S(2)}) %collective-permute-start.16) | collective-permute-done | bytes 4128 | tf_op jit(solution)/shard_map/ppermute | solution.py:526
  38.6 2.6 %collective-permute-start.17 = (f32[8,128]{1,0:T(8,128)S(1)}, f32[8,128]{1,0:T(8,128)S(1)}, u32[]{:S(2)}, u32[]{:S(2)}) collective-permute-start(f32[8,128]{1,0:T(8,128)S(1)} %add.26), channel_id=1, source_target_pairs={{0,16},{4,20},{8,24},{12,28},{16,0},{20,4},{24,8},{28,12},{1,17},{... | collective-permute-start | bytes 12296 | tf_op jit(solution)/shard_map/ppermute | solution.py:526
  41.2 1.9 %collective-permute-done.17 = f32[8,128]{1,0:T(8,128)S(1)} collective-permute-done((f32[8,128]{1,0:T(8,128)S(1)}, f32[8,128]{1,0:T(8,128)S(1)}, u32[]{:S(2)}, u32[]{:S(2)}) %collective-permute-start.17) | collective-permute-done | bytes 4128 | tf_op jit(solution)/shard_map/ppermute | solution.py:526
  43.1 0.5 %slice_bitcast_fusion = (f32[128]{0:T(128)}, f32[128]{0:T(128)}) fusion(f32[8,128]{1,0:T(8,128)S(1)} %add.27), kind=kLoop, calls=%fused_computation.2 | loop fusion | bytes 2048 | tf_op jit(solution)/shard_map/squeeze | solution.py:602
  43.6 0.0 collective-permute-done.9.rest_1_
  43.7 0.0 collective-permute-done.10.rest_2_
  43.7 0.0 collective-permute-done.11.rest_3_
  43.7 1.5 %shard_map.124 = (bf16[2048,128]{1,0:T(8,128)(2,1)}, bf16[1024,128]{1,0:T(8,128)(2,1)}, bf16[1024,128]{1,0:T(8,128)(2,1)}) custom-call(bf16[1024,128]{1,0:T(8,128)(2,1)S(1)} %get-tuple-element.58.rest_0_, bf16[1024,128]{1,0:T(8,128)(2,1)S(1)} %collective-permute-done.9.rest_1_, bf16[1024,128]{1,0:T(8,128)(2,1)S(1)} %collective-permute-done.10.rest_2_, ...), custom_call_target="tpu_custom_call" | custom-call | flops 1048576 | bytes 1048576 | tf_op jit(solution)/shard_map/pallas_call | solution.py:514
  (6 shorter events, 0.0 us)
Async XLA Ops:
  0.6 6.6 %copy-start = (bf16[1,128,16,128]{3,2,1,0:T(8,128)(2,1)S(1)}, bf16[1,128,16,128]{3,2,1,0:T(8,128)(2,1)}, u32[]{:S(2)}) copy-start(bf16[1,128,16,128]{3,2,1,0:T(8,128)(2,1)} %param.8) | copy-start | bytes 1572868
  2.7 10.7 %collective-permute-start.3 = (bf16[528,128]{1,0:T(8,128)(2,1)}, bf16[528,128]{1,0:T(8,128)(2,1)S(1)}, u32[]{:S(2)}, u32[]{:S(2)}) collective-permute-start(bf16[528,128]{1,0:T(8,128)(2,1)} %get-tuple-element.41), channel_id=1, source_target_pairs={{0,1},{1,0},{2,3},{3,2},{4,5},{5,4},{6,7},{7,6},{8,9},{9,8},{10,11... | collective-permute-start | bytes 405512 | tf_op jit(solution)/shard_map/ppermute | solution.py:553
  5.7 7.8 %collective-permute-start.4 = (bf16[528,128]{1,0:T(8,128)(2,1)}, bf16[528,128]{1,0:T(8,128)(2,1)S(1)}, u32[]{:S(2)}, u32[]{:S(2)}) collective-permute-start(bf16[528,128]{1,0:T(8,128)(2,1)} %get-tuple-element.42), channel_id=1, source_target_pairs={{0,2},{1,3},{2,0},{3,1},{4,6},{5,7},{6,4},{7,5},{8,10},{9,11},{10,... | collective-permute-start | bytes 405512 | tf_op jit(solution)/shard_map/ppermute | solution.py:553
  7.2 8.2 %collective-permute-start.5 = (bf16[528,128]{1,0:T(8,128)(2,1)}, bf16[528,128]{1,0:T(8,128)(2,1)S(1)}, u32[]{:S(2)}, u32[]{:S(2)}) collective-permute-start(bf16[528,128]{1,0:T(8,128)(2,1)} %get-tuple-element.43), channel_id=1, source_target_pairs={{0,3},{1,2},{2,1},{3,0},{4,7},{5,6},{6,5},{7,4},{8,11},{9,10},{10,... | collective-permute-start | bytes 405512 | tf_op jit(solution)/shard_map/ppermute | solution.py:553
  7.2 1.0 %copy-start.1 = (bf16[1,128,16,128]{3,2,1,0:T(8,128)(2,1)S(1)}, bf16[1,128,16,128]{3,2,1,0:T(8,128)(2,1)}, u32[]{:S(2)}) copy-start(bf16[1,128,16,128]{3,2,1,0:T(8,128)(2,1)} %param.11) | copy-start | bytes 1572868
  8.3 8.6 %copy-start.2 = (bf16[528,128]{1,0:T(8,128)(2,1)S(1)}, bf16[528,128]{1,0:T(8,128)(2,1)}, u32[]{:S(2)}) copy-start(bf16[528,128]{1,0:T(8,128)(2,1)} %get-tuple-element.40.rest_0_) | copy-start | bytes 405508
  8.3 8.6 %copy-start.3 = (f32[4,2,64,128]{3,2,1,0:T(8,128)S(1)}, f32[4,2,64,128]{3,2,1,0:T(8,128)}, u32[]{:S(2)}) copy-start(f32[4,2,64,128]{3,2,1,0:T(8,128)} %constant.4.clone.rest_4_.rest_10_.rest_14_) | copy-start | bytes 786436
  9.0 8.7 %collective-permute-start = (bf16[512,128]{1,0:T(8,128)(2,1)S(1)}, bf16[512,128]{1,0:T(8,128)(2,1)S(1)}, u32[]{:S(2)}, u32[]{:S(2)}) collective-permute-start(bf16[512,128]{1,0:T(8,128)(2,1)S(1)} %get-tuple-element.37), channel_id=1, source_target_pairs={{0,1},{1,0},{2,3},{3,2},{4,5},{5,4},{6,7},{7,6},{8,9},{9,8},{10,11... | collective-permute-start | bytes 393224 | tf_op jit(solution)/shard_map/ppermute | solution.py:553
  11.0 9.0 %collective-permute-start.1 = (bf16[512,128]{1,0:T(8,128)(2,1)S(1)}, bf16[512,128]{1,0:T(8,128)(2,1)S(1)}, u32[]{:S(2)}, u32[]{:S(2)}) collective-permute-start(bf16[512,128]{1,0:T(8,128)(2,1)S(1)} %get-tuple-element.38), channel_id=1, source_target_pairs={{0,2},{1,3},{2,0},{3,1},{4,6},{5,7},{6,4},{7,5},{8,10},{9,11},{10,... | collective-permute-start | bytes 393224 | tf_op jit(solution)/shard_map/ppermute | solution.py:553
  12.6 0.7 %copy-start.4 = (f32[128]{0:T(128)S(1)}, f32[128]{0:T(128)}, u32[]{:S(2)}) copy-start(f32[128]{0:T(128)} %param.14) | copy-start | bytes 1540
  12.6 0.7 %copy-start.5 = (f32[128]{0:T(128)S(1)}, f32[128]{0:T(128)}, u32[]{:S(2)}) copy-start(f32[128]{0:T(128)} %param.13) | copy-start | bytes 1540
  13.4 7.4 %collective-permute-start.2 = (bf16[512,128]{1,0:T(8,128)(2,1)S(1)}, bf16[512,128]{1,0:T(8,128)(2,1)S(1)}, u32[]{:S(2)}, u32[]{:S(2)}) collective-permute-start(bf16[512,128]{1,0:T(8,128)(2,1)S(1)} %get-tuple-element.39), channel_id=1, source_target_pairs={{0,3},{1,2},{2,1},{3,0},{4,7},{5,6},{6,5},{7,4},{8,11},{9,10},{10,... | collective-permute-start | bytes 393224 | tf_op jit(solution)/shard_map/ppermute | solution.py:553
  13.5 8.9 %collective-permute-start.6 = (bf16[512,128]{1,0:T(8,128)(2,1)S(1)}, bf16[512,128]{1,0:T(8,128)(2,1)S(1)}, u32[]{:S(2)}, u32[]{:S(2)}) collective-permute-start(bf16[512,128]{1,0:T(8,128)(2,1)S(1)} %get-tuple-element.55), channel_id=1, source_target_pairs={{0,1},{1,0},{2,3},{3,2},{4,5},{5,4},{6,7},{7,6},{8,9},{9,8},{10,11... | collective-permute-start | bytes 393224 | tf_op jit(solution)/shard_map/ppermute | solution.py:553
  15.4 9.7 %collective-permute-start.7 = (bf16[512,128]{1,0:T(8,128)(2,1)S(1)}, bf16[512,128]{1,0:T(8,128)(2,1)S(1)}, u32[]{:S(2)}, u32[]{:S(2)}) collective-permute-start(bf16[512,128]{1,0:T(8,128)(2,1)S(1)} %get-tuple-element.56), channel_id=1, source_target_pairs={{0,2},{1,3},{2,0},{3,1},{4,6},{5,7},{6,4},{7,5},{8,10},{9,11},{10,... | collective-permute-start | bytes 393224 | tf_op jit(solution)/shard_map/ppermute | solution.py:553
  17.8 7.3 %collective-permute-start.8 = (bf16[512,128]{1,0:T(8,128)(2,1)S(1)}, bf16[512,128]{1,0:T(8,128)(2,1)S(1)}, u32[]{:S(2)}, u32[]{:S(2)}) collective-permute-start(bf16[512,128]{1,0:T(8,128)(2,1)S(1)} %get-tuple-element.57), channel_id=1, source_target_pairs={{0,3},{1,2},{2,1},{3,0},{4,7},{5,6},{6,5},{7,4},{8,11},{9,10},{10,... | collective-permute-start | bytes 393224 | tf_op jit(solution)/shard_map/ppermute | solution.py:553
  26.7 5.7 %collective-permute-start.14 = (f32[8,128]{1,0:T(8,128)S(1)}, f32[8,128]{1,0:T(8,128)S(1)}, u32[]{:S(2)}, u32[]{:S(2)}) collective-permute-start(f32[8,128]{1,0:T(8,128)S(1)} %add.21), channel_id=1, source_target_pairs={{0,3},{1,2},{2,1},{3,0},{4,7},{5,6},{6,5},{7,4},{8,11},{9,10},{10,... | collective-permute-start | bytes 12296 | tf_op jit(solution)/shard_map/ppermute | solution.py:526
  28.3 5.4 %collective-permute-start.13 = (f32[8,128]{1,0:T(8,128)S(1)}, f32[8,128]{1,0:T(8,128)S(1)}, u32[]{:S(2)}, u32[]{:S(2)}) collective-permute-start(f32[8,128]{1,0:T(8,128)S(1)} %add.21), channel_id=1, source_target_pairs={{0,2},{1,3},{2,0},{3,1},{4,6},{5,7},{6,4},{7,5},{8,10},{9,11},{10,... | collective-permute-start | bytes 12296 | tf_op jit(solution)/shard_map/ppermute | solution.py:526
  29.5 4.3 %collective-permute-start.12 = (f32[8,128]{1,0:T(8,128)S(1)}, f32[8,128]{1,0:T(8,128)S(1)}, u32[]{:S(2)}, u32[]{:S(2)}) collective-permute-start(f32[8,128]{1,0:T(8,128)S(1)} %add.21), channel_id=1, source_target_pairs={{0,1},{1,0},{2,3},{3,2},{4,5},{5,4},{6,7},{7,6},{8,9},{9,8},{10,11... | collective-permute-start | bytes 12296 | tf_op jit(solution)/shard_map/ppermute | solution.py:526
  30.3 13.4 %collective-permute-start.9 = (bf16[1024,128]{1,0:T(8,128)(2,1)S(1)}, bf16[1024,128]{1,0:T(8,128)(2,1)S(1)}, u32[]{:S(2)}, u32[]{:S(2)}) collective-permute-start(bf16[1024,128]{1,0:T(8,128)(2,1)S(1)} %get-tuple-element.59), channel_id=1, source_target_pairs={{0,1},{1,0},{2,3},{3,2},{4,5},{5,4},{6,7},{7,6},{8,9},{9,8},{10,11... | collective-permute-start | bytes 786440 | tf_op jit(solution)/shard_map/ppermute | solution.py:589
  31.5 12.2 %collective-permute-start.10 = (bf16[1024,128]{1,0:T(8,128)(2,1)S(1)}, bf16[1024,128]{1,0:T(8,128)(2,1)S(1)}, u32[]{:S(2)}, u32[]{:S(2)}) collective-permute-start(bf16[1024,128]{1,0:T(8,128)(2,1)S(1)} %get-tuple-element.60), channel_id=1, source_target_pairs={{0,2},{1,3},{2,0},{3,1},{4,6},{5,7},{6,4},{7,5},{8,10},{9,11},{10,... | collective-permute-start | bytes 786440 | tf_op jit(solution)/shard_map/ppermute | solution.py:589
  32.4 11.3 %collective-permute-start.11 = (bf16[1024,128]{1,0:T(8,128)(2,1)S(1)}, bf16[1024,128]{1,0:T(8,128)(2,1)S(1)}, u32[]{:S(2)}, u32[]{:S(2)}) collective-permute-start(bf16[1024,128]{1,0:T(8,128)(2,1)S(1)} %get-tuple-element.61), channel_id=1, source_target_pairs={{0,3},{1,2},{2,1},{3,0},{4,7},{5,6},{6,5},{7,4},{8,11},{9,10},{10,... | collective-permute-start | bytes 786440 | tf_op jit(solution)/shard_map/ppermute | solution.py:589
  33.8 1.2 %collective-permute-start.15 = (f32[8,128]{1,0:T(8,128)S(1)}, f32[8,128]{1,0:T(8,128)S(1)}, u32[]{:S(2)}, u32[]{:S(2)}) collective-permute-start(f32[8,128]{1,0:T(8,128)S(1)} %add_add_fusion), channel_id=1, source_target_pairs={{0,4},{4,0},{8,12},{12,8},{16,20},{20,16},{24,28},{28,24},{1,5},{5... | collective-permute-start | bytes 12296 | tf_op jit(solution)/shard_map/ppermute | solution.py:526
  35.0 3.6 %collective-permute-start.16 = (f32[8,128]{1,0:T(8,128)S(1)}, f32[8,128]{1,0:T(8,128)S(1)}, u32[]{:S(2)}, u32[]{:S(2)}) collective-permute-start(f32[8,128]{1,0:T(8,128)S(1)} %add.25), channel_id=1, source_target_pairs={{0,8},{4,12},{8,0},{12,4},{16,24},{20,28},{24,16},{28,20},{1,9},{5... | collective-permute-start | bytes 12296 | tf_op jit(solution)/shard_map/ppermute | solution.py:526
  38.6 4.5 %collective-permute-start.17 = (f32[8,128]{1,0:T(8,128)S(1)}, f32[8,128]{1,0:T(8,128)S(1)}, u32[]{:S(2)}, u32[]{:S(2)}) collective-permute-start(f32[8,128]{1,0:T(8,128)S(1)} %add.26), channel_id=1, source_target_pairs={{0,16},{4,20},{8,24},{12,28},{16,0},{20,4},{24,8},{28,12},{1,17},{... | collective-permute-start | bytes 12296 | tf_op jit(solution)/shard_map/ppermute | solution.py:526

commit v8 on v7

--- a/solution.py
+++ b/solution.py
@@ -19,7 +19,7 @@
 LOG2E = 1.4426950408889634
 VMEM_LIMIT = 48 * 1024 * 1024
 HEADS_VMEM = 24 * 1024 * 1024
-SPREAD_VMEM = 61 * 1024 * 1024
+SPREAD_VMEM = 426 * 128 * 1024
 NT = (((1,), (1,)), ((), ()))
 TN = (((0,), (0,)), ((), ()))
 
@@ -296,35 +296,26 @@
             yield ref[pl.ds(first + h, block, stride=ref.shape[0] // block), :].astype(jnp.bfloat16)
 
 
-def spread_keys_kernel(axis, parts, per, a_hbm, b_hbm, seg_hbm, *rest):
+def spread_keys_kernel(axis, parts, per, a_hbm, b_hbm, *rest):
     outs = rest[:parts]
-    a_in, b_in, a_f32, b_f32, seg_in, msg, in_sems, out_sems = rest[parts:]
-    block = seg_in.shape[1]
+    a_in, b_in, a_f32, b_f32, in_sems = rest[parts:]
+    block = outs[0].shape[0] // (2 * per)
     me = lax.axis_index(axis)
-    pairs = ((a_hbm, a_in), (b_hbm, b_in), (seg_hbm, seg_in))
-    loads = [pltpu.make_async_copy(src, dst, in_sems.at[i]) for i, (src, dst) in enumerate(pairs)]
+    loads = [pltpu.make_async_copy(src, dst, in_sems.at[i]) for i, (src, dst) in enumerate(((a_hbm, a_in), (b_hbm, b_in)))]
     for copy in loads:
         copy.start()
     for copy, src, dst in zip(loads, (a_in, b_in), (a_f32, b_f32)):
         copy.wait()
         dst[...] = src[...].astype(jnp.float32)
-    loads[2].wait()
-    ids = jnp.broadcast_to(seg_in[...].astype(jnp.float32), (16, block)).astype(jnp.bfloat16)
-    stores = []
-    for m in (*range(1, parts), 0):
+    for m in range(parts):
         for i, rows in enumerate(head_rows((a_f32, b_f32), (me ^ m) * per, per, block)):
-            msg[m, pl.ds(i * block, block), :] = rows
-        msg[m, pl.ds(2 * per * block, 16), :] = ids
-        copy = pltpu.make_async_copy(msg.at[m], outs[m], out_sems.at[m])
-        copy.start()
-        stores.append(copy)
-    for copy in stores:
-        copy.wait()
-
-
-def spread_queries_kernel(axis, parts, groups, per, a_ref, b_ref, *rest):
+            outs[m][pl.ds(i * block, block), :] = rows
+
+
+def spread_queries_kernel(axis, parts, groups, per, a_ref, b_ref, seg_ref, *rest):
     outs, a_f32, b_f32 = rest[-2 - parts * groups : -2], rest[-2], rest[-1]
-    block = outs[0].shape[0] // (2 * per)
+    block = seg_ref.shape[1]
+    ids = jnp.broadcast_to(seg_ref[...].astype(jnp.float32), (16, block)).astype(jnp.bfloat16)
     me = lax.axis_index(axis)
     for src, dst in ((a_ref, a_f32), (b_ref, b_f32)):
         dst[...] = src[...].astype(jnp.float32)
@@ -332,6 +323,7 @@
         for m in range(parts):
             for i, rows in enumerate(head_rows((a_f32, b_f32), ((me ^ m) * groups + grp) * per, per, block)):
                 outs[grp * parts + m][pl.ds(i * block, block), :] = rows
+            outs[m][pl.ds(2 * per * block, 16), :] = ids
 
 
 def turned(x):
@@ -370,7 +362,7 @@
 
 def keys_kernel(axis, parts, *rest):
     msgs, table_ref, gains_ref = rest[:parts], rest[parts], rest[parts + 1]
-    kt_ref, k_ref, v_ref, kn_ref, ks_ref, id_ref = rest[parts + 2 :]
+    kt_ref, k_ref, v_ref, kn_ref, ks_ref = rest[parts + 2 :]
     block = table_ref.shape[3]
     owned = v_ref.shape[1]
     f32, bf16 = jnp.float32, jnp.bfloat16
@@ -378,7 +370,6 @@
     gain = gain_columns(gains_ref, 1, 1)
     for m in range(parts):
         b = me ^ m
-        id_ref[b] = jnp.broadcast_to(msgs[m][pl.ds(2 * owned * block, 16), :].astype(f32)[0:1, :], (8, block))
         for h in range(owned):
             y, normed, scale = embed(turned(msgs[m][pl.ds(h * block, block), :]), gain, *rope(table_ref, b, 1))
             kt_ref[b, h], kn_ref[b, h], ks_ref[b, h] = y, normed, jnp.broadcast_to(scale, (8, block))
@@ -389,9 +380,14 @@
 def heads_kernel(axis, parts, grp, per, group, back, *rest):
     earlier, rest = rest[: grp * parts], rest[grp * parts :]
     msgs, rest = rest[:parts], rest[parts:]
-    kt_ref, k_ref, v_ref, kn_ref, ks_ref, id_ref, table_ref, gains_ref = rest[:8]
-    outs, share_ref = rest[8 : 8 + parts], rest[8 + parts]
-    qt_ref, g_ref, qn_ref, qs_ref, res_ref = rest[9 + parts :]
+    kt_ref, k_ref, v_ref, kn_ref, ks_ref, table_ref, gains_ref = rest[:7]
+    rest = rest[7:]
+    if grp:
+        id_ref, rest = rest[0], rest[1:]
+    outs, share_ref, rest = rest[:parts], rest[parts], rest[parts + 1 :]
+    if not grp:
+        id_ref, rest = rest[0], rest[1:]
+    qt_ref, g_ref, qn_ref, qs_ref, res_ref = rest
     block, width = table_ref.shape[3], gains_ref.shape[1]
     rows = group * block
     f32, bf16 = jnp.float32, jnp.bfloat16
@@ -399,6 +395,9 @@
     q_gain, k_gain = gain_columns(gains_ref, 0, group), gain_columns(gains_ref, 1, 1)
     for m in range(parts):
         b = me ^ m
+        if not grp:
+            ids = msgs[m][pl.ds(2 * per * rows, 16), :].astype(f32)[0:1, :]
+            id_ref[b] = jnp.broadcast_to(ids, (8, block))
         for p in range(per):
             at = b * per + p
             x = turned(msgs[m][pl.ds(p * rows, rows), :])
@@ -543,7 +542,7 @@
     q2, g2 = (x.reshape(block * heads, width) for x in (q_pre, grad_out))
     k2, v2 = (x.reshape(block * kv_heads, width) for x in (k_pre, values))
     owned = kv_heads // parts
-    kv_sent = (2 * owned * block + 16, width)
+    kv_sent = (2 * owned * block, width)
     sent = (per * 2 * rows, width)
     back_sent = (per * (group + 2) * block, width)
     dma = pltpu.SemaphoreType.DMA
@@ -553,16 +552,15 @@
     send = lambda out: [out[0]] + [lax.ppermute(out[m], "seq", xor(m, parts)) for m in range(1, parts)]
     kv_messages = call_in(
         functools.partial(spread_keys_kernel, "seq", parts, owned),
-        [hbm] * 3, [(kv_sent, bf16, hbm)] * parts,
-        [vmem(k_shape, bf16), vmem(k_shape, bf16), vmem(k_shape, f32), vmem(k_shape, f32), vmem((1, block), jnp.int32)]
-        + [vmem((parts, *kv_sent), bf16), dma((3,)), dma((parts,))],
-        1 << 20, k2, v2, segment_ids, limit=SPREAD_VMEM,
+        [hbm] * 2, [(kv_sent, bf16, vmem)] * parts,
+        [vmem(k_shape, bf16), vmem(k_shape, bf16), vmem(k_shape, f32), vmem(k_shape, f32), dma((2,))],
+        1 << 20, k2, v2, limit=SPREAD_VMEM,
     )
     kv_arrived = send(kv_messages)
     messages = call_in(
         functools.partial(spread_queries_kernel, "seq", parts, groups, per * group),
-        [vmem] * 2, [(sent, bf16, vmem)] * (parts * groups),
-        [vmem(q_shape, f32), vmem(q_shape, f32)], 1 << 33, q2, g2,
+        [vmem] * 3, [((sent[0] + 16, width), bf16, vmem)] * (parts * groups),
+        [vmem(q_shape, f32), vmem(q_shape, f32)], 1 << 33, q2, g2, segment_ids,
     )
     arrived = [send(messages[grp * parts : (grp + 1) * parts]) for grp in range(groups)]
     gains = jnp.concatenate([q_gain[None], k_gain[None], jnp.zeros((6, width), f32)], axis=0)
@@ -570,21 +568,22 @@
     keys = call_in(
         functools.partial(keys_kernel, "seq", parts), [vmem] * (parts + 2),
         [((*held, width, block), bf16, vmem), ((*held, block, width), bf16, vmem), ((*held, block, width), bf16, vmem)]
-        + [((*held, width, block), f32, vmem), ((*held, 8, block), f32, vmem), ((parts, 8, block), f32, vmem)],
+        + [((*held, width, block), f32, vmem), ((*held, 8, block), f32, vmem)],
         [], 1 << 33, *kv_arrived, table, gains,
     )
-    results, shares = [], []
+    results, shares, ids = [], [], []
     for grp in range(groups):
-        inputs = [*results, *arrived[grp], *keys, table, gains]
-        *made, share = call_in(
+        inputs = [*results, *arrived[grp], *keys, table, gains, *ids]
+        id_shape = ((parts, 8, block), f32, vmem)
+        made = call_in(
             functools.partial(heads_kernel, "seq", parts, grp, per, group, back),
             [vmem] * len(inputs),
-            [(((grp + 1) * back_sent[0], width), bf16, vmem)] * parts + [((8, width), f32, vmem)],
+            [(((grp + 1) * back_sent[0], width), bf16, vmem)] * parts + [((8, width), f32, vmem)] + [id_shape] * (grp == 0),
             [vmem((parts * per, width, rows), bf16), vmem((parts * per, rows, width), bf16)]
             + [vmem((parts * per, width, rows), f32), vmem((parts * per, 8, rows), f32), vmem((parts, *back_sent), bf16)],
             1 << 34, *inputs,
         )
-        results = made
+        results, share, ids = made[:parts], made[parts], made[parts + 1 :] or ids
         shares.append(share)
     go = lambda m: lax.ppermute(results[m], "seq", xor(m, parts))
     total = functools.reduce(jnp.add, shares)

time: 45.4 us -> 45 us (level)
  starting transfers between devices: 24 us -> 23.2 us
  Pallas kernels: 8.4 us -> 7.72 us
  local copies, waits for them, and re-layouts: 2.32 us -> 2.97 us
    ppermute x9, starting transfers between devices: 12.7 us -> 12 us  [by_heads(): lax.ppermute(out[m], 'seq', xor(m, parts))]
    pallas_call x6, Pallas kernels: 8.4 us -> 7.72 us  [call_in(): pl.pallas_call(kernel, out_shape=[jax.ShapeDtypeStruct(s, t) for s, t, _...]
    unnamed x12, local copies, waits for them, and re-layouts: 1.72 us -> 2.37 us
  transfers between devices with their start and end apart: 18 -> 18, of which waited for: 7 -> 6; matrix products, arithmetic and copies ran while one was open for 2% -> 2% of each run, Pallas kernels for 7% -> 7%
where the time goes in v8:
time: 45 us; the launch traced here: 44.8 us
  starting transfers between devices  23.2 us (52%)
  waiting for transfers between devices  10.1 us (22%)
  Pallas kernels  7.72 us (17%)
  local copies, waits for them, and re-layouts  2.97 us (7%)
  between operations  0.73 us (2%)
    ppermute x9, starting transfers between devices, by_heads(): lax.ppermute(out[m], 'seq', xor(m, parts))  12 us
    ppermute x6, starting transfers between devices, exchange_sum(): lax.ppermute(x, axis, [(i, i ^ m) for i in range(size)])  7.78 us
    pallas_call x6, Pallas kernels, call_in(): pl.pallas_call(kernel, out_shape=[jax.ShapeDtypeStruct(s, t) for s, t, _...  7.72 us
    ppermute x6, waiting for transfers between devices, exchange_sum(): lax.ppermute(x, axis, [(i, i ^ m) for i in range(size)])  5.11 us
    ppermute x9, waiting for transfers between devices, by_heads(): lax.ppermute(out[m], 'seq', xor(m, parts))  4.93 us
    ppermute x3, starting transfers between devices, by_heads(): go = lambda m: lax.ppermute(results[m], 'seq', xor(m, parts))  3.49 us
    unnamed x12, local copies, waits for them, and re-layouts  2.37 us
  transfers between devices with their start and end apart: 18, of which 6 were waited for; matrix products, arithmetic and copies ran while one was open for 2% of the time, Pallas kernels for 7%

profile of v8, /device:TPU:0, one launch (start us, length us, event | category | flops | bytes accessed | tf_op | source)
XLA Modules:
  0.0 44.8 jit_solution(16489699503774240314)
XLA Ops:
  0.6 0.0 copy-start
  0.6 1.3 %shard_map.120 = (bf16[512,128]{1,0:T(8,128)(2,1)S(1)}, bf16[512,128]{1,0:T(8,128)(2,1)S(1)}, bf16[512,128]{1,0:T(8,128)(2,1)S(1)}, bf16[512,128]{1,0:T(8,128)(2,1)S(1)}) custom-call(bf16[1024,128]{1,0:T(8,128)(2,1)} %bitcast.15, bf16[1024,128]{1,0:T(8,128)(2,1)} %bitcast.16), custom_call_target="tpu_custom_call" | custom-call | flops 1048576 | bytes 1048576 | tf_op jit(solution)/shard_map/pallas_call | solution.py:513
  1.9 3.0 %collective-permute-start.3 = (bf16[512,128]{1,0:T(8,128)(2,1)S(1)}, bf16[512,128]{1,0:T(8,128)(2,1)S(1)}, u32[]{:S(2)}, u32[]{:S(2)}) collective-permute-start(bf16[512,128]{1,0:T(8,128)(2,1)S(1)} %get-tuple-element.41), channel_id=1, source_target_pairs={{0,1},{1,0},{2,3},{3,2},{4,5},{5,4},{6,7},{7,6},{8,9},{9,8},{10,11... | collective-permute-start | bytes 393224 | tf_op jit(solution)/shard_map/ppermute | solution.py:552
  4.9 1.5 %collective-permute-start.4 = (bf16[512,128]{1,0:T(8,128)(2,1)S(1)}, bf16[512,128]{1,0:T(8,128)(2,1)S(1)}, u32[]{:S(2)}, u32[]{:S(2)}) collective-permute-start(bf16[512,128]{1,0:T(8,128)(2,1)S(1)} %get-tuple-element.42), channel_id=1, source_target_pairs={{0,2},{1,3},{2,0},{3,1},{4,6},{5,7},{6,4},{7,5},{8,10},{9,11},{10,... | collective-permute-start | bytes 393224 | tf_op jit(solution)/shard_map/ppermute | solution.py:552
  6.5 0.0 collective-permute-start.5
  6.5 0.0 copy-start.2
  6.5 0.0 copy-done
  6.5 0.7 %copy-done.2 = s32[1,128]{1,0:T(1,128)S(1)} copy-done((s32[1,128]{1,0:T(1,128)S(1)}, s32[1,128]{1,0:T(1,128)}, u32[]{:S(2)}) %copy-start.2) | copy-done | bytes 536
  7.1 0.0 copy-start.1
  7.1 1.0 %copy-done.1 = bf16[1,128,16,128]{3,2,1,0:T(8,128)(2,1)S(1)} copy-done((bf16[1,128,16,128]{3,2,1,0:T(8,128)(2,1)S(1)}, bf16[1,128,16,128]{3,2,1,0:T(8,128)(2,1)}, u32[]{:S(2)}) %copy-start.1) | copy-done | bytes 524312
  8.2 0.0 copy-start.3
  8.2 0.8 %shard_map.119 = (bf16[528,128]{1,0:T(8,128)(2,1)S(1)}, bf16[528,128]{1,0:T(8,128)(2,1)S(1)}, bf16[528,128]{1,0:T(8,128)(2,1)S(1)}, bf16[528,128]{1,0:T(8,128)(2...) custom-call(bf16[2048,128]{1,0:T(8,128)(2,1)S(1)} %bitcast.13, ...), custom_call_target="tpu_custom_call" | custom-call | flops 8589934592 | bytes 1048576 | tf_op jit(solution)/shard_map/pallas_call | solution.py:513
  9.0 2.0 %collective-permute-start = (bf16[528,128]{1,0:T(8,128)(2,1)S(1)}, bf16[528,128]{1,0:T(8,128)(2,1)S(1)}, u32[]{:S(2)}, u32[]{:S(2)}) collective-permute-start(bf16[528,128]{1,0:T(8,128)(2,1)S(1)} %get-tuple-element.37), channel_id=1, source_target_pairs={{0,1},{1,0},{2,3},{3,2},{4,5},{5,4},{6,7},{7,6},{8,9},{9,8},{10,11... | collective-permute-start | bytes 405512 | tf_op jit(solution)/shard_map/ppermute | solution.py:552
  11.0 1.5 %collective-permute-start.1 = (bf16[528,128]{1,0:T(8,128)(2,1)S(1)}, bf16[528,128]{1,0:T(8,128)(2,1)S(1)}, u32[]{:S(2)}, u32[]{:S(2)}) collective-permute-start(bf16[528,128]{1,0:T(8,128)(2,1)S(1)} %get-tuple-element.38), channel_id=1, source_target_pairs={{0,2},{1,3},{2,0},{3,1},{4,6},{5,7},{6,4},{7,5},{8,10},{9,11},{10,... | collective-permute-start | bytes 405512 | tf_op jit(solution)/shard_map/ppermute | solution.py:552
  12.5 0.1 pad.2.clone
  12.6 0.0 copy-start.4
  12.6 0.0 copy-start.5
  12.6 0.7 %copy-done.4 = f32[128]{0:T(128)S(1)} copy-done((f32[128]{0:T(128)S(1)}, f32[128]{0:T(128)}, u32[]{:S(2)}) %copy-start.4) | copy-done | bytes 536
  13.2 0.0 copy-done.5
  13.2 0.1 maximum_maximum_fusion.rest_5_.rest_10_.rest_14_
  13.3 0.0 collective-permute-done.3.rest_1_
  13.3 0.0 collective-permute-start.2
  13.4 0.0 collective-permute-done.4.rest_2_
  13.4 1.9 %collective-permute-start.6 = (bf16[528,128]{1,0:T(8,128)(2,1)S(1)}, bf16[528,128]{1,0:T(8,128)(2,1)S(1)}, u32[]{:S(2)}, u32[]{:S(2)}) collective-permute-start(bf16[528,128]{1,0:T(8,128)(2,1)S(1)} %get-tuple-element.54), channel_id=1, source_target_pairs={{0,1},{1,0},{2,3},{3,2},{4,5},{5,4},{6,7},{7,6},{8,9},{9,8},{10,11... | collective-permute-start | bytes 405512 | tf_op jit(solution)/shard_map/ppermute | solution.py:552
  15.3 0.0 collective-permute-done.5.rest_3_
  15.3 1.5 %collective-permute-start.7 = (bf16[528,128]{1,0:T(8,128)(2,1)S(1)}, bf16[528,128]{1,0:T(8,128)(2,1)S(1)}, u32[]{:S(2)}, u32[]{:S(2)}) collective-permute-start(bf16[528,128]{1,0:T(8,128)(2,1)S(1)} %get-tuple-element.55), channel_id=1, source_target_pairs={{0,2},{1,3},{2,0},{3,1},{4,6},{5,7},{6,4},{7,5},{8,10},{9,11},{10,... | collective-permute-start | bytes 405512 | tf_op jit(solution)/shard_map/ppermute | solution.py:552
  16.8 0.0 copy-done.3
  16.8 0.9 %shard_map.121 = (bf16[4,2,128,128]{3,2,1,0:T(8,128)(2,1)S(1)}, bf16[4,2,128,128]{3,2,1,0:T(8,128)(2,1)S(1)}, bf16[4,2,128,128]{3,2,1,0:T(8,128)(2,1)S(1)}, f32[...) custom-call(bf16[512,128]{1,0:T(8,128)(2,1)S(1)} %get-tuple-element.40.rest_0_, ...), custom_call_target="tpu_custom_call" | custom-call | flops 8589934592 | bytes 1048576 | tf_op jit(solution)/shard_map/pallas_call | solution.py:513
  17.7 0.0 collective-permute-done.rest_1_
  17.7 0.4 collective-permute-start.8
  18.1 2.2 %collective-permute-done.1.rest_2_ = bf16[528,128]{1,0:T(8,128)(2,1)S(1)} collective-permute-done((bf16[528,128]{1,0:T(8,128)(2,1)S(1)}, bf16[528,128]{1,0:T(8,128)(2,1)S(1)}, u32[]{:S(2)}, u32[]{:S(2)}) %collective-permute-start.1) | collective-permute-done | bytes 135200 | tf_op jit(solution)/shard_map/ppermute | solution.py:552
  20.3 0.6 %collective-permute-done.2.rest_3_ = bf16[528,128]{1,0:T(8,128)(2,1)S(1)} collective-permute-done((bf16[528,128]{1,0:T(8,128)(2,1)S(1)}, bf16[528,128]{1,0:T(8,128)(2,1)S(1)}, u32[]{:S(2)}, u32[]{:S(2)}) %collective-permute-start.2) | collective-permute-done | bytes 135200 | tf_op jit(solution)/shard_map/ppermute | solution.py:552
  20.9 1.7 %shard_map.122 = (bf16[512,128]{1,0:T(8,128)(2,1)S(1)}, bf16[512,128]{1,0:T(8,128)(2,1)S(1)}, bf16[512,128]{1,0:T(8,128)(2,1)S(1)}, bf16[512,128]{1,0:T(8,128)(2...) custom-call(bf16[528,128]{1,0:T(8,128)(2,1)S(1)} %get-tuple-element.36.rest_0_, ...), custom_call_target="tpu_custom_call" | custom-call | flops 17179869184 | bytes 1048576 | tf_op jit(solution)/shard_map/pallas_call | solution.py:513
  22.5 0.0 collective-permute-done.6.rest_5_
  22.5 2.2 %collective-permute-done.7.rest_6_ = bf16[528,128]{1,0:T(8,128)(2,1)S(1)} collective-permute-done((bf16[528,128]{1,0:T(8,128)(2,1)S(1)}, bf16[528,128]{1,0:T(8,128)(2,1)S(1)}, u32[]{:S(2)}, u32[]{:S(2)}) %collective-permute-start.7) | collective-permute-done | bytes 135200 | tf_op jit(solution)/shard_map/ppermute | solution.py:552
  24.7 0.0 collective-permute-done.8.rest_7_
  24.7 1.6 %shard_map.123 = (bf16[1024,128]{1,0:T(8,128)(2,1)S(1)}, bf16[1024,128]{1,0:T(8,128)(2,1)S(1)}, bf16[1024,128]{1,0:T(8,128)(2,1)S(1)}, bf16[1024,128]{1,0:T(8,128)(2,1)S(1)}, f32[8,128]{1,0:T(8,128)S(1)}) custom-call(bf16[512,128]{1,0:T(8,128)(2,1)S(1)} %get-tuple-element.49.rest_0_, bf16[512,128]{1,0:T(8,128)(2,1)S(1)} %get-tuple-element.50.rest_1_, ...), custom_call_target="tpu_custom_call" | custom-call | flops 17179869184 | bytes 1048576 | tf_op jit(solution)/shard_map/pallas_call | solution.py:513
  26.3 1.4 %collective-permute-start.14 = (f32[8,128]{1,0:T(8,128)S(1)}, f32[8,128]{1,0:T(8,128)S(1)}, u32[]{:S(2)}, u32[]{:S(2)}) collective-permute-start(f32[8,128]{1,0:T(8,128)S(1)} %add.21), channel_id=1, source_target_pairs={{0,3},{1,2},{2,1},{3,0},{4,7},{5,6},{6,5},{7,4},{8,11},{9,10},{10,... | collective-permute-start | bytes 12296 | tf_op jit(solution)/shard_map/ppermute | solution.py:525
  27.7 1.1 %collective-permute-start.13 = (f32[8,128]{1,0:T(8,128)S(1)}, f32[8,128]{1,0:T(8,128)S(1)}, u32[]{:S(2)}, u32[]{:S(2)}) collective-permute-start(f32[8,128]{1,0:T(8,128)S(1)} %add.21), channel_id=1, source_target_pairs={{0,2},{1,3},{2,0},{3,1},{4,6},{5,7},{6,4},{7,5},{8,10},{9,11},{10,... | collective-permute-start | bytes 12296 | tf_op jit(solution)/shard_map/ppermute | solution.py:525
  28.8 1.1 %collective-permute-start.12 = (f32[8,128]{1,0:T(8,128)S(1)}, f32[8,128]{1,0:T(8,128)S(1)}, u32[]{:S(2)}, u32[]{:S(2)}) collective-permute-start(f32[8,128]{1,0:T(8,128)S(1)} %add.21), channel_id=1, source_target_pairs={{0,1},{1,0},{2,3},{3,2},{4,5},{5,4},{6,7},{7,6},{8,9},{9,8},{10,11... | collective-permute-start | bytes 12296 | tf_op jit(solution)/shard_map/ppermute | solution.py:525
  29.9 0.9 %collective-permute-start.9 = (bf16[1024,128]{1,0:T(8,128)(2,1)S(1)}, bf16[1024,128]{1,0:T(8,128)(2,1)S(1)}, u32[]{:S(2)}, u32[]{:S(2)}) collective-permute-start(bf16[1024,128]{1,0:T(8,128)(2,1)S(1)} %get-tuple-element.59), channel_id=1, source_target_pairs={{0,1},{1,0},{2,3},{3,2},{4,5},{5,4},{6,7},{7,6},{8,9},{9,8},{10,11... | collective-permute-start | bytes 786440 | tf_op jit(solution)/shard_map/ppermute | solution.py:588
  30.8 0.9 %collective-permute-start.10 = (bf16[1024,128]{1,0:T(8,128)(2,1)S(1)}, bf16[1024,128]{1,0:T(8,128)(2,1)S(1)}, u32[]{:S(2)}, u32[]{:S(2)}) collective-permute-start(bf16[1024,128]{1,0:T(8,128)(2,1)S(1)} %get-tuple-element.60), channel_id=1, source_target_pairs={{0,2},{1,3},{2,0},{3,1},{4,6},{5,7},{6,4},{7,5},{8,10},{9,11},{10,... | collective-permute-start | bytes 786440 | tf_op jit(solution)/shard_map/ppermute | solution.py:588
  31.8 0.0 collective-permute-done.14
  31.8 1.6 %collective-permute-start.11 = (bf16[1024,128]{1,0:T(8,128)(2,1)S(1)}, bf16[1024,128]{1,0:T(8,128)(2,1)S(1)}, u32[]{:S(2)}, u32[]{:S(2)}) collective-permute-start(bf16[1024,128]{1,0:T(8,128)(2,1)S(1)} %get-tuple-element.61), channel_id=1, source_target_pairs={{0,3},{1,2},{2,1},{3,0},{4,7},{5,6},{6,5},{7,4},{8,11},{9,10},{10,... | collective-permute-start | bytes 786440 | tf_op jit(solution)/shard_map/ppermute | solution.py:588
  33.4 0.0 collective-permute-done.13
  33.4 0.0 collective-permute-done.12
  33.4 0.1 collective-permute-start.15
  33.5 1.2 %collective-permute-done.15 = f32[8,128]{1,0:T(8,128)S(1)} collective-permute-done((f32[8,128]{1,0:T(8,128)S(1)}, f32[8,128]{1,0:T(8,128)S(1)}, u32[]{:S(2)}, u32[]{:S(2)}) %collective-permute-start.15) | collective-permute-done | bytes 4128 | tf_op jit(solution)/shard_map/ppermute | solution.py:525
  34.6 1.6 %collective-permute-start.16 = (f32[8,128]{1,0:T(8,128)S(1)}, f32[8,128]{1,0:T(8,128)S(1)}, u32[]{:S(2)}, u32[]{:S(2)}) collective-permute-start(f32[8,128]{1,0:T(8,128)S(1)} %add.25), channel_id=1, source_target_pairs={{0,8},{4,12},{8,0},{12,4},{16,24},{20,28},{24,16},{28,20},{1,9},{5... | collective-permute-start | bytes 12296 | tf_op jit(solution)/shard_map/ppermute | solution.py:525
  36.2 2.0 %collective-permute-done.16 = f32[8,128]{1,0:T(8,128)S(1)} collective-permute-done((f32[8,128]{1,0:T(8,128)S(1)}, f32[8,128]{1,0:T(8,128)S(1)}, u32[]{:S(2)}, u32[]{:S(2)}) %collective-permute-start.16) | collective-permute-done | bytes 4128 | tf_op jit(solution)/shard_map/ppermute | solution.py:525
  38.3 2.6 %collective-permute-start.17 = (f32[8,128]{1,0:T(8,128)S(1)}, f32[8,128]{1,0:T(8,128)S(1)}, u32[]{:S(2)}, u32[]{:S(2)}) collective-permute-start(f32[8,128]{1,0:T(8,128)S(1)} %add.26), channel_id=1, source_target_pairs={{0,16},{4,20},{8,24},{12,28},{16,0},{20,4},{24,8},{28,12},{1,17},{... | collective-permute-start | bytes 12296 | tf_op jit(solution)/shard_map/ppermute | solution.py:525
  40.8 1.9 %collective-permute-done.17 = f32[8,128]{1,0:T(8,128)S(1)} collective-permute-done((f32[8,128]{1,0:T(8,128)S(1)}, f32[8,128]{1,0:T(8,128)S(1)}, u32[]{:S(2)}, u32[]{:S(2)}) %collective-permute-start.17) | collective-permute-done | bytes 4128 | tf_op jit(solution)/shard_map/ppermute | solution.py:525
  42.8 0.5 %slice_bitcast_fusion = (f32[128]{0:T(128)}, f32[128]{0:T(128)}) fusion(f32[8,128]{1,0:T(8,128)S(1)} %add.27), kind=kLoop, calls=%fused_computation.2 | loop fusion | bytes 2048 | tf_op jit(solution)/shard_map/squeeze | solution.py:601
  43.3 0.0 collective-permute-done.9.rest_1_
  43.3 0.0 collective-permute-done.10.rest_2_
  43.3 0.0 collective-permute-done.11.rest_3_
  43.3 1.5 %shard_map.124 = (bf16[2048,128]{1,0:T(8,128)(2,1)}, bf16[1024,128]{1,0:T(8,128)(2,1)}, bf16[1024,128]{1,0:T(8,128)(2,1)}) custom-call(bf16[1024,128]{1,0:T(8,128)(2,1)S(1)} %get-tuple-element.58.rest_0_, bf16[1024,128]{1,0:T(8,128)(2,1)S(1)} %collective-permute-done.9.rest_1_, bf16[1024,128]{1,0:T(8,128)(2,1)S(1)} %collective-permute-done.10.rest_2_, ...), custom_call_target="tpu_custom_call" | custom-call | flops 1048576 | bytes 1048576 | tf_op jit(solution)/shard_map/pallas_call | solution.py:513
  (6 shorter events, 0.0 us)
Async XLA Ops:
  0.6 5.9 %copy-start = (bf16[1,128,16,128]{3,2,1,0:T(8,128)(2,1)S(1)}, bf16[1,128,16,128]{3,2,1,0:T(8,128)(2,1)}, u32[]{:S(2)}) copy-start(bf16[1,128,16,128]{3,2,1,0:T(8,128)(2,1)} %param.8) | copy-start | bytes 1572868
  1.9 11.4 %collective-permute-start.3 = (bf16[512,128]{1,0:T(8,128)(2,1)S(1)}, bf16[512,128]{1,0:T(8,128)(2,1)S(1)}, u32[]{:S(2)}, u32[]{:S(2)}) collective-permute-start(bf16[512,128]{1,0:T(8,128)(2,1)S(1)} %get-tuple-element.41), channel_id=1, source_target_pairs={{0,1},{1,0},{2,3},{3,2},{4,5},{5,4},{6,7},{7,6},{8,9},{9,8},{10,11... | collective-permute-start | bytes 393224 | tf_op jit(solution)/shard_map/ppermute | solution.py:552
  4.9 8.4 %collective-permute-start.4 = (bf16[512,128]{1,0:T(8,128)(2,1)S(1)}, bf16[512,128]{1,0:T(8,128)(2,1)S(1)}, u32[]{:S(2)}, u32[]{:S(2)}) collective-permute-start(bf16[512,128]{1,0:T(8,128)(2,1)S(1)} %get-tuple-element.42), channel_id=1, source_target_pairs={{0,2},{1,3},{2,0},{3,1},{4,6},{5,7},{6,4},{7,5},{8,10},{9,11},{10,... | collective-permute-start | bytes 393224 | tf_op jit(solution)/shard_map/ppermute | solution.py:552
  6.5 8.8 %collective-permute-start.5 = (bf16[512,128]{1,0:T(8,128)(2,1)S(1)}, bf16[512,128]{1,0:T(8,128)(2,1)S(1)}, u32[]{:S(2)}, u32[]{:S(2)}) collective-permute-start(bf16[512,128]{1,0:T(8,128)(2,1)S(1)} %get-tuple-element.43), channel_id=1, source_target_pairs={{0,3},{1,2},{2,1},{3,0},{4,7},{5,6},{6,5},{7,4},{8,11},{9,10},{10,... | collective-permute-start | bytes 393224 | tf_op jit(solution)/shard_map/ppermute | solution.py:552
  6.5 0.7 %copy-start.2 = (s32[1,128]{1,0:T(1,128)S(1)}, s32[1,128]{1,0:T(1,128)}, u32[]{:S(2)}) copy-start(s32[1,128]{1,0:T(1,128)} %seg_ref.1) | copy-start | bytes 1540
  7.1 1.0 %copy-start.1 = (bf16[1,128,16,128]{3,2,1,0:T(8,128)(2,1)S(1)}, bf16[1,128,16,128]{3,2,1,0:T(8,128)(2,1)}, u32[]{:S(2)}) copy-start(bf16[1,128,16,128]{3,2,1,0:T(8,128)(2,1)} %param.11) | copy-start | bytes 1572868
  8.2 8.6 %copy-start.3 = (f32[4,2,64,128]{3,2,1,0:T(8,128)S(1)}, f32[4,2,64,128]{3,2,1,0:T(8,128)}, u32[]{:S(2)}) copy-start(f32[4,2,64,128]{3,2,1,0:T(8,128)} %constant.4.clone.rest_4_.rest_9_.rest_13_) | copy-start | bytes 786436
  9.0 8.7 %collective-permute-start = (bf16[528,128]{1,0:T(8,128)(2,1)S(1)}, bf16[528,128]{1,0:T(8,128)(2,1)S(1)}, u32[]{:S(2)}, u32[]{:S(2)}) collective-permute-start(bf16[528,128]{1,0:T(8,128)(2,1)S(1)} %get-tuple-element.37), channel_id=1, source_target_pairs={{0,1},{1,0},{2,3},{3,2},{4,5},{5,4},{6,7},{7,6},{8,9},{9,8},{10,11... | collective-permute-start | bytes 405512 | tf_op jit(solution)/shard_map/ppermute | solution.py:552
  11.0 9.3 %collective-permute-start.1 = (bf16[528,128]{1,0:T(8,128)(2,1)S(1)}, bf16[528,128]{1,0:T(8,128)(2,1)S(1)}, u32[]{:S(2)}, u32[]{:S(2)}) collective-permute-start(bf16[528,128]{1,0:T(8,128)(2,1)S(1)} %get-tuple-element.38), channel_id=1, source_target_pairs={{0,2},{1,3},{2,0},{3,1},{4,6},{5,7},{6,4},{7,5},{8,10},{9,11},{10,... | collective-permute-start | bytes 405512 | tf_op jit(solution)/shard_map/ppermute | solution.py:552
  12.6 0.7 %copy-start.4 = (f32[128]{0:T(128)S(1)}, f32[128]{0:T(128)}, u32[]{:S(2)}) copy-start(f32[128]{0:T(128)} %param.14) | copy-start | bytes 1540
  12.6 0.7 %copy-start.5 = (f32[128]{0:T(128)S(1)}, f32[128]{0:T(128)}, u32[]{:S(2)}) copy-start(f32[128]{0:T(128)} %param.13) | copy-start | bytes 1540
  13.3 7.5 %collective-permute-start.2 = (bf16[528,128]{1,0:T(8,128)(2,1)S(1)}, bf16[528,128]{1,0:T(8,128)(2,1)S(1)}, u32[]{:S(2)}, u32[]{:S(2)}) collective-permute-start(bf16[528,128]{1,0:T(8,128)(2,1)S(1)} %get-tuple-element.39), channel_id=1, source_target_pairs={{0,3},{1,2},{2,1},{3,0},{4,7},{5,6},{6,5},{7,4},{8,11},{9,10},{10,... | collective-permute-start | bytes 405512 | tf_op jit(solution)/shard_map/ppermute | solution.py:552
  13.4 9.2 %collective-permute-start.6 = (bf16[528,128]{1,0:T(8,128)(2,1)S(1)}, bf16[528,128]{1,0:T(8,128)(2,1)S(1)}, u32[]{:S(2)}, u32[]{:S(2)}) collective-permute-start(bf16[528,128]{1,0:T(8,128)(2,1)S(1)} %get-tuple-element.54), channel_id=1, source_target_pairs={{0,1},{1,0},{2,3},{3,2},{4,5},{5,4},{6,7},{7,6},{8,9},{9,8},{10,11... | collective-permute-start | bytes 405512 | tf_op jit(solution)/shard_map/ppermute | solution.py:552
  15.3 9.4 %collective-permute-start.7 = (bf16[528,128]{1,0:T(8,128)(2,1)S(1)}, bf16[528,128]{1,0:T(8,128)(2,1)S(1)}, u32[]{:S(2)}, u32[]{:S(2)}) collective-permute-start(bf16[528,128]{1,0:T(8,128)(2,1)S(1)} %get-tuple-element.55), channel_id=1, source_target_pairs={{0,2},{1,3},{2,0},{3,1},{4,6},{5,7},{6,4},{7,5},{8,10},{9,11},{10,... | collective-permute-start | bytes 405512 | tf_op jit(solution)/shard_map/ppermute | solution.py:552
  17.7 7.0 %collective-permute-start.8 = (bf16[528,128]{1,0:T(8,128)(2,1)S(1)}, bf16[528,128]{1,0:T(8,128)(2,1)S(1)}, u32[]{:S(2)}, u32[]{:S(2)}) collective-permute-start(bf16[528,128]{1,0:T(8,128)(2,1)S(1)} %get-tuple-element.56), channel_id=1, source_target_pairs={{0,3},{1,2},{2,1},{3,0},{4,7},{5,6},{6,5},{7,4},{8,11},{9,10},{10,... | collective-permute-start | bytes 405512 | tf_op jit(solution)/shard_map/ppermute | solution.py:552
  26.3 5.4 %collective-permute-start.14 = (f32[8,128]{1,0:T(8,128)S(1)}, f32[8,128]{1,0:T(8,128)S(1)}, u32[]{:S(2)}, u32[]{:S(2)}) collective-permute-start(f32[8,128]{1,0:T(8,128)S(1)} %add.21), channel_id=1, source_target_pairs={{0,3},{1,2},{2,1},{3,0},{4,7},{5,6},{6,5},{7,4},{8,11},{9,10},{10,... | collective-permute-start | bytes 12296 | tf_op jit(solution)/shard_map/ppermute | solution.py:525
  27.7 5.7 %collective-permute-start.13 = (f32[8,128]{1,0:T(8,128)S(1)}, f32[8,128]{1,0:T(8,128)S(1)}, u32[]{:S(2)}, u32[]{:S(2)}) collective-permute-start(f32[8,128]{1,0:T(8,128)S(1)} %add.21), channel_id=1, source_target_pairs={{0,2},{1,3},{2,0},{3,1},{4,6},{5,7},{6,4},{7,5},{8,10},{9,11},{10,... | collective-permute-start | bytes 12296 | tf_op jit(solution)/shard_map/ppermute | solution.py:525
  28.8 4.6 %collective-permute-start.12 = (f32[8,128]{1,0:T(8,128)S(1)}, f32[8,128]{1,0:T(8,128)S(1)}, u32[]{:S(2)}, u32[]{:S(2)}) collective-permute-start(f32[8,128]{1,0:T(8,128)S(1)} %add.21), channel_id=1, source_target_pairs={{0,1},{1,0},{2,3},{3,2},{4,5},{5,4},{6,7},{7,6},{8,9},{9,8},{10,11... | collective-permute-start | bytes 12296 | tf_op jit(solution)/shard_map/ppermute | solution.py:525
  29.9 13.4 %collective-permute-start.9 = (bf16[1024,128]{1,0:T(8,128)(2,1)S(1)}, bf16[1024,128]{1,0:T(8,128)(2,1)S(1)}, u32[]{:S(2)}, u32[]{:S(2)}) collective-permute-start(bf16[1024,128]{1,0:T(8,128)(2,1)S(1)} %get-tuple-element.59), channel_id=1, source_target_pairs={{0,1},{1,0},{2,3},{3,2},{4,5},{5,4},{6,7},{7,6},{8,9},{9,8},{10,11... | collective-permute-start | bytes 786440 | tf_op jit(solution)/shard_map/ppermute | solution.py:588
  30.8 12.4 %collective-permute-start.10 = (bf16[1024,128]{1,0:T(8,128)(2,1)S(1)}, bf16[1024,128]{1,0:T(8,128)(2,1)S(1)}, u32[]{:S(2)}, u32[]{:S(2)}) collective-permute-start(bf16[1024,128]{1,0:T(8,128)(2,1)S(1)} %get-tuple-element.60), channel_id=1, source_target_pairs={{0,2},{1,3},{2,0},{3,1},{4,6},{5,7},{6,4},{7,5},{8,10},{9,11},{10,... | collective-permute-start | bytes 786440 | tf_op jit(solution)/shard_map/ppermute | solution.py:588
  31.8 11.5 %collective-permute-start.11 = (bf16[1024,128]{1,0:T(8,128)(2,1)S(1)}, bf16[1024,128]{1,0:T(8,128)(2,1)S(1)}, u32[]{:S(2)}, u32[]{:S(2)}) collective-permute-start(bf16[1024,128]{1,0:T(8,128)(2,1)S(1)} %get-tuple-element.61), channel_id=1, source_target_pairs={{0,3},{1,2},{2,1},{3,0},{4,7},{5,6},{6,5},{7,4},{8,11},{9,10},{10,... | collective-permute-start | bytes 786440 | tf_op jit(solution)/shard_map/ppermute | solution.py:588
  33.4 1.2 %collective-permute-start.15 = (f32[8,128]{1,0:T(8,128)S(1)}, f32[8,128]{1,0:T(8,128)S(1)}, u32[]{:S(2)}, u32[]{:S(2)}) collective-permute-start(f32[8,128]{1,0:T(8,128)S(1)} %add_add_fusion), channel_id=1, source_target_pairs={{0,4},{4,0},{8,12},{12,8},{16,20},{20,16},{24,28},{28,24},{1,5},{5... | collective-permute-start | bytes 12296 | tf_op jit(solution)/shard_map/ppermute | solution.py:525
  34.6 3.6 %collective-permute-start.16 = (f32[8,128]{1,0:T(8,128)S(1)}, f32[8,128]{1,0:T(8,128)S(1)}, u32[]{:S(2)}, u32[]{:S(2)}) collective-permute-start(f32[8,128]{1,0:T(8,128)S(1)} %add.25), channel_id=1, source_target_pairs={{0,8},{4,12},{8,0},{12,4},{16,24},{20,28},{24,16},{28,20},{1,9},{5... | collective-permute-start | bytes 12296 | tf_op jit(solution)/shard_map/ppermute | solution.py:525
  38.3 4.5 %collective-permute-start.17 = (f32[8,128]{1,0:T(8,128)S(1)}, f32[8,128]{1,0:T(8,128)S(1)}, u32[]{:S(2)}, u32[]{:S(2)}) collective-permute-start(f32[8,128]{1,0:T(8,128)S(1)} %add.26), channel_id=1, source_target_pairs={{0,16},{4,20},{8,24},{12,28},{16,0},{20,4},{24,8},{28,12},{1,17},{... | collective-permute-start | bytes 12296 | tf_op jit(solution)/shard_map/ppermute | solution.py:525

commit v9 on v8

--- a/solution.py
+++ b/solution.py
@@ -362,12 +362,13 @@
 
 def keys_kernel(axis, parts, *rest):
     msgs, table_ref, gains_ref = rest[:parts], rest[parts], rest[parts + 1]
-    kt_ref, k_ref, v_ref, kn_ref, ks_ref = rest[parts + 2 :]
+    kt_ref, k_ref, v_ref, kn_ref, ks_ref, gain_ref = rest[parts + 2 :]
     block = table_ref.shape[3]
     owned = v_ref.shape[1]
     f32, bf16 = jnp.float32, jnp.bfloat16
     me = lax.axis_index(axis)
     gain = gain_columns(gains_ref, 1, 1)
+    gain_ref[0], gain_ref[1] = gain_columns(gains_ref, 0, 1), gain
     for m in range(parts):
         b = me ^ m
         for h in range(owned):
@@ -380,19 +381,19 @@
 def heads_kernel(axis, parts, grp, per, group, back, *rest):
     earlier, rest = rest[: grp * parts], rest[grp * parts :]
     msgs, rest = rest[:parts], rest[parts:]
-    kt_ref, k_ref, v_ref, kn_ref, ks_ref, table_ref, gains_ref = rest[:7]
+    kt_ref, k_ref, v_ref, kn_ref, ks_ref, gain_ref, table_ref = rest[:7]
     rest = rest[7:]
     if grp:
-        id_ref, rest = rest[0], rest[1:]
+        mask_ref, rest = rest[0], rest[1:]
     outs, share_ref, rest = rest[:parts], rest[parts], rest[parts + 1 :]
     if not grp:
-        id_ref, rest = rest[0], rest[1:]
-    qt_ref, g_ref, qn_ref, qs_ref, res_ref = rest
-    block, width = table_ref.shape[3], gains_ref.shape[1]
+        mask_ref, rest = rest[0], rest[1:]
+    qt_ref, g_ref, qn_ref, qs_ref, res_ref, id_ref = rest
+    block, width = table_ref.shape[3], gain_ref.shape[1]
     rows = group * block
     f32, bf16 = jnp.float32, jnp.bfloat16
     me = lax.axis_index(axis)
-    q_gain, k_gain = gain_columns(gains_ref, 0, group), gain_columns(gains_ref, 1, 1)
+    q_gain, k_gain = jnp.concatenate([gain_ref[0]] * group, axis=1), gain_ref[1]
     for m in range(parts):
         b = me ^ m
         if not grp:
@@ -405,17 +406,19 @@
             qt_ref[at], qn_ref[at], qs_ref[at] = y, normed, jnp.broadcast_to(scale, (8, rows))
             g_ref[at] = msgs[m][pl.ds((per + p) * rows, rows), :]
 
-    id_rows = [id_ref[b][0:1, :] for b in range(parts)]
-    id_columns = [jnp.broadcast_to(row, (block, block)).T for row in id_rows]
-    key_at = lax.broadcasted_iota(jnp.int32, (block, block), 0)
-    query_at = lax.broadcasted_iota(jnp.int32, (block, block), 1)
-    causal = jnp.where(key_at <= query_at, 0.0, NEG)
+    if not grp:
+        id_rows = [id_ref[b][0:1, :] for b in range(parts)]
+        id_columns = [jnp.broadcast_to(row, (block, block)).T for row in id_rows]
+        key_at = lax.broadcasted_iota(jnp.int32, (block, block), 0)
+        query_at = lax.broadcasted_iota(jnp.int32, (block, block), 1)
+        causal = jnp.where(key_at <= query_at, 0.0, NEG)
+        for b in range(parts):
+            for j in range(max(0, b - back), b + 1):
+                value = jnp.where(id_columns[j] == id_rows[b], 0.0, NEG)
+                mask_ref[b * (back + 1) + b - j] = value + causal if j == b else value
 
     def bias(key_block, query_block):
-        value = jnp.where(id_columns[key_block] == id_rows[query_block], 0.0, NEG)
-        if key_block == query_block:
-            value = value + causal
-        return jnp.concatenate([value] * group, axis=1)
+        return jnp.concatenate([mask_ref[query_block * (back + 1) + query_block - key_block]] * group, axis=1)
 
     q_total = jnp.zeros((width, rows), f32)
     k_total = jnp.zeros((width, block), f32)
@@ -568,22 +571,23 @@
     keys = call_in(
         functools.partial(keys_kernel, "seq", parts), [vmem] * (parts + 2),
         [((*held, width, block), bf16, vmem), ((*held, block, width), bf16, vmem), ((*held, block, width), bf16, vmem)]
-        + [((*held, width, block), f32, vmem), ((*held, 8, block), f32, vmem)],
+        + [((*held, width, block), f32, vmem), ((*held, 8, block), f32, vmem), ((2, width, block), f32, vmem)],
         [], 1 << 33, *kv_arrived, table, gains,
     )
-    results, shares, ids = [], [], []
+    results, shares, masks = [], [], []
     for grp in range(groups):
-        inputs = [*results, *arrived[grp], *keys, table, gains, *ids]
-        id_shape = ((parts, 8, block), f32, vmem)
+        inputs = [*results, *arrived[grp], *keys, table, *masks]
+        mask_shape = ((parts * (back + 1), block, block), f32, vmem)
         made = call_in(
             functools.partial(heads_kernel, "seq", parts, grp, per, group, back),
             [vmem] * len(inputs),
-            [(((grp + 1) * back_sent[0], width), bf16, vmem)] * parts + [((8, width), f32, vmem)] + [id_shape] * (grp == 0),
+            [(((grp + 1) * back_sent[0], width), bf16, vmem)] * parts + [((8, width), f32, vmem)] + [mask_shape] * (grp == 0),
             [vmem((parts * per, width, rows), bf16), vmem((parts * per, rows, width), bf16)]
-            + [vmem((parts * per, width, rows), f32), vmem((parts * per, 8, rows), f32), vmem((parts, *back_sent), bf16)],
+            + [vmem((parts * per, width, rows), f32), vmem((parts * per, 8, rows), f32), vmem((parts, *back_sent), bf16)]
+            + [vmem((parts, 8, block), f32)],
             1 << 34, *inputs,
         )
-        results, share, ids = made[:parts], made[parts], made[parts + 1 :] or ids
+        results, share, masks = made[:parts], made[parts], made[parts + 1 :] or masks
         shares.append(share)
     go = lambda m: lax.ppermute(results[m], "seq", xor(m, parts))
     total = functools.reduce(jnp.add, shares)

time: 45 us -> 45 us (level)
  no operation moved by 1% of the time
where the time goes in v9:
time: 45 us; the launch traced here: 44.8 us
  starting transfers between devices  23.2 us (52%)
  waiting for transfers between devices  10 us (22%)
  Pallas kernels  7.74 us (17%)
  local copies, waits for them, and re-layouts  2.97 us (7%)
  between operations  0.73 us (2%)
    ppermute x9, starting transfers between devices, by_heads(): lax.ppermute(out[m], 'seq', xor(m, parts))  11.9 us
    ppermute x6, starting transfers between devices, exchange_sum(): lax.ppermute(x, axis, [(i, i ^ m) for i in range(size)])  7.79 us
    pallas_call x6, Pallas kernels, call_in(): pl.pallas_call(kernel, out_shape=[jax.ShapeDtypeStruct(s, t) for s, t, _...  7.74 us
    ppermute x6, waiting for transfers between devices, exchange_sum(): lax.ppermute(x, axis, [(i, i ^ m) for i in range(size)])  5.1 us
    ppermute x9, waiting for transfers between devices, by_heads(): lax.ppermute(out[m], 'seq', xor(m, parts))  4.94 us
    ppermute x3, starting transfers between devices, by_heads(): go = lambda m: lax.ppermute(results[m], 'seq', xor(m, parts))  3.49 us
    unnamed x12, local copies, waits for them, and re-layouts  2.37 us
  transfers between devices with their start and end apart: 18, of which 6 were waited for; matrix products, arithmetic and copies ran while one was open for 2% of the time, Pallas kernels for 7%

profile of v9, /device:TPU:0, one launch (start us, length us, event | category | flops | bytes accessed | tf_op | source)
XLA Modules:
  0.0 44.8 jit_solution(5501475595246427744)
XLA Ops:
  0.6 0.0 copy-start
  0.6 1.3 %shard_map.120 = (bf16[512,128]{1,0:T(8,128)(2,1)S(1)}, bf16[512,128]{1,0:T(8,128)(2,1)S(1)}, bf16[512,128]{1,0:T(8,128)(2,1)S(1)}, bf16[512,128]{1,0:T(8,128)(2,1)S(1)}) custom-call(bf16[1024,128]{1,0:T(8,128)(2,1)} %bitcast.15, bf16[1024,128]{1,0:T(8,128)(2,1)} %bitcast.16), custom_call_target="tpu_custom_call" | custom-call | flops 1048576 | bytes 1048576 | tf_op jit(solution)/shard_map/pallas_call | solution.py:516
  1.9 3.0 %collective-permute-start.3 = (bf16[512,128]{1,0:T(8,128)(2,1)S(1)}, bf16[512,128]{1,0:T(8,128)(2,1)S(1)}, u32[]{:S(2)}, u32[]{:S(2)}) collective-permute-start(bf16[512,128]{1,0:T(8,128)(2,1)S(1)} %get-tuple-element.42), channel_id=1, source_target_pairs={{0,1},{1,0},{2,3},{3,2},{4,5},{5,4},{6,7},{7,6},{8,9},{9,8},{10,11... | collective-permute-start | bytes 393224 | tf_op jit(solution)/shard_map/ppermute | solution.py:555
  4.9 1.5 %collective-permute-start.4 = (bf16[512,128]{1,0:T(8,128)(2,1)S(1)}, bf16[512,128]{1,0:T(8,128)(2,1)S(1)}, u32[]{:S(2)}, u32[]{:S(2)}) collective-permute-start(bf16[512,128]{1,0:T(8,128)(2,1)S(1)} %get-tuple-element.43), channel_id=1, source_target_pairs={{0,2},{1,3},{2,0},{3,1},{4,6},{5,7},{6,4},{7,5},{8,10},{9,11},{10,... | collective-permute-start | bytes 393224 | tf_op jit(solution)/shard_map/ppermute | solution.py:555
  6.5 0.0 collective-permute-start.5
  6.5 0.0 copy-start.2
  6.5 0.0 copy-done
  6.5 0.7 %copy-done.2 = s32[1,128]{1,0:T(1,128)S(1)} copy-done((s32[1,128]{1,0:T(1,128)S(1)}, s32[1,128]{1,0:T(1,128)}, u32[]{:S(2)}) %copy-start.2) | copy-done | bytes 536
  7.1 0.0 copy-start.1
  7.1 1.0 %copy-done.1 = bf16[1,128,16,128]{3,2,1,0:T(8,128)(2,1)S(1)} copy-done((bf16[1,128,16,128]{3,2,1,0:T(8,128)(2,1)S(1)}, bf16[1,128,16,128]{3,2,1,0:T(8,128)(2,1)}, u32[]{:S(2)}) %copy-start.1) | copy-done | bytes 524312
  8.2 0.0 copy-start.3
  8.2 0.8 %shard_map.119 = (bf16[528,128]{1,0:T(8,128)(2,1)S(1)}, bf16[528,128]{1,0:T(8,128)(2,1)S(1)}, bf16[528,128]{1,0:T(8,128)(2,1)S(1)}, bf16[528,128]{1,0:T(8,128)(2...) custom-call(bf16[2048,128]{1,0:T(8,128)(2,1)S(1)} %bitcast.13, ...), custom_call_target="tpu_custom_call" | custom-call | flops 8589934592 | bytes 1048576 | tf_op jit(solution)/shard_map/pallas_call | solution.py:516
  9.0 2.0 %collective-permute-start = (bf16[528,128]{1,0:T(8,128)(2,1)S(1)}, bf16[528,128]{1,0:T(8,128)(2,1)S(1)}, u32[]{:S(2)}, u32[]{:S(2)}) collective-permute-start(bf16[528,128]{1,0:T(8,128)(2,1)S(1)} %get-tuple-element.38), channel_id=1, source_target_pairs={{0,1},{1,0},{2,3},{3,2},{4,5},{5,4},{6,7},{7,6},{8,9},{9,8},{10,11... | collective-permute-start | bytes 405512 | tf_op jit(solution)/shard_map/ppermute | solution.py:555
  11.0 1.5 %collective-permute-start.1 = (bf16[528,128]{1,0:T(8,128)(2,1)S(1)}, bf16[528,128]{1,0:T(8,128)(2,1)S(1)}, u32[]{:S(2)}, u32[]{:S(2)}) collective-permute-start(bf16[528,128]{1,0:T(8,128)(2,1)S(1)} %get-tuple-element.39), channel_id=1, source_target_pairs={{0,2},{1,3},{2,0},{3,1},{4,6},{5,7},{6,4},{7,5},{8,10},{9,11},{10,... | collective-permute-start | bytes 405512 | tf_op jit(solution)/shard_map/ppermute | solution.py:555
  12.5 0.1 pad.2.clone
  12.6 0.0 copy-start.4
  12.6 0.0 copy-start.5
  12.6 0.7 %copy-done.4 = f32[128]{0:T(128)S(1)} copy-done((f32[128]{0:T(128)S(1)}, f32[128]{0:T(128)}, u32[]{:S(2)}) %copy-start.4) | copy-done | bytes 536
  13.2 0.0 copy-done.5
  13.2 0.1 maximum_maximum_fusion.rest_5_
  13.3 0.0 collective-permute-done.3.rest_1_
  13.3 0.0 collective-permute-start.2
  13.4 0.0 collective-permute-done.4.rest_2_
  13.4 1.9 %collective-permute-start.6 = (bf16[528,128]{1,0:T(8,128)(2,1)S(1)}, bf16[528,128]{1,0:T(8,128)(2,1)S(1)}, u32[]{:S(2)}, u32[]{:S(2)}) collective-permute-start(bf16[528,128]{1,0:T(8,128)(2,1)S(1)} %get-tuple-element.56), channel_id=1, source_target_pairs={{0,1},{1,0},{2,3},{3,2},{4,5},{5,4},{6,7},{7,6},{8,9},{9,8},{10,11... | collective-permute-start | bytes 405512 | tf_op jit(solution)/shard_map/ppermute | solution.py:555
  15.3 0.0 collective-permute-done.5.rest_3_
  15.3 1.5 %collective-permute-start.7 = (bf16[528,128]{1,0:T(8,128)(2,1)S(1)}, bf16[528,128]{1,0:T(8,128)(2,1)S(1)}, u32[]{:S(2)}, u32[]{:S(2)}) collective-permute-start(bf16[528,128]{1,0:T(8,128)(2,1)S(1)} %get-tuple-element.57), channel_id=1, source_target_pairs={{0,2},{1,3},{2,0},{3,1},{4,6},{5,7},{6,4},{7,5},{8,10},{9,11},{10,... | collective-permute-start | bytes 405512 | tf_op jit(solution)/shard_map/ppermute | solution.py:555
  16.8 0.0 copy-done.3
  16.8 0.9 %shard_map.121 = (bf16[4,2,128,128]{3,2,1,0:T(8,128)(2,1)S(1)}, bf16[4,2,128,128]{3,2,1,0:T(8,128)(2,1)S(1)}, bf16[4,2,128,128]{3,2,1,0:T(8,128)(2,1)S(1)}, f32[...) custom-call(bf16[512,128]{1,0:T(8,128)(2,1)S(1)} %get-tuple-element.41.rest_0_, ...), custom_call_target="tpu_custom_call" | custom-call | flops 8589934592 | bytes 1048576 | tf_op jit(solution)/shard_map/pallas_call | solution.py:516
  17.7 0.0 collective-permute-done.rest_1_
  17.7 0.3 collective-permute-start.8
  18.1 2.2 %collective-permute-done.1.rest_2_ = bf16[528,128]{1,0:T(8,128)(2,1)S(1)} collective-permute-done((bf16[528,128]{1,0:T(8,128)(2,1)S(1)}, bf16[528,128]{1,0:T(8,128)(2,1)S(1)}, u32[]{:S(2)}, u32[]{:S(2)}) %collective-permute-start.1) | collective-permute-done | bytes 135200 | tf_op jit(solution)/shard_map/ppermute | solution.py:555
  20.3 0.6 %collective-permute-done.2.rest_3_ = bf16[528,128]{1,0:T(8,128)(2,1)S(1)} collective-permute-done((bf16[528,128]{1,0:T(8,128)(2,1)S(1)}, bf16[528,128]{1,0:T(8,128)(2,1)S(1)}, u32[]{:S(2)}, u32[]{:S(2)}) %collective-permute-start.2) | collective-permute-done | bytes 135200 | tf_op jit(solution)/shard_map/ppermute | solution.py:555
  20.8 1.7 %shard_map.122 = (bf16[512,128]{1,0:T(8,128)(2,1)S(1)}, bf16[512,128]{1,0:T(8,128)(2,1)S(1)}, bf16[512,128]{1,0:T(8,128)(2,1)S(1)}, bf16[512,128]{1,0:T(8,128)(2...) custom-call(bf16[528,128]{1,0:T(8,128)(2,1)S(1)} %get-tuple-element.37.rest_0_, ...), custom_call_target="tpu_custom_call" | custom-call | flops 17179869184 | bytes 1048576 | tf_op jit(solution)/shard_map/pallas_call | solution.py:516
  22.5 0.0 collective-permute-done.6.rest_5_
  22.5 2.2 %collective-permute-done.7.rest_6_ = bf16[528,128]{1,0:T(8,128)(2,1)S(1)} collective-permute-done((bf16[528,128]{1,0:T(8,128)(2,1)S(1)}, bf16[528,128]{1,0:T(8,128)(2,1)S(1)}, u32[]{:S(2)}, u32[]{:S(2)}) %collective-permute-start.7) | collective-permute-done | bytes 135200 | tf_op jit(solution)/shard_map/ppermute | solution.py:555
  24.7 0.0 collective-permute-done.8.rest_7_
  24.7 1.6 %shard_map.123 = (bf16[1024,128]{1,0:T(8,128)(2,1)S(1)}, bf16[1024,128]{1,0:T(8,128)(2,1)S(1)}, bf16[1024,128]{1,0:T(8,128)(2,1)S(1)}, bf16[1024,128]{1,0:T(8,128)(2,1)S(1)}, f32[8,128]{1,0:T(8,128)S(1)}) custom-call(bf16[512,128]{1,0:T(8,128)(2,1)S(1)} %get-tuple-element.51.rest_0_, bf16[512,128]{1,0:T(8,128)(2,1)S(1)} %get-tuple-element.52.rest_1_, ...), custom_call_target="tpu_custom_call" | custom-call | flops 17179869184 | bytes 1048576 | tf_op jit(solution)/shard_map/pallas_call | solution.py:516
  26.3 1.4 %collective-permute-start.14 = (f32[8,128]{1,0:T(8,128)S(1)}, f32[8,128]{1,0:T(8,128)S(1)}, u32[]{:S(2)}, u32[]{:S(2)}) collective-permute-start(f32[8,128]{1,0:T(8,128)S(1)} %add.21), channel_id=1, source_target_pairs={{0,3},{1,2},{2,1},{3,0},{4,7},{5,6},{6,5},{7,4},{8,11},{9,10},{10,... | collective-permute-start | bytes 12296 | tf_op jit(solution)/shard_map/ppermute | solution.py:528
  27.7 1.1 %collective-permute-start.13 = (f32[8,128]{1,0:T(8,128)S(1)}, f32[8,128]{1,0:T(8,128)S(1)}, u32[]{:S(2)}, u32[]{:S(2)}) collective-permute-start(f32[8,128]{1,0:T(8,128)S(1)} %add.21), channel_id=1, source_target_pairs={{0,2},{1,3},{2,0},{3,1},{4,6},{5,7},{6,4},{7,5},{8,10},{9,11},{10,... | collective-permute-start | bytes 12296 | tf_op jit(solution)/shard_map/ppermute | solution.py:528
  28.8 1.1 %collective-permute-start.12 = (f32[8,128]{1,0:T(8,128)S(1)}, f32[8,128]{1,0:T(8,128)S(1)}, u32[]{:S(2)}, u32[]{:S(2)}) collective-permute-start(f32[8,128]{1,0:T(8,128)S(1)} %add.21), channel_id=1, source_target_pairs={{0,1},{1,0},{2,3},{3,2},{4,5},{5,4},{6,7},{7,6},{8,9},{9,8},{10,11... | collective-permute-start | bytes 12296 | tf_op jit(solution)/shard_map/ppermute | solution.py:528
  29.9 1.0 %collective-permute-start.9 = (bf16[1024,128]{1,0:T(8,128)(2,1)S(1)}, bf16[1024,128]{1,0:T(8,128)(2,1)S(1)}, u32[]{:S(2)}, u32[]{:S(2)}) collective-permute-start(bf16[1024,128]{1,0:T(8,128)(2,1)S(1)} %get-tuple-element.61), channel_id=1, source_target_pairs={{0,1},{1,0},{2,3},{3,2},{4,5},{5,4},{6,7},{7,6},{8,9},{9,8},{10,11... | collective-permute-start | bytes 786440 | tf_op jit(solution)/shard_map/ppermute | solution.py:592
  30.8 0.9 %collective-permute-start.10 = (bf16[1024,128]{1,0:T(8,128)(2,1)S(1)}, bf16[1024,128]{1,0:T(8,128)(2,1)S(1)}, u32[]{:S(2)}, u32[]{:S(2)}) collective-permute-start(bf16[1024,128]{1,0:T(8,128)(2,1)S(1)} %get-tuple-element.62), channel_id=1, source_target_pairs={{0,2},{1,3},{2,0},{3,1},{4,6},{5,7},{6,4},{7,5},{8,10},{9,11},{10,... | collective-permute-start | bytes 786440 | tf_op jit(solution)/shard_map/ppermute | solution.py:592
  31.7 0.0 collective-permute-done.14
  31.7 1.6 %collective-permute-start.11 = (bf16[1024,128]{1,0:T(8,128)(2,1)S(1)}, bf16[1024,128]{1,0:T(8,128)(2,1)S(1)}, u32[]{:S(2)}, u32[]{:S(2)}) collective-permute-start(bf16[1024,128]{1,0:T(8,128)(2,1)S(1)} %get-tuple-element.63), channel_id=1, source_target_pairs={{0,3},{1,2},{2,1},{3,0},{4,7},{5,6},{6,5},{7,4},{8,11},{9,10},{10,... | collective-permute-start | bytes 786440 | tf_op jit(solution)/shard_map/ppermute | solution.py:592
  33.4 0.0 collective-permute-done.13
  33.4 0.0 collective-permute-done.12
  33.4 0.1 collective-permute-start.15
  33.5 1.2 %collective-permute-done.15 = f32[8,128]{1,0:T(8,128)S(1)} collective-permute-done((f32[8,128]{1,0:T(8,128)S(1)}, f32[8,128]{1,0:T(8,128)S(1)}, u32[]{:S(2)}, u32[]{:S(2)}) %collective-permute-start.15) | collective-permute-done | bytes 4128 | tf_op jit(solution)/shard_map/ppermute | solution.py:528
  34.6 1.6 %collective-permute-start.16 = (f32[8,128]{1,0:T(8,128)S(1)}, f32[8,128]{1,0:T(8,128)S(1)}, u32[]{:S(2)}, u32[]{:S(2)}) collective-permute-start(f32[8,128]{1,0:T(8,128)S(1)} %add.25), channel_id=1, source_target_pairs={{0,8},{4,12},{8,0},{12,4},{16,24},{20,28},{24,16},{28,20},{1,9},{5... | collective-permute-start | bytes 12296 | tf_op jit(solution)/shard_map/ppermute | solution.py:528
  36.2 2.0 %collective-permute-done.16 = f32[8,128]{1,0:T(8,128)S(1)} collective-permute-done((f32[8,128]{1,0:T(8,128)S(1)}, f32[8,128]{1,0:T(8,128)S(1)}, u32[]{:S(2)}, u32[]{:S(2)}) %collective-permute-start.16) | collective-permute-done | bytes 4128 | tf_op jit(solution)/shard_map/ppermute | solution.py:528
  38.2 2.6 %collective-permute-start.17 = (f32[8,128]{1,0:T(8,128)S(1)}, f32[8,128]{1,0:T(8,128)S(1)}, u32[]{:S(2)}, u32[]{:S(2)}) collective-permute-start(f32[8,128]{1,0:T(8,128)S(1)} %add.26), channel_id=1, source_target_pairs={{0,16},{4,20},{8,24},{12,28},{16,0},{20,4},{24,8},{28,12},{1,17},{... | collective-permute-start | bytes 12296 | tf_op jit(solution)/shard_map/ppermute | solution.py:528
  40.8 1.9 %collective-permute-done.17 = f32[8,128]{1,0:T(8,128)S(1)} collective-permute-done((f32[8,128]{1,0:T(8,128)S(1)}, f32[8,128]{1,0:T(8,128)S(1)}, u32[]{:S(2)}, u32[]{:S(2)}) %collective-permute-start.17) | collective-permute-done | bytes 4128 | tf_op jit(solution)/shard_map/ppermute | solution.py:528
  42.8 0.5 %slice_bitcast_fusion = (f32[128]{0:T(128)}, f32[128]{0:T(128)}) fusion(f32[8,128]{1,0:T(8,128)S(1)} %add.27), kind=kLoop, calls=%fused_computation.2 | loop fusion | bytes 2048 | tf_op jit(solution)/shard_map/squeeze | solution.py:605
  43.3 0.0 collective-permute-done.9.rest_1_
  43.3 0.0 collective-permute-done.10.rest_2_
  43.3 0.0 collective-permute-done.11.rest_3_
  43.3 1.5 %shard_map.124 = (bf16[2048,128]{1,0:T(8,128)(2,1)}, bf16[1024,128]{1,0:T(8,128)(2,1)}, bf16[1024,128]{1,0:T(8,128)(2,1)}) custom-call(bf16[1024,128]{1,0:T(8,128)(2,1)S(1)} %get-tuple-element.60.rest_0_, bf16[1024,128]{1,0:T(8,128)(2,1)S(1)} %collective-permute-done.9.rest_1_, bf16[1024,128]{1,0:T(8,128)(2,1)S(1)} %collective-permute-done.10.rest_2_, ...), custom_call_target="tpu_custom_call" | custom-call | flops 1048576 | bytes 1048576 | tf_op jit(solution)/shard_map/pallas_call | solution.py:516
  (6 shorter events, 0.0 us)
Async XLA Ops:
  0.6 5.9 %copy-start = (bf16[1,128,16,128]{3,2,1,0:T(8,128)(2,1)S(1)}, bf16[1,128,16,128]{3,2,1,0:T(8,128)(2,1)}, u32[]{:S(2)}) copy-start(bf16[1,128,16,128]{3,2,1,0:T(8,128)(2,1)} %param.8) | copy-start | bytes 1572868
  1.9 11.4 %collective-permute-start.3 = (bf16[512,128]{1,0:T(8,128)(2,1)S(1)}, bf16[512,128]{1,0:T(8,128)(2,1)S(1)}, u32[]{:S(2)}, u32[]{:S(2)}) collective-permute-start(bf16[512,128]{1,0:T(8,128)(2,1)S(1)} %get-tuple-element.42), channel_id=1, source_target_pairs={{0,1},{1,0},{2,3},{3,2},{4,5},{5,4},{6,7},{7,6},{8,9},{9,8},{10,11... | collective-permute-start | bytes 393224 | tf_op jit(solution)/shard_map/ppermute | solution.py:555
  4.9 8.4 %collective-permute-start.4 = (bf16[512,128]{1,0:T(8,128)(2,1)S(1)}, bf16[512,128]{1,0:T(8,128)(2,1)S(1)}, u32[]{:S(2)}, u32[]{:S(2)}) collective-permute-start(bf16[512,128]{1,0:T(8,128)(2,1)S(1)} %get-tuple-element.43), channel_id=1, source_target_pairs={{0,2},{1,3},{2,0},{3,1},{4,6},{5,7},{6,4},{7,5},{8,10},{9,11},{10,... | collective-permute-start | bytes 393224 | tf_op jit(solution)/shard_map/ppermute | solution.py:555
  6.5 8.8 %collective-permute-start.5 = (bf16[512,128]{1,0:T(8,128)(2,1)S(1)}, bf16[512,128]{1,0:T(8,128)(2,1)S(1)}, u32[]{:S(2)}, u32[]{:S(2)}) collective-permute-start(bf16[512,128]{1,0:T(8,128)(2,1)S(1)} %get-tuple-element.44), channel_id=1, source_target_pairs={{0,3},{1,2},{2,1},{3,0},{4,7},{5,6},{6,5},{7,4},{8,11},{9,10},{10,... | collective-permute-start | bytes 393224 | tf_op jit(solution)/shard_map/ppermute | solution.py:555
  6.5 0.7 %copy-start.2 = (s32[1,128]{1,0:T(1,128)S(1)}, s32[1,128]{1,0:T(1,128)}, u32[]{:S(2)}) copy-start(s32[1,128]{1,0:T(1,128)} %seg_ref.1) | copy-start | bytes 1540
  7.1 1.0 %copy-start.1 = (bf16[1,128,16,128]{3,2,1,0:T(8,128)(2,1)S(1)}, bf16[1,128,16,128]{3,2,1,0:T(8,128)(2,1)}, u32[]{:S(2)}) copy-start(bf16[1,128,16,128]{3,2,1,0:T(8,128)(2,1)} %param.11) | copy-start | bytes 1572868
  8.2 8.6 %copy-start.3 = (f32[4,2,64,128]{3,2,1,0:T(8,128)S(1)}, f32[4,2,64,128]{3,2,1,0:T(8,128)}, u32[]{:S(2)}) copy-start(f32[4,2,64,128]{3,2,1,0:T(8,128)} %constant.4.clone.rest_4_.rest_10_.rest_14_) | copy-start | bytes 786436
  9.0 8.8 %collective-permute-start = (bf16[528,128]{1,0:T(8,128)(2,1)S(1)}, bf16[528,128]{1,0:T(8,128)(2,1)S(1)}, u32[]{:S(2)}, u32[]{:S(2)}) collective-permute-start(bf16[528,128]{1,0:T(8,128)(2,1)S(1)} %get-tuple-element.38), channel_id=1, source_target_pairs={{0,1},{1,0},{2,3},{3,2},{4,5},{5,4},{6,7},{7,6},{8,9},{9,8},{10,11... | collective-permute-start | bytes 405512 | tf_op jit(solution)/shard_map/ppermute | solution.py:555
  11.0 9.3 %collective-permute-start.1 = (bf16[528,128]{1,0:T(8,128)(2,1)S(1)}, bf16[528,128]{1,0:T(8,128)(2,1)S(1)}, u32[]{:S(2)}, u32[]{:S(2)}) collective-permute-start(bf16[528,128]{1,0:T(8,128)(2,1)S(1)} %get-tuple-element.39), channel_id=1, source_target_pairs={{0,2},{1,3},{2,0},{3,1},{4,6},{5,7},{6,4},{7,5},{8,10},{9,11},{10,... | collective-permute-start | bytes 405512 | tf_op jit(solution)/shard_map/ppermute | solution.py:555
  12.6 0.7 %copy-start.4 = (f32[128]{0:T(128)S(1)}, f32[128]{0:T(128)}, u32[]{:S(2)}) copy-start(f32[128]{0:T(128)} %param.14) | copy-start | bytes 1540
  12.6 0.7 %copy-start.5 = (f32[128]{0:T(128)S(1)}, f32[128]{0:T(128)}, u32[]{:S(2)}) copy-start(f32[128]{0:T(128)} %param.13) | copy-start | bytes 1540
  13.3 7.5 %collective-permute-start.2 = (bf16[528,128]{1,0:T(8,128)(2,1)S(1)}, bf16[528,128]{1,0:T(8,128)(2,1)S(1)}, u32[]{:S(2)}, u32[]{:S(2)}) collective-permute-start(bf16[528,128]{1,0:T(8,128)(2,1)S(1)} %get-tuple-element.40), channel_id=1, source_target_pairs={{0,3},{1,2},{2,1},{3,0},{4,7},{5,6},{6,5},{7,4},{8,11},{9,10},{10,... | collective-permute-start | bytes 405512 | tf_op jit(solution)/shard_map/ppermute | solution.py:555
  13.4 9.2 %collective-permute-start.6 = (bf16[528,128]{1,0:T(8,128)(2,1)S(1)}, bf16[528,128]{1,0:T(8,128)(2,1)S(1)}, u32[]{:S(2)}, u32[]{:S(2)}) collective-permute-start(bf16[528,128]{1,0:T(8,128)(2,1)S(1)} %get-tuple-element.56), channel_id=1, source_target_pairs={{0,1},{1,0},{2,3},{3,2},{4,5},{5,4},{6,7},{7,6},{8,9},{9,8},{10,11... | collective-permute-start | bytes 405512 | tf_op jit(solution)/shard_map/ppermute | solution.py:555
  15.3 9.4 %collective-permute-start.7 = (bf16[528,128]{1,0:T(8,128)(2,1)S(1)}, bf16[528,128]{1,0:T(8,128)(2,1)S(1)}, u32[]{:S(2)}, u32[]{:S(2)}) collective-permute-start(bf16[528,128]{1,0:T(8,128)(2,1)S(1)} %get-tuple-element.57), channel_id=1, source_target_pairs={{0,2},{1,3},{2,0},{3,1},{4,6},{5,7},{6,4},{7,5},{8,10},{9,11},{10,... | collective-permute-start | bytes 405512 | tf_op jit(solution)/shard_map/ppermute | solution.py:555
  17.7 6.9 %collective-permute-start.8 = (bf16[528,128]{1,0:T(8,128)(2,1)S(1)}, bf16[528,128]{1,0:T(8,128)(2,1)S(1)}, u32[]{:S(2)}, u32[]{:S(2)}) collective-permute-start(bf16[528,128]{1,0:T(8,128)(2,1)S(1)} %get-tuple-element.58), channel_id=1, source_target_pairs={{0,3},{1,2},{2,1},{3,0},{4,7},{5,6},{6,5},{7,4},{8,11},{9,10},{10,... | collective-permute-start | bytes 405512 | tf_op jit(solution)/shard_map/ppermute | solution.py:555
  26.3 5.4 %collective-permute-start.14 = (f32[8,128]{1,0:T(8,128)S(1)}, f32[8,128]{1,0:T(8,128)S(1)}, u32[]{:S(2)}, u32[]{:S(2)}) collective-permute-start(f32[8,128]{1,0:T(8,128)S(1)} %add.21), channel_id=1, source_target_pairs={{0,3},{1,2},{2,1},{3,0},{4,7},{5,6},{6,5},{7,4},{8,11},{9,10},{10,... | collective-permute-start | bytes 12296 | tf_op jit(solution)/shard_map/ppermute | solution.py:528
  27.7 5.7 %collective-permute-start.13 = (f32[8,128]{1,0:T(8,128)S(1)}, f32[8,128]{1,0:T(8,128)S(1)}, u32[]{:S(2)}, u32[]{:S(2)}) collective-permute-start(f32[8,128]{1,0:T(8,128)S(1)} %add.21), channel_id=1, source_target_pairs={{0,2},{1,3},{2,0},{3,1},{4,6},{5,7},{6,4},{7,5},{8,10},{9,11},{10,... | collective-permute-start | bytes 12296 | tf_op jit(solution)/shard_map/ppermute | solution.py:528
  28.8 4.6 %collective-permute-start.12 = (f32[8,128]{1,0:T(8,128)S(1)}, f32[8,128]{1,0:T(8,128)S(1)}, u32[]{:S(2)}, u32[]{:S(2)}) collective-permute-start(f32[8,128]{1,0:T(8,128)S(1)} %add.21), channel_id=1, source_target_pairs={{0,1},{1,0},{2,3},{3,2},{4,5},{5,4},{6,7},{7,6},{8,9},{9,8},{10,11... | collective-permute-start | bytes 12296 | tf_op jit(solution)/shard_map/ppermute | solution.py:528
  29.9 13.4 %collective-permute-start.9 = (bf16[1024,128]{1,0:T(8,128)(2,1)S(1)}, bf16[1024,128]{1,0:T(8,128)(2,1)S(1)}, u32[]{:S(2)}, u32[]{:S(2)}) collective-permute-start(bf16[1024,128]{1,0:T(8,128)(2,1)S(1)} %get-tuple-element.61), channel_id=1, source_target_pairs={{0,1},{1,0},{2,3},{3,2},{4,5},{5,4},{6,7},{7,6},{8,9},{9,8},{10,11... | collective-permute-start | bytes 786440 | tf_op jit(solution)/shard_map/ppermute | solution.py:592
  30.8 12.4 %collective-permute-start.10 = (bf16[1024,128]{1,0:T(8,128)(2,1)S(1)}, bf16[1024,128]{1,0:T(8,128)(2,1)S(1)}, u32[]{:S(2)}, u32[]{:S(2)}) collective-permute-start(bf16[1024,128]{1,0:T(8,128)(2,1)S(1)} %get-tuple-element.62), channel_id=1, source_target_pairs={{0,2},{1,3},{2,0},{3,1},{4,6},{5,7},{6,4},{7,5},{8,10},{9,11},{10,... | collective-permute-start | bytes 786440 | tf_op jit(solution)/shard_map/ppermute | solution.py:592
  31.7 11.5 %collective-permute-start.11 = (bf16[1024,128]{1,0:T(8,128)(2,1)S(1)}, bf16[1024,128]{1,0:T(8,128)(2,1)S(1)}, u32[]{:S(2)}, u32[]{:S(2)}) collective-permute-start(bf16[1024,128]{1,0:T(8,128)(2,1)S(1)} %get-tuple-element.63), channel_id=1, source_target_pairs={{0,3},{1,2},{2,1},{3,0},{4,7},{5,6},{6,5},{7,4},{8,11},{9,10},{10,... | collective-permute-start | bytes 786440 | tf_op jit(solution)/shard_map/ppermute | solution.py:592
  33.4 1.2 %collective-permute-start.15 = (f32[8,128]{1,0:T(8,128)S(1)}, f32[8,128]{1,0:T(8,128)S(1)}, u32[]{:S(2)}, u32[]{:S(2)}) collective-permute-start(f32[8,128]{1,0:T(8,128)S(1)} %add_add_fusion), channel_id=1, source_target_pairs={{0,4},{4,0},{8,12},{12,8},{16,20},{20,16},{24,28},{28,24},{1,5},{5... | collective-permute-start | bytes 12296 | tf_op jit(solution)/shard_map/ppermute | solution.py:528
  34.6 3.6 %collective-permute-start.16 = (f32[8,128]{1,0:T(8,128)S(1)}, f32[8,128]{1,0:T(8,128)S(1)}, u32[]{:S(2)}, u32[]{:S(2)}) collective-permute-start(f32[8,128]{1,0:T(8,128)S(1)} %add.25), channel_id=1, source_target_pairs={{0,8},{4,12},{8,0},{12,4},{16,24},{20,28},{24,16},{28,20},{1,9},{5... | collective-permute-start | bytes 12296 | tf_op jit(solution)/shard_map/ppermute | solution.py:528
  38.2 4.5 %collective-permute-start.17 = (f32[8,128]{1,0:T(8,128)S(1)}, f32[8,128]{1,0:T(8,128)S(1)}, u32[]{:S(2)}, u32[]{:S(2)}) collective-permute-start(f32[8,128]{1,0:T(8,128)S(1)} %add.26), channel_id=1, source_target_pairs={{0,16},{4,20},{8,24},{12,28},{16,0},{20,4},{24,8},{28,12},{1,17},{... | collective-permute-start | bytes 12296 | tf_op jit(solution)/shard_map/ppermute | solution.py:528

commit v10 on v8

--- a/solution.py
+++ b/solution.py
@@ -587,9 +587,9 @@
         shares.append(share)
     go = lambda m: lax.ppermute(results[m], "seq", xor(m, parts))
     total = functools.reduce(jnp.add, shares)
-    first, second, third = go(1), go(2), go(3)
+    third, first, second = go(3), go(1), go(2)
     total = exchange_sum(total, "seq", parts, 1, 2, 3)
-    total = exchange_sum(exchange_sum(exchange_sum(total, "dp", spans, 1), "dp", spans, 2), "dp", spans, 4)
+    total = exchange_sum(exchange_sum(exchange_sum(total, "dp", spans, 1), "dp", spans, 4), "dp", spans, 2)
     grad_q, grad_k, grad_v = call_in(
         functools.partial(collect_kernel, "seq", parts, groups, heads, kv_heads),
         [vmem] * parts, [(q_shape, bf16, hbm), (k_shape, bf16, hbm), (k_shape, bf16, hbm)],

time: 45 us -> 45 us (level)
  no operation moved by 1% of the time
where the time goes in v10:
time: 45 us; the launch traced here: 44.8 us
  starting transfers between devices  23.2 us (52%)
  waiting for transfers between devices  10.1 us (22%)
  Pallas kernels  7.72 us (17%)
  local copies, waits for them, and re-layouts  2.97 us (7%)
  between operations  0.73 us (2%)
    ppermute x9, starting transfers between devices, by_heads(): lax.ppermute(out[m], 'seq', xor(m, parts))  12 us
    ppermute x6, starting transfers between devices, exchange_sum(): lax.ppermute(x, axis, [(i, i ^ m) for i in range(size)])  7.78 us
    pallas_call x6, Pallas kernels, call_in(): pl.pallas_call(kernel, out_shape=[jax.ShapeDtypeStruct(s, t) for s, t, _...  7.72 us
    ppermute x6, waiting for transfers between devices, exchange_sum(): lax.ppermute(x, axis, [(i, i ^ m) for i in range(size)])  5.11 us
    ppermute x9, waiting for transfers between devices, by_heads(): lax.ppermute(out[m], 'seq', xor(m, parts))  4.93 us
    ppermute x3, starting transfers between devices, by_heads(): go = lambda m: lax.ppermute(results[m], 'seq', xor(m, parts))  3.49 us
    unnamed x12, local copies, waits for them, and re-layouts  2.37 us
  transfers between devices with their start and end apart: 18, of which 6 were waited for; matrix products, arithmetic and copies ran while one was open for 2% of the time, Pallas kernels for 7%

profile of v10, /device:TPU:0, one launch (start us, length us, event | category | flops | bytes accessed | tf_op | source)
XLA Modules:
  0.0 44.8 jit_solution(15311618594006143519)
XLA Ops:
  0.6 0.0 copy-start
  0.6 1.3 %shard_map.120 = (bf16[512,128]{1,0:T(8,128)(2,1)S(1)}, bf16[512,128]{1,0:T(8,128)(2,1)S(1)}, bf16[512,128]{1,0:T(8,128)(2,1)S(1)}, bf16[512,128]{1,0:T(8,128)(2,1)S(1)}) custom-call(bf16[1024,128]{1,0:T(8,128)(2,1)} %bitcast.15, bf16[1024,128]{1,0:T(8,128)(2,1)} %bitcast.16), custom_call_target="tpu_custom_call" | custom-call | flops 1048576 | bytes 1048576 | tf_op jit(solution)/shard_map/pallas_call | solution.py:513
  1.9 3.0 %collective-permute-start.3 = (bf16[512,128]{1,0:T(8,128)(2,1)S(1)}, bf16[512,128]{1,0:T(8,128)(2,1)S(1)}, u32[]{:S(2)}, u32[]{:S(2)}) collective-permute-start(bf16[512,128]{1,0:T(8,128)(2,1)S(1)} %get-tuple-element.41), channel_id=1, source_target_pairs={{0,1},{1,0},{2,3},{3,2},{4,5},{5,4},{6,7},{7,6},{8,9},{9,8},{10,11... | collective-permute-start | bytes 393224 | tf_op jit(solution)/shard_map/ppermute | solution.py:552
  4.9 1.5 %collective-permute-start.4 = (bf16[512,128]{1,0:T(8,128)(2,1)S(1)}, bf16[512,128]{1,0:T(8,128)(2,1)S(1)}, u32[]{:S(2)}, u32[]{:S(2)}) collective-permute-start(bf16[512,128]{1,0:T(8,128)(2,1)S(1)} %get-tuple-element.42), channel_id=1, source_target_pairs={{0,2},{1,3},{2,0},{3,1},{4,6},{5,7},{6,4},{7,5},{8,10},{9,11},{10,... | collective-permute-start | bytes 393224 | tf_op jit(solution)/shard_map/ppermute | solution.py:552
  6.5 0.0 collective-permute-start.5
  6.5 0.0 copy-start.2
  6.5 0.0 copy-done
  6.5 0.7 %copy-done.2 = s32[1,128]{1,0:T(1,128)S(1)} copy-done((s32[1,128]{1,0:T(1,128)S(1)}, s32[1,128]{1,0:T(1,128)}, u32[]{:S(2)}) %copy-start.2) | copy-done | bytes 536
  7.1 0.0 copy-start.1
  7.1 1.0 %copy-done.1 = bf16[1,128,16,128]{3,2,1,0:T(8,128)(2,1)S(1)} copy-done((bf16[1,128,16,128]{3,2,1,0:T(8,128)(2,1)S(1)}, bf16[1,128,16,128]{3,2,1,0:T(8,128)(2,1)}, u32[]{:S(2)}) %copy-start.1) | copy-done | bytes 524312
  8.2 0.0 copy-start.3
  8.2 0.8 %shard_map.119 = (bf16[528,128]{1,0:T(8,128)(2,1)S(1)}, bf16[528,128]{1,0:T(8,128)(2,1)S(1)}, bf16[528,128]{1,0:T(8,128)(2,1)S(1)}, bf16[528,128]{1,0:T(8,128)(2...) custom-call(bf16[2048,128]{1,0:T(8,128)(2,1)S(1)} %bitcast.13, ...), custom_call_target="tpu_custom_call" | custom-call | flops 8589934592 | bytes 1048576 | tf_op jit(solution)/shard_map/pallas_call | solution.py:513
  9.0 2.0 %collective-permute-start = (bf16[528,128]{1,0:T(8,128)(2,1)S(1)}, bf16[528,128]{1,0:T(8,128)(2,1)S(1)}, u32[]{:S(2)}, u32[]{:S(2)}) collective-permute-start(bf16[528,128]{1,0:T(8,128)(2,1)S(1)} %get-tuple-element.37), channel_id=1, source_target_pairs={{0,1},{1,0},{2,3},{3,2},{4,5},{5,4},{6,7},{7,6},{8,9},{9,8},{10,11... | collective-permute-start | bytes 405512 | tf_op jit(solution)/shard_map/ppermute | solution.py:552
  11.0 1.5 %collective-permute-start.1 = (bf16[528,128]{1,0:T(8,128)(2,1)S(1)}, bf16[528,128]{1,0:T(8,128)(2,1)S(1)}, u32[]{:S(2)}, u32[]{:S(2)}) collective-permute-start(bf16[528,128]{1,0:T(8,128)(2,1)S(1)} %get-tuple-element.38), channel_id=1, source_target_pairs={{0,2},{1,3},{2,0},{3,1},{4,6},{5,7},{6,4},{7,5},{8,10},{9,11},{10,... | collective-permute-start | bytes 405512 | tf_op jit(solution)/shard_map/ppermute | solution.py:552
  12.5 0.1 pad.2.clone
  12.6 0.0 copy-start.4
  12.6 0.0 copy-start.5
  12.6 0.7 %copy-done.4 = f32[128]{0:T(128)S(1)} copy-done((f32[128]{0:T(128)S(1)}, f32[128]{0:T(128)}, u32[]{:S(2)}) %copy-start.4) | copy-done | bytes 536
  13.2 0.0 copy-done.5
  13.2 0.1 maximum_maximum_fusion.rest_5_.rest_10_.rest_14_
  13.3 0.0 collective-permute-done.3.rest_1_
  13.3 0.0 collective-permute-start.2
  13.4 0.0 collective-permute-done.4.rest_2_
  13.4 1.9 %collective-permute-start.6 = (bf16[528,128]{1,0:T(8,128)(2,1)S(1)}, bf16[528,128]{1,0:T(8,128)(2,1)S(1)}, u32[]{:S(2)}, u32[]{:S(2)}) collective-permute-start(bf16[528,128]{1,0:T(8,128)(2,1)S(1)} %get-tuple-element.54), channel_id=1, source_target_pairs={{0,1},{1,0},{2,3},{3,2},{4,5},{5,4},{6,7},{7,6},{8,9},{9,8},{10,11... | collective-permute-start | bytes 405512 | tf_op jit(solution)/shard_map/ppermute | solution.py:552
  15.3 0.0 collective-permute-done.5.rest_3_
  15.3 1.5 %collective-permute-start.7 = (bf16[528,128]{1,0:T(8,128)(2,1)S(1)}, bf16[528,128]{1,0:T(8,128)(2,1)S(1)}, u32[]{:S(2)}, u32[]{:S(2)}) collective-permute-start(bf16[528,128]{1,0:T(8,128)(2,1)S(1)} %get-tuple-element.55), channel_id=1, source_target_pairs={{0,2},{1,3},{2,0},{3,1},{4,6},{5,7},{6,4},{7,5},{8,10},{9,11},{10,... | collective-permute-start | bytes 405512 | tf_op jit(solution)/shard_map/ppermute | solution.py:552
  16.8 0.0 copy-done.3
  16.8 0.9 %shard_map.121 = (bf16[4,2,128,128]{3,2,1,0:T(8,128)(2,1)S(1)}, bf16[4,2,128,128]{3,2,1,0:T(8,128)(2,1)S(1)}, bf16[4,2,128,128]{3,2,1,0:T(8,128)(2,1)S(1)}, f32[...) custom-call(bf16[512,128]{1,0:T(8,128)(2,1)S(1)} %get-tuple-element.40.rest_0_, ...), custom_call_target="tpu_custom_call" | custom-call | flops 8589934592 | bytes 1048576 | tf_op jit(solution)/shard_map/pallas_call | solution.py:513
  17.7 0.0 collective-permute-done.rest_1_
  17.7 0.4 collective-permute-start.8
  18.1 2.2 %collective-permute-done.1.rest_2_ = bf16[528,128]{1,0:T(8,128)(2,1)S(1)} collective-permute-done((bf16[528,128]{1,0:T(8,128)(2,1)S(1)}, bf16[528,128]{1,0:T(8,128)(2,1)S(1)}, u32[]{:S(2)}, u32[]{:S(2)}) %collective-permute-start.1) | collective-permute-done | bytes 135200 | tf_op jit(solution)/shard_map/ppermute | solution.py:552
  20.3 0.6 %collective-permute-done.2.rest_3_ = bf16[528,128]{1,0:T(8,128)(2,1)S(1)} collective-permute-done((bf16[528,128]{1,0:T(8,128)(2,1)S(1)}, bf16[528,128]{1,0:T(8,128)(2,1)S(1)}, u32[]{:S(2)}, u32[]{:S(2)}) %collective-permute-start.2) | collective-permute-done | bytes 135200 | tf_op jit(solution)/shard_map/ppermute | solution.py:552
  20.9 1.7 %shard_map.122 = (bf16[512,128]{1,0:T(8,128)(2,1)S(1)}, bf16[512,128]{1,0:T(8,128)(2,1)S(1)}, bf16[512,128]{1,0:T(8,128)(2,1)S(1)}, bf16[512,128]{1,0:T(8,128)(2...) custom-call(bf16[528,128]{1,0:T(8,128)(2,1)S(1)} %get-tuple-element.36.rest_0_, ...), custom_call_target="tpu_custom_call" | custom-call | flops 17179869184 | bytes 1048576 | tf_op jit(solution)/shard_map/pallas_call | solution.py:513
  22.5 0.0 collective-permute-done.6.rest_5_
  22.5 2.2 %collective-permute-done.7.rest_6_ = bf16[528,128]{1,0:T(8,128)(2,1)S(1)} collective-permute-done((bf16[528,128]{1,0:T(8,128)(2,1)S(1)}, bf16[528,128]{1,0:T(8,128)(2,1)S(1)}, u32[]{:S(2)}, u32[]{:S(2)}) %collective-permute-start.7) | collective-permute-done | bytes 135200 | tf_op jit(solution)/shard_map/ppermute | solution.py:552
  24.7 0.0 collective-permute-done.8.rest_7_
  24.7 1.6 %shard_map.123 = (bf16[1024,128]{1,0:T(8,128)(2,1)S(1)}, bf16[1024,128]{1,0:T(8,128)(2,1)S(1)}, bf16[1024,128]{1,0:T(8,128)(2,1)S(1)}, bf16[1024,128]{1,0:T(8,128)(2,1)S(1)}, f32[8,128]{1,0:T(8,128)S(1)}) custom-call(bf16[512,128]{1,0:T(8,128)(2,1)S(1)} %get-tuple-element.49.rest_0_, bf16[512,128]{1,0:T(8,128)(2,1)S(1)} %get-tuple-element.50.rest_1_, ...), custom_call_target="tpu_custom_call" | custom-call | flops 17179869184 | bytes 1048576 | tf_op jit(solution)/shard_map/pallas_call | solution.py:513
  26.3 1.4 %collective-permute-start.14 = (f32[8,128]{1,0:T(8,128)S(1)}, f32[8,128]{1,0:T(8,128)S(1)}, u32[]{:S(2)}, u32[]{:S(2)}) collective-permute-start(f32[8,128]{1,0:T(8,128)S(1)} %add.21), channel_id=1, source_target_pairs={{0,3},{1,2},{2,1},{3,0},{4,7},{5,6},{6,5},{7,4},{8,11},{9,10},{10,... | collective-permute-start | bytes 12296 | tf_op jit(solution)/shard_map/ppermute | solution.py:525
  27.7 1.1 %collective-permute-start.13 = (f32[8,128]{1,0:T(8,128)S(1)}, f32[8,128]{1,0:T(8,128)S(1)}, u32[]{:S(2)}, u32[]{:S(2)}) collective-permute-start(f32[8,128]{1,0:T(8,128)S(1)} %add.21), channel_id=1, source_target_pairs={{0,2},{1,3},{2,0},{3,1},{4,6},{5,7},{6,4},{7,5},{8,10},{9,11},{10,... | collective-permute-start | bytes 12296 | tf_op jit(solution)/shard_map/ppermute | solution.py:525
  28.8 1.1 %collective-permute-start.12 = (f32[8,128]{1,0:T(8,128)S(1)}, f32[8,128]{1,0:T(8,128)S(1)}, u32[]{:S(2)}, u32[]{:S(2)}) collective-permute-start(f32[8,128]{1,0:T(8,128)S(1)} %add.21), channel_id=1, source_target_pairs={{0,1},{1,0},{2,3},{3,2},{4,5},{5,4},{6,7},{7,6},{8,9},{9,8},{10,11... | collective-permute-start | bytes 12296 | tf_op jit(solution)/shard_map/ppermute | solution.py:525
  29.9 0.9 %collective-permute-start.9 = (bf16[1024,128]{1,0:T(8,128)(2,1)S(1)}, bf16[1024,128]{1,0:T(8,128)(2,1)S(1)}, u32[]{:S(2)}, u32[]{:S(2)}) collective-permute-start(bf16[1024,128]{1,0:T(8,128)(2,1)S(1)} %get-tuple-element.59), channel_id=1, source_target_pairs={{0,1},{1,0},{2,3},{3,2},{4,5},{5,4},{6,7},{7,6},{8,9},{9,8},{10,11... | collective-permute-start | bytes 786440 | tf_op jit(solution)/shard_map/ppermute | solution.py:588
  30.8 0.9 %collective-permute-start.10 = (bf16[1024,128]{1,0:T(8,128)(2,1)S(1)}, bf16[1024,128]{1,0:T(8,128)(2,1)S(1)}, u32[]{:S(2)}, u32[]{:S(2)}) collective-permute-start(bf16[1024,128]{1,0:T(8,128)(2,1)S(1)} %get-tuple-element.60), channel_id=1, source_target_pairs={{0,2},{1,3},{2,0},{3,1},{4,6},{5,7},{6,4},{7,5},{8,10},{9,11},{10,... | collective-permute-start | bytes 786440 | tf_op jit(solution)/shard_map/ppermute | solution.py:588
  31.8 0.0 collective-permute-done.14
  31.8 1.6 %collective-permute-start.11 = (bf16[1024,128]{1,0:T(8,128)(2,1)S(1)}, bf16[1024,128]{1,0:T(8,128)(2,1)S(1)}, u32[]{:S(2)}, u32[]{:S(2)}) collective-permute-start(bf16[1024,128]{1,0:T(8,128)(2,1)S(1)} %get-tuple-element.61), channel_id=1, source_target_pairs={{0,3},{1,2},{2,1},{3,0},{4,7},{5,6},{6,5},{7,4},{8,11},{9,10},{10,... | collective-permute-start | bytes 786440 | tf_op jit(solution)/shard_map/ppermute | solution.py:588
  33.4 0.0 collective-permute-done.13
  33.4 0.0 collective-permute-done.12
  33.4 0.1 collective-permute-start.15
  33.5 1.2 %collective-permute-done.15 = f32[8,128]{1,0:T(8,128)S(1)} collective-permute-done((f32[8,128]{1,0:T(8,128)S(1)}, f32[8,128]{1,0:T(8,128)S(1)}, u32[]{:S(2)}, u32[]{:S(2)}) %collective-permute-start.15) | collective-permute-done | bytes 4128 | tf_op jit(solution)/shard_map/ppermute | solution.py:525
  34.6 2.6 %collective-permute-start.16 = (f32[8,128]{1,0:T(8,128)S(1)}, f32[8,128]{1,0:T(8,128)S(1)}, u32[]{:S(2)}, u32[]{:S(2)}) collective-permute-start(f32[8,128]{1,0:T(8,128)S(1)} %add.25), channel_id=1, source_target_pairs={{0,16},{4,20},{8,24},{12,28},{16,0},{20,4},{24,8},{28,12},{1,17},{... | collective-permute-start | bytes 12296 | tf_op jit(solution)/shard_map/ppermute | solution.py:525
  37.2 1.9 %collective-permute-done.16 = f32[8,128]{1,0:T(8,128)S(1)} collective-permute-done((f32[8,128]{1,0:T(8,128)S(1)}, f32[8,128]{1,0:T(8,128)S(1)}, u32[]{:S(2)}, u32[]{:S(2)}) %collective-permute-start.16) | collective-permute-done | bytes 4128 | tf_op jit(solution)/shard_map/ppermute | solution.py:525
  39.1 1.6 %collective-permute-start.17 = (f32[8,128]{1,0:T(8,128)S(1)}, f32[8,128]{1,0:T(8,128)S(1)}, u32[]{:S(2)}, u32[]{:S(2)}) collective-permute-start(f32[8,128]{1,0:T(8,128)S(1)} %add.26), channel_id=1, source_target_pairs={{0,8},{4,12},{8,0},{12,4},{16,24},{20,28},{24,16},{28,20},{1,9},{5... | collective-permute-start | bytes 12296 | tf_op jit(solution)/shard_map/ppermute | solution.py:525
  40.7 2.0 %collective-permute-done.17 = f32[8,128]{1,0:T(8,128)S(1)} collective-permute-done((f32[8,128]{1,0:T(8,128)S(1)}, f32[8,128]{1,0:T(8,128)S(1)}, u32[]{:S(2)}, u32[]{:S(2)}) %collective-permute-start.17) | collective-permute-done | bytes 4128 | tf_op jit(solution)/shard_map/ppermute | solution.py:525
  42.8 0.5 %slice_bitcast_fusion = (f32[128]{0:T(128)}, f32[128]{0:T(128)}) fusion(f32[8,128]{1,0:T(8,128)S(1)} %add.27), kind=kLoop, calls=%fused_computation.2 | loop fusion | bytes 2048 | tf_op jit(solution)/shard_map/squeeze | solution.py:601
  43.3 0.0 collective-permute-done.9.rest_1_
  43.3 0.0 collective-permute-done.10.rest_2_
  43.3 0.0 collective-permute-done.11.rest_3_
  43.3 1.5 %shard_map.124 = (bf16[2048,128]{1,0:T(8,128)(2,1)}, bf16[1024,128]{1,0:T(8,128)(2,1)}, bf16[1024,128]{1,0:T(8,128)(2,1)}) custom-call(bf16[1024,128]{1,0:T(8,128)(2,1)S(1)} %get-tuple-element.58.rest_0_, bf16[1024,128]{1,0:T(8,128)(2,1)S(1)} %collective-permute-done.9.rest_1_, bf16[1024,128]{1,0:T(8,128)(2,1)S(1)} %collective-permute-done.10.rest_2_, ...), custom_call_target="tpu_custom_call" | custom-call | flops 1048576 | bytes 1048576 | tf_op jit(solution)/shard_map/pallas_call | solution.py:513
  (6 shorter events, 0.0 us)
Async XLA Ops:
  0.6 5.9 %copy-start = (bf16[1,128,16,128]{3,2,1,0:T(8,128)(2,1)S(1)}, bf16[1,128,16,128]{3,2,1,0:T(8,128)(2,1)}, u32[]{:S(2)}) copy-start(bf16[1,128,16,128]{3,2,1,0:T(8,128)(2,1)} %param.8) | copy-start | bytes 1572868
  1.9 11.4 %collective-permute-start.3 = (bf16[512,128]{1,0:T(8,128)(2,1)S(1)}, bf16[512,128]{1,0:T(8,128)(2,1)S(1)}, u32[]{:S(2)}, u32[]{:S(2)}) collective-permute-start(bf16[512,128]{1,0:T(8,128)(2,1)S(1)} %get-tuple-element.41), channel_id=1, source_target_pairs={{0,1},{1,0},{2,3},{3,2},{4,5},{5,4},{6,7},{7,6},{8,9},{9,8},{10,11... | collective-permute-start | bytes 393224 | tf_op jit(solution)/shard_map/ppermute | solution.py:552
  4.9 8.4 %collective-permute-start.4 = (bf16[512,128]{1,0:T(8,128)(2,1)S(1)}, bf16[512,128]{1,0:T(8,128)(2,1)S(1)}, u32[]{:S(2)}, u32[]{:S(2)}) collective-permute-start(bf16[512,128]{1,0:T(8,128)(2,1)S(1)} %get-tuple-element.42), channel_id=1, source_target_pairs={{0,2},{1,3},{2,0},{3,1},{4,6},{5,7},{6,4},{7,5},{8,10},{9,11},{10,... | collective-permute-start | bytes 393224 | tf_op jit(solution)/shard_map/ppermute | solution.py:552
  6.5 8.8 %collective-permute-start.5 = (bf16[512,128]{1,0:T(8,128)(2,1)S(1)}, bf16[512,128]{1,0:T(8,128)(2,1)S(1)}, u32[]{:S(2)}, u32[]{:S(2)}) collective-permute-start(bf16[512,128]{1,0:T(8,128)(2,1)S(1)} %get-tuple-element.43), channel_id=1, source_target_pairs={{0,3},{1,2},{2,1},{3,0},{4,7},{5,6},{6,5},{7,4},{8,11},{9,10},{10,... | collective-permute-start | bytes 393224 | tf_op jit(solution)/shard_map/ppermute | solution.py:552
  6.5 0.7 %copy-start.2 = (s32[1,128]{1,0:T(1,128)S(1)}, s32[1,128]{1,0:T(1,128)}, u32[]{:S(2)}) copy-start(s32[1,128]{1,0:T(1,128)} %seg_ref.1) | copy-start | bytes 1540
  7.1 1.0 %copy-start.1 = (bf16[1,128,16,128]{3,2,1,0:T(8,128)(2,1)S(1)}, bf16[1,128,16,128]{3,2,1,0:T(8,128)(2,1)}, u32[]{:S(2)}) copy-start(bf16[1,128,16,128]{3,2,1,0:T(8,128)(2,1)} %param.11) | copy-start | bytes 1572868
  8.2 8.6 %copy-start.3 = (f32[4,2,64,128]{3,2,1,0:T(8,128)S(1)}, f32[4,2,64,128]{3,2,1,0:T(8,128)}, u32[]{:S(2)}) copy-start(f32[4,2,64,128]{3,2,1,0:T(8,128)} %constant.4.clone.rest_4_.rest_9_.rest_13_) | copy-start | bytes 786436
  9.0 8.7 %collective-permute-start = (bf16[528,128]{1,0:T(8,128)(2,1)S(1)}, bf16[528,128]{1,0:T(8,128)(2,1)S(1)}, u32[]{:S(2)}, u32[]{:S(2)}) collective-permute-start(bf16[528,128]{1,0:T(8,128)(2,1)S(1)} %get-tuple-element.37), channel_id=1, source_target_pairs={{0,1},{1,0},{2,3},{3,2},{4,5},{5,4},{6,7},{7,6},{8,9},{9,8},{10,11... | collective-permute-start | bytes 405512 | tf_op jit(solution)/shard_map/ppermute | solution.py:552
  11.0 9.3 %collective-permute-start.1 = (bf16[528,128]{1,0:T(8,128)(2,1)S(1)}, bf16[528,128]{1,0:T(8,128)(2,1)S(1)}, u32[]{:S(2)}, u32[]{:S(2)}) collective-permute-start(bf16[528,128]{1,0:T(8,128)(2,1)S(1)} %get-tuple-element.38), channel_id=1, source_target_pairs={{0,2},{1,3},{2,0},{3,1},{4,6},{5,7},{6,4},{7,5},{8,10},{9,11},{10,... | collective-permute-start | bytes 405512 | tf_op jit(solution)/shard_map/ppermute | solution.py:552
  12.6 0.7 %copy-start.4 = (f32[128]{0:T(128)S(1)}, f32[128]{0:T(128)}, u32[]{:S(2)}) copy-start(f32[128]{0:T(128)} %param.14) | copy-start | bytes 1540
  12.6 0.7 %copy-start.5 = (f32[128]{0:T(128)S(1)}, f32[128]{0:T(128)}, u32[]{:S(2)}) copy-start(f32[128]{0:T(128)} %param.13) | copy-start | bytes 1540
  13.3 7.5 %collective-permute-start.2 = (bf16[528,128]{1,0:T(8,128)(2,1)S(1)}, bf16[528,128]{1,0:T(8,128)(2,1)S(1)}, u32[]{:S(2)}, u32[]{:S(2)}) collective-permute-start(bf16[528,128]{1,0:T(8,128)(2,1)S(1)} %get-tuple-element.39), channel_id=1, source_target_pairs={{0,3},{1,2},{2,1},{3,0},{4,7},{5,6},{6,5},{7,4},{8,11},{9,10},{10,... | collective-permute-start | bytes 405512 | tf_op jit(solution)/shard_map/ppermute | solution.py:552
  13.4 9.2 %collective-permute-start.6 = (bf16[528,128]{1,0:T(8,128)(2,1)S(1)}, bf16[528,128]{1,0:T(8,128)(2,1)S(1)}, u32[]{:S(2)}, u32[]{:S(2)}) collective-permute-start(bf16[528,128]{1,0:T(8,128)(2,1)S(1)} %get-tuple-element.54), channel_id=1, source_target_pairs={{0,1},{1,0},{2,3},{3,2},{4,5},{5,4},{6,7},{7,6},{8,9},{9,8},{10,11... | collective-permute-start | bytes 405512 | tf_op jit(solution)/shard_map/ppermute | solution.py:552
  15.3 9.4 %collective-permute-start.7 = (bf16[528,128]{1,0:T(8,128)(2,1)S(1)}, bf16[528,128]{1,0:T(8,128)(2,1)S(1)}, u32[]{:S(2)}, u32[]{:S(2)}) collective-permute-start(bf16[528,128]{1,0:T(8,128)(2,1)S(1)} %get-tuple-element.55), channel_id=1, source_target_pairs={{0,2},{1,3},{2,0},{3,1},{4,6},{5,7},{6,4},{7,5},{8,10},{9,11},{10,... | collective-permute-start | bytes 405512 | tf_op jit(solution)/shard_map/ppermute | solution.py:552
  17.7 7.0 %collective-permute-start.8 = (bf16[528,128]{1,0:T(8,128)(2,1)S(1)}, bf16[528,128]{1,0:T(8,128)(2,1)S(1)}, u32[]{:S(2)}, u32[]{:S(2)}) collective-permute-start(bf16[528,128]{1,0:T(8,128)(2,1)S(1)} %get-tuple-element.56), channel_id=1, source_target_pairs={{0,3},{1,2},{2,1},{3,0},{4,7},{5,6},{6,5},{7,4},{8,11},{9,10},{10,... | collective-permute-start | bytes 405512 | tf_op jit(solution)/shard_map/ppermute | solution.py:552
  26.3 5.4 %collective-permute-start.14 = (f32[8,128]{1,0:T(8,128)S(1)}, f32[8,128]{1,0:T(8,128)S(1)}, u32[]{:S(2)}, u32[]{:S(2)}) collective-permute-start(f32[8,128]{1,0:T(8,128)S(1)} %add.21), channel_id=1, source_target_pairs={{0,3},{1,2},{2,1},{3,0},{4,7},{5,6},{6,5},{7,4},{8,11},{9,10},{10,... | collective-permute-start | bytes 12296 | tf_op jit(solution)/shard_map/ppermute | solution.py:525
  27.7 5.7 %collective-permute-start.13 = (f32[8,128]{1,0:T(8,128)S(1)}, f32[8,128]{1,0:T(8,128)S(1)}, u32[]{:S(2)}, u32[]{:S(2)}) collective-permute-start(f32[8,128]{1,0:T(8,128)S(1)} %add.21), channel_id=1, source_target_pairs={{0,2},{1,3},{2,0},{3,1},{4,6},{5,7},{6,4},{7,5},{8,10},{9,11},{10,... | collective-permute-start | bytes 12296 | tf_op jit(solution)/shard_map/ppermute | solution.py:525
  28.8 4.6 %collective-permute-start.12 = (f32[8,128]{1,0:T(8,128)S(1)}, f32[8,128]{1,0:T(8,128)S(1)}, u32[]{:S(2)}, u32[]{:S(2)}) collective-permute-start(f32[8,128]{1,0:T(8,128)S(1)} %add.21), channel_id=1, source_target_pairs={{0,1},{1,0},{2,3},{3,2},{4,5},{5,4},{6,7},{7,6},{8,9},{9,8},{10,11... | collective-permute-start | bytes 12296 | tf_op jit(solution)/shard_map/ppermute | solution.py:525
  29.9 13.4 %collective-permute-start.9 = (bf16[1024,128]{1,0:T(8,128)(2,1)S(1)}, bf16[1024,128]{1,0:T(8,128)(2,1)S(1)}, u32[]{:S(2)}, u32[]{:S(2)}) collective-permute-start(bf16[1024,128]{1,0:T(8,128)(2,1)S(1)} %get-tuple-element.59), channel_id=1, source_target_pairs={{0,1},{1,0},{2,3},{3,2},{4,5},{5,4},{6,7},{7,6},{8,9},{9,8},{10,11... | collective-permute-start | bytes 786440 | tf_op jit(solution)/shard_map/ppermute | solution.py:588
  30.8 12.4 %collective-permute-start.10 = (bf16[1024,128]{1,0:T(8,128)(2,1)S(1)}, bf16[1024,128]{1,0:T(8,128)(2,1)S(1)}, u32[]{:S(2)}, u32[]{:S(2)}) collective-permute-start(bf16[1024,128]{1,0:T(8,128)(2,1)S(1)} %get-tuple-element.60), channel_id=1, source_target_pairs={{0,2},{1,3},{2,0},{3,1},{4,6},{5,7},{6,4},{7,5},{8,10},{9,11},{10,... | collective-permute-start | bytes 786440 | tf_op jit(solution)/shard_map/ppermute | solution.py:588
  31.8 11.5 %collective-permute-start.11 = (bf16[1024,128]{1,0:T(8,128)(2,1)S(1)}, bf16[1024,128]{1,0:T(8,128)(2,1)S(1)}, u32[]{:S(2)}, u32[]{:S(2)}) collective-permute-start(bf16[1024,128]{1,0:T(8,128)(2,1)S(1)} %get-tuple-element.61), channel_id=1, source_target_pairs={{0,3},{1,2},{2,1},{3,0},{4,7},{5,6},{6,5},{7,4},{8,11},{9,10},{10,... | collective-permute-start | bytes 786440 | tf_op jit(solution)/shard_map/ppermute | solution.py:588
  33.4 1.2 %collective-permute-start.15 = (f32[8,128]{1,0:T(8,128)S(1)}, f32[8,128]{1,0:T(8,128)S(1)}, u32[]{:S(2)}, u32[]{:S(2)}) collective-permute-start(f32[8,128]{1,0:T(8,128)S(1)} %add_add_fusion), channel_id=1, source_target_pairs={{0,4},{4,0},{8,12},{12,8},{16,20},{20,16},{24,28},{28,24},{1,5},{5... | collective-permute-start | bytes 12296 | tf_op jit(solution)/shard_map/ppermute | solution.py:525
  34.6 4.5 %collective-permute-start.16 = (f32[8,128]{1,0:T(8,128)S(1)}, f32[8,128]{1,0:T(8,128)S(1)}, u32[]{:S(2)}, u32[]{:S(2)}) collective-permute-start(f32[8,128]{1,0:T(8,128)S(1)} %add.25), channel_id=1, source_target_pairs={{0,16},{4,20},{8,24},{12,28},{16,0},{20,4},{24,8},{28,12},{1,17},{... | collective-permute-start | bytes 12296 | tf_op jit(solution)/shard_map/ppermute | solution.py:525
  39.1 3.6 %collective-permute-start.17 = (f32[8,128]{1,0:T(8,128)S(1)}, f32[8,128]{1,0:T(8,128)S(1)}, u32[]{:S(2)}, u32[]{:S(2)}) collective-permute-start(f32[8,128]{1,0:T(8,128)S(1)} %add.26), channel_id=1, source_target_pairs={{0,8},{4,12},{8,0},{12,4},{16,24},{20,28},{24,16},{28,20},{1,9},{5... | collective-permute-start | bytes 12296 | tf_op jit(solution)/shard_map/ppermute | solution.py:525
